TPU v7x, 32 devices: a whole 2x2x4 slice. The times are simulated.
32 devices in a mesh: ctx: 16 (over z, x, core), fsdp: 2 (over y).
Axes of the slice: x: 2, y: 2, z: 4, core: 2. Of those that a mesh axis runs over, the one named last changes fastest.
Arguments:
- queries: bfloat16 [2, 4096, 2048], P(None, 'ctx', 'fsdp'), may hold values from -5.5 to 5.5
- keys_values: bfloat16 [2, 2, 4096, 2048], P(None, None, 'ctx', 'fsdp'), may hold values from -5.5 to 5.5
- block_mask: int32 [64, 32], P('ctx'), may hold values 0 or 1
- out_weight: bfloat16 [2048, 4096], P('fsdp'), may hold values from -3 to 3
Outputs:
- mixed: bfloat16 [2, 4096, 4096], P(None, 'ctx', 'fsdp')
All inputs are finite; a program needn't handle non-finite values. No bound on the sum of `block_mask` on one device may be relied on, other than what follows from the above.
Results may differ from a plain program's by a relative error of at most 0.0058.
Values may be sent and summed in bfloat16 or wider, within the bound.
No kernel may reach another device: no remote copies, remote signals or barrier semaphores. Data moves between devices by JAX's collectives and lax.ppermute only.
A program may use at most 128 MiB of HBM per device.

v0:
```python
import math

import jax
import jax.numpy as jnp
from jax import lax
from jax.sharding import PartitionSpec as P

HD = 128
BLK = 64
WINB = 32


def passed_along(array, axis, by):
    devices = lax.axis_size(axis)
    pairs = [(i, i + by) for i in range(devices) if 0 <= i + by < devices]
    return lax.ppermute(array, axis, pairs)


def block_rules(first_block, query_count, key_start, key_count, mask_rows):
    query_blocks = first_block + jnp.arange(query_count, dtype=jnp.int32)
    key_blocks = key_start + jnp.arange(key_count, dtype=jnp.int32)
    block_gap = query_blocks[:, None] - key_blocks[None, :]
    present = key_blocks[None, :] >= 0
    clean_ok = (block_gap >= 0) & (block_gap < WINB) & present
    offsets = jnp.arange(WINB, dtype=jnp.int32)
    picked = ((block_gap - 1)[:, :, None] == offsets[None, None, :]) & (mask_rows[:, None, :] == 1)
    noisy_ok = jnp.any(picked, axis=2) & present
    own_block = query_blocks[:, None] == query_blocks[None, :]

    def widen(table):
        return jnp.repeat(jnp.repeat(table, BLK, axis=0), BLK, axis=1)

    return (widen(clean_ok), widen(noisy_ok), widen(own_block))


def attend(query, keys, values, allowed):
    count, width = query.shape
    heads = width // HD
    query_three = query.reshape(count, heads, HD)
    key_three = keys.reshape(-1, heads, HD)
    value_three = values.reshape(-1, heads, HD)
    scores = jnp.einsum(
        "qhd,khd->hqk", query_three, key_three, preferred_element_type=jnp.float32
    ) * (1.0 / math.sqrt(HD))
    scores = jnp.where(allowed[None], scores, jnp.float32(-1e30))
    top = jnp.max(scores, axis=-1, keepdims=True)
    expo = jnp.exp(scores - top)
    weights = (expo / jnp.sum(expo, axis=-1, keepdims=True)).astype(jnp.bfloat16)
    result = jnp.einsum("hqk,khd->qhd", weights, value_three, preferred_element_type=jnp.float32)
    return result.reshape(count, width).astype(jnp.bfloat16)


def on_device(queries, keys_values, block_mask, out_weight):
    tokens = queries.shape[1]
    blocks_here = tokens // BLK
    reach = WINB * BLK // tokens
    own = keys_values[:, 0]
    pieces = []
    moving = own
    for step in range(reach):
        moving = passed_along(moving, "ctx", 1)
        pieces.insert(0, moving)
    window = jnp.concatenate(pieces + [own], axis=1)
    first_block = lax.axis_index("ctx") * blocks_here
    clean_ok, noisy_ok, own_ok = block_rules(
        first_block, blocks_here, first_block - WINB, blocks_here + WINB, block_mask
    )
    clean_out = attend(queries[0], window[0], window[1], clean_ok)
    noisy_keys = jnp.concatenate([window[0], keys_values[0, 1]], axis=0)
    noisy_values = jnp.concatenate([window[1], keys_values[1, 1]], axis=0)
    noisy_allowed = jnp.concatenate([noisy_ok, own_ok], axis=1)
    noisy_out = attend(queries[1], noisy_keys, noisy_values, noisy_allowed)
    attended = jnp.stack([clean_out, noisy_out])
    panel = lax.all_to_all(out_weight, "fsdp", split_axis=1, concat_axis=0, tiled=True)
    piece = lax.all_gather(attended, "fsdp", axis=2, tiled=True)
    columns = piece.shape[2]
    mixed = jnp.dot(piece.reshape(-1, columns), panel, preferred_element_type=jnp.float32)
    return mixed.astype(jnp.bfloat16).reshape(2, tokens, panel.shape[1])


def solution(mesh):
    in_specs = (
        P(None, "ctx", "fsdp"),
        P(None, None, "ctx", "fsdp"),
        P("ctx", None),
        P("fsdp", None),
    )
    out_specs = P(None, "ctx", "fsdp")
    return jax.shard_map(
        on_device, mesh=mesh, in_specs=in_specs, out_specs=out_specs, check_vma=False
    )
```

profile of v0, /device:TPU:0, one launch (start us, length us, event | category | flops | bytes accessed | tf_op | source)
XLA Modules:
  0.0 270.3 jit_solution(12736610411490400701)
XLA Ops:
  6.5 1.3 slice.23
  7.8 0.5 copy.65
  8.4 2.4 collective-permute-start
  10.8 2.2 collective-permute-done
  13.0 1.0 copy-done.3
  14.0 14.0 %collective-permute-start.1 = (bf16[2,256,1024]{1,2,0:T(8,128)(2,1)S(1)}, bf16[2,256,1024]{1,2,0:T(8,128)(2,1)S(1)}, u32[]{:S(2)}, u32[]{:S(2)}) collective-permute-start(bf16[2,256,1024]{1,2,0:T(8,128)(2,1)S(1)} %collective-permute-done), channel_id=1, source_target_pairs={{0,2},{2,4},{4,6},{6,8},{8,10},{10,12},{12,14},{14,16},{16,18},{18... | collective-permute-start | bytes 3145736 | tf_op jit(solution)/shard_map/ppermute | solution.py:16
  28.0 2.2 collective-permute-done.1
  30.2 1.0 copy-done.4
  31.2 13.9 %collective-permute-start.2 = (bf16[2,256,1024]{1,2,0:T(8,128)(2,1)S(1)}, bf16[2,256,1024]{1,2,0:T(8,128)(2,1)S(1)}, u32[]{:S(2)}, u32[]{:S(2)}) collective-permute-start(bf16[2,256,1024]{1,2,0:T(8,128)(2,1)S(1)} %collective-permute-done.1), channel_id=1, source_target_pairs={{0,2},{2,4},{4,6},{6,8},{8,10},{10,12},{12,14},{14,16},{16,18},{18... | collective-permute-start | bytes 3145736 | tf_op jit(solution)/shard_map/ppermute | solution.py:16
  45.1 2.2 collective-permute-done.2
  47.3 1.0 copy-done.5
  48.3 13.9 %collective-permute-start.3 = (bf16[2,256,1024]{1,2,0:T(8,128)(2,1)S(1)}, bf16[2,256,1024]{1,2,0:T(8,128)(2,1)S(1)}, u32[]{:S(2)}, u32[]{:S(2)}) collective-permute-start(bf16[2,256,1024]{1,2,0:T(8,128)(2,1)S(1)} %collective-permute-done.2), channel_id=1, source_target_pairs={{0,2},{2,4},{4,6},{6,8},{8,10},{10,12},{12,14},{14,16},{16,18},{18... | collective-permute-start | bytes 3145736 | tf_op jit(solution)/shard_map/ppermute | solution.py:16
  62.2 2.2 collective-permute-done.3
  64.4 1.0 copy-done.7
  65.4 14.8 %collective-permute-start.4 = (bf16[2,256,1024]{1,2,0:T(8,128)(2,1)S(1)}, bf16[2,256,1024]{1,2,0:T(8,128)(2,1)}, u32[]{:S(2)}, u32[]{:S(2)}) collective-permute-start(bf16[2,256,1024]{1,2,0:T(8,128)(2,1)S(1)} %collective-permute-done.3), channel_id=1, source_target_pairs={{0,2},{2,4},{4,6},{6,8},{8,10},{10,12},{12,14},{14,16},{16,18},{18... | collective-permute-start | bytes 3145736 | tf_op jit(solution)/shard_map/ppermute | solution.py:16
  80.2 1.4 collective-permute-done.4
  81.6 14.7 %collective-permute-start.5 = (bf16[2,256,1024]{1,2,0:T(8,128)(2,1)}, bf16[2,256,1024]{1,2,0:T(8,128)(2,1)}, u32[]{:S(2)}, u32[]{:S(2)}) collective-permute-start(bf16[2,256,1024]{1,2,0:T(8,128)(2,1)} %collective-permute-done.4), channel_id=1, source_target_pairs={{0,2},{2,4},{4,6},{6,8},{8,10},{10,12},{12,14},{14,16},{16,18},{18... | collective-permute-start | bytes 3145736 | tf_op jit(solution)/shard_map/ppermute | solution.py:16
  96.3 11.9 %copy.58 = bf16[1024,4096]{0,1:T(8,128)(2,1)} copy(bf16[1024,4096]{1,0:T(8,128)(2,1)} %param.7) | data formatting | bytes 16777216 | tf_op args[3]
  108.3 7.1 %all-to-all-start = ((bf16[1024,2,2048]{0,2,1:T(8,128)(2,1)}), bf16[1024,2,2048]{0,2,1:T(8,128)(2,1)}, u32[]{:S(2)}, u32[]{:S(2)}) async-start(bf16[1024,2,2048]{0,2,1:T(8,128)(2,1)} %bitcast.59), calls=%async_computation | async-start | bytes 16777216 | tf_op jit(solution)/shard_map/all_to_all | solution.py:74
  115.5 4.5 %collective-permute-start.6 = (bf16[2,256,1024]{1,2,0:T(8,128)(2,1)}, bf16[2,256,1024]{1,2,0:T(8,128)(2,1)}, u32[]{:S(2)}, u32[]{:S(2)}) collective-permute-start(bf16[2,256,1024]{1,2,0:T(8,128)(2,1)} %collective-permute-done.5), channel_id=1, source_target_pairs={{0,2},{2,4},{4,6},{6,8},{8,10},{10,12},{12,14},{14,16},{16,18},{18... | collective-permute-start | bytes 3145736 | tf_op jit(solution)/shard_map/ppermute | solution.py:16
  120.6 1.0 collective-permute-done.6
  121.6 15.1 %collective-permute-start.7 = (bf16[2,256,1024]{1,2,0:T(8,128)(2,1)}, bf16[2,256,1024]{1,2,0:T(8,128)(2,1)}, u32[]{:S(2)}, u32[]{:S(2)}) collective-permute-start(bf16[2,256,1024]{1,2,0:T(8,128)(2,1)} %collective-permute-done.6), channel_id=1, source_target_pairs={{0,2},{2,4},{4,6},{6,8},{8,10},{10,12},{12,14},{14,16},{16,18},{18... | collective-permute-start | bytes 3145736 | tf_op jit(solution)/shard_map/ppermute | solution.py:16
  136.6 1.3 fusion.39
  137.9 1.0 copy.66
  139.5 1.0 fusion.38
  140.6 1.2 copy.67
  141.8 1.0 copy.52
  142.8 1.0 copy.68
  143.8 2.0 copy.48
  146.0 1.1 pad_add_fusion
  147.1 1.3 constant_dynamic-update-slice_fusion.8
  148.4 1.3 constant_dynamic-update-slice_fusion.7
  149.7 1.3 constant_dynamic-update-slice_fusion.6
  151.0 1.3 constant_dynamic-update-slice_fusion.5
  152.5 1.3 constant_dynamic-update-slice_fusion.2
  153.8 1.3 constant_dynamic-update-slice_fusion.1
  155.2 4.1 %fusion.37 = (bf16[1,2304,1024]{1,2,0:T(8,128)(2,1)}, bf16[1,2304,1024]{1,2,0:T(8,128)(2,1)}) fusion(bf16[2,2304,1024]{1,2,0:T(8,128)(2,1)S(1)} %constant_dynamic-update-slice_fusion), kind=kLoop, calls=%fused_computation.60 | loop fusion | bytes 18874368 | tf_op jit(solution)/shard_map/slice | solution.py:68
  159.3 6.7 %copy.51 = bf16[2304,8,128]{2,0,1:T(8,128)(2,1)} copy(bf16[2304,8,128]{0,2,1:T(8,128)(2,1)} %bitcast.60) | data formatting | bytes 9437184 | tf_op jit(solution)/shard_map/reshape;squeeze | solution.py:40
  166.1 12.2 %fusion.41 = (f32[8,256]{1,0:T(8,128)S(1)}, f32[8,256,2304]{1,2,0:T(8,128)}) fusion(pred[256,2304]{0,1:T(8,128)(4,1)S(1)} %bitcast.68, bf16[2304,8,128]{0,2,1:T(8,128)(2,1)} %bitcast.61, bf16[256,8,128]{0,2,1:T(8,128)(2,1)S(1)} %bitcast.69), kind=kOutput, calls=%fused_computation.64 | convolution fusion | flops 1226836224 | bytes 24715264 | tf_op jit(solution)/shard_map/sub | solution.py:47
  178.4 9.4 %fusion.20 = bf16[8,128,256]{2,1,0:T(8,128)(2,1)S(1)} fusion(bf16[2304,8,128]{0,2,1:T(8,128)(2,1)} %bitcast.63, f32[8,256,2304]{1,2,0:T(8,128)} %get-tuple-element.16, f32[8,256]{1,0:T(8,128)S(1)} %get-tuple-element.15), kind=kOutput, calls=%fused_computation.27 | convolution fusion | flops 1217658880 | bytes 24125440 | tf_op jit(solution)/shard_map/hqk,khd->qhd/dot_general | solution.py:49
  187.8 0.2 copy.56
  188.0 12.8 %fusion.40 = (f32[8,256]{1,0:T(8,128)S(1)}, f32[8,256,2560]{1,2,0:T(8,128)}) fusion(bf16[256,8,128]{0,2,1:T(8,128)(2,1)S(1)} %bitcast.71, pred[256,2560]{0,1:T(8,128)(4,1)S(1)} %copy-done.9, bf16[256,8,128]{2,0,1:T(8,128)(2,1)S(1)} %copy-done.11, bf16[2304,8,128]{2,0,1:T(8,128)(2,1)} %copy.51), kind=kOutput, calls=%fused_computation.63 | convolution fusion | flops 1373637120 | bytes 27402240 | tf_op jit(solution)/shard_map/sub | solution.py:47
  200.8 10.0 %fusion.21 = bf16[8,128,256]{2,1,0:T(8,128)(2,1)S(1)} fusion(f32[8,256,2560]{1,2,0:T(8,128)} %get-tuple-element.14, f32[8,256]{1,0:T(8,128)S(1)} %get-tuple-element.13, bf16[256,8,128]{0,2,1:T(8,128)(2,1)S(1)} %bitcast.70, bf16[2304,8,128]{0,2,1:T(8,128)(2,1)} %bitcast.64), kind=kOutput, calls=%fused_computation.28 | convolution fusion | flops 1363410944 | bytes 26746880 | tf_op jit(solution)/shard_map/hqk,khd->qhd/dot_general | solution.py:49
  210.8 0.2 copy.57
  211.0 1.1 pad_maximum_fusion.7
  212.1 11.7 %copy.59 = bf16[2,1024,2048]{2,1,0:T(8,128)(2,1)} copy(bf16[2,1024,2048]{1,2,0:T(8,128)(2,1)} %bitcast.18) | data formatting | bytes 16777216 | tf_op jit(solution)/shard_map/all_to_all | solution.py:74
  223.9 29.8 %all-gather.2.cloned.1.call-done = bf16[2,256,2048]{2,1,0:T(8,128)(2,1)} async-done(((bf16[2,256,1024]{2,1,0:T(8,128)(2,1)}), bf16[2,256,2048]{2,1,0:T(8,128)(2,1)}) %all-gather.2.cloned.1.call-update) | async-done | bytes 2097168 | tf_op jit(solution)/shard_map/all_gather | solution.py:75
  253.6 9.8 %convolution_convert_fusion = bf16[512,2048]{1,0:T(8,128)(2,1)} fusion(bf16[512,2048]{1,0:T(8,128)(2,1)} %bitcast.75, bf16[2048,2048]{1,0:T(8,128)(2,1)} %bitcast.62), kind=kOutput, calls=%fused_computation.24 | convolution fusion | flops 4296015872 | bytes 12582912 | tf_op jit(solution)/shard_map/dot_general | solution.py:77
  (53 shorter events, 1.8 us)
Async XLA Ops:
  8.4 99.9 %copy-start = (bf16[2,1,256,1024]{2,3,0,1:T(8,128)(2,1)}, bf16[2,1,256,1024]{2,3,0,1:T(8,128)(2,1)S(1)}, u32[]{:S(2)}) copy-start(bf16[2,1,256,1024]{2,3,0,1:T(8,128)(2,1)S(1)} %copy.65) | copy-start | bytes 3145732
  8.4 4.6 %collective-permute-start = (bf16[2,256,1024]{1,2,0:T(8,128)(2,1)S(1)}, bf16[2,256,1024]{1,2,0:T(8,128)(2,1)S(1)}, u32[]{:S(2)}, u32[]{:S(2)}) collective-permute-start(bf16[2,256,1024]{1,2,0:T(8,128)(2,1)S(1)} %bitcast.65), channel_id=1, source_target_pairs={{0,2},{2,4},{4,6},{6,8},{8,10},{10,12},{12,14},{14,16},{16,18},{18... | collective-permute-start | bytes 3145736 | tf_op jit(solution)/shard_map/ppermute | solution.py:16
  13.0 1.0 copy-start.3
  14.0 16.2 %collective-permute-start.1 = (bf16[2,256,1024]{1,2,0:T(8,128)(2,1)S(1)}, bf16[2,256,1024]{1,2,0:T(8,128)(2,1)S(1)}, u32[]{:S(2)}, u32[]{:S(2)}) collective-permute-start(bf16[2,256,1024]{1,2,0:T(8,128)(2,1)S(1)} %collective-permute-done), channel_id=1, source_target_pairs={{0,2},{2,4},{4,6},{6,8},{8,10},{10,12},{12,14},{14,16},{16,18},{18... | collective-permute-start | bytes 3145736 | tf_op jit(solution)/shard_map/ppermute | solution.py:16
  30.2 1.0 copy-start.4
  31.2 16.1 %collective-permute-start.2 = (bf16[2,256,1024]{1,2,0:T(8,128)(2,1)S(1)}, bf16[2,256,1024]{1,2,0:T(8,128)(2,1)S(1)}, u32[]{:S(2)}, u32[]{:S(2)}) collective-permute-start(bf16[2,256,1024]{1,2,0:T(8,128)(2,1)S(1)} %collective-permute-done.1), channel_id=1, source_target_pairs={{0,2},{2,4},{4,6},{6,8},{8,10},{10,12},{12,14},{14,16},{16,18},{18... | collective-permute-start | bytes 3145736 | tf_op jit(solution)/shard_map/ppermute | solution.py:16
  47.3 1.0 copy-start.5
  48.3 16.1 %collective-permute-start.3 = (bf16[2,256,1024]{1,2,0:T(8,128)(2,1)S(1)}, bf16[2,256,1024]{1,2,0:T(8,128)(2,1)S(1)}, u32[]{:S(2)}, u32[]{:S(2)}) collective-permute-start(bf16[2,256,1024]{1,2,0:T(8,128)(2,1)S(1)} %collective-permute-done.2), channel_id=1, source_target_pairs={{0,2},{2,4},{4,6},{6,8},{8,10},{10,12},{12,14},{14,16},{16,18},{18... | collective-permute-start | bytes 3145736 | tf_op jit(solution)/shard_map/ppermute | solution.py:16
  64.4 1.0 copy-start.7
  65.4 16.2 %collective-permute-start.4 = (bf16[2,256,1024]{1,2,0:T(8,128)(2,1)S(1)}, bf16[2,256,1024]{1,2,0:T(8,128)(2,1)}, u32[]{:S(2)}, u32[]{:S(2)}) collective-permute-start(bf16[2,256,1024]{1,2,0:T(8,128)(2,1)S(1)} %collective-permute-done.3), channel_id=1, source_target_pairs={{0,2},{2,4},{4,6},{6,8},{8,10},{10,12},{12,14},{14,16},{16,18},{18... | collective-permute-start | bytes 3145736 | tf_op jit(solution)/shard_map/ppermute | solution.py:16
  81.6 33.8 %collective-permute-start.5 = (bf16[2,256,1024]{1,2,0:T(8,128)(2,1)}, bf16[2,256,1024]{1,2,0:T(8,128)(2,1)}, u32[]{:S(2)}, u32[]{:S(2)}) collective-permute-start(bf16[2,256,1024]{1,2,0:T(8,128)(2,1)} %collective-permute-done.4), channel_id=1, source_target_pairs={{0,2},{2,4},{4,6},{6,8},{8,10},{10,12},{12,14},{14,16},{16,18},{18... | collective-permute-start | bytes 3145736 | tf_op jit(solution)/shard_map/ppermute | solution.py:16
  108.2 11.7 %copy-start.14 = (s32[4,32]{1,0:T(4,128)S(1)}, s32[4,32]{1,0:T(4,128)}, u32[]{:S(2)}) copy-start(s32[4,32]{1,0:T(4,128)} %param.6) | copy-start | bytes 1540
  108.3 31.3 %copy-start.2 = (bf16[2,2,256,1024]{3,2,1,0:T(8,128)(2,1)S(1)}, bf16[2,2,256,1024]{3,2,1,0:T(8,128)(2,1)}, u32[]{:S(2)}) copy-start(bf16[2,2,256,1024]{3,2,1,0:T(8,128)(2,1)} %param.5) | copy-start | bytes 6291460
  108.3 103.8 %all-to-all-start = ((bf16[1024,2,2048]{0,2,1:T(8,128)(2,1)}), bf16[1024,2,2048]{0,2,1:T(8,128)(2,1)}, u32[]{:S(2)}, u32[]{:S(2)}) async-start(bf16[1024,2,2048]{0,2,1:T(8,128)(2,1)} %bitcast.59), calls=%async_computation | async-start | bytes 16777216 | tf_op jit(solution)/shard_map/all_to_all | solution.py:74
  115.4 138.2 %all-gather.2.cloned.1.call-start = ((), (), s32[]{:S(2)}) async-start(), calls=%async_computation.1 | async-start | bytes 3145728 | tf_op jit(solution)/shard_map/all_gather | solution.py:75
  115.5 6.1 %collective-permute-start.6 = (bf16[2,256,1024]{1,2,0:T(8,128)(2,1)}, bf16[2,256,1024]{1,2,0:T(8,128)(2,1)}, u32[]{:S(2)}, u32[]{:S(2)}) collective-permute-start(bf16[2,256,1024]{1,2,0:T(8,128)(2,1)} %collective-permute-done.5), channel_id=1, source_target_pairs={{0,2},{2,4},{4,6},{6,8},{8,10},{10,12},{12,14},{14,16},{16,18},{18... | collective-permute-start | bytes 3145736 | tf_op jit(solution)/shard_map/ppermute | solution.py:16
  121.6 25.5 %collective-permute-start.7 = (bf16[2,256,1024]{1,2,0:T(8,128)(2,1)}, bf16[2,256,1024]{1,2,0:T(8,128)(2,1)}, u32[]{:S(2)}, u32[]{:S(2)}) collective-permute-start(bf16[2,256,1024]{1,2,0:T(8,128)(2,1)} %collective-permute-done.6), channel_id=1, source_target_pairs={{0,2},{2,4},{4,6},{6,8},{8,10},{10,12},{12,14},{14,16},{16,18},{18... | collective-permute-start | bytes 3145736 | tf_op jit(solution)/shard_map/ppermute | solution.py:16
  145.8 6.5 %copy-start.8 = (bf16[2,256,1024]{1,2,0:T(8,128)(2,1)S(1)}, bf16[2,256,1024]{1,2,0:T(8,128)(2,1)}, u32[]{:S(2)}) copy-start(bf16[2,256,1024]{1,2,0:T(8,128)(2,1)} %copy-done.7) | copy-start | bytes 3145732
  145.8 6.5 %copy-start.6 = (bf16[2,256,1024]{1,2,0:T(8,128)(2,1)S(1)}, bf16[2,256,1024]{1,2,0:T(8,128)(2,1)}, u32[]{:S(2)}) copy-start(bf16[2,256,1024]{1,2,0:T(8,128)(2,1)} %copy-done.5) | copy-start | bytes 3145732
  145.8 9.2 %copy-start.1 = (bf16[2,1,256,1024]{2,3,0,1:T(8,128)(2,1)S(1)}, bf16[2,1,256,1024]{2,3,0,1:T(8,128)(2,1)}, u32[]{:S(2)}) copy-start(bf16[2,1,256,1024]{2,3,0,1:T(8,128)(2,1)} %copy-done) | copy-start | bytes 3145732
  159.3 6.9 %copy-start.10 = (bf16[1,256,1024]{1,2,0:T(8,128)(2,1)S(1)}, bf16[1,256,1024]{1,2,0:T(8,128)(2,1)}, u32[]{:S(2)}) copy-start(bf16[1,256,1024]{1,2,0:T(8,128)(2,1)} %copy.66) | copy-start | bytes 1572868
  178.4 9.6 %copy-start.9 = (pred[256,2560]{0,1:T(8,128)(4,1)S(1)}, pred[256,2560]{0,1:T(8,128)(4,1)}, u32[]{:S(2)}) copy-start(pred[256,2560]{0,1:T(8,128)(4,1)} %pad_add_fusion) | copy-start | bytes 1966084
  178.4 9.6 %copy-start.11 = (bf16[256,8,128]{2,0,1:T(8,128)(2,1)S(1)}, bf16[256,8,128]{2,0,1:T(8,128)(2,1)}, u32[]{:S(2)}) copy-start(bf16[256,8,128]{2,0,1:T(8,128)(2,1)} %copy.52) | copy-start | bytes 1572868
  178.4 9.6 %copy-start.13 = (bf16[1,256,1024]{1,2,0:T(8,128)(2,1)S(1)}, bf16[1,256,1024]{1,2,0:T(8,128)(2,1)}, u32[]{:S(2)}) copy-start(bf16[1,256,1024]{1,2,0:T(8,128)(2,1)} %copy.68) | copy-start | bytes 1572868
  188.0 12.8 %copy-start.12 = (bf16[1,1,256,1024]{2,3,1,0:T(8,128)(2,1)S(1)}, bf16[1,1,256,1024]{2,3,1,0:T(8,128)(2,1)}, u32[]{:S(2)}) copy-start(bf16[1,1,256,1024]{2,3,1,0:T(8,128)(2,1)} %copy.48) | copy-start | bytes 1572868
Sparse Core Ops, SparseCore 0:
  212.2 41.3 all-gather.1
where the time goes:
time: 272 us; the launch traced here: 270 us
  starting transfers between devices  100 us (37%)
  local copies, waits for them, and re-layouts  58.4 us (21%)
  matrix products  54.2 us (20%)
  waiting for transfers between devices  41 us (15%)
  between operations  13.7 us (5%)
    ppermute x8, starting transfers between devices, passed_along(): return lax.ppermute(array, axis, pairs)  93.3 us
    all_gather x1, waiting for transfers between devices, on_device(): piece = lax.all_gather(attended, 'fsdp', axis=2, tiled=True)  29.8 us
    unnamed x43, local copies, waits for them, and re-layouts  27.6 us
    sub x2, matrix products, attend(): expo = jnp.exp(scores - top)  25 us
    dot_general x2, matrix products, attend(): jnp.einsum('hqk,khd->qhd', weights, value_three, preferred_element_type=j...  19.4 us
    all_to_all x1, local copies, waits for them, and re-layouts, on_device(): lax.all_to_all(out_weight, 'fsdp', split_axis=1, concat_axis=0, tiled=True)  11.7 us
    ppermute x8, waiting for transfers between devices, passed_along(): return lax.ppermute(array, axis, pairs)  11.2 us
    dot_general x1, matrix products, on_device(): jnp.dot(piece.reshape(-1, columns), panel, preferred_element_type=jnp.flo...  9.83 us
  transfers between devices with their start and end apart: 10, of which 7 were waited for; matrix products, arithmetic and copies ran while one was open for 37% of the time, Pallas kernels for 0%

commit v1 on v0

v1 whole, which is shorter than its diff:
```python
import math

import jax
import jax.numpy as jnp
from jax import lax
from jax.experimental import pallas as pl
from jax.experimental.pallas import tpu as pltpu
from jax.sharding import PartitionSpec as P

HD = 128
BLK = 64
WINB = 32
MASKED = -1e30
SCALE = math.log2(math.e) / math.sqrt(HD)


def moved(array, n, go):
    pairs = [(i, go(i)) for i in range(n) if go(i) is not None]
    return lax.ppermute(array, "ctx", pairs)


def moved_both(array, n, f, go):
    pairs = [(i * f + k, go(i, k)[0] * f + go(i, k)[1]) for i in range(n) for k in range(f)]
    return lax.ppermute(array, ("ctx", "fsdp"), pairs)


def mask_table(first_block, rows, mask_rows):
    count = WINB + rows
    query = jnp.arange(rows)
    gap = WINB + query[None, :] - jnp.arange(count)[:, None]
    present = (first_block - WINB + jnp.arange(count) >= 0)[:, None]
    clean = (gap >= 0) & (gap < WINB) & present
    offsets = jnp.arange(WINB)
    picked = ((gap - 1)[:, :, None] == offsets[None, None, :]) & (mask_rows[None] == 1)
    noisy = jnp.any(picked, axis=2) & present
    own_clean = jnp.zeros((rows, rows), bool)
    own_noisy = jnp.eye(rows, dtype=bool)
    allowed = jnp.concatenate(
        [jnp.concatenate([clean, noisy], 1), jnp.concatenate([own_clean, own_noisy], 1)], 0
    )
    table = jnp.where(allowed, 0.0, MASKED).astype(jnp.float32)
    return jnp.pad(table, ((0, 0), (0, HD - table.shape[1])))


def attend_kernel(tokens, info, q_here, kn_here, there, own, one, two, swap, extra, table,
                  mine, give, keys, values):
    core, side = info[0], info[1]
    rows = tokens // BLK
    span = WINB * BLK + tokens

    def place(ref, pair):
        for slot in range(2):
            half = core if slot == 0 else 1 - core
            at = pl.multiple_of(pair * 2 * tokens + half * tokens, tokens)
            keys[pl.ds(at, tokens), :] = ref[slot, 0]
            values[pl.ds(at, tokens), :] = ref[slot, 1]

    back = WINB * BLK // (2 * tokens)
    place(two, 0)
    place(extra, jnp.where(side == 0, 1, 3))
    place(one, 2)
    place(swap, jnp.where(side == 0, 3, 1))
    place(own, back)

    spot = lax.broadcasted_iota(jnp.int32, (2 * tokens, HD), 0) // BLK
    lane = lax.broadcasted_iota(jnp.int32, (2 * tokens, HD), 1)
    hot = jnp.where(spot == lane, 1.0, 0.0).astype(jnp.bfloat16)
    contract = (((1,), (1,)), ((), ()))
    for tile in range(2):
        half = core if tile == 0 else 1 - core
        at = pl.multiple_of(half * tokens, tokens)
        if tile == 0:
            query = q_here[...].reshape(2 * tokens, HD)
            key_n, value_n = kn_here[0, 0], kn_here[1, 0]
        else:
            query = there[0:2].reshape(2 * tokens, HD)
            key_n, value_n = there[2], there[3]
        bias = jnp.broadcast_to(
            table[tile][:, None, :], (span // BLK + rows, BLK, HD)
        ).reshape(span + tokens, HD).astype(jnp.bfloat16)
        key = jnp.concatenate([keys[pl.ds(at, span), :], key_n], 0)
        key = jnp.concatenate([key, bias], 1)
        value = jnp.concatenate([values[pl.ds(at, span), :], value_n], 0)
        value = jnp.concatenate([value, jnp.ones_like(value)], 1)
        query = jnp.concatenate([query, hot], 1)
        scores = lax.dot_general(query, key, contract, preferred_element_type=jnp.float32)
        top = jnp.max(scores, axis=1, keepdims=True)
        expo = jnp.exp2((scores - top) * SCALE).astype(jnp.bfloat16)
        total = jnp.dot(expo, value, preferred_element_type=jnp.float32)
        out = (total[:, :HD] / total[:, HD:]).astype(jnp.bfloat16).reshape(2, tokens, HD)
        if tile == 0:
            mine[...] = out
        else:
            give[...] = out


def attend(info, queries, keys_values, there, blocks, table, chunk, heads_chunk, heads_half):
    tokens = queries.shape[1]
    span = WINB * BLK + 2 * tokens

    def col(h, info):
        return info[0] * heads_half + chunk * heads_chunk + h

    pair_spec = pl.BlockSpec((2, 2, tokens, HD), lambda h, info: (0, 0, 0, h))
    out_spec = pl.BlockSpec((2, tokens, HD), lambda h, info: (0, 0, h))
    out = jax.ShapeDtypeStruct((2, tokens, heads_chunk * HD), jnp.bfloat16)
    work = heads_chunk * 2 * 2 * tokens * (WINB * BLK + 2 * tokens)
    return pl.pallas_call(
        lambda *refs: attend_kernel(tokens, *refs),
        grid_spec=pltpu.PrefetchScalarGridSpec(
            num_scalar_prefetch=1,
            grid=(heads_chunk,),
            in_specs=[
                pl.BlockSpec((2, tokens, HD), lambda h, info: (0, 0, col(h, info))),
                pl.BlockSpec((2, 1, tokens, HD), lambda h, info: (0, 1, 0, col(h, info))),
                pl.BlockSpec((4, tokens, HD), lambda h, info: (0, 0, chunk * heads_chunk + h)),
                pair_spec, pair_spec, pair_spec, pair_spec, pair_spec,
                pl.BlockSpec(table.shape, lambda h, info: (0, 0, 0)),
            ],
            out_specs=[out_spec, out_spec],
            scratch_shapes=[
                pltpu.VMEM((span, HD), jnp.bfloat16),
                pltpu.VMEM((span, HD), jnp.bfloat16),
            ],
        ),
        out_shape=[out, out],
        compiler_params=pltpu.CompilerParams(vmem_limit_bytes=48 * 1024 * 1024),
        cost_estimate=pl.CostEstimate(
            flops=work * 4 * 2 * HD, bytes_accessed=4 * 1024 * 1024, transcendentals=work
        ),
    )(info, queries, keys_values, there, *blocks, table)


def project_kernel(pieces, sizes, info, *refs):
    out = refs[-1]
    acts, weights = refs[:pieces], refs[pieces:-1]
    total = None
    place = 0
    for weight, count in zip(weights, sizes):
        row = 0
        for act in acts[place:place + count]:
            wide = act.shape[2]
            part = jnp.dot(
                act[...].reshape(-1, wide), weight[row:row + wide, :],
                preferred_element_type=jnp.float32,
            )
            total = part if total is None else total + part
            row += wide
        place += count
    out[...] = total.astype(jnp.bfloat16).reshape(out.shape)


def project(info, acts, out_weight, others, features):
    tokens = acts[0][0].shape[1]
    half = out_weight.shape[0] // 2
    tile = min(256, features)
    steps = features // tile
    flat = [a for group in acts for a in group]
    weights = [out_weight, out_weight] + others
    specs = [pl.BlockSpec(a.shape, lambda s, info: (0, 0, 0)) for a in flat]
    specs += [
        pl.BlockSpec((half, tile), lambda s, info: (info[0], info[2] * steps + s)),
        pl.BlockSpec((half, tile), lambda s, info: (1 - info[0], info[2] * steps + s)),
    ]
    specs += [pl.BlockSpec((half, tile), lambda s, info: (0, s)) for _ in others]
    sizes = [len(group) for group in acts]
    return pl.pallas_call(
        lambda *refs: project_kernel(len(flat), sizes, *refs),
        grid_spec=pltpu.PrefetchScalarGridSpec(
            num_scalar_prefetch=1,
            grid=(steps,),
            in_specs=specs,
            out_specs=pl.BlockSpec((2, tokens, tile), lambda s, info: (0, 0, s)),
        ),
        out_shape=jax.ShapeDtypeStruct((2, tokens, features), jnp.bfloat16),
        compiler_params=pltpu.CompilerParams(vmem_limit_bytes=32 * 1024 * 1024),
        cost_estimate=pl.CostEstimate(
            flops=2 * 2 * tokens * half * len(weights) * features,
            bytes_accessed=2 * half * len(weights) * features + 8 * tokens * features,
            transcendentals=0,
        ),
    )(info, *flat, *weights)


def on_device(queries, keys_values, block_mask, out_weight):
    tokens = queries.shape[1]
    n, f = lax.axis_size("ctx"), lax.axis_size("fsdp")
    index, place = lax.axis_index("ctx"), lax.axis_index("fsdp")
    core, side = index % 2, (index // 2) % 2
    info = jnp.stack([core, side, place]).astype(jnp.int32)
    width = queries.shape[2] // 2
    heads_half = width // HD
    chunks = 2 if heads_half % 2 == 0 else 1
    heads_chunk = heads_half // chunks
    part = heads_chunk * HD
    rows = tokens // BLK
    features = out_weight.shape[1] // f

    def columns(array, start, size):
        return lax.dynamic_slice_in_dim(array, start, size, array.ndim - 1)

    clean = keys_values[:, 0]
    pair = lambda i: i ^ 1
    got = moved(columns(clean, (1 - core) * width, width), n, pair)
    keep = columns(clean, core * width, width)
    later = jnp.concatenate(
        [columns(queries, (1 - core) * width, width),
         columns(keys_values[:, 1], (1 - core) * width, width)], 0
    )
    there = moved(later, n, pair)
    mask_there = moved(block_mask, n, pair)

    others = []
    for r in range(1, f):
        block = lax.dynamic_slice(
            out_weight, (core * width, ((place + r) % f) * features), (width, features)
        )
        same = moved_both(block, n, f, lambda i, k: (i, (k + r) % f))
        others += [same, moved(same, n, pair)]

    first = index * rows
    sibling = (index ^ 1) * rows
    table = jnp.stack([
        mask_table(first, rows, block_mask), mask_table(sibling, rows, mask_there)
    ])

    ahead = lambda i: i + 4 if i + 4 < n else None
    across = lambda i: i ^ 2
    acts = [[] for _ in range(2 * f)]
    for chunk in range(chunks):
        cut = slice(chunk * part, (chunk + 1) * part)
        own = jnp.stack([keep[:, :, cut], got[:, :, cut]])
        one = moved(own, n, ahead)
        two = moved(one, n, ahead)
        swap = moved(one, n, across)
        extra = moved(jnp.where(side == 0, own, two), n, across)
        mine, give = attend(
            info, queries, keys_values, there, [own, one, two, swap, extra], table,
            chunk, heads_chunk, heads_half,
        )
        acts[0].append(mine)
        acts[1].append(moved(give, n, pair))
        for r in range(1, f):
            acts[2 * r].append(moved_both(mine, n, f, lambda i, k: (i, (k + r) % f)))
            acts[2 * r + 1].append(moved_both(give, n, f, lambda i, k: (i ^ 1, (k + r) % f)))
    return project(info, acts, out_weight, others, features)


def solution(mesh):
    in_specs = (
        P(None, "ctx", "fsdp"),
        P(None, None, "ctx", "fsdp"),
        P("ctx", None),
        P("fsdp", None),
    )
    out_specs = P(None, "ctx", "fsdp")
    return jax.shard_map(
        on_device, mesh=mesh, in_specs=in_specs, out_specs=out_specs, check_vma=False
    )
```

time: 272 us -> 132 us (0.49)
  starting transfers between devices: 100 us -> 31.2 us
  matrix products: 54.2 us -> 0 us
  local copies, waits for them, and re-layouts: 58.4 us -> 11.4 us
  Pallas kernels: 0 us -> 32.2 us
  between operations: 13.7 us -> 0.23 us
  waiting for transfers between devices: 41 us -> 53.1 us
    ppermute x8 -> x19, starting transfers between devices: 93.3 us -> 31.2 us  [the longest x14 24.2 us: moved(): return lax.ppermute(array, 'ctx', pairs)]
    ppermute x8 -> x19, waiting for transfers between devices: 11.2 us -> 53.1 us  [the longest x14 30.7 us: moved(): return lax.ppermute(array, 'ctx', pairs)]
    pallas_call x0 -> x3, Pallas kernels: none -> 32.2 us  [the longest x2 22.7 us: attend(): pl.pallas_call(lambda *refs: attend_kernel(tokens, *refs), grid_spec=pltp...]
    all_gather x1 -> x0, waiting for transfers between devices: 29.8 us -> none  [on_device(): piece = lax.all_gather(attended, 'fsdp', axis=2, tiled=True)]
    dot_general x3 -> x0, matrix products: 29.2 us -> none  [the longest x2 19.4 us: attend(): jnp.einsum('hqk,khd->qhd', weights, value_three, preferred_element_type=j...]
    sub x2 -> x0, matrix products: 25 us -> none  [attend(): expo = jnp.exp(scores - top)]
    unnamed x43 -> x22, local copies, waits for them, and re-layouts: 27.6 us -> 2.94 us
    all_to_all x1 -> x0, local copies, waits for them, and re-layouts: 11.7 us -> none  [on_device(): lax.all_to_all(out_weight, 'fsdp', split_axis=1, concat_axis=0, tiled=True)]
  transfers between devices with their start and end apart: 10 -> 19, of which waited for: 7 -> 8; matrix products, arithmetic and copies ran while one was open for 37% -> 6% of each run, Pallas kernels for 0% -> 17%
where the time goes in v1:
time: 132 us; the launch traced here: 131 us
  waiting for transfers between devices  53.1 us (40%)
  Pallas kernels  32.2 us (24%)
  starting transfers between devices  31.2 us (24%)
  local copies, waits for them, and re-layouts  11.4 us (9%)
  other arithmetic  2.81 us (2%)
    ppermute x14, waiting for transfers between devices, moved(): return lax.ppermute(array, 'ctx', pairs)  30.7 us
    ppermute x14, starting transfers between devices, moved(): return lax.ppermute(array, 'ctx', pairs)  24.2 us
    pallas_call x2, Pallas kernels, attend(): pl.pallas_call(lambda *refs: attend_kernel(tokens, *refs), grid_spec=pltp...  22.7 us
    ppermute x5, waiting for transfers between devices, moved_both(): return lax.ppermute(array, ('ctx', 'fsdp'), pairs)  22.4 us
    pallas_call x1, Pallas kernels, project(): pl.pallas_call(lambda *refs: project_kernel(len(flat), sizes, *refs), gri...  9.48 us
    ppermute x5, starting transfers between devices, moved_both(): return lax.ppermute(array, ('ctx', 'fsdp'), pairs)  6.95 us
    dynamic_slice x1, local copies, waits for them, and re-layouts, on_device(): lax.dynamic_slice(out_weight, (core * width, (place + r) % f * features),...  3.16 us
    unnamed x22, local copies, waits for them, and re-layouts  2.94 us
  transfers between devices with their start and end apart: 19, of which 8 were waited for; matrix products, arithmetic and copies ran while one was open for 6% of the time, Pallas kernels for 17%

profile of v1, /device:TPU:0, one launch (start us, length us, event | category | flops | bytes accessed | tf_op | source)
XLA Modules:
  0.0 130.9 jit_solution(9445713774609042322)
XLA Ops:
  0.0 1.7 %fusion.8 = (bf16[2,1,256,1024]{3,2,1,0:T(8,128)(2,1)S(1)}, bf16[2,1,256,1024]{3,2,1,0:T(8,128)(2,1)S(1)}) fusion(bf16[2,2,256,1024]{3,2,1,0:T(8,128)(2,1)} %refs_2_.3), kind=kLoop, calls=%fused_computation.41 | loop fusion | bytes 4194304 | tf_op jit(solution)/shard_map/slice | solution.py:202
  1.7 1.1 dynamic-slice_bitcast_fusion.1
  2.8 0.5 collective-permute-start.1
  3.4 1.1 pad_maximum_fusion
  4.4 0.4 collective-permute-start
  4.9 0.1 collective-permute-start.6
  5.0 3.2 %dynamic_slice.28 = bf16[512,2048]{1,0:T(8,128)(2,1)} dynamic-slice(bf16[1024,4096]{1,0:T(8,128)(2,1)} %refs_10_.1, s32[]{:T(128)S(6)} %select_n.54, s32[]{:T(128)S(6)} %select_n.61), dynamic_slice_sizes={512,2048} | dynamic-slice | bytes 4194308 | tf_op jit(solution)/shard_map/dynamic_slice | solution.py:215
  8.1 3.0 %collective-permute-start.17 = (bf16[512,2048]{1,0:T(8,128)(2,1)}, bf16[512,2048]{1,0:T(8,128)(2,1)S(1)}, u32[]{:S(2)}, u32[]{:S(2)}) collective-permute-start(bf16[512,2048]{1,0:T(8,128)(2,1)} %dynamic_slice.28), channel_id=1, source_target_pairs={{0,1},{1,0},{2,3},{3,2},{4,5},{5,4},{6,7},{7,6},{8,9},{9,8},{10,11... | collective-permute-start | bytes 6291464 | tf_op jit(solution)/shard_map/ppermute | solution.py:24
  11.1 0.1 pad_add_fusion.2.refs_0_
  11.2 0.1 fusion.4
  11.3 1.1 slice_bitcast_fusion.1
  12.4 1.2 slice_bitcast_fusion
  13.5 0.1 pad_maximum_fusion.2.refs_4_
  13.6 4.3 %collective-permute-start.7 = (bf16[2,2,256,256]{3,2,1,0:T(8,128)(2,1)S(1)}, bf16[2,2,256,256]{3,2,1,0:T(8,128)(2,1)}, u32[]{:S(2)}, u32[]{:S(2)}) collective-permute-start(bf16[2,2,256,256]{3,2,1,0:T(8,128)(2,1)S(1)} %pad_maximum_fusion.2.refs_4_), channel_id=1, source_target_pairs={{0,8},{2,10},{4,12},{6,14},{8,16},{10,18},{12,20},{14,22},{16,24},... | collective-permute-start | bytes 1572872 | tf_op jit(solution)/shard_map/ppermute | solution.py:19
  17.9 0.8 copy-done
  18.7 0.1 fusion.2
  18.9 0.1 pad_maximum_fusion.1.refs_4_
  18.9 3.5 %collective-permute-start.2 = (bf16[2,2,256,256]{3,2,1,0:T(8,128)(2,1)S(1)}, bf16[2,2,256,256]{3,2,1,0:T(8,128)(2,1)}, u32[]{:S(2)}, u32[]{:S(2)}) collective-permute-start(bf16[2,2,256,256]{3,2,1,0:T(8,128)(2,1)S(1)} %pad_maximum_fusion.1.refs_4_), channel_id=1, source_target_pairs={{0,8},{2,10},{4,12},{6,14},{8,16},{10,18},{12,20},{14,22},{16,24},... | collective-permute-start | bytes 1572872 | tf_op jit(solution)/shard_map/ppermute | solution.py:19
  22.4 0.1 broadcast_and_fusion.3
  22.5 6.9 %collective-permute-done.7.refs_5_ = bf16[2,2,256,256]{3,2,1,0:T(8,128)(2,1)} collective-permute-done((bf16[2,2,256,256]{3,2,1,0:T(8,128)(2,1)S(1)}, bf16[2,2,256,256]{3,2,1,0:T(8,128)(2,1)}, u32[]{:S(2)}, u32[]{:S(2)}) %collective-permute-start.7) | collective-permute-done | bytes 524320 | tf_op jit(solution)/shard_map/ppermute | solution.py:19
  29.4 5.3 %collective-permute-start.8 = (bf16[2,2,256,256]{3,2,1,0:T(8,128)(2,1)}, bf16[2,2,256,256]{3,2,1,0:T(8,128)(2,1)}, u32[]{:S(2)}, u32[]{:S(2)}) collective-permute-start(bf16[2,2,256,256]{3,2,1,0:T(8,128)(2,1)} %collective-permute-done.7.refs_5_), channel_id=1, source_target_pairs={{0,8},{2,10},{4,12},{6,14},{8,16},{10,18},{12,20},{14,22},{16,24},... | collective-permute-start | bytes 1572872 | tf_op jit(solution)/shard_map/ppermute | solution.py:19
  34.7 0.1 pad_add_fusion
  34.8 0.1 copy.9
  34.9 0.1 copy.8
  35.0 5.7 %collective-permute-done.2.refs_5_ = bf16[2,2,256,256]{3,2,1,0:T(8,128)(2,1)} collective-permute-done((bf16[2,2,256,256]{3,2,1,0:T(8,128)(2,1)S(1)}, bf16[2,2,256,256]{3,2,1,0:T(8,128)(2,1)}, u32[]{:S(2)}, u32[]{:S(2)}) %collective-permute-start.2) | collective-permute-done | bytes 524320 | tf_op jit(solution)/shard_map/ppermute | solution.py:19
  40.6 4.5 %collective-permute-start.3 = (bf16[2,2,256,256]{3,2,1,0:T(8,128)(2,1)}, bf16[2,2,256,256]{3,2,1,0:T(8,128)(2,1)S(1)}, u32[]{:S(2)}, u32[]{:S(2)}) collective-permute-start(bf16[2,2,256,256]{3,2,1,0:T(8,128)(2,1)} %collective-permute-done.2.refs_5_), channel_id=1, source_target_pairs={{0,8},{2,10},{4,12},{6,14},{8,16},{10,18},{12,20},{14,22},{16,24},... | collective-permute-start | bytes 1572872 | tf_op jit(solution)/shard_map/ppermute | solution.py:19
  45.2 1.6 %collective-permute-start.9 = (bf16[2,2,256,256]{3,2,1,0:T(8,128)(2,1)}, bf16[2,2,256,256]{3,2,1,0:T(8,128)(2,1)S(1)}, u32[]{:S(2)}, u32[]{:S(2)}) collective-permute-start(bf16[2,2,256,256]{3,2,1,0:T(8,128)(2,1)} %collective-permute-done.7.refs_5_), channel_id=1, source_target_pairs={{0,4},{2,6},{4,0},{6,2},{8,12},{10,14},{12,8},{14,10},{16,20},{18,... | collective-permute-start | bytes 1572872 | tf_op jit(solution)/shard_map/ppermute | solution.py:19
  46.7 10.4 %collective-permute-done.17.refs_11_ = bf16[512,2048]{1,0:T(8,128)(2,1)S(1)} collective-permute-done((bf16[512,2048]{1,0:T(8,128)(2,1)}, bf16[512,2048]{1,0:T(8,128)(2,1)S(1)}, u32[]{:S(2)}, u32[]{:S(2)}) %collective-permute-start.17) | collective-permute-done | bytes 2097184 | tf_op jit(solution)/shard_map/ppermute | solution.py:24
  57.1 1.1 broadcast_select_fusion
  58.3 1.9 %collective-permute-start.10 = (bf16[2,2,256,256]{3,2,1,0:T(8,128)(2,1)S(1)}, bf16[2,2,256,256]{3,2,1,0:T(8,128)(2,1)S(1)}, u32[]{:S(2)}, u32[]{:S(2)}) collective-permute-start(bf16[2,2,256,256]{3,2,1,0:T(8,128)(2,1)S(1)} %broadcast_select_fusion), channel_id=1, source_target_pairs={{0,4},{2,6},{4,0},{6,2},{8,12},{10,14},{12,8},{14,10},{16,20},{18,... | collective-permute-start | bytes 1572872 | tf_op jit(solution)/shard_map/ppermute | solution.py:19
  60.2 1.8 %collective-permute-done.3.refs_6_ = bf16[2,2,256,256]{3,2,1,0:T(8,128)(2,1)S(1)} collective-permute-done((bf16[2,2,256,256]{3,2,1,0:T(8,128)(2,1)}, bf16[2,2,256,256]{3,2,1,0:T(8,128)(2,1)S(1)}, u32[]{:S(2)}, u32[]{:S(2)}) %collective-permute-start.3) | collective-permute-done | bytes 524320 | tf_op jit(solution)/shard_map/ppermute | solution.py:19
  62.0 1.5 %collective-permute-start.4 = (bf16[2,2,256,256]{3,2,1,0:T(8,128)(2,1)}, bf16[2,2,256,256]{3,2,1,0:T(8,128)(2,1)S(1)}, u32[]{:S(2)}, u32[]{:S(2)}) collective-permute-start(bf16[2,2,256,256]{3,2,1,0:T(8,128)(2,1)} %collective-permute-done.2.refs_5_), channel_id=1, source_target_pairs={{0,4},{2,6},{4,0},{6,2},{8,12},{10,14},{12,8},{14,10},{16,20},{18,... | collective-permute-start | bytes 1572872 | tf_op jit(solution)/shard_map/ppermute | solution.py:19
  63.5 0.1 broadcast_select_fusion.1
  63.6 0.6 collective-permute-start.5
  64.2 8.9 %collective-permute-done.10.refs_8_ = bf16[2,2,256,256]{3,2,1,0:T(8,128)(2,1)S(1)} collective-permute-done((bf16[2,2,256,256]{3,2,1,0:T(8,128)(2,1)S(1)}, bf16[2,2,256,256]{3,2,1,0:T(8,128)(2,1)S(1)}, u32[]{:S(2)}, u32[]{:S(2)}) %collective-permute-start.10) | collective-permute-done | bytes 524320 | tf_op jit(solution)/shard_map/ppermute | solution.py:19
  73.1 1.0 copy-done.1
  74.2 11.6 %shard_map.47 = (bf16[2,256,256]{2,1,0:T(8,128)(2,1)S(1)}, bf16[2,256,256]{2,1,0:T(8,128)(2,1)}) custom-call(s32[3]{0:T(128)S(1)} %pad_add_fusion.2.refs_0_, bf16[2,256,1024]{2,1,0:T(8,128)(2,1)S(1)} %copy-done.5, bf16[2,2,256,1024]{3,2,1,0:T(8,128)(2,1)} %refs_2_.3, bf16[4,256,512]{2,1,0:T(8,128)(2,1)} %collective-permute-done.refs_3_, ...), custom_call_target="tpu_custom_call" | custom-call | flops 5368709120 | bytes 4194304 | tf_op jit(solution)/shard_map/pallas_call | solution.py:108
  85.8 1.8 %collective-permute-start.16 = (bf16[2,256,256]{2,1,0:T(8,128)(2,1)}, bf16[2,256,256]{2,1,0:T(8,128)(2,1)S(1)}, u32[]{:S(2)}, u32[]{:S(2)}) collective-permute-start(bf16[2,256,256]{2,1,0:T(8,128)(2,1)} %get-tuple-element.12), channel_id=1, source_target_pairs={{0,3},{1,2},{2,1},{3,0},{4,7},{5,6},{6,5},{7,4},{8,11},{9,10},{10,... | collective-permute-start | bytes 786440 | tf_op jit(solution)/shard_map/ppermute | solution.py:24
  87.6 0.4 collective-permute-start.14
  88.0 7.4 %collective-permute-done.5.refs_8_ = bf16[2,2,256,256]{3,2,1,0:T(8,128)(2,1)} collective-permute-done((bf16[2,2,256,256]{3,2,1,0:T(8,128)(2,1)S(1)}, bf16[2,2,256,256]{3,2,1,0:T(8,128)(2,1)}, u32[]{:S(2)}, u32[]{:S(2)}) %collective-permute-start.5) | collective-permute-done | bytes 524320 | tf_op jit(solution)/shard_map/ppermute | solution.py:19
  95.4 1.0 copy-done.3
  96.4 11.0 %shard_map.46 = (bf16[2,256,256]{2,1,0:T(8,128)(2,1)S(1)}, bf16[2,256,256]{2,1,0:T(8,128)(2,1)S(1)}) custom-call(s32[3]{0:T(128)S(1)} %pad_add_fusion.2.refs_0_, bf16[2,256,1024]{2,1,0:T(8,128)(2,1)S(1)} %copy-done.5, bf16[2,2,256,1024]{3,2,1,0:T(8,128)(2,1)} %refs_2_.3, bf16[4,256,512]{2,1,0:T(8,128)(2,1)} %collective-permute-done.refs_3_, ...), custom_call_target="tpu_custom_call" | custom-call | flops 5368709120 | bytes 4194304 | tf_op jit(solution)/shard_map/pallas_call | solution.py:108
  107.5 0.1 collective-permute-start.11
  107.5 1.7 %collective-permute-start.13 = (bf16[2,256,256]{2,1,0:T(8,128)(2,1)S(1)}, bf16[2,256,256]{2,1,0:T(8,128)(2,1)S(1)}, u32[]{:S(2)}, u32[]{:S(2)}) collective-permute-start(bf16[2,256,256]{2,1,0:T(8,128)(2,1)S(1)} %get-tuple-element.9.refs_1_), channel_id=1, source_target_pairs={{0,1},{1,0},{2,3},{3,2},{4,5},{5,4},{6,7},{7,6},{8,9},{9,8},{10,11... | collective-permute-start | bytes 786440 | tf_op jit(solution)/shard_map/ppermute | solution.py:24
  109.2 0.2 collective-permute-start.15
  109.4 7.3 %collective-permute-done.13.refs_5_ = bf16[2,256,256]{2,1,0:T(8,128)(2,1)S(1)} collective-permute-done((bf16[2,256,256]{2,1,0:T(8,128)(2,1)S(1)}, bf16[2,256,256]{2,1,0:T(8,128)(2,1)S(1)}, u32[]{:S(2)}, u32[]{:S(2)}) %collective-permute-start.13) | collective-permute-done | bytes 262176 | tf_op jit(solution)/shard_map/ppermute | solution.py:24
  116.7 4.7 %collective-permute-done.15.refs_7_ = bf16[2,256,256]{2,1,0:T(8,128)(2,1)S(1)} collective-permute-done((bf16[2,256,256]{2,1,0:T(8,128)(2,1)S(1)}, bf16[2,256,256]{2,1,0:T(8,128)(2,1)S(1)}, u32[]{:S(2)}, u32[]{:S(2)}) %collective-permute-start.15) | collective-permute-done | bytes 262176 | tf_op jit(solution)/shard_map/ppermute | solution.py:24
  121.4 9.5 %shard_map.48 = bf16[2,256,2048]{2,1,0:T(8,128)(2,1)} custom-call(s32[3]{0:T(128)S(1)} %pad_add_fusion.2.refs_0_, bf16[2,256,256]{2,1,0:T(8,128)(2,1)S(1)} %get-tuple-element.9.refs_1_, bf16[2,256,256]{2,1,0:T(8,128)(2,1)S(1)} %get-tuple-element.10.refs_2_, bf16[2,256,256]{2,1,0:T(8,128)(2,1)S(1)} %collective-permute-done.11.refs_3_, ...), custom_call_target="tpu_custom_call" | custom-call | flops 4294967296 | bytes 12582912 | tf_op jit(solution)/shard_map/pallas_call | solution.py:167
  (45 shorter events, 0.2 us)
Async XLA Ops:
  1.7 1.6 %copy-start.4 = (bf16[2,256,1024]{2,1,0:T(8,128)(2,1)S(1)}, bf16[2,256,1024]{2,1,0:T(8,128)(2,1)}, u32[]{:S(2)}) copy-start(bf16[2,256,1024]{2,1,0:T(8,128)(2,1)} %refs_1_.3) | copy-start | bytes 3145732
  2.8 9.5 %collective-permute-start.1 = (bf16[2,256,512]{2,1,0:T(8,128)(2,1)}, bf16[2,256,512]{2,1,0:T(8,128)(2,1)}, u32[]{:S(2)}, u32[]{:S(2)}) collective-permute-start(bf16[2,256,512]{2,1,0:T(8,128)(2,1)} %get-tuple-element.18), channel_id=1, source_target_pairs={{0,2},{2,0},{4,6},{6,4},{8,10},{10,8},{12,14},{14,12},{16,18},{18,... | collective-permute-start | bytes 1572872 | tf_op jit(solution)/shard_map/ppermute | solution.py:19
  3.3 1.6 %copy-start.8 = (s32[4,32]{1,0:T(4,128)S(1)}, s32[4,32]{1,0:T(4,128)}, u32[]{:S(2)}) copy-start(s32[4,32]{1,0:T(4,128)} %param.6) | copy-start | bytes 1540
  4.4 59.1 %collective-permute-start = (bf16[4,256,512]{2,1,0:T(8,128)(2,1)}, bf16[4,256,512]{2,1,0:T(8,128)(2,1)}, u32[]{:S(2)}, u32[]{:S(2)}) collective-permute-start(bf16[4,256,512]{2,1,0:T(8,128)(2,1)} %pad_maximum_fusion), channel_id=1, source_target_pairs={{0,2},{2,0},{4,6},{6,4},{8,10},{10,8},{12,14},{14,12},{16,18},{18,... | collective-permute-start | bytes 3145736 | tf_op jit(solution)/shard_map/ppermute | solution.py:19
  4.9 13.8 %collective-permute-start.6 = (s32[4,32]{1,0:T(4,128)S(1)}, s32[4,32]{1,0:T(4,128)S(1)}, u32[]{:S(2)}, u32[]{:S(2)}) collective-permute-start(s32[4,32]{1,0:T(4,128)S(1)} %copy-done.8), channel_id=1, source_target_pairs={{0,2},{2,0},{4,6},{6,4},{8,10},{10,8},{12,14},{14,12},{16,18},{18,... | collective-permute-start | bytes 1544 | tf_op jit(solution)/shard_map/ppermute | solution.py:19
  8.1 49.0 %collective-permute-start.17 = (bf16[512,2048]{1,0:T(8,128)(2,1)}, bf16[512,2048]{1,0:T(8,128)(2,1)S(1)}, u32[]{:S(2)}, u32[]{:S(2)}) collective-permute-start(bf16[512,2048]{1,0:T(8,128)(2,1)} %dynamic_slice.28), channel_id=1, source_target_pairs={{0,1},{1,0},{2,3},{3,2},{4,5},{5,4},{6,7},{7,6},{8,9},{9,8},{10,11... | collective-permute-start | bytes 6291464 | tf_op jit(solution)/shard_map/ppermute | solution.py:24
  12.3 6.5 %copy-start.6 = (bf16[1,2,256,256]{3,2,1,0:T(8,128)(2,1)}, bf16[1,2,256,256]{3,2,1,0:T(8,128)(2,1)S(1)}, u32[]{:S(2)}) copy-start(bf16[1,2,256,256]{3,2,1,0:T(8,128)(2,1)S(1)} %get-tuple-element.19) | copy-start | bytes 786436
  13.5 5.3 %copy-start.7 = (bf16[1,2,256,256]{3,2,1,0:T(8,128)(2,1)}, bf16[1,2,256,256]{3,2,1,0:T(8,128)(2,1)S(1)}, u32[]{:S(2)}) copy-start(bf16[1,2,256,256]{3,2,1,0:T(8,128)(2,1)S(1)} %get-tuple-element.21) | copy-start | bytes 786436
  13.6 15.8 %collective-permute-start.7 = (bf16[2,2,256,256]{3,2,1,0:T(8,128)(2,1)S(1)}, bf16[2,2,256,256]{3,2,1,0:T(8,128)(2,1)}, u32[]{:S(2)}, u32[]{:S(2)}) collective-permute-start(bf16[2,2,256,256]{3,2,1,0:T(8,128)(2,1)S(1)} %pad_maximum_fusion.2.refs_4_), channel_id=1, source_target_pairs={{0,8},{2,10},{4,12},{6,14},{8,16},{10,18},{12,20},{14,22},{16,24},... | collective-permute-start | bytes 1572872 | tf_op jit(solution)/shard_map/ppermute | solution.py:19
  17.9 0.8 copy-start
  18.9 21.7 %collective-permute-start.2 = (bf16[2,2,256,256]{3,2,1,0:T(8,128)(2,1)S(1)}, bf16[2,2,256,256]{3,2,1,0:T(8,128)(2,1)}, u32[]{:S(2)}, u32[]{:S(2)}) collective-permute-start(bf16[2,2,256,256]{3,2,1,0:T(8,128)(2,1)S(1)} %pad_maximum_fusion.1.refs_4_), channel_id=1, source_target_pairs={{0,8},{2,10},{4,12},{6,14},{8,16},{10,18},{12,20},{14,22},{16,24},... | collective-permute-start | bytes 1572872 | tf_op jit(solution)/shard_map/ppermute | solution.py:19
  29.4 27.8 %collective-permute-start.8 = (bf16[2,2,256,256]{3,2,1,0:T(8,128)(2,1)}, bf16[2,2,256,256]{3,2,1,0:T(8,128)(2,1)}, u32[]{:S(2)}, u32[]{:S(2)}) collective-permute-start(bf16[2,2,256,256]{3,2,1,0:T(8,128)(2,1)} %collective-permute-done.7.refs_5_), channel_id=1, source_target_pairs={{0,8},{2,10},{4,12},{6,14},{8,16},{10,18},{12,20},{14,22},{16,24},... | collective-permute-start | bytes 1572872 | tf_op jit(solution)/shard_map/ppermute | solution.py:19
  35.0 38.2 %copy-start.5 = (bf16[2,256,1024]{2,1,0:T(8,128)(2,1)S(1)}, bf16[2,256,1024]{2,1,0:T(8,128)(2,1)}, u32[]{:S(2)}) copy-start(bf16[2,256,1024]{2,1,0:T(8,128)(2,1)} %refs_1_.3) | copy-start | bytes 3145732
  40.6 21.4 %collective-permute-start.3 = (bf16[2,2,256,256]{3,2,1,0:T(8,128)(2,1)}, bf16[2,2,256,256]{3,2,1,0:T(8,128)(2,1)S(1)}, u32[]{:S(2)}, u32[]{:S(2)}) collective-permute-start(bf16[2,2,256,256]{3,2,1,0:T(8,128)(2,1)} %collective-permute-done.2.refs_5_), channel_id=1, source_target_pairs={{0,8},{2,10},{4,12},{6,14},{8,16},{10,18},{12,20},{14,22},{16,24},... | collective-permute-start | bytes 1572872 | tf_op jit(solution)/shard_map/ppermute | solution.py:19
  45.2 19.0 %collective-permute-start.9 = (bf16[2,2,256,256]{3,2,1,0:T(8,128)(2,1)}, bf16[2,2,256,256]{3,2,1,0:T(8,128)(2,1)S(1)}, u32[]{:S(2)}, u32[]{:S(2)}) collective-permute-start(bf16[2,2,256,256]{3,2,1,0:T(8,128)(2,1)} %collective-permute-done.7.refs_5_), channel_id=1, source_target_pairs={{0,4},{2,6},{4,0},{6,2},{8,12},{10,14},{12,8},{14,10},{16,20},{18,... | collective-permute-start | bytes 1572872 | tf_op jit(solution)/shard_map/ppermute | solution.py:19
  57.1 64.3 %collective-permute-start.18 = (bf16[512,2048]{1,0:T(8,128)(2,1)S(1)}, bf16[512,2048]{1,0:T(8,128)(2,1)}, u32[]{:S(2)}, u32[]{:S(2)}) collective-permute-start(bf16[512,2048]{1,0:T(8,128)(2,1)S(1)} %collective-permute-done.17.refs_11_), channel_id=1, source_target_pairs={{0,2},{2,0},{4,6},{6,4},{8,10},{10,8},{12,14},{14,12},{16,18},{18,... | collective-permute-start | bytes 6291464 | tf_op jit(solution)/shard_map/ppermute | solution.py:19
  58.3 14.9 %collective-permute-start.10 = (bf16[2,2,256,256]{3,2,1,0:T(8,128)(2,1)S(1)}, bf16[2,2,256,256]{3,2,1,0:T(8,128)(2,1)S(1)}, u32[]{:S(2)}, u32[]{:S(2)}) collective-permute-start(bf16[2,2,256,256]{3,2,1,0:T(8,128)(2,1)S(1)} %broadcast_select_fusion), channel_id=1, source_target_pairs={{0,4},{2,6},{4,0},{6,2},{8,12},{10,14},{12,8},{14,10},{16,20},{18,... | collective-permute-start | bytes 1572872 | tf_op jit(solution)/shard_map/ppermute | solution.py:19
  62.0 2.2 %copy-start.2 = (bf16[2,2,256,256]{3,2,1,0:T(8,128)(2,1)}, bf16[2,2,256,256]{3,2,1,0:T(8,128)(2,1)S(1)}, u32[]{:S(2)}) copy-start(bf16[2,2,256,256]{3,2,1,0:T(8,128)(2,1)S(1)} %collective-permute-done.3.refs_6_) | copy-start | bytes 1572868
  62.0 25.6 %collective-permute-start.4 = (bf16[2,2,256,256]{3,2,1,0:T(8,128)(2,1)}, bf16[2,2,256,256]{3,2,1,0:T(8,128)(2,1)S(1)}, u32[]{:S(2)}, u32[]{:S(2)}) collective-permute-start(bf16[2,2,256,256]{3,2,1,0:T(8,128)(2,1)} %collective-permute-done.2.refs_5_), channel_id=1, source_target_pairs={{0,4},{2,6},{4,0},{6,2},{8,12},{10,14},{12,8},{14,10},{16,20},{18,... | collective-permute-start | bytes 1572872 | tf_op jit(solution)/shard_map/ppermute | solution.py:19
  63.6 31.8 %collective-permute-start.5 = (bf16[2,2,256,256]{3,2,1,0:T(8,128)(2,1)S(1)}, bf16[2,2,256,256]{3,2,1,0:T(8,128)(2,1)}, u32[]{:S(2)}, u32[]{:S(2)}) collective-permute-start(bf16[2,2,256,256]{3,2,1,0:T(8,128)(2,1)S(1)} %broadcast_select_fusion.1), channel_id=1, source_target_pairs={{0,4},{2,6},{4,0},{6,2},{8,12},{10,14},{12,8},{14,10},{16,20},{18,... | collective-permute-start | bytes 1572872 | tf_op jit(solution)/shard_map/ppermute | solution.py:19
  73.1 1.0 copy-start.1
  85.8 21.7 %collective-permute-start.12 = (bf16[2,256,256]{2,1,0:T(8,128)(2,1)}, bf16[2,256,256]{2,1,0:T(8,128)(2,1)S(1)}, u32[]{:S(2)}, u32[]{:S(2)}) collective-permute-start(bf16[2,256,256]{2,1,0:T(8,128)(2,1)} %get-tuple-element.12), channel_id=1, source_target_pairs={{0,2},{2,0},{4,6},{6,4},{8,10},{10,8},{12,14},{14,12},{16,18},{18,... | collective-permute-start | bytes 786440 | tf_op jit(solution)/shard_map/ppermute | solution.py:19
  85.8 23.6 %collective-permute-start.16 = (bf16[2,256,256]{2,1,0:T(8,128)(2,1)}, bf16[2,256,256]{2,1,0:T(8,128)(2,1)S(1)}, u32[]{:S(2)}, u32[]{:S(2)}) collective-permute-start(bf16[2,256,256]{2,1,0:T(8,128)(2,1)} %get-tuple-element.12), channel_id=1, source_target_pairs={{0,3},{1,2},{2,1},{3,0},{4,7},{5,6},{6,5},{7,4},{8,11},{9,10},{10,... | collective-permute-start | bytes 786440 | tf_op jit(solution)/shard_map/ppermute | solution.py:24
  87.6 33.8 %slice-start = ((s8[8388608]{0:T(1024)(128)(4,1)}), s8[4194304]{0:T(1024)(128)(4,1)S(1)}, s32[]{:S(2)}) async-start(s8[8388608]{0:T(1024)(128)(4,1)} %bitcast.21), calls=%async_computation | async-start | bytes 8388608
  87.6 33.8 %slice-start.1 = ((s8[8388608]{0:T(1024)(128)(4,1)}), s8[4194304]{0:T(1024)(128)(4,1)S(1)}, s32[]{:S(2)}) async-start(s8[8388608]{0:T(1024)(128)(4,1)} %bitcast.21), calls=%async_computation.1 | async-start | bytes 8388608
  87.6 21.6 %collective-permute-start.14 = (bf16[2,256,256]{2,1,0:T(8,128)(2,1)S(1)}, bf16[2,256,256]{2,1,0:T(8,128)(2,1)}, u32[]{:S(2)}, u32[]{:S(2)}) collective-permute-start(bf16[2,256,256]{2,1,0:T(8,128)(2,1)S(1)} %get-tuple-element.10.refs_2_), channel_id=1, source_target_pairs={{0,1},{1,0},{2,3},{3,2},{4,5},{5,4},{6,7},{7,6},{8,9},{9,8},{10,11... | collective-permute-start | bytes 786440 | tf_op jit(solution)/shard_map/ppermute | solution.py:24
  95.4 1.0 copy-start.3
  107.5 2.0 %collective-permute-start.11 = (bf16[2,256,256]{2,1,0:T(8,128)(2,1)S(1)}, bf16[2,256,256]{2,1,0:T(8,128)(2,1)S(1)}, u32[]{:S(2)}, u32[]{:S(2)}) collective-permute-start(bf16[2,256,256]{2,1,0:T(8,128)(2,1)S(1)} %get-tuple-element.11), channel_id=1, source_target_pairs={{0,2},{2,0},{4,6},{6,4},{8,10},{10,8},{12,14},{14,12},{16,18},{18,... | collective-permute-start | bytes 786440 | tf_op jit(solution)/shard_map/ppermute | solution.py:19
  107.5 9.2 %collective-permute-start.13 = (bf16[2,256,256]{2,1,0:T(8,128)(2,1)S(1)}, bf16[2,256,256]{2,1,0:T(8,128)(2,1)S(1)}, u32[]{:S(2)}, u32[]{:S(2)}) collective-permute-start(bf16[2,256,256]{2,1,0:T(8,128)(2,1)S(1)} %get-tuple-element.9.refs_1_), channel_id=1, source_target_pairs={{0,1},{1,0},{2,3},{3,2},{4,5},{5,4},{6,7},{7,6},{8,9},{9,8},{10,11... | collective-permute-start | bytes 786440 | tf_op jit(solution)/shard_map/ppermute | solution.py:24
  109.2 12.2 %collective-permute-start.15 = (bf16[2,256,256]{2,1,0:T(8,128)(2,1)S(1)}, bf16[2,256,256]{2,1,0:T(8,128)(2,1)S(1)}, u32[]{:S(2)}, u32[]{:S(2)}) collective-permute-start(bf16[2,256,256]{2,1,0:T(8,128)(2,1)S(1)} %get-tuple-element.11), channel_id=1, source_target_pairs={{0,3},{1,2},{2,1},{3,0},{4,7},{5,6},{6,5},{7,4},{8,11},{9,10},{10,... | collective-permute-start | bytes 786440 | tf_op jit(solution)/shard_map/ppermute | solution.py:24

commit v2 on v1

v2 whole, which is shorter than its diff:
```python
import math

import jax
import jax.numpy as jnp
from jax import lax
from jax.experimental import pallas as pl
from jax.experimental.pallas import tpu as pltpu
from jax.sharding import PartitionSpec as P

HD = 128
BLK = 64
WINB = 32
MASKED = -1e30
SCALE = math.log2(math.e) / math.sqrt(HD)
VMEM = 60 * 1024 * 1024


def moved(array, n, go):
    pairs = [(i, go(i)) for i in range(n) if go(i) is not None]
    return lax.ppermute(array, "ctx", pairs)


def moved_both(array, n, f, go):
    pairs = [(i * f + k, go(i, k)[0] * f + go(i, k)[1]) for i in range(n) for k in range(f)]
    return lax.ppermute(array, ("ctx", "fsdp"), pairs)


def mask_table(first_block, rows, mask_rows):
    count = WINB + rows
    query = jnp.arange(rows)
    gap = WINB + query[None, :] - jnp.arange(count)[:, None]
    present = (first_block - WINB + jnp.arange(count) >= 0)[:, None]
    clean = (gap >= 0) & (gap < WINB) & present
    offsets = jnp.arange(WINB)
    picked = ((gap - 1)[:, :, None] == offsets[None, None, :]) & (mask_rows[None] == 1)
    noisy = jnp.any(picked, axis=2) & present
    own_clean = jnp.zeros((rows, rows), bool)
    own_noisy = jnp.eye(rows, dtype=bool)
    allowed = jnp.concatenate(
        [jnp.concatenate([clean, noisy], 1), jnp.concatenate([own_clean, own_noisy], 1)], 0
    )
    table = jnp.where(allowed, 0.0, MASKED).astype(jnp.float32)
    return jnp.pad(table, ((0, 0), (0, HD - table.shape[1])))


def behind(array, *others):
    return lax.optimization_barrier((array,) + others)[0]


def cut_kernel(info, source, out):
    out[...] = source[...]


def cut_weight(info, out_weight, features, step):
    half = out_weight.shape[0] // 2
    tiles = 4 if half % 64 == 0 else 1
    count = out_weight.shape[1] // features
    return pl.pallas_call(
        cut_kernel,
        grid_spec=pltpu.PrefetchScalarGridSpec(
            num_scalar_prefetch=1,
            grid=(tiles,),
            in_specs=[pl.BlockSpec(
                (half // tiles, features),
                lambda s, info: (info[0] * tiles + s, lax.rem(info[2] + step, count)),
            )],
            out_specs=pl.BlockSpec((half // tiles, features), lambda s, info: (s, 0)),
        ),
        out_shape=jax.ShapeDtypeStruct((half, features), out_weight.dtype),
        compiler_params=pltpu.CompilerParams(vmem_limit_bytes=VMEM),
        cost_estimate=pl.CostEstimate(
            flops=0, bytes_accessed=4 * half * features, transcendentals=0
        ),
    )(info, out_weight)


def join_kernel(info, here, got, out):
    out[0] = here[:, 0]
    out[1] = got[...]


def join_pair(info, keys_values, got, first, heads, heads_half):
    tokens = keys_values.shape[2]
    return pl.pallas_call(
        join_kernel,
        grid_spec=pltpu.PrefetchScalarGridSpec(
            num_scalar_prefetch=1,
            grid=(heads,),
            in_specs=[
                pl.BlockSpec(
                    (2, 1, tokens, HD),
                    lambda h, info: (0, 0, 0, info[0] * heads_half + first + h),
                ),
                pl.BlockSpec((2, tokens, HD), lambda h, info: (0, 0, first + h)),
            ],
            out_specs=pl.BlockSpec((2, 2, tokens, HD), lambda h, info: (0, 0, 0, h)),
        ),
        out_shape=jax.ShapeDtypeStruct((2, 2, tokens, heads * HD), keys_values.dtype),
        compiler_params=pltpu.CompilerParams(vmem_limit_bytes=VMEM),
        cost_estimate=pl.CostEstimate(
            flops=0, bytes_accessed=16 * tokens * heads * HD, transcendentals=0
        ),
    )(info, keys_values, got)


def attend_kernel(tokens, count, info, *refs):
    core, side = info[0], info[1]
    refs = refs[:6 + 4 * count] + refs[-4:]
    q_here, kn_here, there, own, low = refs[:5]
    blocks = [refs[5 + 4 * h:9 + 4 * h] for h in range(count)]
    table, mine, give, keys, values = refs[5 + 4 * count:]
    rows = tokens // BLK
    span = WINB * BLK + tokens
    back = WINB * BLK // (2 * tokens)

    def place(head, ref, pair, lanes):
        for slot in range(2):
            half = core if slot == 0 else 1 - core
            at = pl.multiple_of(pair * 2 * tokens + half * tokens, tokens)
            keys[head, pl.ds(at, tokens), :] = ref[slot, 0, :, lanes]
            values[head, pl.ds(at, tokens), :] = ref[slot, 1, :, lanes]

    only = slice(0, HD)
    for head, (one, two, swap, far) in enumerate(blocks):
        lanes = slice(head * HD, (head + 1) * HD)
        place(head, two, 0, only)
        place(head, one, 2, only)
        place(head, swap, jnp.where(side == 0, 3, 1), only)
        place(head, own, back, lanes)

    @pl.when(side == 0)
    def _():
        for head in range(count):
            place(head, blocks[head][3], 1, only)

    @pl.when(side != 0)
    def _():
        for head in range(count):
            place(head, low, 3, slice(head * HD, (head + 1) * HD))

    spot = lax.broadcasted_iota(jnp.int32, (2 * tokens, HD), 0) // BLK
    lane = lax.broadcasted_iota(jnp.int32, (2 * tokens, HD), 1)
    hot = jnp.where(spot == lane, 1.0, 0.0).astype(jnp.bfloat16)
    contract = (((1,), (1,)), ((), ()))
    biases = [
        jnp.broadcast_to(table[tile][:, None, :], (span // BLK + rows, BLK, HD))
        .reshape(span + tokens, HD).astype(jnp.bfloat16)
        for tile in range(2)
    ]

    def scores_of(head, tile):
        lanes = slice(head * HD, (head + 1) * HD)
        half = core if tile == 0 else 1 - core
        at = pl.multiple_of(half * tokens, tokens)
        if tile == 0:
            query = q_here[:, :, lanes].reshape(2 * tokens, HD)
            key_n = kn_here[0, 0, :, lanes]
        else:
            query = there[0:2, :, lanes].reshape(2 * tokens, HD)
            key_n = there[2, :, lanes]
        key = jnp.concatenate([keys[head, pl.ds(at, span), :], key_n], 0)
        key = jnp.concatenate([key, biases[tile]], 1)
        query = jnp.concatenate([query, hot], 1)
        return lax.dot_general(query, key, contract, preferred_element_type=jnp.float32)

    def attended(head, tile, scores):
        lanes = slice(head * HD, (head + 1) * HD)
        half = core if tile == 0 else 1 - core
        at = pl.multiple_of(half * tokens, tokens)
        value_n = kn_here[1, 0, :, lanes] if tile == 0 else there[3, :, lanes]
        value = jnp.concatenate([values[head, pl.ds(at, span), :], value_n], 0)
        value = jnp.concatenate([value, jnp.ones_like(value)], 1)
        top = jnp.max(scores, axis=1, keepdims=True)
        expo = jnp.exp2((scores - top) * SCALE).astype(jnp.bfloat16)
        total = jnp.dot(expo, value, preferred_element_type=jnp.float32)
        out = (total[:, :HD] / total[:, HD:]).astype(jnp.bfloat16).reshape(2, tokens, HD)
        (mine if tile == 0 else give)[:, :, lanes] = out

    jobs = [(head, tile) for head in range(count) for tile in range(2)]
    scores = scores_of(*jobs[0])
    for job, later in zip(jobs, jobs[1:] + [None]):
        upcoming = scores_of(*later) if later else None
        attended(*job, scores)
        scores = upcoming


def attend(info, queries, keys_values, there, own, low, blocks, table, first, heads_half,
           room, at, into):
    tokens = queries.shape[1]
    span = WINB * BLK + 2 * tokens
    count = len(blocks)
    wide = count * HD
    per = heads_half // count if heads_half % count == 0 and first % count == 0 else None
    assert per is not None
    here = lambda s, info: (0, 0, info[0] * per + first // count)
    out_spec = pl.BlockSpec((2, tokens, wide), lambda s, info: (0, 0, at // count))
    out = jax.ShapeDtypeStruct((2, tokens, room * HD), jnp.bfloat16)
    work = count * 2 * 2 * tokens * (WINB * BLK + 2 * tokens)
    whole = pl.BlockSpec((2, 2, tokens, wide), lambda s, info: (0, 0, 0, first // count))
    one_head = pl.BlockSpec((2, 2, tokens, HD), lambda s, info: (0, 0, 0, 0))
    return pl.pallas_call(
        lambda *refs: attend_kernel(tokens, count, *refs),
        grid_spec=pltpu.PrefetchScalarGridSpec(
            num_scalar_prefetch=1,
            grid=(1,),
            in_specs=[
                pl.BlockSpec((2, tokens, wide), here),
                pl.BlockSpec((2, 1, tokens, wide), lambda s, info: (0, 1) + here(s, info)[1:]),
                pl.BlockSpec((4, tokens, wide), lambda s, info: (0, 0, first // count)),
                whole, whole,
                *[one_head] * (4 * count),
                pl.BlockSpec(table.shape, lambda s, info: (0, 0, 0)),
                *[pl.BlockSpec(memory_space=pl.ANY) for _ in into],
            ],
            out_specs=[out_spec, out_spec],
            scratch_shapes=[
                pltpu.VMEM((count, span, HD), jnp.bfloat16),
                pltpu.VMEM((count, span, HD), jnp.bfloat16),
            ],
        ),
        out_shape=[out, out],
        input_output_aliases={7 + 4 * count + k: k for k in range(len(into))},
        compiler_params=pltpu.CompilerParams(vmem_limit_bytes=VMEM),
        cost_estimate=pl.CostEstimate(
            flops=work * 8, bytes_accessed=count * 64 * 1024, transcendentals=0
        ),
    )(info, queries, keys_values, there, own, low, *[b for group in blocks for b in group], table,
      *into)


def project_kernel(count, groups, add, info, *refs):
    out = refs[-1]
    acts, weights = refs[:count], refs[count:count + groups]
    act = jnp.concatenate([a[...].reshape(-1, a.shape[2]) for a in acts], 1)
    weight = jnp.concatenate([w[...] for w in weights], 0)
    total = jnp.dot(act, weight, preferred_element_type=jnp.float32)
    if add:
        total = total + refs[count + groups][...].reshape(total.shape)
    out[...] = total.astype(out.dtype).reshape(out.shape)


def project(info, pieces, weights, features, dtype, before=None):
    tokens = pieces[0][2].shape[1]
    tile = min(256, features)
    steps = features // tile
    half = weights[0].shape[0] // 2 // HD
    used, rows = [], []
    for group, first, act in pieces:
        for head in range(first, first + act.shape[2] // HD):
            used.append(weights[group])
            if group == 0:
                row = lambda s, info, at=head: (info[0] * half + at, info[2] * steps + s)
            elif group == 1:
                row = lambda s, info, at=head: ((1 - info[0]) * half + at, info[2] * steps + s)
            else:
                row = lambda s, info, at=head: (at, s)
            rows.append(pl.BlockSpec((HD, tile), row))
    flat = [act for _, _, act in pieces]
    spec = pl.BlockSpec((2, tokens, tile), lambda s, info: (0, 0, s))
    specs = [pl.BlockSpec(a.shape, lambda s, info: (0, 0, 0)) for a in flat] + rows
    operands = flat + used
    if before is not None:
        specs.append(spec)
        operands.append(before)
    depth = HD * len(used)
    return pl.pallas_call(
        lambda *refs: project_kernel(len(flat), len(used), before is not None, *refs),
        grid_spec=pltpu.PrefetchScalarGridSpec(
            num_scalar_prefetch=1, grid=(steps,), in_specs=specs, out_specs=spec
        ),
        out_shape=jax.ShapeDtypeStruct((2, tokens, features), dtype),
        compiler_params=pltpu.CompilerParams(vmem_limit_bytes=VMEM),
        cost_estimate=pl.CostEstimate(
            flops=2 * 2 * tokens * depth * features,
            bytes_accessed=2 * depth * features + 8 * tokens * features,
            transcendentals=0,
        ),
    )(info, *operands)


def on_device(queries, keys_values, block_mask, out_weight):
    tokens = queries.shape[1]
    n, f = lax.axis_size("ctx"), lax.axis_size("fsdp")
    index, place = lax.axis_index("ctx"), lax.axis_index("fsdp")
    core, side = index % 2, (index // 2) % 2
    info = jnp.stack([core, side, place]).astype(jnp.int32)
    width = queries.shape[2] // 2
    heads_half = width // HD
    rows = tokens // BLK
    features = out_weight.shape[1] // f
    shares = [[0, 1], [2, 3]] if heads_half == 4 else [[h] for h in range(heads_half)]

    pair = lambda i: i ^ 1
    ahead = lambda i: i + 4 if i + 4 < n else None
    across = lambda i: i ^ 2
    upper = lambda i: i + 2 if i & 2 == 0 else None
    lower = lambda i: i - 2 if i & 2 else None

    clean = lax.dynamic_slice(
        keys_values, (0, 0, 0, (1 - core) * width), (2, 1, tokens, width)
    ).reshape(2, tokens, width)
    got = moved(clean, n, pair)
    own = [join_pair(info, keys_values, got, h, 1, heads_half) for h in range(1)]
    own.append(join_pair(info, keys_values, got, 0, heads_half, heads_half))
    own, whole = own[:1], own[1]
    for h in range(1, heads_half):
        own.append(join_pair(info, keys_values, got, h, 1, heads_half))

    low = moved(whole, n, upper)
    blocks = []
    for h in range(heads_half):
        last = blocks[-1] if blocks else None
        in_turn = lambda array, k: behind(array, last[k]) if last else array
        one = moved(in_turn(own[h], 0), n, ahead)
        two = moved(in_turn(one, 1), n, ahead)
        swap = moved(in_turn(one, 2), n, across)
        far = moved(in_turn(two, 3), n, lower)
        blocks.append((one, two, swap, far))

    later = jnp.concatenate(
        [lax.dynamic_slice(queries, (0, 0, (1 - core) * width), (2, tokens, width)),
         lax.dynamic_slice(
             keys_values, (0, 1, 0, (1 - core) * width), (2, 1, tokens, width)
         ).reshape(2, tokens, width)], 0
    )
    there = moved(behind(later, own[0]), n, pair)
    mask_there = moved(behind(block_mask, own[0]), n, pair)
    table = jnp.stack([
        mask_table(index * rows, rows, block_mask),
        mask_table((index ^ 1) * rows, rows, mask_there),
    ])

    sames = [
        moved_both(
            cut_weight(behind(info, own[0]), out_weight, features, r),
            n, f, lambda i, k: (i, (k + r) % f),
        )
        for r in range(1, f)
    ]

    acts = [[] for _ in range(2 * f)]
    for k, share in enumerate(shares):
        final = k == len(shares) - 1
        runs = [[h] for h in share] if final else [share]
        into = ()
        for run in runs:
            if run[-1] < heads_half - 1:
                after = [blocks[-1][1 if final else 0]]
            else:
                after = [a[0] for a in acts[1:] if a]
            into = attend(
                behind(info, *after, *into, *acts[0][-1:]), queries, keys_values, there, whole, low,
                [blocks[h] for h in run], table, run[0], heads_half,
                len(share), run[0] - share[0], into,
            )
        mine, give = into
        acts[0].append(mine)
        for r in range(1, f):
            acts[2 * r].append(moved_both(mine, n, f, lambda i, k: (i, (k + r) % f)))
            acts[2 * r + 1].append(moved_both(give, n, f, lambda i, k: (i ^ 1, (k + r) % f)))
        acts[1].append(moved(give, n, pair))
    others = []
    for same in sames:
        same = behind(same, blocks[-1][3])
        others += [same, moved(same, n, pair)]

    weights = [out_weight, out_weight] + others
    early, late = [], []
    for g in range(2 * f):
        for k, (share, act) in enumerate(zip(shares, acts[g])):
            (late if g % 2 and g > 1 or g and k == len(shares) - 1 else early).append((g, share[0], act))
    before = project(info, early, weights, features, jnp.float32)
    return project(info, late, weights, features, jnp.bfloat16, before)


def solution(mesh):
    in_specs = (
        P(None, "ctx", "fsdp"),
        P(None, None, "ctx", "fsdp"),
        P("ctx", None),
        P("fsdp", None),
    )
    out_specs = P(None, "ctx", "fsdp")
    return jax.shard_map(
        on_device, mesh=mesh, in_specs=in_specs, out_specs=out_specs, check_vma=False
    )
```

time: 132 us -> 186 us (1.41)
  Pallas kernels: 32.2 us -> 59.5 us
  starting transfers between devices: 31.2 us -> 52.6 us
  waiting for transfers between devices: 53.1 us -> 63.6 us
  local copies, waits for them, and re-layouts: 11.4 us -> 6.22 us
    pallas_call x3 -> x11, Pallas kernels: 32.2 us -> 59.5 us  [the longest x3 22.3 us: attend(): pl.pallas_call(lambda *refs: attend_kernel(tokens, count, *refs), grid_sp...]
    ppermute x14 -> x23, waiting for transfers between devices: 30.7 us -> 56.8 us  [moved(): return lax.ppermute(array, 'ctx', pairs)]
    ppermute x14 -> x23, starting transfers between devices: 24.2 us -> 46 us  [moved(): return lax.ppermute(array, 'ctx', pairs)]
    ppermute x5, waiting for transfers between devices: 22.4 us -> 6.77 us  [moved_both(): return lax.ppermute(array, ('ctx', 'fsdp'), pairs)]
    dynamic_slice x4 -> x1, local copies, waits for them, and re-layouts: 4.32 us -> 0.04 us  [on_device(): lax.dynamic_slice(queries, (0, 0, (1 - core) * width), (2, tokens, width))]
    another operation x4 -> x2, local copies, waits for them, and re-layouts: 2.23 us -> 0.01 us  [on_device(): jnp.stack([mask_table(index * rows, rows, block_mask), mask_table((index...]
    reshape x0 -> x1, local copies, waits for them, and re-layouts: none -> 2.08 us  [on_device(): later = jnp.concatenate([lax.dynamic_slice(queries, (0, 0, (1 - core) * w...]
    unnamed x22 -> x40, local copies, waits for them, and re-layouts: 2.94 us -> 3.88 us
  transfers between devices with their start and end apart: 19 -> 28, of which waited for: 8 -> 12; matrix products, arithmetic and copies ran while one was open for 6% -> 2% of each run, Pallas kernels for 17% -> 23%
where the time goes in v2:
time: 186 us; the launch traced here: 185 us
  waiting for transfers between devices  63.6 us (34%)
  Pallas kernels  59.5 us (32%)
  starting transfers between devices  52.6 us (28%)
  local copies, waits for them, and re-layouts  6.22 us (3%)
  other arithmetic  2.63 us (1%)
    ppermute x23, waiting for transfers between devices, moved(): return lax.ppermute(array, 'ctx', pairs)  56.8 us
    ppermute x23, starting transfers between devices, moved(): return lax.ppermute(array, 'ctx', pairs)  46 us
    pallas_call x3, Pallas kernels, attend(): pl.pallas_call(lambda *refs: attend_kernel(tokens, count, *refs), grid_sp...  22.3 us
    pallas_call x2, Pallas kernels, project(): pl.pallas_call(lambda *refs: project_kernel(len(flat), len(used), before...  18.9 us
    pallas_call x5, Pallas kernels, join_pair(): pl.pallas_call(join_kernel, grid_spec=pltpu.PrefetchScalarGridSpec(num_sc...  13.7 us
    ppermute x5, waiting for transfers between devices, moved_both(): return lax.ppermute(array, ('ctx', 'fsdp'), pairs)  6.77 us
    ppermute x5, starting transfers between devices, moved_both(): return lax.ppermute(array, ('ctx', 'fsdp'), pairs)  6.58 us
    pallas_call x1, Pallas kernels, cut_weight(): pl.pallas_call(cut_kernel, grid_spec=pltpu.PrefetchScalarGridSpec(num_sca...  4.58 us
  transfers between devices with their start and end apart: 28, of which 12 were waited for; matrix products, arithmetic and copies ran while one was open for 2% of the time, Pallas kernels for 23%

profile of v2, /device:TPU:0, one launch (start us, length us, event | category | flops | bytes accessed | tf_op | source)
XLA Modules:
  0.0 184.8 jit_solution(6496796416006631337)
XLA Ops:
  0.0 2.1 %dynamic-slice_bitcast_fusion = (bf16[2,256,512]{2,1,0:T(8,128)(2,1)}, bf16[2,256,512]{2,1,0:T(8,128)(2,1)S(1)}) fusion(bf16[2,2,256,1024]{3,2,1,0:T(8,128)(2,1)} %refs_2_.5, s32[]{:T(128)S(6)} %select_n.30), kind=kLoop, calls=%fused_computation.1 | loop fusion | bytes 2097156 | tf_op jit(solution)/shard_map/reshape | solution.py:324
  3.1 1.0 collective-permute-done.got
  4.1 0.8 copy-done.1
  4.9 2.4 %shard_map.49 = bf16[2,2,256,128]{3,2,1,0:T(8,128)(2,1)} custom-call(s32[3]{0:T(128)} %pad_add_fusion.2.info.refs_0_, bf16[2,2,256,1024]{3,2,1,0:T(8,128)(2,1)} %refs_2_.5, bf16[2,256,512]{2,1,0:T(8,128)(2,1)} %copy-done.1), custom_call_target="tpu_custom_call" | custom-call | bytes 524288 | tf_op jit(solution)/shard_map/pallas_call | solution.py:84
  7.2 4.6 %shard_map.54 = bf16[512,2048]{1,0:T(8,128)(2,1)} custom-call(s32[3]{0:T(128)} %pad_add_fusion.2.info.refs_0_, bf16[1024,4096]{1,0:T(8,128)(2,1)} %refs_6_.3), custom_call_target="tpu_custom_call" | custom-call | bytes 4194304 | tf_op jit(solution)/shard_map/pallas_call | solution.py:58
  11.8 2.9 %collective-permute-start.26 = (bf16[512,2048]{1,0:T(8,128)(2,1)}, bf16[512,2048]{1,0:T(8,128)(2,1)S(1)}, u32[]{:S(2)}, u32[]{:S(2)}) collective-permute-start(bf16[512,2048]{1,0:T(8,128)(2,1)} %shard_map.54), channel_id=1, source_target_pairs={{0,1},{1,0},{2,3},{3,2},{4,5},{5,4},{6,7},{7,6},{8,9},{9,8},{10,11... | collective-permute-start | bytes 6291464 | tf_op jit(solution)/shard_map/ppermute | solution.py:25
  14.7 4.2 %collective-permute-start.1 = (bf16[2,2,256,128]{3,2,1,0:T(8,128)(2,1)S(1)}, bf16[2,2,256,128]{3,2,1,0:T(8,128)(2,1)}, u32[]{:S(2)}, u32[]{:S(2)}) collective-permute-start(bf16[2,2,256,128]{3,2,1,0:T(8,128)(2,1)S(1)} %copy-done.18), channel_id=1, source_target_pairs={{0,8},{2,10},{4,12},{6,14},{8,16},{10,18},{12,20},{14,22},{16,24},... | collective-permute-start | bytes 786440 | tf_op jit(solution)/shard_map/ppermute | solution.py:20
  18.9 2.4 %shard_map.48 = bf16[2,2,256,128]{3,2,1,0:T(8,128)(2,1)} custom-call(s32[3]{0:T(128)} %pad_add_fusion.2.info.refs_0_, bf16[2,2,256,1024]{3,2,1,0:T(8,128)(2,1)} %refs_2_.5, bf16[2,256,512]{2,1,0:T(8,128)(2,1)} %copy-done.1), custom_call_target="tpu_custom_call" | custom-call | bytes 524288 | tf_op jit(solution)/shard_map/pallas_call | solution.py:84
  21.3 2.5 %collective-permute-done.1.refs_6_ = bf16[2,2,256,128]{3,2,1,0:T(8,128)(2,1)} collective-permute-done((bf16[2,2,256,128]{3,2,1,0:T(8,128)(2,1)S(1)}, bf16[2,2,256,128]{3,2,1,0:T(8,128)(2,1)}, u32[]{:S(2)}, u32[]{:S(2)}) %collective-permute-start.1) | collective-permute-done | bytes 262176 | tf_op jit(solution)/shard_map/ppermute | solution.py:20
  23.8 5.2 %collective-permute-start.2 = (bf16[2,2,256,128]{3,2,1,0:T(8,128)(2,1)}, bf16[2,2,256,128]{3,2,1,0:T(8,128)(2,1)}, u32[]{:S(2)}, u32[]{:S(2)}) collective-permute-start(bf16[2,2,256,128]{3,2,1,0:T(8,128)(2,1)} %shard_map.48), channel_id=1, source_target_pairs={{0,8},{2,10},{4,12},{6,14},{8,16},{10,18},{12,20},{14,22},{16,24},... | collective-permute-start | bytes 786440 | tf_op jit(solution)/shard_map/ppermute | solution.py:20
  29.0 3.5 %collective-permute-start.7 = (bf16[2,2,256,128]{3,2,1,0:T(8,128)(2,1)}, bf16[2,2,256,128]{3,2,1,0:T(8,128)(2,1)}, u32[]{:S(2)}, u32[]{:S(2)}) collective-permute-start(bf16[2,2,256,128]{3,2,1,0:T(8,128)(2,1)} %collective-permute-done.1.refs_6_), channel_id=1, source_target_pairs={{0,8},{2,10},{4,12},{6,14},{8,16},{10,18},{12,20},{14,22},{16,24},... | collective-permute-start | bytes 786440 | tf_op jit(solution)/shard_map/ppermute | solution.py:20
  32.4 2.4 %shard_map.47 = bf16[2,2,256,128]{3,2,1,0:T(8,128)(2,1)} custom-call(s32[3]{0:T(128)} %pad_add_fusion.2.info.refs_0_, bf16[2,2,256,1024]{3,2,1,0:T(8,128)(2,1)} %refs_2_.5, bf16[2,256,512]{2,1,0:T(8,128)(2,1)} %copy-done.1), custom_call_target="tpu_custom_call" | custom-call | bytes 524288 | tf_op jit(solution)/shard_map/pallas_call | solution.py:84
  35.3 4.4 %collective-permute-start.3 = (bf16[2,2,256,128]{3,2,1,0:T(8,128)(2,1)}, bf16[2,2,256,128]{3,2,1,0:T(8,128)(2,1)S(1)}, u32[]{:S(2)}, u32[]{:S(2)}) collective-permute-start(bf16[2,2,256,128]{3,2,1,0:T(8,128)(2,1)} %shard_map.47), channel_id=1, source_target_pairs={{0,8},{2,10},{4,12},{6,14},{8,16},{10,18},{12,20},{14,22},{16,24},... | collective-permute-start | bytes 786440 | tf_op jit(solution)/shard_map/ppermute | solution.py:20
  39.7 1.2 collective-permute-done.7.refs_7_
  40.9 5.1 %collective-permute-start.10 = (bf16[2,2,256,128]{3,2,1,0:T(8,128)(2,1)}, bf16[2,2,256,128]{3,2,1,0:T(8,128)(2,1)}, u32[]{:S(2)}, u32[]{:S(2)}) collective-permute-start(bf16[2,2,256,128]{3,2,1,0:T(8,128)(2,1)} %collective-permute-done.2.refs_10_), channel_id=1, source_target_pairs={{0,8},{2,10},{4,12},{6,14},{8,16},{10,18},{12,20},{14,22},{16,24},... | collective-permute-start | bytes 786440 | tf_op jit(solution)/shard_map/ppermute | solution.py:20
  46.0 1.3 collective-permute-start.9
  47.3 2.5 %shard_map.46 = bf16[2,2,256,128]{3,2,1,0:T(8,128)(2,1)} custom-call(s32[3]{0:T(128)} %pad_add_fusion.2.info.refs_0_, bf16[2,2,256,1024]{3,2,1,0:T(8,128)(2,1)} %refs_2_.5, bf16[2,256,512]{2,1,0:T(8,128)(2,1)} %copy-done.1), custom_call_target="tpu_custom_call" | custom-call | bytes 524288 | tf_op jit(solution)/shard_map/pallas_call | solution.py:84
  49.8 2.8 %collective-permute-start.4 = (bf16[2,2,256,128]{3,2,1,0:T(8,128)(2,1)}, bf16[2,2,256,128]{3,2,1,0:T(8,128)(2,1)S(1)}, u32[]{:S(2)}, u32[]{:S(2)}) collective-permute-start(bf16[2,2,256,128]{3,2,1,0:T(8,128)(2,1)} %shard_map.46), channel_id=1, source_target_pairs={{0,8},{2,10},{4,12},{6,14},{8,16},{10,18},{12,20},{14,22},{16,24},... | collective-permute-start | bytes 786440 | tf_op jit(solution)/shard_map/ppermute | solution.py:20
  52.7 3.5 %collective-permute-start.17 = (bf16[2,2,256,128]{3,2,1,0:T(8,128)(2,1)S(1)}, bf16[2,2,256,128]{3,2,1,0:T(8,128)(2,1)S(1)}, u32[]{:S(2)}, u32[]{:S(2)}) collective-permute-start(bf16[2,2,256,128]{3,2,1,0:T(8,128)(2,1)S(1)} %collective-permute-done.3.refs_6_), channel_id=1, source_target_pairs={{0,8},{2,10},{4,12},{6,14},{8,16},{10,18},{12,20},{14,22},{16,24},... | collective-permute-start | bytes 786440 | tf_op jit(solution)/shard_map/ppermute | solution.py:20
  56.2 1.3 collective-permute-start.12
  57.5 1.1 pad_maximum_fusion
  58.6 2.7 %collective-permute-done.17.refs_7_ = bf16[2,2,256,128]{3,2,1,0:T(8,128)(2,1)S(1)} collective-permute-done((bf16[2,2,256,128]{3,2,1,0:T(8,128)(2,1)S(1)}, bf16[2,2,256,128]{3,2,1,0:T(8,128)(2,1)S(1)}, u32[]{:S(2)}, u32[]{:S(2)}) %collective-permute-start.17) | collective-permute-done | bytes 262176 | tf_op jit(solution)/shard_map/ppermute | solution.py:20
  61.2 4.4 %collective-permute-start.18 = (bf16[2,2,256,128]{3,2,1,0:T(8,128)(2,1)S(1)}, bf16[2,2,256,128]{3,2,1,0:T(8,128)(2,1)S(1)}, u32[]{:S(2)}, u32[]{:S(2)}) collective-permute-start(bf16[2,2,256,128]{3,2,1,0:T(8,128)(2,1)S(1)} %collective-permute-done.4.refs_6_), channel_id=1, source_target_pairs={{0,8},{2,10},{4,12},{6,14},{8,16},{10,18},{12,20},{14,22},{16,24},... | collective-permute-start | bytes 786440 | tf_op jit(solution)/shard_map/ppermute | solution.py:20
  65.7 1.3 collective-permute-start.20
  67.0 2.5 %collective-permute-done.18.refs_7_ = bf16[2,2,256,128]{3,2,1,0:T(8,128)(2,1)S(1)} collective-permute-done((bf16[2,2,256,128]{3,2,1,0:T(8,128)(2,1)S(1)}, bf16[2,2,256,128]{3,2,1,0:T(8,128)(2,1)S(1)}, u32[]{:S(2)}, u32[]{:S(2)}) %collective-permute-start.18) | collective-permute-done | bytes 262176 | tf_op jit(solution)/shard_map/ppermute | solution.py:20
  69.5 5.8 %collective-permute-done.20.refs_9_ = bf16[2,2,256,128]{3,2,1,0:T(8,128)(2,1)} collective-permute-done((bf16[2,2,256,128]{3,2,1,0:T(8,128)(2,1)S(1)}, bf16[2,2,256,128]{3,2,1,0:T(8,128)(2,1)}, u32[]{:S(2)}, u32[]{:S(2)}) %collective-permute-start.20) | collective-permute-done | bytes 262176 | tf_op jit(solution)/shard_map/ppermute | solution.py:20
  75.3 1.3 collective-permute-start.22
  76.7 6.9 %collective-permute-done.22.refs_9_ = bf16[2,2,256,128]{3,2,1,0:T(8,128)(2,1)S(1)} collective-permute-done((bf16[2,2,256,128]{3,2,1,0:T(8,128)(2,1)S(1)}, bf16[2,2,256,128]{3,2,1,0:T(8,128)(2,1)S(1)}, u32[]{:S(2)}, u32[]{:S(2)}) %collective-permute-start.22) | collective-permute-done | bytes 262176 | tf_op jit(solution)/shard_map/ppermute | solution.py:20
  84.3 4.1 %shard_map.50.refs_4_ = bf16[2,2,256,512]{3,2,1,0:T(8,128)(2,1)} custom-call(s32[3]{0:T(128)} %pad_add_fusion.2.info.refs_0_, bf16[2,2,256,1024]{3,2,1,0:T(8,128)(2,1)} %refs_2_.5, bf16[2,256,512]{2,1,0:T(8,128)(2,1)} %copy-done.1), custom_call_target="tpu_custom_call" | custom-call | bytes 2097152 | tf_op jit(solution)/shard_map/pallas_call | solution.py:84
  88.4 1.5 collective-permute-start.6
  90.5 27.9 %collective-permute-done.8.refs_8_ = bf16[2,2,256,128]{3,2,1,0:T(8,128)(2,1)} collective-permute-done((bf16[2,2,256,128]{3,2,1,0:T(8,128)(2,1)}, bf16[2,2,256,128]{3,2,1,0:T(8,128)(2,1)}, u32[]{:S(2)}, u32[]{:S(2)}) %collective-permute-start.8) | collective-permute-done | bytes 262176 | tf_op jit(solution)/shard_map/ppermute | solution.py:20
  118.4 2.5 %collective-permute-start.11 = (bf16[2,2,256,128]{3,2,1,0:T(8,128)(2,1)}, bf16[2,2,256,128]{3,2,1,0:T(8,128)(2,1)}, u32[]{:S(2)}, u32[]{:S(2)}) collective-permute-start(bf16[2,2,256,128]{3,2,1,0:T(8,128)(2,1)} %collective-permute-done.2.refs_10_), channel_id=1, source_target_pairs={{0,4},{2,6},{4,0},{6,2},{8,12},{10,14},{12,8},{14,10},{16,20},{18,... | collective-permute-start | bytes 786440 | tf_op jit(solution)/shard_map/ppermute | solution.py:20
  121.0 5.8 %collective-permute-done.11.refs_12_ = bf16[2,2,256,128]{3,2,1,0:T(8,128)(2,1)} collective-permute-done((bf16[2,2,256,128]{3,2,1,0:T(8,128)(2,1)}, bf16[2,2,256,128]{3,2,1,0:T(8,128)(2,1)}, u32[]{:S(2)}, u32[]{:S(2)}) %collective-permute-start.11) | collective-permute-done | bytes 262176 | tf_op jit(solution)/shard_map/ppermute | solution.py:20
  126.8 1.7 collective-permute-start.19
  128.6 0.6 pad_maximum_fusion.1.refs_14_.refs_10_
  129.2 1.0 copy-done.3
  130.2 10.0 %shard_map.51 = (bf16[2,256,256]{2,1,0:T(8,128)(2,1)}, bf16[2,256,256]{2,1,0:T(8,128)(2,1)}) custom-call(s32[3]{0:T(128)} %pad_add_fusion.2.info.refs_0_, bf16[2,256,1024]{2,1,0:T(8,128)(2,1)} %refs_1_.5, bf16[2,2,256,1024]{3,2,1,0:T(8,128)(2,1)} %refs_2_.5, bf16[4,256,512]{2,1,0:T(8,128)(2,1)} %collective-permute-done.5.refs_3_, ...), custom_call_target="tpu_custom_call" | custom-call | flops 41943040 | bytes 131072 | tf_op jit(solution)/shard_map/pallas_call | solution.py:201
  140.2 0.6 collective-permute-start.14
  140.8 1.5 collective-permute-start.15
  142.7 6.3 %shard_map.52 = (bf16[2,256,256]{2,1,0:T(8,128)(2,1)}, bf16[2,256,256]{2,1,0:T(8,128)(2,1)}) custom-call(s32[3]{0:T(128)} %pad_add_fusion.2.info.refs_0_, bf16[2,256,1024]{2,1,0:T(8,128)(2,1)} %refs_1_.5, bf16[2,2,256,1024]{3,2,1,0:T(8,128)(2,1)} %refs_2_.5, bf16[4,256,512]{2,1,0:T(8,128)(2,1)} %collective-permute-done.5.refs_3_, ...), custom_call_target="tpu_custom_call" | custom-call | flops 20971520 | bytes 65536 | tf_op jit(solution)/shard_map/pallas_call | solution.py:201
  149.0 3.8 %collective-permute-done.15.refs_4_ = bf16[2,256,256]{2,1,0:T(8,128)(2,1)S(1)} collective-permute-done((bf16[2,256,256]{2,1,0:T(8,128)(2,1)}, bf16[2,256,256]{2,1,0:T(8,128)(2,1)S(1)}, u32[]{:S(2)}, u32[]{:S(2)}) %collective-permute-start.15) | collective-permute-done | bytes 262176 | tf_op jit(solution)/shard_map/ppermute | solution.py:25
  152.8 0.8 copy-done.17
  153.5 6.1 %shard_map.53 = (bf16[2,256,256]{2,1,0:T(8,128)(2,1)}, bf16[2,256,256]{2,1,0:T(8,128)(2,1)}) custom-call(s32[3]{0:T(128)} %pad_add_fusion.2.info.refs_0_, bf16[2,256,1024]{2,1,0:T(8,128)(2,1)} %refs_1_.5, bf16[2,2,256,1024]{3,2,1,0:T(8,128)(2,1)} %refs_2_.5, ...), custom_call_target="tpu_custom_call", output_to_operand_aliasing={{0}: (11, {}), {1}: (12, {})} | custom-call | flops 20971520 | bytes 65536 | tf_op jit(solution)/shard_map/pallas_call | solution.py:201
  159.7 2.1 %collective-permute-start.25 = (bf16[2,256,256]{2,1,0:T(8,128)(2,1)}, bf16[2,256,256]{2,1,0:T(8,128)(2,1)S(1)}, u32[]{:S(2)}, u32[]{:S(2)}) collective-permute-start(bf16[2,256,256]{2,1,0:T(8,128)(2,1)} %get-tuple-element.51), channel_id=1, source_target_pairs={{0,3},{1,2},{2,1},{3,0},{4,7},{5,6},{6,5},{7,4},{8,11},{9,10},{10,... | collective-permute-start | bytes 786440 | tf_op jit(solution)/shard_map/ppermute | solution.py:25
  162.3 9.2 %shard_map.55.refs_13_ = f32[2,256,2048]{2,1,0:T(8,128)} custom-call(s32[3]{0:T(128)} %pad_add_fusion.2.info.refs_0_, bf16[2,256,256]{2,1,0:T(8,128)(2,1)} %get-tuple-element.40.refs_1_, bf16[2,256,256]{2,1,0:T(8,128)(2,1)} %get-tuple-element.52.refs_2_, bf16[2,256,256]{2,1,0:T(8,128)(2,1)} %copy-done.6, bf16[2,256,256]{2,1,0:T(8,128)(2,1)} %copy-done.7, ...), custom_call_target="tpu_custom_call" | custom-call | flops 2147483648 | bytes 8388608 | tf_op jit(solution)/shard_map/pallas_call | solution.py:266
  171.5 3.0 %collective-permute-done.24.refs_2_ = bf16[2,256,256]{2,1,0:T(8,128)(2,1)S(1)} collective-permute-done((bf16[2,256,256]{2,1,0:T(8,128)(2,1)}, bf16[2,256,256]{2,1,0:T(8,128)(2,1)S(1)}, u32[]{:S(2)}, u32[]{:S(2)}) %collective-permute-start.24) | collective-permute-done | bytes 262176 | tf_op jit(solution)/shard_map/ppermute | solution.py:25
  174.5 0.7 copy-done.10
  175.2 9.7 %shard_map.56 = bf16[2,256,2048]{2,1,0:T(8,128)(2,1)} custom-call(s32[3]{0:T(128)} %pad_add_fusion.2.info.refs_0_, bf16[2,256,256]{2,1,0:T(8,128)(2,1)} %copy-done.9, bf16[2,256,256]{2,1,0:T(8,128)(2,1)} %copy-done.10, bf16[2,256,256]{2,1,0:T(8,128)(2,1)} %copy-done.5, bf16[2,256,256]{2,1,0:T(8,128)(2,1)} %copy-done.8, bf16[1024,4096]{1,0:T(8,128)(2,1)} %refs_6_.3, ...), custom_call_target="tpu_custom_call" | custom-call | flops 2147483648 | bytes 8388608 | tf_op jit(solution)/shard_map/pallas_call | solution.py:266
  (79 shorter events, 4.0 us)
Async XLA Ops:
  2.1 2.0 %collective-permute-start = (bf16[2,256,512]{2,1,0:T(8,128)(2,1)S(1)}, bf16[2,256,512]{2,1,0:T(8,128)(2,1)S(1)}, u32[]{:S(2)}, u32[]{:S(2)}) collective-permute-start(bf16[2,256,512]{2,1,0:T(8,128)(2,1)S(1)} %get-tuple-element.58), channel_id=1, source_target_pairs={{0,2},{2,0},{4,6},{6,4},{8,10},{10,8},{12,14},{14,12},{16,18},{18,... | collective-permute-start | bytes 1572872 | tf_op jit(solution)/shard_map/ppermute | solution.py:20
  4.1 0.8 copy-start.1
  7.2 7.5 %copy-start.18 = (bf16[2,2,256,128]{3,2,1,0:T(8,128)(2,1)S(1)}, bf16[2,2,256,128]{3,2,1,0:T(8,128)(2,1)}, u32[]{:S(2)}) copy-start(bf16[2,2,256,128]{3,2,1,0:T(8,128)(2,1)} %shard_map.49) | copy-start | bytes 786436
  11.8 71.8 %collective-permute-start.26 = (bf16[512,2048]{1,0:T(8,128)(2,1)}, bf16[512,2048]{1,0:T(8,128)(2,1)S(1)}, u32[]{:S(2)}, u32[]{:S(2)}) collective-permute-start(bf16[512,2048]{1,0:T(8,128)(2,1)} %shard_map.54), channel_id=1, source_target_pairs={{0,1},{1,0},{2,3},{3,2},{4,5},{5,4},{6,7},{7,6},{8,9},{9,8},{10,11... | collective-permute-start | bytes 6291464 | tf_op jit(solution)/shard_map/ppermute | solution.py:25
  14.7 9.0 %collective-permute-start.1 = (bf16[2,2,256,128]{3,2,1,0:T(8,128)(2,1)S(1)}, bf16[2,2,256,128]{3,2,1,0:T(8,128)(2,1)}, u32[]{:S(2)}, u32[]{:S(2)}) collective-permute-start(bf16[2,2,256,128]{3,2,1,0:T(8,128)(2,1)S(1)} %copy-done.18), channel_id=1, source_target_pairs={{0,8},{2,10},{4,12},{6,14},{8,16},{10,18},{12,20},{14,22},{16,24},... | collective-permute-start | bytes 786440 | tf_op jit(solution)/shard_map/ppermute | solution.py:20
  23.8 11.5 %collective-permute-start.2 = (bf16[2,2,256,128]{3,2,1,0:T(8,128)(2,1)}, bf16[2,2,256,128]{3,2,1,0:T(8,128)(2,1)}, u32[]{:S(2)}, u32[]{:S(2)}) collective-permute-start(bf16[2,2,256,128]{3,2,1,0:T(8,128)(2,1)} %shard_map.48), channel_id=1, source_target_pairs={{0,8},{2,10},{4,12},{6,14},{8,16},{10,18},{12,20},{14,22},{16,24},... | collective-permute-start | bytes 786440 | tf_op jit(solution)/shard_map/ppermute | solution.py:20
  29.0 12.0 %collective-permute-start.7 = (bf16[2,2,256,128]{3,2,1,0:T(8,128)(2,1)}, bf16[2,2,256,128]{3,2,1,0:T(8,128)(2,1)}, u32[]{:S(2)}, u32[]{:S(2)}) collective-permute-start(bf16[2,2,256,128]{3,2,1,0:T(8,128)(2,1)} %collective-permute-done.1.refs_6_), channel_id=1, source_target_pairs={{0,8},{2,10},{4,12},{6,14},{8,16},{10,18},{12,20},{14,22},{16,24},... | collective-permute-start | bytes 786440 | tf_op jit(solution)/shard_map/ppermute | solution.py:20
  34.8 22.7 %copy-start.2 = (bf16[2,256,1024]{2,1,0:T(8,128)(2,1)S(1)}, bf16[2,256,1024]{2,1,0:T(8,128)(2,1)}, u32[]{:S(2)}) copy-start(bf16[2,256,1024]{2,1,0:T(8,128)(2,1)} %refs_1_.5) | copy-start | bytes 3145732
  35.3 14.5 %collective-permute-start.3 = (bf16[2,2,256,128]{3,2,1,0:T(8,128)(2,1)}, bf16[2,2,256,128]{3,2,1,0:T(8,128)(2,1)S(1)}, u32[]{:S(2)}, u32[]{:S(2)}) collective-permute-start(bf16[2,2,256,128]{3,2,1,0:T(8,128)(2,1)} %shard_map.47), channel_id=1, source_target_pairs={{0,8},{2,10},{4,12},{6,14},{8,16},{10,18},{12,20},{14,22},{16,24},... | collective-permute-start | bytes 786440 | tf_op jit(solution)/shard_map/ppermute | solution.py:20
  40.9 11.7 %collective-permute-start.10 = (bf16[2,2,256,128]{3,2,1,0:T(8,128)(2,1)}, bf16[2,2,256,128]{3,2,1,0:T(8,128)(2,1)}, u32[]{:S(2)}, u32[]{:S(2)}) collective-permute-start(bf16[2,2,256,128]{3,2,1,0:T(8,128)(2,1)} %collective-permute-done.2.refs_10_), channel_id=1, source_target_pairs={{0,8},{2,10},{4,12},{6,14},{8,16},{10,18},{12,20},{14,22},{16,24},... | collective-permute-start | bytes 786440 | tf_op jit(solution)/shard_map/ppermute | solution.py:20
  46.0 10.1 %collective-permute-start.9 = (bf16[2,2,256,128]{3,2,1,0:T(8,128)(2,1)}, bf16[2,2,256,128]{3,2,1,0:T(8,128)(2,1)}, u32[]{:S(2)}, u32[]{:S(2)}) collective-permute-start(bf16[2,2,256,128]{3,2,1,0:T(8,128)(2,1)} %collective-permute-done.7.refs_7_), channel_id=1, source_target_pairs={{4,0},{6,2},{12,8},{14,10},{20,16},{22,18},{28,24},{30,26},{5,1},{... | collective-permute-start | bytes 786440 | tf_op jit(solution)/shard_map/ppermute | solution.py:20
  47.3 10.2 %copy-start.4 = (bf16[2,256,512]{2,1,0:T(8,128)(2,1)S(1)}, bf16[2,256,512]{2,1,0:T(8,128)(2,1)}, u32[]{:S(2)}) copy-start(bf16[2,256,512]{2,1,0:T(8,128)(2,1)} %get-tuple-element.57) | copy-start | bytes 1572868
  49.8 17.1 %copy-start.19 = (s32[4,32]{1,0:T(4,128)S(1)}, s32[4,32]{1,0:T(4,128)}, u32[]{:S(2)}) copy-start(s32[4,32]{1,0:T(4,128)} %param.6) | copy-start | bytes 1540
  49.8 77.0 %copy-start.11 = (bf16[2,2,256,128]{3,2,1,0:T(8,128)(2,1)}, bf16[2,2,256,128]{3,2,1,0:T(8,128)(2,1)S(1)}, u32[]{:S(2)}) copy-start(bf16[2,2,256,128]{3,2,1,0:T(8,128)(2,1)S(1)} %collective-permute-done.3.refs_6_) | copy-start | bytes 786436
  49.8 8.7 %collective-permute-start.4 = (bf16[2,2,256,128]{3,2,1,0:T(8,128)(2,1)}, bf16[2,2,256,128]{3,2,1,0:T(8,128)(2,1)S(1)}, u32[]{:S(2)}, u32[]{:S(2)}) collective-permute-start(bf16[2,2,256,128]{3,2,1,0:T(8,128)(2,1)} %shard_map.46), channel_id=1, source_target_pairs={{0,8},{2,10},{4,12},{6,14},{8,16},{10,18},{12,20},{14,22},{16,24},... | collective-permute-start | bytes 786440 | tf_op jit(solution)/shard_map/ppermute | solution.py:20
  52.7 8.6 %collective-permute-start.17 = (bf16[2,2,256,128]{3,2,1,0:T(8,128)(2,1)S(1)}, bf16[2,2,256,128]{3,2,1,0:T(8,128)(2,1)S(1)}, u32[]{:S(2)}, u32[]{:S(2)}) collective-permute-start(bf16[2,2,256,128]{3,2,1,0:T(8,128)(2,1)S(1)} %collective-permute-done.3.refs_6_), channel_id=1, source_target_pairs={{0,8},{2,10},{4,12},{6,14},{8,16},{10,18},{12,20},{14,22},{16,24},... | collective-permute-start | bytes 786440 | tf_op jit(solution)/shard_map/ppermute | solution.py:20
  56.2 9.5 %collective-permute-start.12 = (bf16[2,2,256,128]{3,2,1,0:T(8,128)(2,1)}, bf16[2,2,256,128]{3,2,1,0:T(8,128)(2,1)S(1)}, u32[]{:S(2)}, u32[]{:S(2)}) collective-permute-start(bf16[2,2,256,128]{3,2,1,0:T(8,128)(2,1)} %collective-permute-done.10.refs_11_), channel_id=1, source_target_pairs={{4,0},{6,2},{12,8},{14,10},{20,16},{22,18},{28,24},{30,26},{5,1},{... | collective-permute-start | bytes 786440 | tf_op jit(solution)/shard_map/ppermute | solution.py:20
  58.6 25.0 %copy-start.12 = (bf16[2,2,256,128]{3,2,1,0:T(8,128)(2,1)}, bf16[2,2,256,128]{3,2,1,0:T(8,128)(2,1)S(1)}, u32[]{:S(2)}) copy-start(bf16[2,2,256,128]{3,2,1,0:T(8,128)(2,1)S(1)} %collective-permute-done.4.refs_6_) | copy-start | bytes 786436
  61.2 22.5 %copy-start.13 = (bf16[2,2,256,128]{3,2,1,0:T(8,128)(2,1)}, bf16[2,2,256,128]{3,2,1,0:T(8,128)(2,1)S(1)}, u32[]{:S(2)}) copy-start(bf16[2,2,256,128]{3,2,1,0:T(8,128)(2,1)S(1)} %collective-permute-done.17.refs_7_) | copy-start | bytes 786436
  61.2 8.3 %collective-permute-start.18 = (bf16[2,2,256,128]{3,2,1,0:T(8,128)(2,1)S(1)}, bf16[2,2,256,128]{3,2,1,0:T(8,128)(2,1)S(1)}, u32[]{:S(2)}, u32[]{:S(2)}) collective-permute-start(bf16[2,2,256,128]{3,2,1,0:T(8,128)(2,1)S(1)} %collective-permute-done.4.refs_6_), channel_id=1, source_target_pairs={{0,8},{2,10},{4,12},{6,14},{8,16},{10,18},{12,20},{14,22},{16,24},... | collective-permute-start | bytes 786440 | tf_op jit(solution)/shard_map/ppermute | solution.py:20
  65.7 18.1 %copy-start.16 = (bf16[2,2,256,128]{3,2,1,0:T(8,128)(2,1)}, bf16[2,2,256,128]{3,2,1,0:T(8,128)(2,1)S(1)}, u32[]{:S(2)}) copy-start(bf16[2,2,256,128]{3,2,1,0:T(8,128)(2,1)S(1)} %collective-permute-done.12.refs_13_) | copy-start | bytes 786436
  65.7 9.7 %collective-permute-start.20 = (bf16[2,2,256,128]{3,2,1,0:T(8,128)(2,1)S(1)}, bf16[2,2,256,128]{3,2,1,0:T(8,128)(2,1)}, u32[]{:S(2)}, u32[]{:S(2)}) collective-permute-start(bf16[2,2,256,128]{3,2,1,0:T(8,128)(2,1)S(1)} %collective-permute-done.17.refs_7_), channel_id=1, source_target_pairs={{4,0},{6,2},{12,8},{14,10},{20,16},{22,18},{28,24},{30,26},{5,1},{... | collective-permute-start | bytes 786440 | tf_op jit(solution)/shard_map/ppermute | solution.py:20
  69.5 14.2 %copy-start.14 = (bf16[2,2,256,128]{3,2,1,0:T(8,128)(2,1)}, bf16[2,2,256,128]{3,2,1,0:T(8,128)(2,1)S(1)}, u32[]{:S(2)}) copy-start(bf16[2,2,256,128]{3,2,1,0:T(8,128)(2,1)S(1)} %collective-permute-done.18.refs_7_) | copy-start | bytes 786436
  75.3 8.3 %collective-permute-start.22 = (bf16[2,2,256,128]{3,2,1,0:T(8,128)(2,1)S(1)}, bf16[2,2,256,128]{3,2,1,0:T(8,128)(2,1)S(1)}, u32[]{:S(2)}, u32[]{:S(2)}) collective-permute-start(bf16[2,2,256,128]{3,2,1,0:T(8,128)(2,1)S(1)} %collective-permute-done.18.refs_7_), channel_id=1, source_target_pairs={{4,0},{6,2},{12,8},{14,10},{20,16},{22,18},{28,24},{30,26},{5,1},{... | collective-permute-start | bytes 786440 | tf_op jit(solution)/shard_map/ppermute | solution.py:20
  76.7 13.3 %collective-permute-start.13 = (s32[4,32]{1,0:T(4,128)S(1)}, s32[4,32]{1,0:T(4,128)S(1)}, u32[]{:S(2)}, u32[]{:S(2)}) collective-permute-start(s32[4,32]{1,0:T(4,128)S(1)} %copy-done.19), channel_id=1, source_target_pairs={{0,2},{2,0},{4,6},{6,4},{8,10},{10,8},{12,14},{14,12},{16,18},{18,... | collective-permute-start | bytes 1544 | tf_op jit(solution)/shard_map/ppermute | solution.py:20
  83.6 0.7 copy-start.15
  83.6 56.5 %copy-start = (bf16[512,2048]{1,0:T(8,128)(2,1)}, bf16[512,2048]{1,0:T(8,128)(2,1)S(1)}, u32[]{:S(2)}) copy-start(bf16[512,2048]{1,0:T(8,128)(2,1)S(1)} %collective-permute-done.26.refs_11_.refs_12_.refs_7_.refs_8_) | copy-start | bytes 6291460
  83.6 90.8 %collective-permute-start.27 = (bf16[512,2048]{1,0:T(8,128)(2,1)S(1)}, bf16[512,2048]{1,0:T(8,128)(2,1)}, u32[]{:S(2)}, u32[]{:S(2)}) collective-permute-start(bf16[512,2048]{1,0:T(8,128)(2,1)S(1)} %collective-permute-done.26.refs_11_.refs_12_.refs_7_.refs_8_), channel_id=1, source_target_pairs={{0,2},{2,0},{4,6},{6,4},{8,10},{10,8},{12,14},{14,12},{16,18},{18,... | collective-permute-start | bytes 6291464 | tf_op jit(solution)/shard_map/ppermute | solution.py:20
  88.4 40.8 %collective-permute-start.6 = (bf16[2,2,256,512]{3,2,1,0:T(8,128)(2,1)}, bf16[2,2,256,512]{3,2,1,0:T(8,128)(2,1)S(1)}, u32[]{:S(2)}, u32[]{:S(2)}) collective-permute-start(bf16[2,2,256,512]{3,2,1,0:T(8,128)(2,1)} %shard_map.50.refs_4_), channel_id=1, source_target_pairs={{0,4},{2,6},{8,12},{10,14},{16,20},{18,22},{24,28},{26,30},{1,5},{... | collective-permute-start | bytes 3145736 | tf_op jit(solution)/shard_map/ppermute | solution.py:20
  89.9 39.3 %collective-permute-start.5 = (bf16[4,256,512]{2,1,0:T(8,128)(2,1)}, bf16[4,256,512]{2,1,0:T(8,128)(2,1)}, u32[]{:S(2)}, u32[]{:S(2)}) collective-permute-start(bf16[4,256,512]{2,1,0:T(8,128)(2,1)} %pad_maximum_fusion), channel_id=1, source_target_pairs={{0,2},{2,0},{4,6},{6,4},{8,10},{10,8},{12,14},{14,12},{16,18},{18,... | collective-permute-start | bytes 3145736 | tf_op jit(solution)/shard_map/ppermute | solution.py:20
  90.2 28.2 %collective-permute-start.8 = (bf16[2,2,256,128]{3,2,1,0:T(8,128)(2,1)}, bf16[2,2,256,128]{3,2,1,0:T(8,128)(2,1)}, u32[]{:S(2)}, u32[]{:S(2)}) collective-permute-start(bf16[2,2,256,128]{3,2,1,0:T(8,128)(2,1)} %collective-permute-done.1.refs_6_), channel_id=1, source_target_pairs={{0,4},{2,6},{4,0},{6,2},{8,12},{10,14},{12,8},{14,10},{16,20},{18,... | collective-permute-start | bytes 786440 | tf_op jit(solution)/shard_map/ppermute | solution.py:20
  118.4 8.4 %collective-permute-start.11 = (bf16[2,2,256,128]{3,2,1,0:T(8,128)(2,1)}, bf16[2,2,256,128]{3,2,1,0:T(8,128)(2,1)}, u32[]{:S(2)}, u32[]{:S(2)}) collective-permute-start(bf16[2,2,256,128]{3,2,1,0:T(8,128)(2,1)} %collective-permute-done.2.refs_10_), channel_id=1, source_target_pairs={{0,4},{2,6},{4,0},{6,2},{8,12},{10,14},{12,8},{14,10},{16,20},{18,... | collective-permute-start | bytes 786440 | tf_op jit(solution)/shard_map/ppermute | solution.py:20
  126.8 15.5 %collective-permute-start.19 = (bf16[2,2,256,128]{3,2,1,0:T(8,128)(2,1)S(1)}, bf16[2,2,256,128]{3,2,1,0:T(8,128)(2,1)}, u32[]{:S(2)}, u32[]{:S(2)}) collective-permute-start(bf16[2,2,256,128]{3,2,1,0:T(8,128)(2,1)S(1)} %collective-permute-done.3.refs_6_), channel_id=1, source_target_pairs={{0,4},{2,6},{4,0},{6,2},{8,12},{10,14},{12,8},{14,10},{16,20},{18,... | collective-permute-start | bytes 786440 | tf_op jit(solution)/shard_map/ppermute | solution.py:20
  129.2 1.0 copy-start.3
  140.2 8.8 %collective-permute-start.16 = (bf16[2,256,256]{2,1,0:T(8,128)(2,1)}, bf16[2,256,256]{2,1,0:T(8,128)(2,1)S(1)}, u32[]{:S(2)}, u32[]{:S(2)}) collective-permute-start(bf16[2,256,256]{2,1,0:T(8,128)(2,1)} %get-tuple-element.39), channel_id=1, source_target_pairs={{0,3},{1,2},{2,1},{3,0},{4,7},{5,6},{6,5},{7,4},{8,11},{9,10},{10,... | collective-permute-start | bytes 786440 | tf_op jit(solution)/shard_map/ppermute | solution.py:25
  140.2 8.8 %collective-permute-start.14 = (bf16[2,256,256]{2,1,0:T(8,128)(2,1)}, bf16[2,256,256]{2,1,0:T(8,128)(2,1)S(1)}, u32[]{:S(2)}, u32[]{:S(2)}) collective-permute-start(bf16[2,256,256]{2,1,0:T(8,128)(2,1)} %get-tuple-element.39), channel_id=1, source_target_pairs={{0,2},{2,0},{4,6},{6,4},{8,10},{10,8},{12,14},{14,12},{16,18},{18,... | collective-permute-start | bytes 786440 | tf_op jit(solution)/shard_map/ppermute | solution.py:20
  140.8 11.9 %collective-permute-start.15 = (bf16[2,256,256]{2,1,0:T(8,128)(2,1)}, bf16[2,256,256]{2,1,0:T(8,128)(2,1)S(1)}, u32[]{:S(2)}, u32[]{:S(2)}) collective-permute-start(bf16[2,256,256]{2,1,0:T(8,128)(2,1)} %get-tuple-element.40.refs_1_), channel_id=1, source_target_pairs={{0,1},{1,0},{2,3},{3,2},{4,5},{5,4},{6,7},{7,6},{8,9},{9,8},{10,11... | collective-permute-start | bytes 786440 | tf_op jit(solution)/shard_map/ppermute | solution.py:25
  142.3 10.4 %collective-permute-start.21 = (bf16[2,2,256,128]{3,2,1,0:T(8,128)(2,1)}, bf16[2,2,256,128]{3,2,1,0:T(8,128)(2,1)S(1)}, u32[]{:S(2)}, u32[]{:S(2)}) collective-permute-start(bf16[2,2,256,128]{3,2,1,0:T(8,128)(2,1)} %copy-done.12), channel_id=1, source_target_pairs={{0,4},{2,6},{4,0},{6,2},{8,12},{10,14},{12,8},{14,10},{16,20},{18,... | collective-permute-start | bytes 786440 | tf_op jit(solution)/shard_map/ppermute | solution.py:20
  149.0 10.7 %copy-start.5 = (bf16[2,256,256]{2,1,0:T(8,128)(2,1)}, bf16[2,256,256]{2,1,0:T(8,128)(2,1)S(1)}, u32[]{:S(2)}) copy-start(bf16[2,256,256]{2,1,0:T(8,128)(2,1)S(1)} %collective-permute-done.16.refs_3_) | copy-start | bytes 786436
  149.0 10.6 %copy-start.6 = (bf16[2,256,256]{2,1,0:T(8,128)(2,1)}, bf16[2,256,256]{2,1,0:T(8,128)(2,1)S(1)}, u32[]{:S(2)}) copy-start(bf16[2,256,256]{2,1,0:T(8,128)(2,1)S(1)} %collective-permute-done.14.refs_3_) | copy-start | bytes 786436
  152.8 6.9 %copy-start.7 = (bf16[2,256,256]{2,1,0:T(8,128)(2,1)}, bf16[2,256,256]{2,1,0:T(8,128)(2,1)S(1)}, u32[]{:S(2)}) copy-start(bf16[2,256,256]{2,1,0:T(8,128)(2,1)S(1)} %collective-permute-done.15.refs_4_) | copy-start | bytes 786436
  152.8 0.8 copy-start.17
  159.7 11.8 %collective-permute-start.25 = (bf16[2,256,256]{2,1,0:T(8,128)(2,1)}, bf16[2,256,256]{2,1,0:T(8,128)(2,1)S(1)}, u32[]{:S(2)}, u32[]{:S(2)}) collective-permute-start(bf16[2,256,256]{2,1,0:T(8,128)(2,1)} %get-tuple-element.51), channel_id=1, source_target_pairs={{0,3},{1,2},{2,1},{3,0},{4,7},{5,6},{6,5},{7,4},{8,11},{9,10},{10,... | collective-permute-start | bytes 786440 | tf_op jit(solution)/shard_map/ppermute | solution.py:25
  161.8 9.7 %collective-permute-start.23 = (bf16[2,256,256]{2,1,0:T(8,128)(2,1)}, bf16[2,256,256]{2,1,0:T(8,128)(2,1)S(1)}, u32[]{:S(2)}, u32[]{:S(2)}) collective-permute-start(bf16[2,256,256]{2,1,0:T(8,128)(2,1)} %get-tuple-element.51), channel_id=1, source_target_pairs={{0,2},{2,0},{4,6},{6,4},{8,10},{10,8},{12,14},{14,12},{16,18},{18,... | collective-permute-start | bytes 786440 | tf_op jit(solution)/shard_map/ppermute | solution.py:20
  162.2 12.2 %collective-permute-start.24 = (bf16[2,256,256]{2,1,0:T(8,128)(2,1)}, bf16[2,256,256]{2,1,0:T(8,128)(2,1)S(1)}, u32[]{:S(2)}, u32[]{:S(2)}) collective-permute-start(bf16[2,256,256]{2,1,0:T(8,128)(2,1)} %get-tuple-element.52.refs_2_), channel_id=1, source_target_pairs={{0,1},{1,0},{2,3},{3,2},{4,5},{5,4},{6,7},{7,6},{8,9},{9,8},{10,11... | collective-permute-start | bytes 786440 | tf_op jit(solution)/shard_map/ppermute | solution.py:25
  171.5 3.0 %copy-start.8 = (bf16[2,256,256]{2,1,0:T(8,128)(2,1)}, bf16[2,256,256]{2,1,0:T(8,128)(2,1)S(1)}, u32[]{:S(2)}) copy-start(bf16[2,256,256]{2,1,0:T(8,128)(2,1)S(1)} %collective-permute-done.25.refs_4_) | copy-start | bytes 786436
  171.5 3.0 %copy-start.9 = (bf16[2,256,256]{2,1,0:T(8,128)(2,1)}, bf16[2,256,256]{2,1,0:T(8,128)(2,1)S(1)}, u32[]{:S(2)}) copy-start(bf16[2,256,256]{2,1,0:T(8,128)(2,1)S(1)} %collective-permute-done.23.refs_1_) | copy-start | bytes 786436
  174.5 0.7 copy-start.10

commit v3 on v2

--- a/solution.py
+++ b/solution.py
@@ -23,6 +23,22 @@
 def moved_both(array, n, f, go):
     pairs = [(i * f + k, go(i, k)[0] * f + go(i, k)[1]) for i in range(n) for k in range(f)]
     return lax.ppermute(array, ("ctx", "fsdp"), pairs)
+
+
+def behind(array, *others):
+    return lax.optimization_barrier((array,) + others)[0] if others else array
+
+
+def gated(array, tie):
+    return pl.pallas_call(
+        lambda *refs: None,
+        in_specs=[pl.BlockSpec(memory_space=pl.ANY)] * 2,
+        out_specs=pl.BlockSpec(memory_space=pl.ANY),
+        out_shape=jax.ShapeDtypeStruct(array.shape, array.dtype),
+        input_output_aliases={0: 0},
+        compiler_params=pltpu.CompilerParams(vmem_limit_bytes=VMEM),
+        cost_estimate=pl.CostEstimate(flops=0, bytes_accessed=0, transcendentals=0),
+    )(array, tie)
 
 
 def mask_table(first_block, rows, mask_rows):
@@ -43,72 +59,42 @@
     return jnp.pad(table, ((0, 0), (0, HD - table.shape[1])))
 
 
-def behind(array, *others):
-    return lax.optimization_barrier((array,) + others)[0]
-
-
-def cut_kernel(info, source, out):
-    out[...] = source[...]
-
-
-def cut_weight(info, out_weight, features, step):
-    half = out_weight.shape[0] // 2
-    tiles = 4 if half % 64 == 0 else 1
-    count = out_weight.shape[1] // features
+def copies(info, sources, outs, plan):
+    total = sum(math.prod(o.shape) for o in outs)
+
+    def kernel(info, *refs):
+        ins, rest = refs[:len(sources)], refs[len(sources):]
+        pairs = plan(info[0], info[2], ins, rest[:len(outs)])
+        started = [
+            pltpu.make_async_copy(a, b, rest[-1].at[k]) for k, (a, b) in enumerate(pairs)
+        ]
+        for copy in started:
+            copy.start()
+        for copy in started:
+            copy.wait()
+
     return pl.pallas_call(
-        cut_kernel,
+        kernel,
         grid_spec=pltpu.PrefetchScalarGridSpec(
             num_scalar_prefetch=1,
-            grid=(tiles,),
-            in_specs=[pl.BlockSpec(
-                (half // tiles, features),
-                lambda s, info: (info[0] * tiles + s, lax.rem(info[2] + step, count)),
-            )],
-            out_specs=pl.BlockSpec((half // tiles, features), lambda s, info: (s, 0)),
+            grid=(),
+            in_specs=[pl.BlockSpec(memory_space=pl.ANY)] * len(sources),
+            out_specs=[pl.BlockSpec(memory_space=pl.ANY)] * len(outs),
+            scratch_shapes=[pltpu.SemaphoreType.DMA((32,))],
         ),
-        out_shape=jax.ShapeDtypeStruct((half, features), out_weight.dtype),
+        out_shape=[jax.ShapeDtypeStruct(o.shape, o.dtype) for o in outs],
         compiler_params=pltpu.CompilerParams(vmem_limit_bytes=VMEM),
-        cost_estimate=pl.CostEstimate(
-            flops=0, bytes_accessed=4 * half * features, transcendentals=0
-        ),
-    )(info, out_weight)
-
-
-def join_kernel(info, here, got, out):
-    out[0] = here[:, 0]
-    out[1] = got[...]
-
-
-def join_pair(info, keys_values, got, first, heads, heads_half):
-    tokens = keys_values.shape[2]
-    return pl.pallas_call(
-        join_kernel,
-        grid_spec=pltpu.PrefetchScalarGridSpec(
-            num_scalar_prefetch=1,
-            grid=(heads,),
-            in_specs=[
-                pl.BlockSpec(
-                    (2, 1, tokens, HD),
-                    lambda h, info: (0, 0, 0, info[0] * heads_half + first + h),
-                ),
-                pl.BlockSpec((2, tokens, HD), lambda h, info: (0, 0, first + h)),
-            ],
-            out_specs=pl.BlockSpec((2, 2, tokens, HD), lambda h, info: (0, 0, 0, h)),
-        ),
-        out_shape=jax.ShapeDtypeStruct((2, 2, tokens, heads * HD), keys_values.dtype),
-        compiler_params=pltpu.CompilerParams(vmem_limit_bytes=VMEM),
-        cost_estimate=pl.CostEstimate(
-            flops=0, bytes_accessed=16 * tokens * heads * HD, transcendentals=0
-        ),
-    )(info, keys_values, got)
+        cost_estimate=pl.CostEstimate(flops=0, bytes_accessed=total, transcendentals=0),
+    )(info, *sources)
 
 
 def attend_kernel(tokens, count, info, *refs):
     core, side = info[0], info[1]
-    refs = refs[:6 + 4 * count] + refs[-4:]
+    refs = refs[:6 + 4 * count] + refs[-5:]
     q_here, kn_here, there, own, low = refs[:5]
     blocks = [refs[5 + 4 * h:9 + 4 * h] for h in range(count)]
-    table, mine, give, keys, values = refs[5 + 4 * count:]
+    table, mine, give, tie, keys, values = refs[5 + 4 * count:]
+    tie[...] = jnp.zeros_like(tie)
     rows = tokens // BLK
     span = WINB * BLK + tokens
     back = WINB * BLK // (2 * tokens)
@@ -185,7 +171,7 @@
 
 
 def attend(info, queries, keys_values, there, own, low, blocks, table, first, heads_half,
-           room, at, into):
+           room, at, into, after):
     tokens = queries.shape[1]
     span = WINB * BLK + 2 * tokens
     count = len(blocks)
@@ -210,23 +196,22 @@
                 whole, whole,
                 *[one_head] * (4 * count),
                 pl.BlockSpec(table.shape, lambda s, info: (0, 0, 0)),
-                *[pl.BlockSpec(memory_space=pl.ANY) for _ in into],
+                *[pl.BlockSpec(memory_space=pl.ANY)] * (len(into) + len(after)),
             ],
-            out_specs=[out_spec, out_spec],
+            out_specs=[out_spec, out_spec, pl.BlockSpec((8, HD), lambda s, info: (0, 0))],
             scratch_shapes=[
                 pltpu.VMEM((count, span, HD), jnp.bfloat16),
                 pltpu.VMEM((count, span, HD), jnp.bfloat16),
             ],
         ),
-        out_shape=[out, out],
+        out_shape=[out, out, jax.ShapeDtypeStruct((8, HD), jnp.float32)],
         input_output_aliases={7 + 4 * count + k: k for k in range(len(into))},
         compiler_params=pltpu.CompilerParams(vmem_limit_bytes=VMEM),
         cost_estimate=pl.CostEstimate(
             flops=work * 8, bytes_accessed=count * 64 * 1024, transcendentals=0
         ),
     )(info, queries, keys_values, there, own, low, *[b for group in blocks for b in group], table,
-      *into)
-
+      *into, *after)
 
 def project_kernel(count, groups, add, info, *refs):
     out = refs[-1]
@@ -241,38 +226,39 @@
 
 def project(info, pieces, weights, features, dtype, before=None):
     tokens = pieces[0][2].shape[1]
-    tile = min(256, features)
+    tile = min(512, features)
     steps = features // tile
-    half = weights[0].shape[0] // 2 // HD
-    used, rows = [], []
+    half = weights[0].shape[0] // 2
+    used, specs = [], []
     for group, first, act in pieces:
-        for head in range(first, first + act.shape[2] // HD):
-            used.append(weights[group])
-            if group == 0:
-                row = lambda s, info, at=head: (info[0] * half + at, info[2] * steps + s)
-            elif group == 1:
-                row = lambda s, info, at=head: ((1 - info[0]) * half + at, info[2] * steps + s)
-            else:
-                row = lambda s, info, at=head: (at, s)
-            rows.append(pl.BlockSpec((HD, tile), row))
+        wide = act.shape[2]
+        per, at = half // wide, first * HD // wide
+        used.append(weights[group])
+        if group == 0:
+            row = lambda s, info, at=at, per=per: (info[0] * per + at, info[2] * steps + s)
+        elif group == 1:
+            row = lambda s, info, at=at, per=per: ((1 - info[0]) * per + at, info[2] * steps + s)
+        else:
+            row = lambda s, info, at=at: (at, s)
+        specs.append(pl.BlockSpec((wide, tile), row))
     flat = [act for _, _, act in pieces]
     spec = pl.BlockSpec((2, tokens, tile), lambda s, info: (0, 0, s))
-    specs = [pl.BlockSpec(a.shape, lambda s, info: (0, 0, 0)) for a in flat] + rows
+    specs = [pl.BlockSpec(a.shape, lambda s, info: (0, 0, 0)) for a in flat] + specs
     operands = flat + used
     if before is not None:
         specs.append(spec)
         operands.append(before)
-    depth = HD * len(used)
+    depth = sum(a.shape[2] for a in flat)
     return pl.pallas_call(
         lambda *refs: project_kernel(len(flat), len(used), before is not None, *refs),
         grid_spec=pltpu.PrefetchScalarGridSpec(
             num_scalar_prefetch=1, grid=(steps,), in_specs=specs, out_specs=spec
         ),
         out_shape=jax.ShapeDtypeStruct((2, tokens, features), dtype),
-        compiler_params=pltpu.CompilerParams(vmem_limit_bytes=VMEM),
+        compiler_params=pltpu.CompilerParams(vmem_limit_bytes=40 * 1024 * 1024),
         cost_estimate=pl.CostEstimate(
-            flops=2 * 2 * tokens * depth * features,
-            bytes_accessed=2 * depth * features + 8 * tokens * features,
+            flops=2 * 2 * tokens * depth * features // 8,
+            bytes_accessed=2 * depth * features // 8,
             transcendentals=0,
         ),
     )(info, *operands)
@@ -288,6 +274,7 @@
     heads_half = width // HD
     rows = tokens // BLK
     features = out_weight.shape[1] // f
+    bf16 = jnp.bfloat16
     shares = [[0, 1], [2, 3]] if heads_half == 4 else [[h] for h in range(heads_half)]
 
     pair = lambda i: i ^ 1
@@ -295,65 +282,96 @@
     across = lambda i: i ^ 2
     upper = lambda i: i + 2 if i & 2 == 0 else None
     lower = lambda i: i - 2 if i & 2 else None
-
-    clean = lax.dynamic_slice(
-        keys_values, (0, 0, 0, (1 - core) * width), (2, 1, tokens, width)
-    ).reshape(2, tokens, width)
+    lanes = lambda start, size: pl.ds(pl.multiple_of(start, HD), size)
+
+    def cut_clean(core, place, ins, outs):
+        return [(ins[0].at[:, 0, :, lanes((1 - core) * width, width)], outs[0])]
+
+    clean, = copies(info, [keys_values], [jax.ShapeDtypeStruct((2, tokens, width), bf16)], cut_clean)
     got = moved(clean, n, pair)
-    own = [join_pair(info, keys_values, got, h, 1, heads_half) for h in range(1)]
-    own.append(join_pair(info, keys_values, got, 0, heads_half, heads_half))
-    own, whole = own[:1], own[1]
-    for h in range(1, heads_half):
-        own.append(join_pair(info, keys_values, got, h, 1, heads_half))
-
-    low = moved(whole, n, upper)
+
+    def join(head, heads, kv, got, out):
+        def pairs(core):
+            return [
+                (kv.at[:, 0, :, lanes(core * width + head * HD, heads * HD)], out.at[0]),
+                (got.at[:, :, head * HD:(head + heads) * HD], out.at[1]),
+            ]
+        return pairs
+
+    pair_shape = lambda heads: jax.ShapeDtypeStruct((2, 2, tokens, heads * HD), bf16)
+    first, = copies(
+        info, [keys_values, got], [pair_shape(1)],
+        lambda core, place, ins, outs: join(0, 1, ins[0], ins[1], outs[0])(core),
+    )
+    one = moved(first, n, ahead)
+
+    def cut_rest(core, place, ins, outs):
+        kv, got, q, w, _ = ins
+        give = lanes((1 - core) * width, width)
+        plan = join(0, heads_half, kv, got, outs[0])(core)
+        for h in range(1, heads_half):
+            plan += join(h, 1, kv, got, outs[h])(core)
+        plan += [(q.at[:, :, give], outs[heads_half].at[0:2]),
+                 (kv.at[:, 1, :, give], outs[heads_half].at[2:4])]
+        for r in range(1, f):
+            out = outs[heads_half + r]
+            column = pl.multiple_of(lax.rem(place + r, f) * features, HD)
+            pieces = max(1, 4 // f)
+            step = width // pieces
+            for p in range(pieces):
+                row = pl.multiple_of(core * width + p * step, step)
+                plan.append((w.at[pl.ds(row, step), pl.ds(column, features)],
+                             out.at[p * step:(p + 1) * step]))
+        return plan
+
+    whole, *rest = copies(
+        info, [keys_values, got, queries, out_weight, first],
+        [pair_shape(heads_half)] + [pair_shape(1)] * (heads_half - 1)
+        + [jax.ShapeDtypeStruct((4, tokens, width), bf16)]
+        + [jax.ShapeDtypeStruct((width, features), bf16)] * (f - 1),
+        cut_rest,
+    )
+    own = [first] + rest[:heads_half - 1]
+    later, panels = rest[heads_half - 1], rest[heads_half:]
+
+    sames = [
+        moved_both(panel, n, f, lambda i, k: (i, (k + r) % f))
+        for r, panel in enumerate(panels, 1)
+    ]
+
     blocks = []
     for h in range(heads_half):
         last = blocks[-1] if blocks else None
         in_turn = lambda array, k: behind(array, last[k]) if last else array
-        one = moved(in_turn(own[h], 0), n, ahead)
+        if h:
+            one = moved(in_turn(own[h], 0), n, ahead)
         two = moved(in_turn(one, 1), n, ahead)
         swap = moved(in_turn(one, 2), n, across)
         far = moved(in_turn(two, 3), n, lower)
         blocks.append((one, two, swap, far))
-
-    later = jnp.concatenate(
-        [lax.dynamic_slice(queries, (0, 0, (1 - core) * width), (2, tokens, width)),
-         lax.dynamic_slice(
-             keys_values, (0, 1, 0, (1 - core) * width), (2, 1, tokens, width)
-         ).reshape(2, tokens, width)], 0
-    )
-    there = moved(behind(later, own[0]), n, pair)
-    mask_there = moved(behind(block_mask, own[0]), n, pair)
+    low = moved(whole, n, upper)
+    there = moved(later, n, pair)
+    mask_there = moved(behind(block_mask, first), n, pair)
     table = jnp.stack([
         mask_table(index * rows, rows, block_mask),
         mask_table((index ^ 1) * rows, rows, mask_there),
     ])
 
-    sames = [
-        moved_both(
-            cut_weight(behind(info, own[0]), out_weight, features, r),
-            n, f, lambda i, k: (i, (k + r) % f),
-        )
-        for r in range(1, f)
-    ]
-
     acts = [[] for _ in range(2 * f)]
+    ties = []
     for k, share in enumerate(shares):
         final = k == len(shares) - 1
-        runs = [[h] for h in share] if final else [share]
         into = ()
-        for run in runs:
-            if run[-1] < heads_half - 1:
-                after = [blocks[-1][1 if final else 0]]
-            else:
-                after = [a[0] for a in acts[1:] if a]
-            into = attend(
-                behind(info, *after, *into, *acts[0][-1:]), queries, keys_values, there, whole, low,
+        for run in [[h] for h in share] if final else [share]:
+            after = ([blocks[-1][0], blocks[-2][1]] if not final else [blocks[-1][1]]) \
+                if run[-1] < heads_half - 1 else [a[0] for a in acts[1:] if a]
+            mine, give, tie = attend(
+                info, queries, keys_values, there, whole, low,
                 [blocks[h] for h in run], table, run[0], heads_half,
-                len(share), run[0] - share[0], into,
+                len(share), run[0] - share[0], into, after + ties[-1:],
             )
-        mine, give = into
+            into = (mine, give)
+            ties.append(tie)
         acts[0].append(mine)
         for r in range(1, f):
             acts[2 * r].append(moved_both(mine, n, f, lambda i, k: (i, (k + r) % f)))
@@ -361,14 +379,14 @@
         acts[1].append(moved(give, n, pair))
     others = []
     for same in sames:
-        same = behind(same, blocks[-1][3])
+        same = gated(same, ties[-1])
         others += [same, moved(same, n, pair)]
 
     weights = [out_weight, out_weight] + others
     early, late = [], []
     for g in range(2 * f):
         for k, (share, act) in enumerate(zip(shares, acts[g])):
-            (late if g % 2 and g > 1 or g and k == len(shares) - 1 else early).append((g, share[0], act))
+            (late if g and k == len(shares) - 1 else early).append((g, share[0], act))
     before = project(info, early, weights, features, jnp.float32)
     return project(info, late, weights, features, jnp.bfloat16, before)
 

time: 186 us -> 306 us (1.65)
  Pallas kernels: 59.5 us -> 214 us
  waiting for transfers between devices: 63.6 us -> 27.4 us
    pallas_call x6 -> x4, Pallas kernels: 18.3 us -> 181 us  [the longest x3 181 us: copies(): pl.pallas_call(kernel, grid_spec=pltpu.PrefetchScalarGridSpec(num_scalar_...]
    ppermute x23, waiting for transfers between devices: 56.8 us -> 19.6 us  [moved(): return lax.ppermute(array, 'ctx', pairs)]
    pallas_call x2, Pallas kernels: 18.9 us -> 11 us  [project(): pl.pallas_call(lambda *refs: project_kernel(len(flat), len(used), before...]
    ppermute x23, starting transfers between devices: 46 us -> 49.8 us  [moved(): return lax.ppermute(array, 'ctx', pairs)]
    unnamed x40 -> x50, local copies, waits for them, and re-layouts: 3.88 us -> 6.65 us
  transfers between devices with their start and end apart: 28 -> 28, of which waited for: 12 -> 11; matrix products, arithmetic and copies ran while one was open for 2% -> 0% of each run, Pallas kernels for 23% -> 59%
where the time goes in v3:
time: 306 us; the launch traced here: 305 us
  Pallas kernels  214 us (70%)
  starting transfers between devices  54.3 us (18%)
  waiting for transfers between devices  27.4 us (9%)
  local copies, waits for them, and re-layouts  6.86 us (2%)
    pallas_call x3, Pallas kernels, copies(): pl.pallas_call(kernel, grid_spec=pltpu.PrefetchScalarGridSpec(num_scalar_...  181 us
    ppermute x23, starting transfers between devices, moved(): return lax.ppermute(array, 'ctx', pairs)  49.8 us
    pallas_call x3, Pallas kernels, attend(): pl.pallas_call(lambda *refs: attend_kernel(tokens, count, *refs), grid_sp...  22.4 us
    ppermute x23, waiting for transfers between devices, moved(): return lax.ppermute(array, 'ctx', pairs)  19.6 us
    pallas_call x2, Pallas kernels, project(): pl.pallas_call(lambda *refs: project_kernel(len(flat), len(used), before...  11 us
    ppermute x5, waiting for transfers between devices, moved_both(): return lax.ppermute(array, ('ctx', 'fsdp'), pairs)  7.83 us
    unnamed x50, local copies, waits for them, and re-layouts  6.65 us
  transfers between devices with their start and end apart: 28, of which 11 were waited for; matrix products, arithmetic and copies ran while one was open for 0% of the time, Pallas kernels for 59%

profile of v3, /device:TPU:0, one launch (start us, length us, event | category | flops | bytes accessed | tf_op | source)
XLA Modules:
  0.0 304.8 jit_solution(8184825035111275064)
XLA Ops:
  0.6 17.9 %shard_map.46 = bf16[2,256,512]{2,1,0:T(8,128)(2,1)} custom-call(s32[3]{0:T(128)} %pad_add_fusion.2.info.refs_0_, bf16[2,2,256,1024]{3,2,1,0:T(8,128)(2,1)} %refs_2_.7), custom_call_target="tpu_custom_call" | custom-call | bytes 262144 | tf_op jit(solution)/shard_map/pallas_call | solution.py:76
  19.0 1.7 collective-permute-done.refs_1_
  20.8 0.8 copy-done.12
  21.6 10.0 %shard_map.47.refs_4_ = bf16[2,2,256,128]{3,2,1,0:T(8,128)(2,1)} custom-call(s32[3]{0:T(128)} %pad_add_fusion.2.info.refs_0_, bf16[2,2,256,1024]{3,2,1,0:T(8,128)(2,1)} %refs_2_.7, bf16[2,256,512]{2,1,0:T(8,128)(2,1)} %copy-done.12), custom_call_target="tpu_custom_call" | custom-call | bytes 131072 | tf_op jit(solution)/shard_map/pallas_call | solution.py:76
  31.6 4.9 %collective-permute-start.3 = (bf16[2,2,256,128]{3,2,1,0:T(8,128)(2,1)}, bf16[2,2,256,128]{3,2,1,0:T(8,128)(2,1)S(1)}, u32[]{:S(2)}, u32[]{:S(2)}) collective-permute-start(bf16[2,2,256,128]{3,2,1,0:T(8,128)(2,1)} %shard_map.47.refs_4_), channel_id=1, source_target_pairs={{0,8},{2,10},{4,12},{6,14},{8,16},{10,18},{12,20},{14,22},{16,24},... | collective-permute-start | bytes 786440 | tf_op jit(solution)/shard_map/ppermute | solution.py:20
  36.5 152.9 %shard_map.48 = (bf16[2,2,256,512]{3,2,1,0:T(8,128)(2,1)}, bf16[2,2,256,128]{3,2,1,0:T(8,128)(2,1)}, bf16[2,2,256,128]{3,2,1,0:T(8,128)(2,1)}, bf16[2,2,256,128]...) custom-call(s32[3]{0:T(128)} %pad_add_fusion.2.info.refs_0_, ...), custom_call_target="tpu_custom_call" | custom-call | bytes 2490368 | tf_op jit(solution)/shard_map/pallas_call | solution.py:76
  189.5 3.5 %collective-permute-start.4 = (bf16[2,2,256,128]{3,2,1,0:T(8,128)(2,1)}, bf16[2,2,256,128]{3,2,1,0:T(8,128)(2,1)S(1)}, u32[]{:S(2)}, u32[]{:S(2)}) collective-permute-start(bf16[2,2,256,128]{3,2,1,0:T(8,128)(2,1)} %get-tuple-element.38), channel_id=1, source_target_pairs={{0,8},{2,10},{4,12},{6,14},{8,16},{10,18},{12,20},{14,22},{16,24},... | collective-permute-start | bytes 786440 | tf_op jit(solution)/shard_map/ppermute | solution.py:20
  193.0 1.6 collective-permute-start.26
  194.6 1.5 collective-permute-start.11
  196.1 3.5 %collective-permute-start.7 = (bf16[2,2,256,128]{3,2,1,0:T(8,128)(2,1)S(1)}, bf16[2,2,256,128]{3,2,1,0:T(8,128)(2,1)S(1)}, u32[]{:S(2)}, u32[]{:S(2)}) collective-permute-start(bf16[2,2,256,128]{3,2,1,0:T(8,128)(2,1)S(1)} %collective-permute-done.3.refs_6_), channel_id=1, source_target_pairs={{0,8},{2,10},{4,12},{6,14},{8,16},{10,18},{12,20},{14,22},{16,24},... | collective-permute-start | bytes 786440 | tf_op jit(solution)/shard_map/ppermute | solution.py:20
  199.6 4.6 %collective-permute-start.5 = (bf16[2,2,256,128]{3,2,1,0:T(8,128)(2,1)}, bf16[2,2,256,128]{3,2,1,0:T(8,128)(2,1)}, u32[]{:S(2)}, u32[]{:S(2)}) collective-permute-start(bf16[2,2,256,128]{3,2,1,0:T(8,128)(2,1)} %get-tuple-element.39), channel_id=1, source_target_pairs={{0,8},{2,10},{4,12},{6,14},{8,16},{10,18},{12,20},{14,22},{16,24},... | collective-permute-start | bytes 786440 | tf_op jit(solution)/shard_map/ppermute | solution.py:20
  204.3 0.7 copy-done.19
  205.4 0.8 collective-permute-done.7.refs_7_
  206.2 4.4 %collective-permute-start.8 = (bf16[2,2,256,128]{3,2,1,0:T(8,128)(2,1)}, bf16[2,2,256,128]{3,2,1,0:T(8,128)(2,1)S(1)}, u32[]{:S(2)}, u32[]{:S(2)}) collective-permute-start(bf16[2,2,256,128]{3,2,1,0:T(8,128)(2,1)} %copy-done.18), channel_id=1, source_target_pairs={{0,8},{2,10},{4,12},{6,14},{8,16},{10,18},{12,20},{14,22},{16,24},... | collective-permute-start | bytes 786440 | tf_op jit(solution)/shard_map/ppermute | solution.py:20
  210.6 0.6 collective-permute-start.12
  211.3 1.3 collective-permute-start.15
  212.7 3.0 collective-permute-done.8.refs_11_
  215.7 4.4 %collective-permute-start.2 = (bf16[2,2,256,512]{3,2,1,0:T(8,128)(2,1)}, bf16[2,2,256,512]{3,2,1,0:T(8,128)(2,1)}, u32[]{:S(2)}, u32[]{:S(2)}) collective-permute-start(bf16[2,2,256,512]{3,2,1,0:T(8,128)(2,1)} %get-tuple-element.34.refs_4_), channel_id=1, source_target_pairs={{0,4},{2,6},{8,12},{10,14},{16,20},{18,22},{24,28},{26,30},{1,5},{... | collective-permute-start | bytes 3145736 | tf_op jit(solution)/shard_map/ppermute | solution.py:20
  220.0 2.9 collective-permute-done.15.refs_9_
  222.9 2.7 collective-permute-start.6
  225.6 0.7 copy-done.22
  226.3 2.9 collective-permute-start.9
  229.5 2.8 collective-permute-done.6.refs_15_.refs_6_
  232.3 1.3 collective-permute-start.16
  233.6 1.8 collective-permute-done.9.refs_16_.refs_7_
  235.4 1.5 collective-permute-start.13
  237.0 4.5 %collective-permute-done.16.refs_13_ = bf16[2,2,256,128]{3,2,1,0:T(8,128)(2,1)} collective-permute-done((bf16[2,2,256,128]{3,2,1,0:T(8,128)(2,1)}, bf16[2,2,256,128]{3,2,1,0:T(8,128)(2,1)}, u32[]{:S(2)}, u32[]{:S(2)}) %collective-permute-start.16) | collective-permute-done | bytes 262176 | tf_op jit(solution)/shard_map/ppermute | solution.py:20
  241.5 4.4 %collective-permute-start.10 = (bf16[2,2,256,128]{3,2,1,0:T(8,128)(2,1)S(1)}, bf16[2,2,256,128]{3,2,1,0:T(8,128)(2,1)S(1)}, u32[]{:S(2)}, u32[]{:S(2)}) collective-permute-start(bf16[2,2,256,128]{3,2,1,0:T(8,128)(2,1)S(1)} %collective-permute-done.6.refs_15_.refs_6_), channel_id=1, source_target_pairs={{0,8},{2,10},{4,12},{6,14},{8,16},{10,18},{12,20},{14,22},{16,24},... | collective-permute-start | bytes 786440 | tf_op jit(solution)/shard_map/ppermute | solution.py:20
  245.9 0.7 collective-permute-done.13.refs_8_
  246.6 1.3 collective-permute-start.17
  247.9 3.3 %collective-permute-start.14 = (bf16[2,2,256,128]{3,2,1,0:T(8,128)(2,1)S(1)}, bf16[2,2,256,128]{3,2,1,0:T(8,128)(2,1)}, u32[]{:S(2)}, u32[]{:S(2)}) collective-permute-start(bf16[2,2,256,128]{3,2,1,0:T(8,128)(2,1)S(1)} %collective-permute-done.6.refs_15_.refs_6_), channel_id=1, source_target_pairs={{0,4},{2,6},{4,0},{6,2},{8,12},{10,14},{12,8},{14,10},{16,20},{18,... | collective-permute-start | bytes 786440 | tf_op jit(solution)/shard_map/ppermute | solution.py:20
  251.3 0.6 pad_maximum_fusion.refs_14_.refs_10_
  251.9 10.0 %shard_map.49 = (bf16[2,256,256]{2,1,0:T(8,128)(2,1)}, bf16[2,256,256]{2,1,0:T(8,128)(2,1)}, f32[8,128]{1,0:T(8,128)}) custom-call(s32[3]{0:T(128)} %pad_add_fusion.2.info.refs_0_, bf16[2,256,1024]{2,1,0:T(8,128)(2,1)} %refs_1_.5, bf16[2,2,256,1024]{3,2,1,0:T(8,128)(2,1)} %refs_2_.7, bf16[4,256,512]{2,1,0:T(8,128)(2,1)} %copy-done.11, ...), custom_call_target="tpu_custom_call" | custom-call | flops 41943040 | bytes 131072 | tf_op jit(solution)/shard_map/pallas_call | solution.py:187
  261.9 1.4 collective-permute-start.20
  263.3 0.7 collective-permute-start.21
  264.0 1.3 collective-permute-start.18
  265.3 6.3 %shard_map.50 = (bf16[2,256,256]{2,1,0:T(8,128)(2,1)}, bf16[2,256,256]{2,1,0:T(8,128)(2,1)}, f32[8,128]{1,0:T(8,128)}) custom-call(s32[3]{0:T(128)} %pad_add_fusion.2.info.refs_0_, bf16[2,256,1024]{2,1,0:T(8,128)(2,1)} %refs_1_.5, bf16[2,2,256,1024]{3,2,1,0:T(8,128)(2,1)} %refs_2_.7, bf16[4,256,512]{2,1,0:T(8,128)(2,1)} %copy-done.11, ...), custom_call_target="tpu_custom_call" | custom-call | flops 20971520 | bytes 65536 | tf_op jit(solution)/shard_map/pallas_call | solution.py:187
  271.6 4.5 %collective-permute-done.21.refs_14_.refs_4_ = bf16[2,256,256]{2,1,0:T(8,128)(2,1)S(1)} collective-permute-done((bf16[2,256,256]{2,1,0:T(8,128)(2,1)}, bf16[2,256,256]{2,1,0:T(8,128)(2,1)S(1)}, u32[]{:S(2)}, u32[]{:S(2)}) %collective-permute-start.21) | collective-permute-done | bytes 262176 | tf_op jit(solution)/shard_map/ppermute | solution.py:25
  276.1 0.7 copy-done.6
  276.9 6.1 %shard_map.51 = (bf16[2,256,256]{2,1,0:T(8,128)(2,1)}, bf16[2,256,256]{2,1,0:T(8,128)(2,1)}, f32[8,128]{1,0:T(8,128)}) custom-call(s32[3]{0:T(128)} %pad_add_fusion.2.info.refs_0_, bf16[2,256,1024]{2,1,0:T(8,128)(2,1)} %refs_1_.5, bf16[2,2,256,1024]{3,2,1,0:T(8,128)(2,1)} %refs_2_.7, ...), custom_call_target="tpu_custom_call", output_to_operand_aliasing={{0}: (11, {}), {1}: (12, {})} | custom-call | flops 20971520 | bytes 65536 | tf_op jit(solution)/shard_map/pallas_call | solution.py:187
  283.0 1.3 copy-done
  284.6 0.7 copy-done.16
  285.5 1.9 collective-permute-start.24
  287.4 1.4 collective-permute-done.27.refs_10_.refs_6_
  288.9 1.6 copy-done.1
  290.4 5.7 %shard_map.53.refs_7_ = f32[2,256,2048]{2,1,0:T(8,128)S(1)} custom-call(s32[3]{0:T(128)S(1)} %copy-done.10, bf16[2,256,256]{2,1,0:T(8,128)(2,1)S(1)} %copy-done.9, bf16[2,256,256]{2,1,0:T(8,128)(2,1)S(1)} %copy-done.8, bf16[2,256,256]{2,1,0:T(8,128)(2,1)S(1)} %copy-done.5, bf16[2,256,256]{2,1,0:T(8,128)(2,1)S(1)} %copy-done.7, ...), custom_call_target="tpu_custom_call" | custom-call | flops 335544320 | bytes 655360 | tf_op jit(solution)/shard_map/pallas_call | solution.py:252
  296.1 3.4 %collective-permute-done.24.refs_2_ = bf16[2,256,256]{2,1,0:T(8,128)(2,1)S(1)} collective-permute-done((bf16[2,256,256]{2,1,0:T(8,128)(2,1)S(1)}, bf16[2,256,256]{2,1,0:T(8,128)(2,1)S(1)}, u32[]{:S(2)}, u32[]{:S(2)}) %collective-permute-start.24) | collective-permute-done | bytes 262176 | tf_op jit(solution)/shard_map/ppermute | solution.py:25
  299.5 5.3 %shard_map.54 = bf16[2,256,2048]{2,1,0:T(8,128)(2,1)} custom-call(s32[3]{0:T(128)S(1)} %copy-done.10, bf16[2,256,256]{2,1,0:T(8,128)(2,1)S(1)} %collective-permute-done.23.refs_1_, bf16[2,256,256]{2,1,0:T(8,128)(2,1)S(1)} %collective-permute-done.24.refs_2_, bf16[2,256,256]{2,1,0:T(8,128)(2,1)S(1)} %collective-permute-done.25.refs_3_, ...), custom_call_target="tpu_custom_call" | custom-call | flops 201326592 | bytes 393216 | tf_op jit(solution)/shard_map/pallas_call | solution.py:252
  (84 shorter events, 2.8 us)
Async XLA Ops:
  18.5 2.3 collective-permute-start
  31.6 161.3 %copy-start.24 = (s32[4,32]{1,0:T(4,128)S(1)}, s32[4,32]{1,0:T(4,128)}, u32[]{:S(2)}) copy-start(s32[4,32]{1,0:T(4,128)} %param.6) | copy-start | bytes 1540
  31.6 157.8 %collective-permute-start.3 = (bf16[2,2,256,128]{3,2,1,0:T(8,128)(2,1)}, bf16[2,2,256,128]{3,2,1,0:T(8,128)(2,1)S(1)}, u32[]{:S(2)}, u32[]{:S(2)}) collective-permute-start(bf16[2,2,256,128]{3,2,1,0:T(8,128)(2,1)} %shard_map.47.refs_4_), channel_id=1, source_target_pairs={{0,8},{2,10},{4,12},{6,14},{8,16},{10,18},{12,20},{14,22},{16,24},... | collective-permute-start | bytes 786440 | tf_op jit(solution)/shard_map/ppermute | solution.py:20
  189.4 30.6 %copy-start.17 = (bf16[2,2,256,128]{3,2,1,0:T(8,128)(2,1)}, bf16[2,2,256,128]{3,2,1,0:T(8,128)(2,1)S(1)}, u32[]{:S(2)}) copy-start(bf16[2,2,256,128]{3,2,1,0:T(8,128)(2,1)S(1)} %collective-permute-done.3.refs_6_) | copy-start | bytes 786436
  189.5 10.1 %collective-permute-start.4 = (bf16[2,2,256,128]{3,2,1,0:T(8,128)(2,1)}, bf16[2,2,256,128]{3,2,1,0:T(8,128)(2,1)S(1)}, u32[]{:S(2)}, u32[]{:S(2)}) collective-permute-start(bf16[2,2,256,128]{3,2,1,0:T(8,128)(2,1)} %get-tuple-element.38), channel_id=1, source_target_pairs={{0,8},{2,10},{4,12},{6,14},{8,16},{10,18},{12,20},{14,22},{16,24},... | collective-permute-start | bytes 786440 | tf_op jit(solution)/shard_map/ppermute | solution.py:20
  193.0 90.0 %collective-permute-start.26 = (bf16[512,2048]{1,0:T(8,128)(2,1)}, bf16[512,2048]{1,0:T(8,128)(2,1)S(1)}, u32[]{:S(2)}, u32[]{:S(2)}) collective-permute-start(bf16[512,2048]{1,0:T(8,128)(2,1)} %get-tuple-element.59), channel_id=1, source_target_pairs={{0,1},{1,0},{2,3},{3,2},{4,5},{5,4},{6,7},{7,6},{8,9},{9,8},{10,11... | collective-permute-start | bytes 6291464 | tf_op jit(solution)/shard_map/ppermute | solution.py:25
  194.6 9.7 %collective-permute-start.11 = (bf16[2,2,256,128]{3,2,1,0:T(8,128)(2,1)S(1)}, bf16[2,2,256,128]{3,2,1,0:T(8,128)(2,1)S(1)}, u32[]{:S(2)}, u32[]{:S(2)}) collective-permute-start(bf16[2,2,256,128]{3,2,1,0:T(8,128)(2,1)S(1)} %collective-permute-done.3.refs_6_), channel_id=1, source_target_pairs={{0,4},{2,6},{4,0},{6,2},{8,12},{10,14},{12,8},{14,10},{16,20},{18,... | collective-permute-start | bytes 786440 | tf_op jit(solution)/shard_map/ppermute | solution.py:20
  196.1 10.1 %collective-permute-start.7 = (bf16[2,2,256,128]{3,2,1,0:T(8,128)(2,1)S(1)}, bf16[2,2,256,128]{3,2,1,0:T(8,128)(2,1)S(1)}, u32[]{:S(2)}, u32[]{:S(2)}) collective-permute-start(bf16[2,2,256,128]{3,2,1,0:T(8,128)(2,1)S(1)} %collective-permute-done.3.refs_6_), channel_id=1, source_target_pairs={{0,8},{2,10},{4,12},{6,14},{8,16},{10,18},{12,20},{14,22},{16,24},... | collective-permute-start | bytes 786440 | tf_op jit(solution)/shard_map/ppermute | solution.py:20
  199.6 4.7 %copy-start.18 = (bf16[2,2,256,128]{3,2,1,0:T(8,128)(2,1)}, bf16[2,2,256,128]{3,2,1,0:T(8,128)(2,1)S(1)}, u32[]{:S(2)}) copy-start(bf16[2,2,256,128]{3,2,1,0:T(8,128)(2,1)S(1)} %collective-permute-done.4.refs_10_) | copy-start | bytes 786436
  199.6 11.7 %collective-permute-start.5 = (bf16[2,2,256,128]{3,2,1,0:T(8,128)(2,1)}, bf16[2,2,256,128]{3,2,1,0:T(8,128)(2,1)}, u32[]{:S(2)}, u32[]{:S(2)}) collective-permute-start(bf16[2,2,256,128]{3,2,1,0:T(8,128)(2,1)} %get-tuple-element.39), channel_id=1, source_target_pairs={{0,8},{2,10},{4,12},{6,14},{8,16},{10,18},{12,20},{14,22},{16,24},... | collective-permute-start | bytes 786440 | tf_op jit(solution)/shard_map/ppermute | solution.py:20
  204.2 6.4 %collective-permute-start.19 = (s32[4,32]{1,0:T(4,128)S(1)}, s32[4,32]{1,0:T(4,128)S(1)}, u32[]{:S(2)}, u32[]{:S(2)}) collective-permute-start(s32[4,32]{1,0:T(4,128)S(1)} %copy-done.24), channel_id=1, source_target_pairs={{0,2},{2,0},{4,6},{6,4},{8,10},{10,8},{12,14},{14,12},{16,18},{18,... | collective-permute-start | bytes 1544 | tf_op jit(solution)/shard_map/ppermute | solution.py:20
  205.0 42.9 %collective-permute-start.1 = (bf16[4,256,512]{2,1,0:T(8,128)(2,1)}, bf16[4,256,512]{2,1,0:T(8,128)(2,1)S(1)}, u32[]{:S(2)}, u32[]{:S(2)}) collective-permute-start(bf16[4,256,512]{2,1,0:T(8,128)(2,1)} %get-tuple-element.33), channel_id=1, source_target_pairs={{0,2},{2,0},{4,6},{6,4},{8,10},{10,8},{12,14},{14,12},{16,18},{18,... | collective-permute-start | bytes 3145736 | tf_op jit(solution)/shard_map/ppermute | solution.py:20
  206.2 16.7 %copy-start.20 = (bf16[2,2,256,128]{3,2,1,0:T(8,128)(2,1)}, bf16[2,2,256,128]{3,2,1,0:T(8,128)(2,1)S(1)}, u32[]{:S(2)}) copy-start(bf16[2,2,256,128]{3,2,1,0:T(8,128)(2,1)S(1)} %collective-permute-done.7.refs_7_) | copy-start | bytes 786436
  206.2 9.5 %collective-permute-start.8 = (bf16[2,2,256,128]{3,2,1,0:T(8,128)(2,1)}, bf16[2,2,256,128]{3,2,1,0:T(8,128)(2,1)S(1)}, u32[]{:S(2)}, u32[]{:S(2)}) collective-permute-start(bf16[2,2,256,128]{3,2,1,0:T(8,128)(2,1)} %copy-done.18), channel_id=1, source_target_pairs={{0,8},{2,10},{4,12},{6,14},{8,16},{10,18},{12,20},{14,22},{16,24},... | collective-permute-start | bytes 786440 | tf_op jit(solution)/shard_map/ppermute | solution.py:20
  210.6 15.0 %collective-permute-start.12 = (bf16[2,2,256,128]{3,2,1,0:T(8,128)(2,1)}, bf16[2,2,256,128]{3,2,1,0:T(8,128)(2,1)S(1)}, u32[]{:S(2)}, u32[]{:S(2)}) collective-permute-start(bf16[2,2,256,128]{3,2,1,0:T(8,128)(2,1)} %copy-done.18), channel_id=1, source_target_pairs={{0,4},{2,6},{4,0},{6,2},{8,12},{10,14},{12,8},{14,10},{16,20},{18,... | collective-permute-start | bytes 786440 | tf_op jit(solution)/shard_map/ppermute | solution.py:20
  211.3 11.6 %collective-permute-start.15 = (bf16[2,2,256,128]{3,2,1,0:T(8,128)(2,1)S(1)}, bf16[2,2,256,128]{3,2,1,0:T(8,128)(2,1)S(1)}, u32[]{:S(2)}, u32[]{:S(2)}) collective-permute-start(bf16[2,2,256,128]{3,2,1,0:T(8,128)(2,1)S(1)} %collective-permute-done.7.refs_7_), channel_id=1, source_target_pairs={{4,0},{6,2},{12,8},{14,10},{20,16},{22,18},{28,24},{30,26},{5,1},{... | collective-permute-start | bytes 786440 | tf_op jit(solution)/shard_map/ppermute | solution.py:20
  215.7 9.9 %copy-start.21 = (bf16[2,2,256,128]{3,2,1,0:T(8,128)(2,1)}, bf16[2,2,256,128]{3,2,1,0:T(8,128)(2,1)S(1)}, u32[]{:S(2)}) copy-start(bf16[2,2,256,128]{3,2,1,0:T(8,128)(2,1)S(1)} %collective-permute-done.8.refs_11_) | copy-start | bytes 786436
  215.7 36.2 %collective-permute-start.2 = (bf16[2,2,256,512]{3,2,1,0:T(8,128)(2,1)}, bf16[2,2,256,512]{3,2,1,0:T(8,128)(2,1)}, u32[]{:S(2)}, u32[]{:S(2)}) collective-permute-start(bf16[2,2,256,512]{3,2,1,0:T(8,128)(2,1)} %get-tuple-element.34.refs_4_), channel_id=1, source_target_pairs={{0,4},{2,6},{8,12},{10,14},{16,20},{18,22},{24,28},{26,30},{1,5},{... | collective-permute-start | bytes 3145736 | tf_op jit(solution)/shard_map/ppermute | solution.py:20
  222.9 6.3 %copy-start.23 = (bf16[2,2,256,128]{3,2,1,0:T(8,128)(2,1)}, bf16[2,2,256,128]{3,2,1,0:T(8,128)(2,1)S(1)}, u32[]{:S(2)}) copy-start(bf16[2,2,256,128]{3,2,1,0:T(8,128)(2,1)S(1)} %collective-permute-done.15.refs_9_) | copy-start | bytes 786436
  222.9 9.4 %collective-permute-start.6 = (bf16[2,2,256,128]{3,2,1,0:T(8,128)(2,1)}, bf16[2,2,256,128]{3,2,1,0:T(8,128)(2,1)S(1)}, u32[]{:S(2)}, u32[]{:S(2)}) collective-permute-start(bf16[2,2,256,128]{3,2,1,0:T(8,128)(2,1)} %get-tuple-element.40), channel_id=1, source_target_pairs={{0,8},{2,10},{4,12},{6,14},{8,16},{10,18},{12,20},{14,22},{16,24},... | collective-permute-start | bytes 786440 | tf_op jit(solution)/shard_map/ppermute | solution.py:20
  226.3 9.1 %collective-permute-start.9 = (bf16[2,2,256,128]{3,2,1,0:T(8,128)(2,1)}, bf16[2,2,256,128]{3,2,1,0:T(8,128)(2,1)}, u32[]{:S(2)}, u32[]{:S(2)}) collective-permute-start(bf16[2,2,256,128]{3,2,1,0:T(8,128)(2,1)} %collective-permute-done.5.refs_6_), channel_id=1, source_target_pairs={{0,8},{2,10},{4,12},{6,14},{8,16},{10,18},{12,20},{14,22},{16,24},... | collective-permute-start | bytes 786440 | tf_op jit(solution)/shard_map/ppermute | solution.py:20
  232.3 19.6 %copy-start.14 = (bf16[2,2,256,128]{3,2,1,0:T(8,128)(2,1)}, bf16[2,2,256,128]{3,2,1,0:T(8,128)(2,1)S(1)}, u32[]{:S(2)}) copy-start(bf16[2,2,256,128]{3,2,1,0:T(8,128)(2,1)S(1)} %collective-permute-done.6.refs_15_.refs_6_) | copy-start | bytes 786436
  232.3 9.2 %collective-permute-start.16 = (bf16[2,2,256,128]{3,2,1,0:T(8,128)(2,1)}, bf16[2,2,256,128]{3,2,1,0:T(8,128)(2,1)}, u32[]{:S(2)}, u32[]{:S(2)}) collective-permute-start(bf16[2,2,256,128]{3,2,1,0:T(8,128)(2,1)} %copy-done.21), channel_id=1, source_target_pairs={{4,0},{6,2},{12,8},{14,10},{20,16},{22,18},{28,24},{30,26},{5,1},{... | collective-permute-start | bytes 786440 | tf_op jit(solution)/shard_map/ppermute | solution.py:20
  235.4 11.2 %collective-permute-start.13 = (bf16[2,2,256,128]{3,2,1,0:T(8,128)(2,1)}, bf16[2,2,256,128]{3,2,1,0:T(8,128)(2,1)}, u32[]{:S(2)}, u32[]{:S(2)}) collective-permute-start(bf16[2,2,256,128]{3,2,1,0:T(8,128)(2,1)} %collective-permute-done.5.refs_6_), channel_id=1, source_target_pairs={{0,4},{2,6},{4,0},{6,2},{8,12},{10,14},{12,8},{14,10},{16,20},{18,... | collective-permute-start | bytes 786440 | tf_op jit(solution)/shard_map/ppermute | solution.py:20
  241.5 20.3 %collective-permute-start.10 = (bf16[2,2,256,128]{3,2,1,0:T(8,128)(2,1)S(1)}, bf16[2,2,256,128]{3,2,1,0:T(8,128)(2,1)S(1)}, u32[]{:S(2)}, u32[]{:S(2)}) collective-permute-start(bf16[2,2,256,128]{3,2,1,0:T(8,128)(2,1)S(1)} %collective-permute-done.6.refs_15_.refs_6_), channel_id=1, source_target_pairs={{0,8},{2,10},{4,12},{6,14},{8,16},{10,18},{12,20},{14,22},{16,24},... | collective-permute-start | bytes 786440 | tf_op jit(solution)/shard_map/ppermute | solution.py:20
  246.6 16.7 %collective-permute-start.17 = (bf16[2,2,256,128]{3,2,1,0:T(8,128)(2,1)}, bf16[2,2,256,128]{3,2,1,0:T(8,128)(2,1)}, u32[]{:S(2)}, u32[]{:S(2)}) collective-permute-start(bf16[2,2,256,128]{3,2,1,0:T(8,128)(2,1)} %collective-permute-done.9.refs_16_.refs_7_), channel_id=1, source_target_pairs={{4,0},{6,2},{12,8},{14,10},{20,16},{22,18},{28,24},{30,26},{5,1},{... | collective-permute-start | bytes 786440 | tf_op jit(solution)/shard_map/ppermute | solution.py:20
  247.9 4.0 %copy-start.11 = (bf16[4,256,512]{2,1,0:T(8,128)(2,1)}, bf16[4,256,512]{2,1,0:T(8,128)(2,1)S(1)}, u32[]{:S(2)}) copy-start(bf16[4,256,512]{2,1,0:T(8,128)(2,1)S(1)} %collective-permute-done.1.refs_3_) | copy-start | bytes 3145732
  247.9 16.1 %collective-permute-start.14 = (bf16[2,2,256,128]{3,2,1,0:T(8,128)(2,1)S(1)}, bf16[2,2,256,128]{3,2,1,0:T(8,128)(2,1)}, u32[]{:S(2)}, u32[]{:S(2)}) collective-permute-start(bf16[2,2,256,128]{3,2,1,0:T(8,128)(2,1)S(1)} %collective-permute-done.6.refs_15_.refs_6_), channel_id=1, source_target_pairs={{0,4},{2,6},{4,0},{6,2},{8,12},{10,14},{12,8},{14,10},{16,20},{18,... | collective-permute-start | bytes 786440 | tf_op jit(solution)/shard_map/ppermute | solution.py:20
  261.8 9.7 %collective-permute-start.22 = (bf16[2,256,256]{2,1,0:T(8,128)(2,1)}, bf16[2,256,256]{2,1,0:T(8,128)(2,1)S(1)}, u32[]{:S(2)}, u32[]{:S(2)}) collective-permute-start(bf16[2,256,256]{2,1,0:T(8,128)(2,1)} %get-tuple-element.54), channel_id=1, source_target_pairs={{0,3},{1,2},{2,1},{3,0},{4,7},{5,6},{6,5},{7,4},{8,11},{9,10},{10,... | collective-permute-start | bytes 786440 | tf_op jit(solution)/shard_map/ppermute | solution.py:25
  261.9 3.4 %copy-start.13 = (bf16[2,2,256,128]{3,2,1,0:T(8,128)(2,1)}, bf16[2,2,256,128]{3,2,1,0:T(8,128)(2,1)S(1)}, u32[]{:S(2)}) copy-start(bf16[2,2,256,128]{3,2,1,0:T(8,128)(2,1)S(1)} %collective-permute-done.10.refs_11_.refs_7_) | copy-start | bytes 786436
  261.9 9.7 %collective-permute-start.20 = (bf16[2,256,256]{2,1,0:T(8,128)(2,1)}, bf16[2,256,256]{2,1,0:T(8,128)(2,1)S(1)}, u32[]{:S(2)}, u32[]{:S(2)}) collective-permute-start(bf16[2,256,256]{2,1,0:T(8,128)(2,1)} %get-tuple-element.54), channel_id=1, source_target_pairs={{0,2},{2,0},{4,6},{6,4},{8,10},{10,8},{12,14},{14,12},{16,18},{18,... | collective-permute-start | bytes 786440 | tf_op jit(solution)/shard_map/ppermute | solution.py:20
  263.3 12.8 %collective-permute-start.21 = (bf16[2,256,256]{2,1,0:T(8,128)(2,1)}, bf16[2,256,256]{2,1,0:T(8,128)(2,1)S(1)}, u32[]{:S(2)}, u32[]{:S(2)}) collective-permute-start(bf16[2,256,256]{2,1,0:T(8,128)(2,1)} %get-tuple-element.55.refs_1_), channel_id=1, source_target_pairs={{0,1},{1,0},{2,3},{3,2},{4,5},{5,4},{6,7},{7,6},{8,9},{9,8},{10,11... | collective-permute-start | bytes 786440 | tf_op jit(solution)/shard_map/ppermute | solution.py:25
  264.0 12.1 %collective-permute-start.18 = (bf16[2,2,256,128]{3,2,1,0:T(8,128)(2,1)S(1)}, bf16[2,2,256,128]{3,2,1,0:T(8,128)(2,1)S(1)}, u32[]{:S(2)}, u32[]{:S(2)}) collective-permute-start(bf16[2,2,256,128]{3,2,1,0:T(8,128)(2,1)S(1)} %collective-permute-done.10.refs_11_.refs_7_), channel_id=1, source_target_pairs={{4,0},{6,2},{12,8},{14,10},{20,16},{22,18},{28,24},{30,26},{5,1},{... | collective-permute-start | bytes 786440 | tf_op jit(solution)/shard_map/ppermute | solution.py:20
  271.6 4.5 %copy-start.2 = (bf16[2,256,256]{2,1,0:T(8,128)(2,1)}, bf16[2,256,256]{2,1,0:T(8,128)(2,1)S(1)}, u32[]{:S(2)}) copy-start(bf16[2,256,256]{2,1,0:T(8,128)(2,1)S(1)} %collective-permute-done.22.refs_15_.refs_5_) | copy-start | bytes 786436
  271.6 4.5 %copy-start.4 = (bf16[2,256,256]{2,1,0:T(8,128)(2,1)}, bf16[2,256,256]{2,1,0:T(8,128)(2,1)S(1)}, u32[]{:S(2)}) copy-start(bf16[2,256,256]{2,1,0:T(8,128)(2,1)S(1)} %collective-permute-done.20.refs_13_.refs_3_) | copy-start | bytes 786436
  283.0 1.3 copy-start
  284.3 0.9 copy-start.16
  284.3 1.2 copy-start.8
  284.3 4.5 %copy-start.3 = (bf16[2,256,256]{2,1,0:T(8,128)(2,1)S(1)}, bf16[2,256,256]{2,1,0:T(8,128)(2,1)}, u32[]{:S(2)}) copy-start(bf16[2,256,256]{2,1,0:T(8,128)(2,1)} %copy-done.2) | copy-start | bytes 786436
  284.3 4.5 %copy-start.5 = (bf16[2,256,256]{2,1,0:T(8,128)(2,1)S(1)}, bf16[2,256,256]{2,1,0:T(8,128)(2,1)}, u32[]{:S(2)}) copy-start(bf16[2,256,256]{2,1,0:T(8,128)(2,1)} %copy-done.4) | copy-start | bytes 786436
  284.3 4.5 %copy-start.7 = (bf16[2,256,256]{2,1,0:T(8,128)(2,1)S(1)}, bf16[2,256,256]{2,1,0:T(8,128)(2,1)}, u32[]{:S(2)}) copy-start(bf16[2,256,256]{2,1,0:T(8,128)(2,1)} %copy-done.6) | copy-start | bytes 786436
  284.3 4.5 %copy-start.9 = (bf16[2,256,256]{2,1,0:T(8,128)(2,1)S(1)}, bf16[2,256,256]{2,1,0:T(8,128)(2,1)}, u32[]{:S(2)}) copy-start(bf16[2,256,256]{2,1,0:T(8,128)(2,1)} %get-tuple-element.55.refs_1_) | copy-start | bytes 786436
  284.3 4.5 %copy-start.10 = (s32[3]{0:T(128)S(1)}, s32[3]{0:T(128)}, u32[]{:S(2)}) copy-start(s32[3]{0:T(128)} %pad_add_fusion.2.info.refs_0_) | copy-start | bytes 40
  284.4 4.4 %collective-permute-start.27 = (bf16[512,2048]{1,0:T(8,128)(2,1)}, bf16[512,2048]{1,0:T(8,128)(2,1)S(1)}, u32[]{:S(2)}, u32[]{:S(2)}) collective-permute-start(bf16[512,2048]{1,0:T(8,128)(2,1)} %shard_map.52.refs_9_.refs_5_), channel_id=1, source_target_pairs={{0,2},{2,0},{4,6},{6,4},{8,10},{10,8},{12,14},{14,12},{16,18},{18,... | collective-permute-start | bytes 6291464 | tf_op jit(solution)/shard_map/ppermute | solution.py:20
  285.3 10.8 %collective-permute-start.25 = (bf16[2,256,256]{2,1,0:T(8,128)(2,1)S(1)}, bf16[2,256,256]{2,1,0:T(8,128)(2,1)S(1)}, u32[]{:S(2)}, u32[]{:S(2)}) collective-permute-start(bf16[2,256,256]{2,1,0:T(8,128)(2,1)S(1)} %copy-done.16), channel_id=1, source_target_pairs={{0,3},{1,2},{2,1},{3,0},{4,7},{5,6},{6,5},{7,4},{8,11},{9,10},{10,... | collective-permute-start | bytes 786440 | tf_op jit(solution)/shard_map/ppermute | solution.py:25
  285.5 10.7 %collective-permute-start.23 = (bf16[2,256,256]{2,1,0:T(8,128)(2,1)S(1)}, bf16[2,256,256]{2,1,0:T(8,128)(2,1)S(1)}, u32[]{:S(2)}, u32[]{:S(2)}) collective-permute-start(bf16[2,256,256]{2,1,0:T(8,128)(2,1)S(1)} %copy-done.16), channel_id=1, source_target_pairs={{0,2},{2,0},{4,6},{6,4},{8,10},{10,8},{12,14},{14,12},{16,18},{18,... | collective-permute-start | bytes 786440 | tf_op jit(solution)/shard_map/ppermute | solution.py:20
  285.5 14.0 %collective-permute-start.24 = (bf16[2,256,256]{2,1,0:T(8,128)(2,1)S(1)}, bf16[2,256,256]{2,1,0:T(8,128)(2,1)S(1)}, u32[]{:S(2)}, u32[]{:S(2)}) collective-permute-start(bf16[2,256,256]{2,1,0:T(8,128)(2,1)S(1)} %copy-done.8), channel_id=1, source_target_pairs={{0,1},{1,0},{2,3},{3,2},{4,5},{5,4},{6,7},{7,6},{8,9},{9,8},{10,11... | collective-permute-start | bytes 786440 | tf_op jit(solution)/shard_map/ppermute | solution.py:25
  288.8 1.6 copy-start.1
  (5 other events, 3.7 us)

commit v4 on v3

--- a/solution.py
+++ b/solution.py
@@ -56,22 +56,32 @@
         [jnp.concatenate([clean, noisy], 1), jnp.concatenate([own_clean, own_noisy], 1)], 0
     )
     table = jnp.where(allowed, 0.0, MASKED).astype(jnp.float32)
+    table = jnp.concatenate([table, jnp.ones((count + rows, 1), jnp.float32)], 1)
     return jnp.pad(table, ((0, 0), (0, HD - table.shape[1])))
 
 
-def copies(info, sources, outs, plan):
+def copies(info, sources, outs, shapes, plan):
     total = sum(math.prod(o.shape) for o in outs)
 
     def kernel(info, *refs):
         ins, rest = refs[:len(sources)], refs[len(sources):]
-        pairs = plan(info[0], info[2], ins, rest[:len(outs)])
-        started = [
-            pltpu.make_async_copy(a, b, rest[-1].at[k]) for k, (a, b) in enumerate(pairs)
+        pieces = plan(info[0], info[2], ins, rest[:len(outs)])
+        room, arrive, leave = rest[len(outs):-2], rest[-2], rest[-1]
+        reads = [
+            pltpu.make_async_copy(source, held, arrive.at[k])
+            for k, ((source, _), held) in enumerate(zip(pieces, room))
         ]
-        for copy in started:
-            copy.start()
-        for copy in started:
-            copy.wait()
+        for read in reads:
+            read.start()
+        writes = []
+        for read, (_, targets), held in zip(reads, pieces, room):
+            read.wait()
+            for part, target in targets:
+                write = pltpu.make_async_copy(held.at[part], target, leave.at[len(writes)])
+                write.start()
+                writes.append(write)
+        for write in writes:
+            write.wait()
 
     return pl.pallas_call(
         kernel,
@@ -80,7 +90,11 @@
             grid=(),
             in_specs=[pl.BlockSpec(memory_space=pl.ANY)] * len(sources),
             out_specs=[pl.BlockSpec(memory_space=pl.ANY)] * len(outs),
-            scratch_shapes=[pltpu.SemaphoreType.DMA((32,))],
+            scratch_shapes=[
+                *[pltpu.VMEM(shape, jnp.bfloat16) for shape in shapes],
+                pltpu.SemaphoreType.DMA((len(shapes),)),
+                pltpu.SemaphoreType.DMA((32,)),
+            ],
         ),
         out_shape=[jax.ShapeDtypeStruct(o.shape, o.dtype) for o in outs],
         compiler_params=pltpu.CompilerParams(vmem_limit_bytes=VMEM),
@@ -90,10 +104,10 @@
 
 def attend_kernel(tokens, count, info, *refs):
     core, side = info[0], info[1]
-    refs = refs[:6 + 4 * count] + refs[-5:]
-    q_here, kn_here, there, own, low = refs[:5]
-    blocks = [refs[5 + 4 * h:9 + 4 * h] for h in range(count)]
-    table, mine, give, tie, keys, values = refs[5 + 4 * count:]
+    refs = refs[:7 + 4 * count] + refs[-6:]
+    q_here, n_here, q_there, n_there, own, low = refs[:6]
+    blocks = [refs[6 + 4 * h:10 + 4 * h] for h in range(count)]
+    table, mine, give, tie, keys, values, least = refs[6 + 4 * count:]
     tie[...] = jnp.zeros_like(tie)
     rows = tokens // BLK
     span = WINB * BLK + tokens
@@ -126,51 +140,86 @@
 
     spot = lax.broadcasted_iota(jnp.int32, (2 * tokens, HD), 0) // BLK
     lane = lax.broadcasted_iota(jnp.int32, (2 * tokens, HD), 1)
-    hot = jnp.where(spot == lane, 1.0, 0.0).astype(jnp.bfloat16)
+    hot = jnp.where(spot == lane, 1.0, 0.0)
     contract = (((1,), (1,)), ((), ()))
-    biases = [
-        jnp.broadcast_to(table[tile][:, None, :], (span // BLK + rows, BLK, HD))
-        .reshape(span + tokens, HD).astype(jnp.bfloat16)
-        for tile in range(2)
-    ]
-
-    def scores_of(head, tile):
+    step = tokens
+    tiles = (span + tokens) // step
+
+    def operands(head, tile):
         lanes = slice(head * HD, (head + 1) * HD)
         half = core if tile == 0 else 1 - core
-        at = pl.multiple_of(half * tokens, tokens)
-        if tile == 0:
-            query = q_here[:, :, lanes].reshape(2 * tokens, HD)
-            key_n = kn_here[0, 0, :, lanes]
-        else:
-            query = there[0:2, :, lanes].reshape(2 * tokens, HD)
-            key_n = there[2, :, lanes]
-        key = jnp.concatenate([keys[head, pl.ds(at, span), :], key_n], 0)
-        key = jnp.concatenate([key, biases[tile]], 1)
-        query = jnp.concatenate([query, hot], 1)
-        return lax.dot_general(query, key, contract, preferred_element_type=jnp.float32)
-
-    def attended(head, tile, scores):
+        q_ref, n_ref = (q_here, n_here) if tile == 0 else (q_there, n_there)
+        query = q_ref[:, :, lanes].reshape(2 * tokens, HD)
+        key, value = [], []
+        for k in range(tiles):
+            at = pl.multiple_of((half + k) * tokens, tokens)
+            if k == tiles - 1:
+                key.append(n_ref[0, 0, :, lanes])
+                value.append(n_ref[1, 0, :, lanes])
+            else:
+                key.append(keys[head, pl.ds(at, step), :])
+                value.append(values[head, pl.ds(at, step), :])
+        bias = [
+            jnp.broadcast_to(
+                table[tile, k * rows:(k + 1) * rows][:, None, :], (rows, BLK, HD)
+            ).reshape(step, HD).astype(jnp.bfloat16)
+            for k in range(tiles)
+        ]
+        return query, key, bias, value
+
+    def store(head, tile, out):
         lanes = slice(head * HD, (head + 1) * HD)
-        half = core if tile == 0 else 1 - core
-        at = pl.multiple_of(half * tokens, tokens)
-        value_n = kn_here[1, 0, :, lanes] if tile == 0 else there[3, :, lanes]
-        value = jnp.concatenate([values[head, pl.ds(at, span), :], value_n], 0)
+        (mine if tile == 0 else give)[:, :, lanes] = out.astype(jnp.bfloat16).reshape(
+            2, tokens, HD)
+
+    shift_lane = 2 * rows
+    jobs = [(head, tile) for head in range(count) for tile in range(2)]
+    low_sum = None
+    for head, tile in jobs:
+        query, key, bias, value = operands(head, tile)
+        wide = query.astype(jnp.float32)
+        longest = None
+        for k in key:
+            k = k.astype(jnp.float32)
+            size = jnp.max(jnp.sum(k * k, axis=1, keepdims=True), axis=0, keepdims=True)
+            longest = size if longest is None else jnp.maximum(longest, size)
+        bound = jnp.sqrt(jnp.sum(wide * wide, axis=1, keepdims=True) * longest)
+        extra = jnp.where(lane == shift_lane, -bound, hot).astype(jnp.bfloat16)
+        query = jnp.concatenate([query, extra], 1)
+        parts = []
+        for k in range(tiles):
+            scores = lax.dot_general(
+                query, jnp.concatenate([key[k], bias[k]], 1), contract,
+                preferred_element_type=jnp.float32,
+            )
+            parts.append(jnp.exp2(scores * SCALE).astype(jnp.bfloat16))
+        expo = jnp.concatenate(parts, 1)
+        value = jnp.concatenate(value, 0)
         value = jnp.concatenate([value, jnp.ones_like(value)], 1)
-        top = jnp.max(scores, axis=1, keepdims=True)
-        expo = jnp.exp2((scores - top) * SCALE).astype(jnp.bfloat16)
         total = jnp.dot(expo, value, preferred_element_type=jnp.float32)
-        out = (total[:, :HD] / total[:, HD:]).astype(jnp.bfloat16).reshape(2, tokens, HD)
-        (mine if tile == 0 else give)[:, :, lanes] = out
-
-    jobs = [(head, tile) for head in range(count) for tile in range(2)]
-    scores = scores_of(*jobs[0])
-    for job, later in zip(jobs, jobs[1:] + [None]):
-        upcoming = scores_of(*later) if later else None
-        attended(*job, scores)
-        scores = upcoming
-
-
-def attend(info, queries, keys_values, there, own, low, blocks, table, first, heads_half,
+        sums = total[:, HD:]
+        store(head, tile, total[:, :HD] / sums)
+        smallest = jnp.min(sums.reshape(-1, 8, HD), axis=0)
+        low_sum = smallest if low_sum is None else jnp.minimum(low_sum, smallest)
+    least[...] = low_sum
+
+    @pl.when(jnp.logical_not(jnp.min(least[...]) > 2.0 ** -40))
+    def _():
+        for head, tile in jobs:
+            query, key, bias, value = operands(head, tile)
+            query = jnp.concatenate([query, hot.astype(jnp.bfloat16)], 1)
+            key = jnp.concatenate(
+                [jnp.concatenate(key, 0), jnp.concatenate(bias, 0)], 1)
+            scores = lax.dot_general(query, key, contract, preferred_element_type=jnp.float32)
+            top = jnp.max(scores, axis=1, keepdims=True)
+            expo = jnp.exp2((scores - top) * SCALE).astype(jnp.bfloat16)
+            value = jnp.concatenate(value, 0)
+            value = jnp.concatenate([value, jnp.ones_like(value)], 1)
+            total = jnp.dot(expo, value, preferred_element_type=jnp.float32)
+            store(head, tile, total[:, :HD] / total[:, HD:])
+
+
+def attend(info, queries, keys_values, there, got, own, low, blocks, table, first, heads_half,
            room, at, into, after):
     tokens = queries.shape[1]
     span = WINB * BLK + 2 * tokens
@@ -190,9 +239,10 @@
             num_scalar_prefetch=1,
             grid=(1,),
             in_specs=[
-                pl.BlockSpec((2, tokens, wide), here),
-                pl.BlockSpec((2, 1, tokens, wide), lambda s, info: (0, 1) + here(s, info)[1:]),
-                pl.BlockSpec((4, tokens, wide), lambda s, info: (0, 0, first // count)),
+                *[
+                    pl.BlockSpec((2, tokens, wide), here),
+                    pl.BlockSpec((2, 1, tokens, wide), lambda s, info: (0, 1) + here(s, info)[1:]),
+                ] * 2,
                 whole, whole,
                 *[one_head] * (4 * count),
                 pl.BlockSpec(table.shape, lambda s, info: (0, 0, 0)),
@@ -202,15 +252,16 @@
             scratch_shapes=[
                 pltpu.VMEM((count, span, HD), jnp.bfloat16),
                 pltpu.VMEM((count, span, HD), jnp.bfloat16),
+                pltpu.VMEM((8, HD), jnp.float32),
             ],
         ),
         out_shape=[out, out, jax.ShapeDtypeStruct((8, HD), jnp.float32)],
-        input_output_aliases={7 + 4 * count + k: k for k in range(len(into))},
+        input_output_aliases={8 + 4 * count + k: k for k in range(len(into))},
         compiler_params=pltpu.CompilerParams(vmem_limit_bytes=VMEM),
         cost_estimate=pl.CostEstimate(
             flops=work * 8, bytes_accessed=count * 64 * 1024, transcendentals=0
         ),
-    )(info, queries, keys_values, there, own, low, *[b for group in blocks for b in group], table,
+    )(info, queries, keys_values, there, got, own, low, *[b for group in blocks for b in group], table,
       *into, *after)
 
 def project_kernel(count, groups, add, info, *refs):
@@ -284,55 +335,51 @@
     lower = lambda i: i - 2 if i & 2 else None
     lanes = lambda start, size: pl.ds(pl.multiple_of(start, HD), size)
 
-    def cut_clean(core, place, ins, outs):
-        return [(ins[0].at[:, 0, :, lanes((1 - core) * width, width)], outs[0])]
-
-    clean, = copies(info, [keys_values], [jax.ShapeDtypeStruct((2, tokens, width), bf16)], cut_clean)
-    got = moved(clean, n, pair)
-
-    def join(head, heads, kv, got, out):
-        def pairs(core):
-            return [
-                (kv.at[:, 0, :, lanes(core * width + head * HD, heads * HD)], out.at[0]),
-                (got.at[:, :, head * HD:(head + heads) * HD], out.at[1]),
-            ]
-        return pairs
+    got = moved(keys_values, n, pair)
+    there = moved(queries, n, pair)
+
+    def cut_panels(core, place, ins, outs):
+        pieces = []
+        for r in range(1, f):
+            column = pl.multiple_of(lax.rem(place + r, f) * features, HD)
+            for p in range(cuts):
+                row = pl.multiple_of(core * width + p * (width // cuts), width // cuts)
+                at = pl.ds(p * (width // cuts), width // cuts)
+                pieces.append((ins[0].at[pl.ds(row, width // cuts), pl.ds(column, features)],
+                               [(slice(None), outs[r - 1].at[at])]))
+        return pieces
+
+    cuts = 4 if f == 2 else 1
+    panels = copies(
+        info, [out_weight], [jax.ShapeDtypeStruct((width, features), bf16)] * (f - 1),
+        [(width // cuts, features)] * (cuts * (f - 1)), cut_panels,
+    )
+
+    def join(core, ins, outs):
+        pieces = []
+        for slot, source in enumerate(ins[:2]):
+            for head_at, target in outs:
+                wide = target.shape[-1]
+                here = lanes(core * width + head_at * HD, wide)
+                pieces.append((source.at[:, 0, :, here], [(slice(None), target.at[slot])]))
+        return pieces
 
     pair_shape = lambda heads: jax.ShapeDtypeStruct((2, 2, tokens, heads * HD), bf16)
+    held = lambda heads: (2, tokens, heads * HD)
     first, = copies(
-        info, [keys_values, got], [pair_shape(1)],
-        lambda core, place, ins, outs: join(0, 1, ins[0], ins[1], outs[0])(core),
+        info, [keys_values, got], [pair_shape(1)], [held(1)] * 2,
+        lambda core, place, ins, outs: join(core, ins, [(0, outs[0])]),
     )
     one = moved(first, n, ahead)
-
-    def cut_rest(core, place, ins, outs):
-        kv, got, q, w, _ = ins
-        give = lanes((1 - core) * width, width)
-        plan = join(0, heads_half, kv, got, outs[0])(core)
-        for h in range(1, heads_half):
-            plan += join(h, 1, kv, got, outs[h])(core)
-        plan += [(q.at[:, :, give], outs[heads_half].at[0:2]),
-                 (kv.at[:, 1, :, give], outs[heads_half].at[2:4])]
-        for r in range(1, f):
-            out = outs[heads_half + r]
-            column = pl.multiple_of(lax.rem(place + r, f) * features, HD)
-            pieces = max(1, 4 // f)
-            step = width // pieces
-            for p in range(pieces):
-                row = pl.multiple_of(core * width + p * step, step)
-                plan.append((w.at[pl.ds(row, step), pl.ds(column, features)],
-                             out.at[p * step:(p + 1) * step]))
-        return plan
-
     whole, *rest = copies(
-        info, [keys_values, got, queries, out_weight, first],
-        [pair_shape(heads_half)] + [pair_shape(1)] * (heads_half - 1)
-        + [jax.ShapeDtypeStruct((4, tokens, width), bf16)]
-        + [jax.ShapeDtypeStruct((width, features), bf16)] * (f - 1),
-        cut_rest,
-    )
-    own = [first] + rest[:heads_half - 1]
-    later, panels = rest[heads_half - 1], rest[heads_half:]
+        info, [keys_values, got, first], [pair_shape(heads_half)] + [pair_shape(1)] * (heads_half - 1),
+        [held(heads_half)] + [held(1)] * (heads_half - 1) + [held(heads_half)]
+        + [held(1)] * (heads_half - 1),
+        lambda core, place, ins, outs: join(
+            core, ins,
+            [(0, outs[0])] + [(h, outs[h]) for h in range(1, heads_half)]),
+    )
+    own = [first] + rest
 
     sames = [
         moved_both(panel, n, f, lambda i, k: (i, (k + r) % f))
@@ -344,13 +391,12 @@
         last = blocks[-1] if blocks else None
         in_turn = lambda array, k: behind(array, last[k]) if last else array
         if h:
-            one = moved(in_turn(own[h], 0), n, ahead)
+            one = moved(behind(own[h], blocks[-2][0]) if h > 1 else own[h], n, ahead)
         two = moved(in_turn(one, 1), n, ahead)
         swap = moved(in_turn(one, 2), n, across)
         far = moved(in_turn(two, 3), n, lower)
         blocks.append((one, two, swap, far))
     low = moved(whole, n, upper)
-    there = moved(later, n, pair)
     mask_there = moved(behind(block_mask, first), n, pair)
     table = jnp.stack([
         mask_table(index * rows, rows, block_mask),
@@ -366,7 +412,7 @@
             after = ([blocks[-1][0], blocks[-2][1]] if not final else [blocks[-1][1]]) \
                 if run[-1] < heads_half - 1 else [a[0] for a in acts[1:] if a]
             mine, give, tie = attend(
-                info, queries, keys_values, there, whole, low,
+                info, queries, keys_values, there, got, whole, low,
                 [blocks[h] for h in run], table, run[0], heads_half,
                 len(share), run[0] - share[0], into, after + ties[-1:],
             )

time: 306 us -> 163 us (0.53)
  Pallas kernels: 214 us -> 60.9 us
  waiting for transfers between devices: 27.4 us -> 44.8 us
  starting transfers between devices: 54.3 us -> 47.2 us
    pallas_call x3, Pallas kernels: 181 us -> 9.38 us  [copies(): pl.pallas_call(kernel, grid_spec=pltpu.PrefetchScalarGridSpec(num_scalar_...]
    ppermute x23, waiting for transfers between devices: 19.6 us -> 41.7 us  [moved(): return lax.ppermute(array, 'ctx', pairs)]
    pallas_call x3, Pallas kernels: 22.4 us -> 40.5 us  [attend(): pl.pallas_call(lambda *refs: attend_kernel(tokens, count, *refs), grid_sp...]
    ppermute x23, starting transfers between devices: 49.8 us -> 41.6 us  [moved(): return lax.ppermute(array, 'ctx', pairs)]
    ppermute x5, waiting for transfers between devices: 7.83 us -> 3.05 us  [moved_both(): return lax.ppermute(array, ('ctx', 'fsdp'), pairs)]
    unnamed x50 -> x40, local copies, waits for them, and re-layouts: 6.65 us -> 6.8 us
  transfers between devices with their start and end apart: 28 -> 28, of which waited for: 11 -> 10; matrix products, arithmetic and copies ran while one was open for 0% -> 1% of each run, Pallas kernels for 59% -> 33%
where the time goes in v4:
time: 163 us; the launch traced here: 162 us
  Pallas kernels  60.9 us (37%)
  starting transfers between devices  47.2 us (29%)
  waiting for transfers between devices  44.8 us (27%)
  local copies, waits for them, and re-layouts  7 us (4%)
    ppermute x23, waiting for transfers between devices, moved(): return lax.ppermute(array, 'ctx', pairs)  41.7 us
    ppermute x23, starting transfers between devices, moved(): return lax.ppermute(array, 'ctx', pairs)  41.6 us
    pallas_call x3, Pallas kernels, attend(): pl.pallas_call(lambda *refs: attend_kernel(tokens, count, *refs), grid_sp...  40.5 us
    pallas_call x2, Pallas kernels, project(): pl.pallas_call(lambda *refs: project_kernel(len(flat), len(used), before...  11 us
    pallas_call x3, Pallas kernels, copies(): pl.pallas_call(kernel, grid_spec=pltpu.PrefetchScalarGridSpec(num_scalar_...  9.38 us
    unnamed x40, local copies, waits for them, and re-layouts  6.8 us
    ppermute x5, starting transfers between devices, moved_both(): return lax.ppermute(array, ('ctx', 'fsdp'), pairs)  5.52 us
  transfers between devices with their start and end apart: 28, of which 10 were waited for; matrix products, arithmetic and copies ran while one was open for 1% of the time, Pallas kernels for 33%

profile of v4, /device:TPU:0, one launch (start us, length us, event | category | flops | bytes accessed | tf_op | source)
XLA Modules:
  0.0 161.8 jit_solution(8848385144707666933)
XLA Ops:
  0.0 0.5 collective-permute-start.1
  0.5 0.6 pad_add_fusion.2.info.refs_0_
  1.1 3.4 %collective-permute-done.1.refs_1_.refs_4_ = bf16[2,2,256,1024]{3,2,1,0:T(8,128)(2,1)S(1)} collective-permute-done((bf16[2,2,256,1024]{3,2,1,0:T(8,128)(2,1)}, bf16[2,2,256,1024]{3,2,1,0:T(8,128)(2,1)S(1)}, u32[]{:S(2)}, u32[]{:S(2)}) %collective-permute-start.1) | collective-permute-done | bytes 2097184 | tf_op jit(solution)/shard_map/ppermute | solution.py:20
  4.5 1.3 copy-done.11
  5.8 2.6 %shard_map.46.refs_2_ = bf16[2,2,256,128]{3,2,1,0:T(8,128)(2,1)} custom-call(s32[3]{0:T(128)} %pad_add_fusion.2.info.refs_0_, bf16[2,2,256,1024]{3,2,1,0:T(8,128)(2,1)} %refs_2_.5, bf16[2,2,256,1024]{3,2,1,0:T(8,128)(2,1)} %copy-done.11), custom_call_target="tpu_custom_call" | custom-call | bytes 131072 | tf_op jit(solution)/shard_map/pallas_call | solution.py:86
  8.4 4.9 %collective-permute-start.5 = (bf16[2,2,256,128]{3,2,1,0:T(8,128)(2,1)}, bf16[2,2,256,128]{3,2,1,0:T(8,128)(2,1)S(1)}, u32[]{:S(2)}, u32[]{:S(2)}) collective-permute-start(bf16[2,2,256,128]{3,2,1,0:T(8,128)(2,1)} %shard_map.46.refs_2_), channel_id=1, source_target_pairs={{0,8},{2,10},{4,12},{6,14},{8,16},{10,18},{12,20},{14,22},{16,24},... | collective-permute-start | bytes 786440 | tf_op jit(solution)/shard_map/ppermute | solution.py:20
  13.3 3.4 %shard_map.51 = bf16[512,2048]{1,0:T(8,128)(2,1)} custom-call(s32[3]{0:T(128)} %pad_add_fusion.2.info.refs_0_, bf16[1024,4096]{1,0:T(8,128)(2,1)} %refs_4_.1), custom_call_target="tpu_custom_call" | custom-call | bytes 1048576 | tf_op jit(solution)/shard_map/pallas_call | solution.py:86
  16.7 1.6 collective-permute-start.26
  18.3 3.4 %shard_map.47 = (bf16[2,2,256,512]{3,2,1,0:T(8,128)(2,1)}, bf16[2,2,256,128]{3,2,1,0:T(8,128)(2,1)}, bf16[2,2,256,128]{3,2,1,0:T(8,128)(2,1)}, bf16[2,2,256,128]{3,2,1,0:T(8,128)(2,1)}) custom-call(s32[3]{0:T(128)} %pad_add_fusion.2.info.refs_0_, bf16[2,2,256,1024]{3,2,1,0:T(8,128)(2,1)} %refs_2_.5, bf16[2,2,256,1024]{3,2,1,0:T(8,128)(2,1)} %copy-done.11, ...), custom_call_target="tpu_custom_call" | custom-call | bytes 917504 | tf_op jit(solution)/shard_map/pallas_call | solution.py:86
  21.7 4.2 %collective-permute-start.3 = (bf16[2,2,256,128]{3,2,1,0:T(8,128)(2,1)}, bf16[2,2,256,128]{3,2,1,0:T(8,128)(2,1)}, u32[]{:S(2)}, u32[]{:S(2)}) collective-permute-start(bf16[2,2,256,128]{3,2,1,0:T(8,128)(2,1)} %get-tuple-element.32), channel_id=1, source_target_pairs={{0,8},{2,10},{4,12},{6,14},{8,16},{10,18},{12,20},{14,22},{16,24},... | collective-permute-start | bytes 786440 | tf_op jit(solution)/shard_map/ppermute | solution.py:20
  25.9 2.8 %collective-permute-start.7 = (bf16[2,2,256,128]{3,2,1,0:T(8,128)(2,1)S(1)}, bf16[2,2,256,128]{3,2,1,0:T(8,128)(2,1)S(1)}, u32[]{:S(2)}, u32[]{:S(2)}) collective-permute-start(bf16[2,2,256,128]{3,2,1,0:T(8,128)(2,1)S(1)} %collective-permute-done.5.refs_7_), channel_id=1, source_target_pairs={{0,8},{2,10},{4,12},{6,14},{8,16},{10,18},{12,20},{14,22},{16,24},... | collective-permute-start | bytes 786440 | tf_op jit(solution)/shard_map/ppermute | solution.py:20
  28.8 1.5 collective-permute-start.11
  30.3 1.8 %collective-permute-done.3.refs_11_ = bf16[2,2,256,128]{3,2,1,0:T(8,128)(2,1)} collective-permute-done((bf16[2,2,256,128]{3,2,1,0:T(8,128)(2,1)}, bf16[2,2,256,128]{3,2,1,0:T(8,128)(2,1)}, u32[]{:S(2)}, u32[]{:S(2)}) %collective-permute-start.3) | collective-permute-done | bytes 262176 | tf_op jit(solution)/shard_map/ppermute | solution.py:20
  32.2 4.8 %collective-permute-done.7.refs_8_ = bf16[2,2,256,128]{3,2,1,0:T(8,128)(2,1)S(1)} collective-permute-done((bf16[2,2,256,128]{3,2,1,0:T(8,128)(2,1)S(1)}, bf16[2,2,256,128]{3,2,1,0:T(8,128)(2,1)S(1)}, u32[]{:S(2)}, u32[]{:S(2)}) %collective-permute-start.7) | collective-permute-done | bytes 262176 | tf_op jit(solution)/shard_map/ppermute | solution.py:20
  37.0 0.7 copy-done.15
  37.7 5.1 %collective-permute-start.8 = (bf16[2,2,256,128]{3,2,1,0:T(8,128)(2,1)}, bf16[2,2,256,128]{3,2,1,0:T(8,128)(2,1)}, u32[]{:S(2)}, u32[]{:S(2)}) collective-permute-start(bf16[2,2,256,128]{3,2,1,0:T(8,128)(2,1)} %collective-permute-done.3.refs_11_), channel_id=1, source_target_pairs={{0,8},{2,10},{4,12},{6,14},{8,16},{10,18},{12,20},{14,22},{16,24},... | collective-permute-start | bytes 786440 | tf_op jit(solution)/shard_map/ppermute | solution.py:20
  42.9 3.5 %collective-permute-start.6 = (bf16[2,2,256,128]{3,2,1,0:T(8,128)(2,1)}, bf16[2,2,256,128]{3,2,1,0:T(8,128)(2,1)}, u32[]{:S(2)}, u32[]{:S(2)}) collective-permute-start(bf16[2,2,256,128]{3,2,1,0:T(8,128)(2,1)} %get-tuple-element.35), channel_id=1, source_target_pairs={{0,8},{2,10},{4,12},{6,14},{8,16},{10,18},{12,20},{14,22},{16,24},... | collective-permute-start | bytes 786440 | tf_op jit(solution)/shard_map/ppermute | solution.py:20
  46.4 1.5 collective-permute-start.12
  48.3 1.3 collective-permute-start.15
  49.7 11.0 %collective-permute-done.15.refs_10_ = bf16[2,2,256,128]{3,2,1,0:T(8,128)(2,1)} collective-permute-done((bf16[2,2,256,128]{3,2,1,0:T(8,128)(2,1)}, bf16[2,2,256,128]{3,2,1,0:T(8,128)(2,1)}, u32[]{:S(2)}, u32[]{:S(2)}) %collective-permute-start.15) | collective-permute-done | bytes 262176 | tf_op jit(solution)/shard_map/ppermute | solution.py:20
  60.8 2.4 %collective-permute-start.2 = (bf16[2,2,256,512]{3,2,1,0:T(8,128)(2,1)}, bf16[2,2,256,512]{3,2,1,0:T(8,128)(2,1)}, u32[]{:S(2)}, u32[]{:S(2)}) collective-permute-start(bf16[2,2,256,512]{3,2,1,0:T(8,128)(2,1)} %get-tuple-element.30.refs_5_), channel_id=1, source_target_pairs={{0,4},{2,6},{8,12},{10,14},{16,20},{18,22},{24,28},{26,30},{1,5},{... | collective-permute-start | bytes 3145736 | tf_op jit(solution)/shard_map/ppermute | solution.py:20
  63.2 1.3 collective-permute-start.16
  64.5 2.3 %collective-permute-start.9 = (bf16[2,2,256,128]{3,2,1,0:T(8,128)(2,1)}, bf16[2,2,256,128]{3,2,1,0:T(8,128)(2,1)}, u32[]{:S(2)}, u32[]{:S(2)}) collective-permute-start(bf16[2,2,256,128]{3,2,1,0:T(8,128)(2,1)} %collective-permute-done.6.refs_7_), channel_id=1, source_target_pairs={{0,8},{2,10},{4,12},{6,14},{8,16},{10,18},{12,20},{14,22},{16,24},... | collective-permute-start | bytes 786440 | tf_op jit(solution)/shard_map/ppermute | solution.py:20
  67.0 5.8 %collective-permute-done.16.refs_14_ = bf16[2,2,256,128]{3,2,1,0:T(8,128)(2,1)} collective-permute-done((bf16[2,2,256,128]{3,2,1,0:T(8,128)(2,1)}, bf16[2,2,256,128]{3,2,1,0:T(8,128)(2,1)}, u32[]{:S(2)}, u32[]{:S(2)}) %collective-permute-start.16) | collective-permute-done | bytes 262176 | tf_op jit(solution)/shard_map/ppermute | solution.py:20
  72.8 1.3 collective-permute-start.4
  74.1 1.9 %collective-permute-start.13 = (bf16[2,2,256,128]{3,2,1,0:T(8,128)(2,1)}, bf16[2,2,256,128]{3,2,1,0:T(8,128)(2,1)}, u32[]{:S(2)}, u32[]{:S(2)}) collective-permute-start(bf16[2,2,256,128]{3,2,1,0:T(8,128)(2,1)} %collective-permute-done.6.refs_7_), channel_id=1, source_target_pairs={{0,4},{2,6},{4,0},{6,2},{8,12},{10,14},{12,8},{14,10},{16,20},{18,... | collective-permute-start | bytes 786440 | tf_op jit(solution)/shard_map/ppermute | solution.py:20
  76.2 2.6 %collective-permute-done.4.refs_16_.refs_7_ = bf16[2,2,256,128]{3,2,1,0:T(8,128)(2,1)S(1)} collective-permute-done((bf16[2,2,256,128]{3,2,1,0:T(8,128)(2,1)}, bf16[2,2,256,128]{3,2,1,0:T(8,128)(2,1)S(1)}, u32[]{:S(2)}, u32[]{:S(2)}) %collective-permute-start.4) | collective-permute-done | bytes 262176 | tf_op jit(solution)/shard_map/ppermute | solution.py:20
  78.7 1.3 collective-permute-start.17
  80.0 10.2 %collective-permute-done.13.refs_9_ = bf16[2,2,256,128]{3,2,1,0:T(8,128)(2,1)} collective-permute-done((bf16[2,2,256,128]{3,2,1,0:T(8,128)(2,1)}, bf16[2,2,256,128]{3,2,1,0:T(8,128)(2,1)}, u32[]{:S(2)}, u32[]{:S(2)}) %collective-permute-start.13) | collective-permute-done | bytes 262176 | tf_op jit(solution)/shard_map/ppermute | solution.py:20
  90.2 2.0 %collective-permute-start.10 = (bf16[2,2,256,128]{3,2,1,0:T(8,128)(2,1)S(1)}, bf16[2,2,256,128]{3,2,1,0:T(8,128)(2,1)}, u32[]{:S(2)}, u32[]{:S(2)}) collective-permute-start(bf16[2,2,256,128]{3,2,1,0:T(8,128)(2,1)S(1)} %collective-permute-done.4.refs_16_.refs_7_), channel_id=1, source_target_pairs={{0,8},{2,10},{4,12},{6,14},{8,16},{10,18},{12,20},{14,22},{16,24},... | collective-permute-start | bytes 786440 | tf_op jit(solution)/shard_map/ppermute | solution.py:20
  92.2 2.5 %collective-permute-start.14 = (bf16[2,2,256,128]{3,2,1,0:T(8,128)(2,1)S(1)}, bf16[2,2,256,128]{3,2,1,0:T(8,128)(2,1)S(1)}, u32[]{:S(2)}, u32[]{:S(2)}) collective-permute-start(bf16[2,2,256,128]{3,2,1,0:T(8,128)(2,1)S(1)} %collective-permute-done.4.refs_16_.refs_7_), channel_id=1, source_target_pairs={{0,4},{2,6},{4,0},{6,2},{8,12},{10,14},{12,8},{14,10},{16,20},{18,... | collective-permute-start | bytes 786440 | tf_op jit(solution)/shard_map/ppermute | solution.py:20
  94.7 0.6 pad_maximum_fusion.refs_15_.refs_11_
  95.3 17.7 %shard_map.48 = (bf16[2,256,256]{2,1,0:T(8,128)(2,1)}, bf16[2,256,256]{2,1,0:T(8,128)(2,1)}, f32[8,128]{1,0:T(8,128)}) custom-call(s32[3]{0:T(128)} %pad_add_fusion.2.info.refs_0_, bf16[2,256,1024]{2,1,0:T(8,128)(2,1)} %refs_1_.5, bf16[2,2,256,1024]{3,2,1,0:T(8,128)(2,1)} %refs_2_.5, bf16[2,256,1024]{2,1,0:T(8,128)(2,1)} %collective-permute-done.refs_3_, ...), custom_call_target="tpu_custom_call" | custom-call | flops 41943040 | bytes 131072 | tf_op jit(solution)/shard_map/pallas_call | solution.py:236
  113.1 0.6 collective-permute-start.22
  113.7 1.5 collective-permute-start.21
  115.2 1.3 collective-permute-start.18
  116.5 11.4 %shard_map.49 = (bf16[2,256,256]{2,1,0:T(8,128)(2,1)}, bf16[2,256,256]{2,1,0:T(8,128)(2,1)}, f32[8,128]{1,0:T(8,128)}) custom-call(s32[3]{0:T(128)} %pad_add_fusion.2.info.refs_0_, bf16[2,256,1024]{2,1,0:T(8,128)(2,1)} %refs_1_.5, bf16[2,2,256,1024]{3,2,1,0:T(8,128)(2,1)} %refs_2_.5, bf16[2,256,1024]{2,1,0:T(8,128)(2,1)} %collective-permute-done.refs_3_, ...), custom_call_target="tpu_custom_call" | custom-call | flops 20971520 | bytes 65536 | tf_op jit(solution)/shard_map/pallas_call | solution.py:236
  128.0 0.6 copy-done.2
  128.9 11.4 %shard_map.50 = (bf16[2,256,256]{2,1,0:T(8,128)(2,1)}, bf16[2,256,256]{2,1,0:T(8,128)(2,1)}, f32[8,128]{1,0:T(8,128)}) custom-call(s32[3]{0:T(128)} %pad_add_fusion.2.info.refs_0_, bf16[2,256,1024]{2,1,0:T(8,128)(2,1)} %refs_1_.5, bf16[2,2,256,1024]{3,2,1,0:T(8,128)(2,1)} %refs_2_.5, ...), custom_call_target="tpu_custom_call", output_to_operand_aliasing={{0}: (12, {}), {1}: (13, {})} | custom-call | flops 20971520 | bytes 65536 | tf_op jit(solution)/shard_map/pallas_call | solution.py:236
  140.3 1.3 copy-done
  141.8 0.8 copy-done.18
  142.7 0.5 collective-permute-start.24
  143.2 1.3 collective-permute-start.25
  144.5 1.7 %collective-permute-done.27.refs_10_.refs_6_ = bf16[512,2048]{1,0:T(8,128)(2,1)S(1)} collective-permute-done((bf16[512,2048]{1,0:T(8,128)(2,1)}, bf16[512,2048]{1,0:T(8,128)(2,1)S(1)}, u32[]{:S(2)}, u32[]{:S(2)}) %collective-permute-start.27) | collective-permute-done | bytes 2097184 | tf_op jit(solution)/shard_map/ppermute | solution.py:20
  146.2 1.6 copy-done.1
  147.7 5.7 %shard_map.53.refs_7_ = f32[2,256,2048]{2,1,0:T(8,128)S(1)} custom-call(s32[3]{0:T(128)S(1)} %copy-done.10, bf16[2,256,256]{2,1,0:T(8,128)(2,1)S(1)} %copy-done.9, bf16[2,256,256]{2,1,0:T(8,128)(2,1)S(1)} %copy-done.8, bf16[2,256,256]{2,1,0:T(8,128)(2,1)S(1)} %copy-done.3, bf16[2,256,256]{2,1,0:T(8,128)(2,1)S(1)} %copy-done.7, ...), custom_call_target="tpu_custom_call" | custom-call | flops 335544320 | bytes 655360 | tf_op jit(solution)/shard_map/pallas_call | solution.py:303
  153.4 3.0 %collective-permute-done.25.refs_3_ = bf16[2,256,256]{2,1,0:T(8,128)(2,1)S(1)} collective-permute-done((bf16[2,256,256]{2,1,0:T(8,128)(2,1)S(1)}, bf16[2,256,256]{2,1,0:T(8,128)(2,1)S(1)}, u32[]{:S(2)}, u32[]{:S(2)}) %collective-permute-start.25) | collective-permute-done | bytes 262176 | tf_op jit(solution)/shard_map/ppermute | solution.py:25
  156.5 5.3 %shard_map.54 = bf16[2,256,2048]{2,1,0:T(8,128)(2,1)} custom-call(s32[3]{0:T(128)S(1)} %copy-done.10, bf16[2,256,256]{2,1,0:T(8,128)(2,1)S(1)} %collective-permute-done.23.refs_1_, bf16[2,256,256]{2,1,0:T(8,128)(2,1)S(1)} %collective-permute-done.24.refs_2_, bf16[2,256,256]{2,1,0:T(8,128)(2,1)S(1)} %collective-permute-done.25.refs_3_, ...), custom_call_target="tpu_custom_call" | custom-call | flops 201326592 | bytes 393216 | tf_op jit(solution)/shard_map/pallas_call | solution.py:303
  (74 shorter events, 1.7 us)
Async XLA Ops:
  0.0 4.5 %collective-permute-start.1 = (bf16[2,2,256,1024]{3,2,1,0:T(8,128)(2,1)}, bf16[2,2,256,1024]{3,2,1,0:T(8,128)(2,1)S(1)}, u32[]{:S(2)}, u32[]{:S(2)}) collective-permute-start(bf16[2,2,256,1024]{3,2,1,0:T(8,128)(2,1)} %refs_2_.5), channel_id=1, source_target_pairs={{0,2},{2,0},{4,6},{6,4},{8,10},{10,8},{12,14},{14,12},{16,18},{18,... | collective-permute-start | bytes 6291464 | tf_op jit(solution)/shard_map/ppermute | solution.py:20
  1.1 12.2 %copy-start.12 = (bf16[2,256,1024]{2,1,0:T(8,128)(2,1)S(1)}, bf16[2,256,1024]{2,1,0:T(8,128)(2,1)}, u32[]{:S(2)}) copy-start(bf16[2,256,1024]{2,1,0:T(8,128)(2,1)} %refs_1_.5) | copy-start | bytes 3145732
  4.5 1.3 copy-start.11
  8.4 17.6 %collective-permute-start.5 = (bf16[2,2,256,128]{3,2,1,0:T(8,128)(2,1)}, bf16[2,2,256,128]{3,2,1,0:T(8,128)(2,1)S(1)}, u32[]{:S(2)}, u32[]{:S(2)}) collective-permute-start(bf16[2,2,256,128]{3,2,1,0:T(8,128)(2,1)} %shard_map.46.refs_2_), channel_id=1, source_target_pairs={{0,8},{2,10},{4,12},{6,14},{8,16},{10,18},{12,20},{14,22},{16,24},... | collective-permute-start | bytes 786440 | tf_op jit(solution)/shard_map/ppermute | solution.py:20
  13.3 78.9 %collective-permute-start = (bf16[2,256,1024]{2,1,0:T(8,128)(2,1)S(1)}, bf16[2,256,1024]{2,1,0:T(8,128)(2,1)}, u32[]{:S(2)}, u32[]{:S(2)}) collective-permute-start(bf16[2,256,1024]{2,1,0:T(8,128)(2,1)S(1)} %copy-done.12), channel_id=1, source_target_pairs={{0,2},{2,0},{4,6},{6,4},{8,10},{10,8},{12,14},{14,12},{16,18},{18,... | collective-permute-start | bytes 3145736 | tf_op jit(solution)/shard_map/ppermute | solution.py:20
  16.7 26.0 %copy-start.19 = (s32[4,32]{1,0:T(4,128)S(1)}, s32[4,32]{1,0:T(4,128)}, u32[]{:S(2)}) copy-start(s32[4,32]{1,0:T(4,128)} %param.6) | copy-start | bytes 1540
  16.7 123.6 %collective-permute-start.26 = (bf16[512,2048]{1,0:T(8,128)(2,1)}, bf16[512,2048]{1,0:T(8,128)(2,1)S(1)}, u32[]{:S(2)}, u32[]{:S(2)}) collective-permute-start(bf16[512,2048]{1,0:T(8,128)(2,1)} %shard_map.51), channel_id=1, source_target_pairs={{0,1},{1,0},{2,3},{3,2},{4,5},{5,4},{6,7},{7,6},{8,9},{9,8},{10,11... | collective-permute-start | bytes 6291464 | tf_op jit(solution)/shard_map/ppermute | solution.py:25
  21.7 10.4 %collective-permute-start.3 = (bf16[2,2,256,128]{3,2,1,0:T(8,128)(2,1)}, bf16[2,2,256,128]{3,2,1,0:T(8,128)(2,1)}, u32[]{:S(2)}, u32[]{:S(2)}) collective-permute-start(bf16[2,2,256,128]{3,2,1,0:T(8,128)(2,1)} %get-tuple-element.32), channel_id=1, source_target_pairs={{0,8},{2,10},{4,12},{6,14},{8,16},{10,18},{12,20},{14,22},{16,24},... | collective-permute-start | bytes 786440 | tf_op jit(solution)/shard_map/ppermute | solution.py:20
  25.9 41.1 %copy-start.14 = (bf16[2,2,256,128]{3,2,1,0:T(8,128)(2,1)}, bf16[2,2,256,128]{3,2,1,0:T(8,128)(2,1)S(1)}, u32[]{:S(2)}) copy-start(bf16[2,2,256,128]{3,2,1,0:T(8,128)(2,1)S(1)} %collective-permute-done.5.refs_7_) | copy-start | bytes 786436
  25.9 11.0 %collective-permute-start.7 = (bf16[2,2,256,128]{3,2,1,0:T(8,128)(2,1)S(1)}, bf16[2,2,256,128]{3,2,1,0:T(8,128)(2,1)S(1)}, u32[]{:S(2)}, u32[]{:S(2)}) collective-permute-start(bf16[2,2,256,128]{3,2,1,0:T(8,128)(2,1)S(1)} %collective-permute-done.5.refs_7_), channel_id=1, source_target_pairs={{0,8},{2,10},{4,12},{6,14},{8,16},{10,18},{12,20},{14,22},{16,24},... | collective-permute-start | bytes 786440 | tf_op jit(solution)/shard_map/ppermute | solution.py:20
  28.8 14.1 %collective-permute-start.11 = (bf16[2,2,256,128]{3,2,1,0:T(8,128)(2,1)S(1)}, bf16[2,2,256,128]{3,2,1,0:T(8,128)(2,1)}, u32[]{:S(2)}, u32[]{:S(2)}) collective-permute-start(bf16[2,2,256,128]{3,2,1,0:T(8,128)(2,1)S(1)} %collective-permute-done.5.refs_7_), channel_id=1, source_target_pairs={{0,4},{2,6},{4,0},{6,2},{8,12},{10,14},{12,8},{14,10},{16,20},{18,... | collective-permute-start | bytes 786440 | tf_op jit(solution)/shard_map/ppermute | solution.py:20
  37.0 0.7 copy-start.15
  37.7 10.6 %collective-permute-start.8 = (bf16[2,2,256,128]{3,2,1,0:T(8,128)(2,1)}, bf16[2,2,256,128]{3,2,1,0:T(8,128)(2,1)}, u32[]{:S(2)}, u32[]{:S(2)}) collective-permute-start(bf16[2,2,256,128]{3,2,1,0:T(8,128)(2,1)} %collective-permute-done.3.refs_11_), channel_id=1, source_target_pairs={{0,8},{2,10},{4,12},{6,14},{8,16},{10,18},{12,20},{14,22},{16,24},... | collective-permute-start | bytes 786440 | tf_op jit(solution)/shard_map/ppermute | solution.py:20
  42.8 3.6 %collective-permute-start.19 = (s32[4,32]{1,0:T(4,128)S(1)}, s32[4,32]{1,0:T(4,128)S(1)}, u32[]{:S(2)}, u32[]{:S(2)}) collective-permute-start(s32[4,32]{1,0:T(4,128)S(1)} %copy-done.19), channel_id=1, source_target_pairs={{0,2},{2,0},{4,6},{6,4},{8,10},{10,8},{12,14},{14,12},{16,18},{18,... | collective-permute-start | bytes 1544 | tf_op jit(solution)/shard_map/ppermute | solution.py:20
  42.9 20.3 %collective-permute-start.6 = (bf16[2,2,256,128]{3,2,1,0:T(8,128)(2,1)}, bf16[2,2,256,128]{3,2,1,0:T(8,128)(2,1)}, u32[]{:S(2)}, u32[]{:S(2)}) collective-permute-start(bf16[2,2,256,128]{3,2,1,0:T(8,128)(2,1)} %get-tuple-element.35), channel_id=1, source_target_pairs={{0,8},{2,10},{4,12},{6,14},{8,16},{10,18},{12,20},{14,22},{16,24},... | collective-permute-start | bytes 786440 | tf_op jit(solution)/shard_map/ppermute | solution.py:20
  46.4 18.1 %collective-permute-start.12 = (bf16[2,2,256,128]{3,2,1,0:T(8,128)(2,1)}, bf16[2,2,256,128]{3,2,1,0:T(8,128)(2,1)}, u32[]{:S(2)}, u32[]{:S(2)}) collective-permute-start(bf16[2,2,256,128]{3,2,1,0:T(8,128)(2,1)} %collective-permute-done.3.refs_11_), channel_id=1, source_target_pairs={{0,4},{2,6},{4,0},{6,2},{8,12},{10,14},{12,8},{14,10},{16,20},{18,... | collective-permute-start | bytes 786440 | tf_op jit(solution)/shard_map/ppermute | solution.py:20
  48.3 12.4 %collective-permute-start.15 = (bf16[2,2,256,128]{3,2,1,0:T(8,128)(2,1)}, bf16[2,2,256,128]{3,2,1,0:T(8,128)(2,1)}, u32[]{:S(2)}, u32[]{:S(2)}) collective-permute-start(bf16[2,2,256,128]{3,2,1,0:T(8,128)(2,1)} %copy-done.15), channel_id=1, source_target_pairs={{4,0},{6,2},{12,8},{14,10},{20,16},{22,18},{28,24},{30,26},{5,1},{... | collective-permute-start | bytes 786440 | tf_op jit(solution)/shard_map/ppermute | solution.py:20
  60.8 34.6 %collective-permute-start.2 = (bf16[2,2,256,512]{3,2,1,0:T(8,128)(2,1)}, bf16[2,2,256,512]{3,2,1,0:T(8,128)(2,1)}, u32[]{:S(2)}, u32[]{:S(2)}) collective-permute-start(bf16[2,2,256,512]{3,2,1,0:T(8,128)(2,1)} %get-tuple-element.30.refs_5_), channel_id=1, source_target_pairs={{0,4},{2,6},{8,12},{10,14},{16,20},{18,22},{24,28},{26,30},{1,5},{... | collective-permute-start | bytes 3145736 | tf_op jit(solution)/shard_map/ppermute | solution.py:20
  63.2 9.6 %collective-permute-start.16 = (bf16[2,2,256,128]{3,2,1,0:T(8,128)(2,1)}, bf16[2,2,256,128]{3,2,1,0:T(8,128)(2,1)}, u32[]{:S(2)}, u32[]{:S(2)}) collective-permute-start(bf16[2,2,256,128]{3,2,1,0:T(8,128)(2,1)} %collective-permute-done.8.refs_12_), channel_id=1, source_target_pairs={{4,0},{6,2},{12,8},{14,10},{20,16},{22,18},{28,24},{30,26},{5,1},{... | collective-permute-start | bytes 786440 | tf_op jit(solution)/shard_map/ppermute | solution.py:20
  64.5 9.6 %collective-permute-start.9 = (bf16[2,2,256,128]{3,2,1,0:T(8,128)(2,1)}, bf16[2,2,256,128]{3,2,1,0:T(8,128)(2,1)}, u32[]{:S(2)}, u32[]{:S(2)}) collective-permute-start(bf16[2,2,256,128]{3,2,1,0:T(8,128)(2,1)} %collective-permute-done.6.refs_7_), channel_id=1, source_target_pairs={{0,8},{2,10},{4,12},{6,14},{8,16},{10,18},{12,20},{14,22},{16,24},... | collective-permute-start | bytes 786440 | tf_op jit(solution)/shard_map/ppermute | solution.py:20
  72.8 5.9 %collective-permute-start.4 = (bf16[2,2,256,128]{3,2,1,0:T(8,128)(2,1)}, bf16[2,2,256,128]{3,2,1,0:T(8,128)(2,1)S(1)}, u32[]{:S(2)}, u32[]{:S(2)}) collective-permute-start(bf16[2,2,256,128]{3,2,1,0:T(8,128)(2,1)} %get-tuple-element.33), channel_id=1, source_target_pairs={{0,8},{2,10},{4,12},{6,14},{8,16},{10,18},{12,20},{14,22},{16,24},... | collective-permute-start | bytes 786440 | tf_op jit(solution)/shard_map/ppermute | solution.py:20
  74.1 16.1 %collective-permute-start.13 = (bf16[2,2,256,128]{3,2,1,0:T(8,128)(2,1)}, bf16[2,2,256,128]{3,2,1,0:T(8,128)(2,1)}, u32[]{:S(2)}, u32[]{:S(2)}) collective-permute-start(bf16[2,2,256,128]{3,2,1,0:T(8,128)(2,1)} %collective-permute-done.6.refs_7_), channel_id=1, source_target_pairs={{0,4},{2,6},{4,0},{6,2},{8,12},{10,14},{12,8},{14,10},{16,20},{18,... | collective-permute-start | bytes 786440 | tf_op jit(solution)/shard_map/ppermute | solution.py:20
  78.7 16.6 %copy-start.13 = (bf16[2,2,256,128]{3,2,1,0:T(8,128)(2,1)}, bf16[2,2,256,128]{3,2,1,0:T(8,128)(2,1)S(1)}, u32[]{:S(2)}) copy-start(bf16[2,2,256,128]{3,2,1,0:T(8,128)(2,1)S(1)} %collective-permute-done.4.refs_16_.refs_7_) | copy-start | bytes 786436
  78.7 34.3 %collective-permute-start.17 = (bf16[2,2,256,128]{3,2,1,0:T(8,128)(2,1)}, bf16[2,2,256,128]{3,2,1,0:T(8,128)(2,1)}, u32[]{:S(2)}, u32[]{:S(2)}) collective-permute-start(bf16[2,2,256,128]{3,2,1,0:T(8,128)(2,1)} %collective-permute-done.9.refs_17_.refs_8_), channel_id=1, source_target_pairs={{4,0},{6,2},{12,8},{14,10},{20,16},{22,18},{28,24},{30,26},{5,1},{... | collective-permute-start | bytes 786440 | tf_op jit(solution)/shard_map/ppermute | solution.py:20
  90.2 23.5 %collective-permute-start.10 = (bf16[2,2,256,128]{3,2,1,0:T(8,128)(2,1)S(1)}, bf16[2,2,256,128]{3,2,1,0:T(8,128)(2,1)}, u32[]{:S(2)}, u32[]{:S(2)}) collective-permute-start(bf16[2,2,256,128]{3,2,1,0:T(8,128)(2,1)S(1)} %collective-permute-done.4.refs_16_.refs_7_), channel_id=1, source_target_pairs={{0,8},{2,10},{4,12},{6,14},{8,16},{10,18},{12,20},{14,22},{16,24},... | collective-permute-start | bytes 786440 | tf_op jit(solution)/shard_map/ppermute | solution.py:20
  92.2 23.0 %collective-permute-start.14 = (bf16[2,2,256,128]{3,2,1,0:T(8,128)(2,1)S(1)}, bf16[2,2,256,128]{3,2,1,0:T(8,128)(2,1)S(1)}, u32[]{:S(2)}, u32[]{:S(2)}) collective-permute-start(bf16[2,2,256,128]{3,2,1,0:T(8,128)(2,1)S(1)} %collective-permute-done.4.refs_16_.refs_7_), channel_id=1, source_target_pairs={{0,4},{2,6},{4,0},{6,2},{8,12},{10,14},{12,8},{14,10},{16,20},{18,... | collective-permute-start | bytes 786440 | tf_op jit(solution)/shard_map/ppermute | solution.py:20
  113.0 14.8 %collective-permute-start.20 = (bf16[2,256,256]{2,1,0:T(8,128)(2,1)}, bf16[2,256,256]{2,1,0:T(8,128)(2,1)S(1)}, u32[]{:S(2)}, u32[]{:S(2)}) collective-permute-start(bf16[2,256,256]{2,1,0:T(8,128)(2,1)} %get-tuple-element.49), channel_id=1, source_target_pairs={{0,2},{2,0},{4,6},{6,4},{8,10},{10,8},{12,14},{14,12},{16,18},{18,... | collective-permute-start | bytes 786440 | tf_op jit(solution)/shard_map/ppermute | solution.py:20
  113.1 14.9 %collective-permute-start.22 = (bf16[2,256,256]{2,1,0:T(8,128)(2,1)}, bf16[2,256,256]{2,1,0:T(8,128)(2,1)S(1)}, u32[]{:S(2)}, u32[]{:S(2)}) collective-permute-start(bf16[2,256,256]{2,1,0:T(8,128)(2,1)} %get-tuple-element.49), channel_id=1, source_target_pairs={{0,3},{1,2},{2,1},{3,0},{4,7},{5,6},{6,5},{7,4},{8,11},{9,10},{10,... | collective-permute-start | bytes 786440 | tf_op jit(solution)/shard_map/ppermute | solution.py:25
  113.7 14.2 %collective-permute-start.21 = (bf16[2,256,256]{2,1,0:T(8,128)(2,1)}, bf16[2,256,256]{2,1,0:T(8,128)(2,1)S(1)}, u32[]{:S(2)}, u32[]{:S(2)}) collective-permute-start(bf16[2,256,256]{2,1,0:T(8,128)(2,1)} %get-tuple-element.50.refs_1_), channel_id=1, source_target_pairs={{0,1},{1,0},{2,3},{3,2},{4,5},{5,4},{6,7},{7,6},{8,9},{9,8},{10,11... | collective-permute-start | bytes 786440 | tf_op jit(solution)/shard_map/ppermute | solution.py:25
  115.2 12.7 %copy-start.16 = (bf16[2,2,256,128]{3,2,1,0:T(8,128)(2,1)}, bf16[2,2,256,128]{3,2,1,0:T(8,128)(2,1)S(1)}, u32[]{:S(2)}) copy-start(bf16[2,2,256,128]{3,2,1,0:T(8,128)(2,1)S(1)} %collective-permute-done.14.refs_9_) | copy-start | bytes 786436
  115.2 12.7 %collective-permute-start.18 = (bf16[2,2,256,128]{3,2,1,0:T(8,128)(2,1)}, bf16[2,2,256,128]{3,2,1,0:T(8,128)(2,1)S(1)}, u32[]{:S(2)}, u32[]{:S(2)}) collective-permute-start(bf16[2,2,256,128]{3,2,1,0:T(8,128)(2,1)} %collective-permute-done.10.refs_12_.refs_8_), channel_id=1, source_target_pairs={{4,0},{6,2},{12,8},{14,10},{20,16},{22,18},{28,24},{30,26},{5,1},{... | collective-permute-start | bytes 786440 | tf_op jit(solution)/shard_map/ppermute | solution.py:20
  127.9 0.7 copy-start.2
  127.9 0.8 copy-start.6
  127.9 0.8 copy-start.4
  127.9 0.9 copy-start.17
  140.3 1.3 copy-start
  141.6 0.9 copy-start.18
  141.6 1.0 copy-start.8
  141.6 4.5 %copy-start.3 = (bf16[2,256,256]{2,1,0:T(8,128)(2,1)S(1)}, bf16[2,256,256]{2,1,0:T(8,128)(2,1)}, u32[]{:S(2)}) copy-start(bf16[2,256,256]{2,1,0:T(8,128)(2,1)} %copy-done.2) | copy-start | bytes 786436
  141.6 4.5 %copy-start.5 = (bf16[2,256,256]{2,1,0:T(8,128)(2,1)S(1)}, bf16[2,256,256]{2,1,0:T(8,128)(2,1)}, u32[]{:S(2)}) copy-start(bf16[2,256,256]{2,1,0:T(8,128)(2,1)} %copy-done.4) | copy-start | bytes 786436
  141.6 4.5 %copy-start.7 = (bf16[2,256,256]{2,1,0:T(8,128)(2,1)S(1)}, bf16[2,256,256]{2,1,0:T(8,128)(2,1)}, u32[]{:S(2)}) copy-start(bf16[2,256,256]{2,1,0:T(8,128)(2,1)} %copy-done.6) | copy-start | bytes 786436
  141.6 4.5 %copy-start.9 = (bf16[2,256,256]{2,1,0:T(8,128)(2,1)S(1)}, bf16[2,256,256]{2,1,0:T(8,128)(2,1)}, u32[]{:S(2)}) copy-start(bf16[2,256,256]{2,1,0:T(8,128)(2,1)} %get-tuple-element.50.refs_1_) | copy-start | bytes 786436
  141.7 4.5 %copy-start.10 = (s32[3]{0:T(128)S(1)}, s32[3]{0:T(128)}, u32[]{:S(2)}) copy-start(s32[3]{0:T(128)} %pad_add_fusion.2.info.refs_0_) | copy-start | bytes 40
  141.7 4.4 %collective-permute-start.27 = (bf16[512,2048]{1,0:T(8,128)(2,1)}, bf16[512,2048]{1,0:T(8,128)(2,1)S(1)}, u32[]{:S(2)}, u32[]{:S(2)}) collective-permute-start(bf16[512,2048]{1,0:T(8,128)(2,1)} %shard_map.52.refs_9_.refs_5_), channel_id=1, source_target_pairs={{0,2},{2,0},{4,6},{6,4},{8,10},{10,8},{12,14},{14,12},{16,18},{18,... | collective-permute-start | bytes 6291464 | tf_op jit(solution)/shard_map/ppermute | solution.py:20
  142.6 10.8 %collective-permute-start.23 = (bf16[2,256,256]{2,1,0:T(8,128)(2,1)S(1)}, bf16[2,256,256]{2,1,0:T(8,128)(2,1)S(1)}, u32[]{:S(2)}, u32[]{:S(2)}) collective-permute-start(bf16[2,256,256]{2,1,0:T(8,128)(2,1)S(1)} %copy-done.18), channel_id=1, source_target_pairs={{0,2},{2,0},{4,6},{6,4},{8,10},{10,8},{12,14},{14,12},{16,18},{18,... | collective-permute-start | bytes 786440 | tf_op jit(solution)/shard_map/ppermute | solution.py:20
  142.7 10.8 %collective-permute-start.24 = (bf16[2,256,256]{2,1,0:T(8,128)(2,1)S(1)}, bf16[2,256,256]{2,1,0:T(8,128)(2,1)S(1)}, u32[]{:S(2)}, u32[]{:S(2)}) collective-permute-start(bf16[2,256,256]{2,1,0:T(8,128)(2,1)S(1)} %copy-done.8), channel_id=1, source_target_pairs={{0,1},{1,0},{2,3},{3,2},{4,5},{5,4},{6,7},{7,6},{8,9},{9,8},{10,11... | collective-permute-start | bytes 786440 | tf_op jit(solution)/shard_map/ppermute | solution.py:25
  143.2 13.3 %collective-permute-start.25 = (bf16[2,256,256]{2,1,0:T(8,128)(2,1)S(1)}, bf16[2,256,256]{2,1,0:T(8,128)(2,1)S(1)}, u32[]{:S(2)}, u32[]{:S(2)}) collective-permute-start(bf16[2,256,256]{2,1,0:T(8,128)(2,1)S(1)} %copy-done.18), channel_id=1, source_target_pairs={{0,3},{1,2},{2,1},{3,0},{4,7},{5,6},{6,5},{7,4},{8,11},{9,10},{10,... | collective-permute-start | bytes 786440 | tf_op jit(solution)/shard_map/ppermute | solution.py:25
  146.1 1.6 copy-start.1

commit v5 on v4

--- a/solution.py
+++ b/solution.py
@@ -15,30 +15,33 @@
 VMEM = 60 * 1024 * 1024
 
 
-def moved(array, n, go):
+def moved(array, n, go, name):
     pairs = [(i, go(i)) for i in range(n) if go(i) is not None]
-    return lax.ppermute(array, "ctx", pairs)
-
-
-def moved_both(array, n, f, go):
+    with jax.named_scope(name):
+        return lax.ppermute(array, "ctx", pairs)
+
+
+def moved_both(array, n, f, go, name):
     pairs = [(i * f + k, go(i, k)[0] * f + go(i, k)[1]) for i in range(n) for k in range(f)]
-    return lax.ppermute(array, ("ctx", "fsdp"), pairs)
+    with jax.named_scope(name):
+        return lax.ppermute(array, ("ctx", "fsdp"), pairs)
 
 
 def behind(array, *others):
     return lax.optimization_barrier((array,) + others)[0] if others else array
 
 
-def gated(array, tie):
+def gated(arrays, *ties):
+    some = pl.BlockSpec(memory_space=pl.ANY)
     return pl.pallas_call(
         lambda *refs: None,
-        in_specs=[pl.BlockSpec(memory_space=pl.ANY)] * 2,
-        out_specs=pl.BlockSpec(memory_space=pl.ANY),
-        out_shape=jax.ShapeDtypeStruct(array.shape, array.dtype),
-        input_output_aliases={0: 0},
+        in_specs=[some] * (len(arrays) + len(ties)),
+        out_specs=[some] * len(arrays),
+        out_shape=[jax.ShapeDtypeStruct(a.shape, a.dtype) for a in arrays],
+        input_output_aliases={k: k for k in range(len(arrays))},
         compiler_params=pltpu.CompilerParams(vmem_limit_bytes=VMEM),
         cost_estimate=pl.CostEstimate(flops=0, bytes_accessed=0, transcendentals=0),
-    )(array, tie)
+    )(*arrays, *ties)
 
 
 def mask_table(first_block, rows, mask_rows):
@@ -104,10 +107,9 @@
 
 def attend_kernel(tokens, count, info, *refs):
     core, side = info[0], info[1]
-    refs = refs[:7 + 4 * count] + refs[-6:]
-    q_here, n_here, q_there, n_there, own, low = refs[:6]
-    blocks = [refs[6 + 4 * h:10 + 4 * h] for h in range(count)]
-    table, mine, give, tie, keys, values, least = refs[6 + 4 * count:]
+    ins, refs = refs[:4 * count + 2 * count + 4], refs[-7:]
+    views, pairs, blocks = ins[:4 * count], ins[4 * count:6 * count], ins[6 * count:]
+    table, mine, give, tie, keys, values, least = refs
     tie[...] = jnp.zeros_like(tie)
     rows = tokens // BLK
     span = WINB * BLK + tokens
@@ -120,23 +122,23 @@
             keys[head, pl.ds(at, tokens), :] = ref[slot, 0, :, lanes]
             values[head, pl.ds(at, tokens), :] = ref[slot, 1, :, lanes]
 
-    only = slice(0, HD)
-    for head, (one, two, swap, far) in enumerate(blocks):
+    one, two, swap, far = blocks
+    for head in range(count):
         lanes = slice(head * HD, (head + 1) * HD)
-        place(head, two, 0, only)
-        place(head, one, 2, only)
-        place(head, swap, jnp.where(side == 0, 3, 1), only)
-        place(head, own, back, lanes)
+        place(head, two, 0, lanes)
+        place(head, one, 2, lanes)
+        place(head, swap, jnp.where(side == 0, 3, 1), lanes)
+        place(head, pairs[2 * head], back, slice(None))
 
     @pl.when(side == 0)
     def _():
         for head in range(count):
-            place(head, blocks[head][3], 1, only)
+            place(head, far, 1, slice(head * HD, (head + 1) * HD))
 
     @pl.when(side != 0)
     def _():
         for head in range(count):
-            place(head, low, 3, slice(head * HD, (head + 1) * HD))
+            place(head, pairs[2 * head + 1], 3, slice(None))
 
     spot = lax.broadcasted_iota(jnp.int32, (2 * tokens, HD), 0) // BLK
     lane = lax.broadcasted_iota(jnp.int32, (2 * tokens, HD), 1)
@@ -146,16 +148,15 @@
     tiles = (span + tokens) // step
 
     def operands(head, tile):
-        lanes = slice(head * HD, (head + 1) * HD)
         half = core if tile == 0 else 1 - core
-        q_ref, n_ref = (q_here, n_here) if tile == 0 else (q_there, n_there)
-        query = q_ref[:, :, lanes].reshape(2 * tokens, HD)
+        q_ref, n_ref = views[4 * head + 2 * tile:4 * head + 2 * tile + 2]
+        query = q_ref[...].reshape(2 * tokens, HD)
         key, value = [], []
         for k in range(tiles):
             at = pl.multiple_of((half + k) * tokens, tokens)
             if k == tiles - 1:
-                key.append(n_ref[0, 0, :, lanes])
-                value.append(n_ref[1, 0, :, lanes])
+                key.append(n_ref[0, 0])
+                value.append(n_ref[1, 0])
             else:
                 key.append(keys[head, pl.ds(at, step), :])
                 value.append(values[head, pl.ds(at, step), :])
@@ -219,34 +220,35 @@
             store(head, tile, total[:, :HD] / total[:, HD:])
 
 
-def attend(info, queries, keys_values, there, got, own, low, blocks, table, first, heads_half,
-           room, at, into, after):
+def attend(info, queries, keys_values, there, got, own, low, blocks, table, part, heads_half, after):
     tokens = queries.shape[1]
     span = WINB * BLK + 2 * tokens
-    count = len(blocks)
+    count = len(part)
     wide = count * HD
-    per = heads_half // count if heads_half % count == 0 and first % count == 0 else None
-    assert per is not None
-    here = lambda s, info: (0, 0, info[0] * per + first // count)
-    out_spec = pl.BlockSpec((2, tokens, wide), lambda s, info: (0, 0, at // count))
-    out = jax.ShapeDtypeStruct((2, tokens, room * HD), jnp.bfloat16)
-    work = count * 2 * 2 * tokens * (WINB * BLK + 2 * tokens)
-    whole = pl.BlockSpec((2, 2, tokens, wide), lambda s, info: (0, 0, 0, first // count))
-    one_head = pl.BlockSpec((2, 2, tokens, HD), lambda s, info: (0, 0, 0, 0))
+    views, view_specs, pairs, pair_specs = [], [], [], []
+    for head in part:
+        here = lambda s, info, head=head: (0, 0, info[0] * heads_half + head)
+        noisy = lambda s, info, head=head: (0, 1, 0, info[0] * heads_half + head)
+        views += [queries, keys_values, there, got]
+        view_specs += [
+            pl.BlockSpec((2, tokens, HD), here), pl.BlockSpec((2, 1, tokens, HD), noisy)
+        ] * 2
+        pairs += [own, low]
+        pair_specs += [
+            pl.BlockSpec((2, 2, tokens, HD), lambda s, info, head=head: (0, 0, 0, head))] * 2
+    out_spec = pl.BlockSpec((2, tokens, wide), lambda s, info: (0, 0, 0))
+    out = jax.ShapeDtypeStruct((2, tokens, wide), jnp.bfloat16)
+    work = count * 2 * 2 * tokens * span
     return pl.pallas_call(
         lambda *refs: attend_kernel(tokens, count, *refs),
         grid_spec=pltpu.PrefetchScalarGridSpec(
             num_scalar_prefetch=1,
             grid=(1,),
             in_specs=[
-                *[
-                    pl.BlockSpec((2, tokens, wide), here),
-                    pl.BlockSpec((2, 1, tokens, wide), lambda s, info: (0, 1) + here(s, info)[1:]),
-                ] * 2,
-                whole, whole,
-                *[one_head] * (4 * count),
+                *view_specs, *pair_specs,
+                *[pl.BlockSpec((2, 2, tokens, wide), lambda s, info: (0, 0, 0, 0))] * 4,
+                *[pl.BlockSpec(memory_space=pl.ANY)] * len(after),
                 pl.BlockSpec(table.shape, lambda s, info: (0, 0, 0)),
-                *[pl.BlockSpec(memory_space=pl.ANY)] * (len(into) + len(after)),
             ],
             out_specs=[out_spec, out_spec, pl.BlockSpec((8, HD), lambda s, info: (0, 0))],
             scratch_shapes=[
@@ -256,13 +258,12 @@
             ],
         ),
         out_shape=[out, out, jax.ShapeDtypeStruct((8, HD), jnp.float32)],
-        input_output_aliases={8 + 4 * count + k: k for k in range(len(into))},
         compiler_params=pltpu.CompilerParams(vmem_limit_bytes=VMEM),
         cost_estimate=pl.CostEstimate(
             flops=work * 8, bytes_accessed=count * 64 * 1024, transcendentals=0
         ),
-    )(info, queries, keys_values, there, got, own, low, *[b for group in blocks for b in group], table,
-      *into, *after)
+    )(info, *views, *pairs, *blocks, *after, table)
+
 
 def project_kernel(count, groups, add, info, *refs):
     out = refs[-1]
@@ -282,16 +283,18 @@
     half = weights[0].shape[0] // 2
     used, specs = [], []
     for group, first, act in pieces:
-        wide = act.shape[2]
-        per, at = half // wide, first * HD // wide
-        used.append(weights[group])
-        if group == 0:
-            row = lambda s, info, at=at, per=per: (info[0] * per + at, info[2] * steps + s)
-        elif group == 1:
-            row = lambda s, info, at=at, per=per: ((1 - info[0]) * per + at, info[2] * steps + s)
-        else:
-            row = lambda s, info, at=at: (at, s)
-        specs.append(pl.BlockSpec((wide, tile), row))
+        wide = act.shape[2] if first * HD % act.shape[2] == 0 else HD
+        per = half // wide
+        for at in range(first * HD // wide, (first * HD + act.shape[2]) // wide):
+            used.append(weights[group])
+            if group == 0:
+                row = lambda s, info, at=at, per=per: (info[0] * per + at, info[2] * steps + s)
+            elif group == 1:
+                row = lambda s, info, at=at, per=per: (
+                    (1 - info[0]) * per + at, info[2] * steps + s)
+            else:
+                row = lambda s, info, at=at: (at, s)
+            specs.append(pl.BlockSpec((wide, tile), row))
     flat = [act for _, _, act in pieces]
     spec = pl.BlockSpec((2, tokens, tile), lambda s, info: (0, 0, s))
     specs = [pl.BlockSpec(a.shape, lambda s, info: (0, 0, 0)) for a in flat] + specs
@@ -326,7 +329,7 @@
     rows = tokens // BLK
     features = out_weight.shape[1] // f
     bf16 = jnp.bfloat16
-    shares = [[0, 1], [2, 3]] if heads_half == 4 else [[h] for h in range(heads_half)]
+    parts = [[0,1],[2,3]] if heads_half == 4 else [[h] for h in range(heads_half)]
 
     pair = lambda i: i ^ 1
     ahead = lambda i: i + 4 if i + 4 < n else None
@@ -335,8 +338,8 @@
     lower = lambda i: i - 2 if i & 2 else None
     lanes = lambda start, size: pl.ds(pl.multiple_of(start, HD), size)
 
-    got = moved(keys_values, n, pair)
-    there = moved(queries, n, pair)
+    got = moved(keys_values, n, pair, "pair_kv")
+    there = moved(queries, n, pair, "pair_q")
 
     def cut_panels(core, place, ins, outs):
         pieces = []
@@ -366,38 +369,26 @@
 
     pair_shape = lambda heads: jax.ShapeDtypeStruct((2, 2, tokens, heads * HD), bf16)
     held = lambda heads: (2, tokens, heads * HD)
-    first, = copies(
-        info, [keys_values, got], [pair_shape(1)], [held(1)] * 2,
-        lambda core, place, ins, outs: join(core, ins, [(0, outs[0])]),
+    sizes = [heads_half] + [len(part) for part in parts]
+    whole, *own = copies(
+        info, [keys_values, got, *panels], [pair_shape(size) for size in sizes],
+        [held(size) for size in sizes] * 2,
+        lambda core, place, ins, outs: join(
+            core, ins, [(0, outs[0])] + [(p[0], out) for p, out in zip(parts, outs[1:])]),
     )
-    one = moved(first, n, ahead)
-    whole, *rest = copies(
-        info, [keys_values, got, first], [pair_shape(heads_half)] + [pair_shape(1)] * (heads_half - 1),
-        [held(heads_half)] + [held(1)] * (heads_half - 1) + [held(heads_half)]
-        + [held(1)] * (heads_half - 1),
-        lambda core, place, ins, outs: join(
-            core, ins,
-            [(0, outs[0])] + [(h, outs[h]) for h in range(1, heads_half)]),
-    )
-    own = [first] + rest
 
     sames = [
-        moved_both(panel, n, f, lambda i, k: (i, (k + r) % f))
+        moved_both(panel, n, f, lambda i, k: (i, (k + r) % f), "panel")
         for r, panel in enumerate(panels, 1)
     ]
 
     blocks = []
-    for h in range(heads_half):
-        last = blocks[-1] if blocks else None
-        in_turn = lambda array, k: behind(array, last[k]) if last else array
-        if h:
-            one = moved(behind(own[h], blocks[-2][0]) if h > 1 else own[h], n, ahead)
-        two = moved(in_turn(one, 1), n, ahead)
-        swap = moved(in_turn(one, 2), n, across)
-        far = moved(in_turn(two, 3), n, lower)
-        blocks.append((one, two, swap, far))
-    low = moved(whole, n, upper)
-    mask_there = moved(behind(block_mask, first), n, pair)
+    for k, mine in enumerate(own):
+        one = moved(mine, n, ahead, f"near{k}")
+        two = moved(one, n, ahead, f"far{k}")
+        blocks.append((one, two, moved(one, n, across, f"nearx{k}"), moved(two, n, lower, f"farx{k}")))
+    low = moved(whole, n, upper, "ownx")
+    mask_there = moved(block_mask, n, pair, "pair_mask")
     table = jnp.stack([
         mask_table(index * rows, rows, block_mask),
         mask_table((index ^ 1) * rows, rows, mask_there),
@@ -405,34 +396,28 @@
 
     acts = [[] for _ in range(2 * f)]
     ties = []
-    for k, share in enumerate(shares):
-        final = k == len(shares) - 1
-        into = ()
-        for run in [[h] for h in share] if final else [share]:
-            after = ([blocks[-1][0], blocks[-2][1]] if not final else [blocks[-1][1]]) \
-                if run[-1] < heads_half - 1 else [a[0] for a in acts[1:] if a]
-            mine, give, tie = attend(
-                info, queries, keys_values, there, got, whole, low,
-                [blocks[h] for h in run], table, run[0], heads_half,
-                len(share), run[0] - share[0], into, after + ties[-1:],
-            )
-            into = (mine, give)
-            ties.append(tie)
+    for k, part in enumerate(parts):
+        after = []
+        mine, give, tie = attend(
+            info, queries, keys_values, there, got, whole, low, blocks[k], table,
+            part, heads_half, after + ties[-1:],
+        )
+        ties.append(tie)
         acts[0].append(mine)
         for r in range(1, f):
-            acts[2 * r].append(moved_both(mine, n, f, lambda i, k: (i, (k + r) % f)))
-            acts[2 * r + 1].append(moved_both(give, n, f, lambda i, k: (i ^ 1, (k + r) % f)))
-        acts[1].append(moved(give, n, pair))
+            acts[2 * r].append(moved_both(mine, n, f, lambda i, k: (i, (k + r) % f), f"same{k}"))
+            acts[2 * r + 1].append(moved_both(give, n, f, lambda i, k: (i ^ 1, (k + r) % f), f"cross{k}"))
+        acts[1].append(moved(give, n, pair, f"pair{k}"))
     others = []
     for same in sames:
-        same = gated(same, ties[-1])
-        others += [same, moved(same, n, pair)]
+        same, = gated([same], ties[-1])
+        others += [same, moved(same, n, pair, "panel_pair")]
 
     weights = [out_weight, out_weight] + others
     early, late = [], []
     for g in range(2 * f):
-        for k, (share, act) in enumerate(zip(shares, acts[g])):
-            (late if g and k == len(shares) - 1 else early).append((g, share[0], act))
+        for k, (part, act) in enumerate(zip(parts, acts[g])):
+            (late if g and k == len(parts) - 1 else early).append((g, part[0], act))
     before = project(info, early, weights, features, jnp.float32)
     return project(info, late, weights, features, jnp.bfloat16, before)
 

time: 163 us -> 151 us (0.926)
  starting transfers between devices: 47.2 us -> 33.9 us
  waiting for transfers between devices: 44.8 us -> 55.8 us
  Pallas kernels: 60.9 us -> 54.2 us
  local copies, waits for them, and re-layouts: 7 us -> 4.25 us
    ppermute x23 -> x15, starting transfers between devices: 41.6 us -> 29.8 us  [moved(): return lax.ppermute(array, 'ctx', pairs)]
    ppermute x5, waiting for transfers between devices: 3.05 us -> 11.5 us  [moved_both(): return lax.ppermute(array, ('ctx', 'fsdp'), pairs)]
    pallas_call x3 -> x2, Pallas kernels: 40.5 us -> 36.3 us  [attend(): pl.pallas_call(lambda *refs: attend_kernel(tokens, count, *refs), grid_sp...]
    unnamed x40 -> x18, local copies, waits for them, and re-layouts: 6.8 us -> 4.05 us
    ppermute x23 -> x15, waiting for transfers between devices: 41.7 us -> 44.3 us  [moved(): return lax.ppermute(array, 'ctx', pairs)]
    pallas_call x3 -> x2, Pallas kernels: 9.38 us -> 6.89 us  [copies(): pl.pallas_call(kernel, grid_spec=pltpu.PrefetchScalarGridSpec(num_scalar_...]
  transfers between devices with their start and end apart: 28 -> 20, of which waited for: 10 -> 10; matrix products, arithmetic and copies ran while one was open for 1% -> 1% of each run, Pallas kernels for 33% -> 33%
where the time goes in v5:
time: 151 us; the launch traced here: 150 us
  waiting for transfers between devices  55.8 us (37%)
  Pallas kernels  54.2 us (36%)
  starting transfers between devices  33.9 us (22%)
  local copies, waits for them, and re-layouts  4.25 us (3%)
  other arithmetic  1.59 us (1%)
    ppermute x15, waiting for transfers between devices, moved(): return lax.ppermute(array, 'ctx', pairs)  44.3 us
    pallas_call x2, Pallas kernels, attend(): pl.pallas_call(lambda *refs: attend_kernel(tokens, count, *refs), grid_sp...  36.3 us
    ppermute x15, starting transfers between devices, moved(): return lax.ppermute(array, 'ctx', pairs)  29.8 us
    ppermute x5, waiting for transfers between devices, moved_both(): return lax.ppermute(array, ('ctx', 'fsdp'), pairs)  11.5 us
    pallas_call x2, Pallas kernels, project(): pl.pallas_call(lambda *refs: project_kernel(len(flat), len(used), before...  11 us
    pallas_call x2, Pallas kernels, copies(): pl.pallas_call(kernel, grid_spec=pltpu.PrefetchScalarGridSpec(num_scalar_...  6.89 us
    ppermute x5, starting transfers between devices, moved_both(): return lax.ppermute(array, ('ctx', 'fsdp'), pairs)  4.17 us
    unnamed x18, local copies, waits for them, and re-layouts  4.05 us
  transfers between devices with their start and end apart: 20, of which 10 were waited for; matrix products, arithmetic and copies ran while one was open for 1% of the time, Pallas kernels for 33%

profile of v5, /device:TPU:0, one launch (start us, length us, event | category | flops | bytes accessed | tf_op | source)
XLA Modules:
  0.0 150.0 jit_solution(4079713175372830401)
XLA Ops:
  0.0 0.5 collective-permute-start.1
  0.5 0.1 collective-permute-start.11
  0.5 0.5 collective-permute-start
  1.0 0.6 pad_add_fusion.2.info.refs_0_
  1.6 3.5 %shard_map.46.refs_2_ = bf16[512,2048]{1,0:T(8,128)(2,1)} custom-call(s32[3]{0:T(128)} %pad_add_fusion.2.info.refs_0_, bf16[1024,4096]{1,0:T(8,128)(2,1)} %refs_4_.1), custom_call_target="tpu_custom_call" | custom-call | bytes 1048576 | tf_op jit(solution)/shard_map/pallas_call | solution.py:89
  5.0 2.6 %collective-permute-start.15 = (bf16[512,2048]{1,0:T(8,128)(2,1)}, bf16[512,2048]{1,0:T(8,128)(2,1)S(1)}, u32[]{:S(2)}, u32[]{:S(2)}) collective-permute-start(bf16[512,2048]{1,0:T(8,128)(2,1)} %shard_map.46.refs_2_), channel_id=1, source_target_pairs={{0,1},{1,0},{2,3},{3,2},{4,5},{5,4},{6,7},{7,6},{8,9},{9,8},{10,11... | collective-permute-start | bytes 6291464 | tf_op jit(solution)/shard_map/panel/ppermute | solution.py:27
  7.6 0.1 fusion.4
  7.7 3.4 %shard_map.47 = (bf16[2,2,256,512]{3,2,1,0:T(8,128)(2,1)}, bf16[2,2,256,256]{3,2,1,0:T(8,128)(2,1)}, bf16[2,2,256,256]{3,2,1,0:T(8,128)(2,1)}) custom-call(s32[3]{0:T(128)} %pad_add_fusion.2.info.refs_0_, bf16[2,2,256,1024]{3,2,1,0:T(8,128)(2,1)} %refs_6_.4, bf16[2,2,256,1024]{3,2,1,0:T(8,128)(2,1)} %collective-permute-done.1.refs_1_.refs_4_.refs_8_, ...), custom_call_target="tpu_custom_call" | custom-call | bytes 1048576 | tf_op jit(solution)/shard_map/pallas_call | solution.py:89
  11.1 4.3 %collective-permute-start.7 = (bf16[2,2,256,256]{3,2,1,0:T(8,128)(2,1)}, bf16[2,2,256,256]{3,2,1,0:T(8,128)(2,1)}, u32[]{:S(2)}, u32[]{:S(2)}) collective-permute-start(bf16[2,2,256,256]{3,2,1,0:T(8,128)(2,1)} %get-tuple-element.16), channel_id=1, source_target_pairs={{0,8},{2,10},{4,12},{6,14},{8,16},{10,18},{12,20},{14,22},{16,24},... | collective-permute-start | bytes 1572872 | tf_op jit(solution)/shard_map/near0/ppermute | solution.py:21
  15.4 4.4 %collective-permute-start.2 = (bf16[2,2,256,512]{3,2,1,0:T(8,128)(2,1)}, bf16[2,2,256,512]{3,2,1,0:T(8,128)(2,1)}, u32[]{:S(2)}, u32[]{:S(2)}) collective-permute-start(bf16[2,2,256,512]{3,2,1,0:T(8,128)(2,1)} %get-tuple-element.14.refs_9_.refs_11_), channel_id=1, source_target_pairs={{0,4},{2,6},{8,12},{10,14},{16,20},{18,22},{24,28},{26,30},{1,5},{... | collective-permute-start | bytes 3145736 | tf_op jit(solution)/shard_map/ownx/ppermute | solution.py:21
  19.8 3.5 %collective-permute-start.3 = (bf16[2,2,256,256]{3,2,1,0:T(8,128)(2,1)}, bf16[2,2,256,256]{3,2,1,0:T(8,128)(2,1)}, u32[]{:S(2)}, u32[]{:S(2)}) collective-permute-start(bf16[2,2,256,256]{3,2,1,0:T(8,128)(2,1)} %get-tuple-element.15), channel_id=1, source_target_pairs={{0,8},{2,10},{4,12},{6,14},{8,16},{10,18},{12,20},{14,22},{16,24},... | collective-permute-start | bytes 1572872 | tf_op jit(solution)/shard_map/near1/ppermute | solution.py:21
  23.3 0.1 fusion.2
  23.4 3.8 %collective-permute-done.7.refs_13_ = bf16[2,2,256,256]{3,2,1,0:T(8,128)(2,1)} collective-permute-done((bf16[2,2,256,256]{3,2,1,0:T(8,128)(2,1)}, bf16[2,2,256,256]{3,2,1,0:T(8,128)(2,1)}, u32[]{:S(2)}, u32[]{:S(2)}) %collective-permute-start.7) | collective-permute-done | bytes 524320 | tf_op jit(solution)/shard_map/near0/ppermute | solution.py:21
  27.2 5.2 %collective-permute-start.8 = (bf16[2,2,256,256]{3,2,1,0:T(8,128)(2,1)}, bf16[2,2,256,256]{3,2,1,0:T(8,128)(2,1)}, u32[]{:S(2)}, u32[]{:S(2)}) collective-permute-start(bf16[2,2,256,256]{3,2,1,0:T(8,128)(2,1)} %collective-permute-done.7.refs_13_), channel_id=1, source_target_pairs={{0,8},{2,10},{4,12},{6,14},{8,16},{10,18},{12,20},{14,22},{16,24},... | collective-permute-start | bytes 1572872 | tf_op jit(solution)/shard_map/far0/ppermute | solution.py:21
  32.4 6.0 %collective-permute-done.3.refs_13_ = bf16[2,2,256,256]{3,2,1,0:T(8,128)(2,1)} collective-permute-done((bf16[2,2,256,256]{3,2,1,0:T(8,128)(2,1)}, bf16[2,2,256,256]{3,2,1,0:T(8,128)(2,1)}, u32[]{:S(2)}, u32[]{:S(2)}) %collective-permute-start.3) | collective-permute-done | bytes 524320 | tf_op jit(solution)/shard_map/near1/ppermute | solution.py:21
  38.4 5.2 %collective-permute-start.4 = (bf16[2,2,256,256]{3,2,1,0:T(8,128)(2,1)}, bf16[2,2,256,256]{3,2,1,0:T(8,128)(2,1)}, u32[]{:S(2)}, u32[]{:S(2)}) collective-permute-start(bf16[2,2,256,256]{3,2,1,0:T(8,128)(2,1)} %collective-permute-done.3.refs_13_), channel_id=1, source_target_pairs={{0,8},{2,10},{4,12},{6,14},{8,16},{10,18},{12,20},{14,22},{16,24},... | collective-permute-start | bytes 1572872 | tf_op jit(solution)/shard_map/far1/ppermute | solution.py:21
  43.6 0.1 broadcast_and_fusion.3
  43.7 0.1 pad_add_fusion
  43.8 0.1 copy.10
  43.9 0.1 copy.9
  44.0 1.6 %collective-permute-start.9 = (bf16[2,2,256,256]{3,2,1,0:T(8,128)(2,1)}, bf16[2,2,256,256]{3,2,1,0:T(8,128)(2,1)}, u32[]{:S(2)}, u32[]{:S(2)}) collective-permute-start(bf16[2,2,256,256]{3,2,1,0:T(8,128)(2,1)} %collective-permute-done.7.refs_13_), channel_id=1, source_target_pairs={{0,4},{2,6},{4,0},{6,2},{8,12},{10,14},{12,8},{14,10},{16,20},{18,... | collective-permute-start | bytes 1572872 | tf_op jit(solution)/shard_map/nearx0/ppermute | solution.py:21
  45.6 0.5 collective-permute-start.5
  46.1 3.6 %collective-permute-done.8.refs_14_ = bf16[2,2,256,256]{3,2,1,0:T(8,128)(2,1)} collective-permute-done((bf16[2,2,256,256]{3,2,1,0:T(8,128)(2,1)}, bf16[2,2,256,256]{3,2,1,0:T(8,128)(2,1)}, u32[]{:S(2)}, u32[]{:S(2)}) %collective-permute-start.8) | collective-permute-done | bytes 524320 | tf_op jit(solution)/shard_map/far0/ppermute | solution.py:21
  49.7 1.3 collective-permute-start.10
  51.0 9.2 %collective-permute-done.4.refs_14_ = bf16[2,2,256,256]{3,2,1,0:T(8,128)(2,1)} collective-permute-done((bf16[2,2,256,256]{3,2,1,0:T(8,128)(2,1)}, bf16[2,2,256,256]{3,2,1,0:T(8,128)(2,1)}, u32[]{:S(2)}, u32[]{:S(2)}) %collective-permute-start.4) | collective-permute-done | bytes 524320 | tf_op jit(solution)/shard_map/far1/ppermute | solution.py:21
  60.2 1.3 collective-permute-start.6
  61.5 0.6 pad_maximum_fusion.refs_17_.refs_18_
  62.1 19.6 %collective-permute-done.10.refs_16_ = bf16[2,2,256,256]{3,2,1,0:T(8,128)(2,1)} collective-permute-done((bf16[2,2,256,256]{3,2,1,0:T(8,128)(2,1)}, bf16[2,2,256,256]{3,2,1,0:T(8,128)(2,1)}, u32[]{:S(2)}, u32[]{:S(2)}) %collective-permute-start.10) | collective-permute-done | bytes 524320 | tf_op jit(solution)/shard_map/farx0/ppermute | solution.py:21
  81.7 18.0 %shard_map.48 = (bf16[2,256,256]{2,1,0:T(8,128)(2,1)}, bf16[2,256,256]{2,1,0:T(8,128)(2,1)}, f32[8,128]{1,0:T(8,128)}) custom-call(s32[3]{0:T(128)} %pad_add_fusion.2.info.refs_0_, bf16[2,256,1024]{2,1,0:T(8,128)(2,1)} %refs_5_.3, bf16[2,2,256,1024]{3,2,1,0:T(8,128)(2,1)} %refs_6_.4, bf16[2,256,1024]{2,1,0:T(8,128)(2,1)} %copy-done.5, ...), custom_call_target="tpu_custom_call" | custom-call | flops 41943040 | bytes 131072 | tf_op jit(solution)/shard_map/pallas_call | solution.py:242
  99.7 0.8 copy-done.6
  100.5 18.3 %shard_map.49 = (bf16[2,256,256]{2,1,0:T(8,128)(2,1)}, bf16[2,256,256]{2,1,0:T(8,128)(2,1)}, f32[8,128]{1,0:T(8,128)}) custom-call(s32[3]{0:T(128)} %pad_add_fusion.2.info.refs_0_, bf16[2,256,1024]{2,1,0:T(8,128)(2,1)} %refs_5_.3, bf16[2,2,256,1024]{3,2,1,0:T(8,128)(2,1)} %refs_6_.4, bf16[2,256,1024]{2,1,0:T(8,128)(2,1)} %copy-done.5, ...), custom_call_target="tpu_custom_call" | custom-call | flops 41943040 | bytes 131072 | tf_op jit(solution)/shard_map/pallas_call | solution.py:242
  118.8 0.0 copy-start
  118.8 1.3 copy-done
  120.2 0.1 collective-permute-start.16
  120.3 0.5 collective-permute-start.17
  120.8 0.3 copy-done.2
  121.1 0.5 collective-permute-start.18
  121.6 0.6 collective-permute-start.19
  122.2 1.1 collective-permute-start.12
  123.3 2.1 %collective-permute-done.17.refs_3_ = bf16[2,256,256]{2,1,0:T(8,128)(2,1)S(1)} collective-permute-done((bf16[2,256,256]{2,1,0:T(8,128)(2,1)}, bf16[2,256,256]{2,1,0:T(8,128)(2,1)S(1)}, u32[]{:S(2)}, u32[]{:S(2)}) %collective-permute-start.17) | collective-permute-done | bytes 262176 | tf_op jit(solution)/shard_map/pair0/ppermute | solution.py:21
  125.4 0.5 collective-permute-start.13
  125.9 4.4 %collective-permute-done.18.refs_4_ = bf16[2,256,256]{2,1,0:T(8,128)(2,1)S(1)} collective-permute-done((bf16[2,256,256]{2,1,0:T(8,128)(2,1)S(1)}, bf16[2,256,256]{2,1,0:T(8,128)(2,1)S(1)}, u32[]{:S(2)}, u32[]{:S(2)}) %collective-permute-start.18) | collective-permute-done | bytes 262176 | tf_op jit(solution)/shard_map/same0/ppermute | solution.py:27
  130.3 3.7 %collective-permute-done.19.refs_5_ = bf16[2,256,256]{2,1,0:T(8,128)(2,1)S(1)} collective-permute-done((bf16[2,256,256]{2,1,0:T(8,128)(2,1)}, bf16[2,256,256]{2,1,0:T(8,128)(2,1)S(1)}, u32[]{:S(2)}, u32[]{:S(2)}) %collective-permute-start.19) | collective-permute-done | bytes 262176 | tf_op jit(solution)/shard_map/cross0/ppermute | solution.py:27
  134.1 1.6 %copy-done.1 = bf16[512,2048]{1,0:T(8,128)(2,1)S(1)} copy-done((bf16[512,2048]{1,0:T(8,128)(2,1)S(1)}, bf16[512,2048]{1,0:T(8,128)(2,1)}, u32[]{:S(2)}) %copy-start.1) | copy-done | bytes 2097176
  135.7 5.7 %shard_map.51.refs_7_ = f32[2,256,2048]{2,1,0:T(8,128)S(1)} custom-call(s32[3]{0:T(128)S(1)} %copy-done.4, bf16[2,256,256]{2,1,0:T(8,128)(2,1)S(1)} %copy-done.2, bf16[2,256,256]{2,1,0:T(8,128)(2,1)S(1)} %copy-done.3, bf16[2,256,256]{2,1,0:T(8,128)(2,1)S(1)} %collective-permute-done.17.refs_3_, bf16[2,256,256]{2,1,0:T(8,128)(2,1)S(1)} %collective-permute-done.18.refs_4_, ...), custom_call_target="tpu_custom_call" | custom-call | flops 335544320 | bytes 655360 | tf_op jit(solution)/shard_map/pallas_call | solution.py:306
  141.4 0.2 collective-permute-done.13.refs_2_
  141.6 3.1 %collective-permute-done.14.refs_3_ = bf16[2,256,256]{2,1,0:T(8,128)(2,1)S(1)} collective-permute-done((bf16[2,256,256]{2,1,0:T(8,128)(2,1)S(1)}, bf16[2,256,256]{2,1,0:T(8,128)(2,1)S(1)}, u32[]{:S(2)}, u32[]{:S(2)}) %collective-permute-start.14) | collective-permute-done | bytes 262176 | tf_op jit(solution)/shard_map/cross1/ppermute | solution.py:27
  144.6 5.3 %shard_map.52 = bf16[2,256,2048]{2,1,0:T(8,128)(2,1)} custom-call(s32[3]{0:T(128)S(1)} %copy-done.4, bf16[2,256,256]{2,1,0:T(8,128)(2,1)S(1)} %collective-permute-done.12.refs_1_, bf16[2,256,256]{2,1,0:T(8,128)(2,1)S(1)} %collective-permute-done.13.refs_2_, bf16[2,256,256]{2,1,0:T(8,128)(2,1)S(1)} %collective-permute-done.14.refs_3_, ...), custom_call_target="tpu_custom_call" | custom-call | flops 201326592 | bytes 393216 | tf_op jit(solution)/shard_map/pallas_call | solution.py:306
  (34 shorter events, 0.1 us)
Async XLA Ops:
  0.0 7.7 %collective-permute-start.1 = (bf16[2,2,256,1024]{3,2,1,0:T(8,128)(2,1)}, bf16[2,2,256,1024]{3,2,1,0:T(8,128)(2,1)}, u32[]{:S(2)}, u32[]{:S(2)}) collective-permute-start(bf16[2,2,256,1024]{3,2,1,0:T(8,128)(2,1)} %refs_6_.4), channel_id=1, source_target_pairs={{0,2},{2,0},{4,6},{6,4},{8,10},{10,8},{12,14},{14,12},{16,18},{18,... | collective-permute-start | bytes 6291464 | tf_op jit(solution)/shard_map/pair_kv/ppermute | solution.py:21
  0.5 19.3 %collective-permute-start.11 = (s32[4,32]{1,0:T(4,128)}, s32[4,32]{1,0:T(4,128)S(1)}, u32[]{:S(2)}, u32[]{:S(2)}) collective-permute-start(s32[4,32]{1,0:T(4,128)} %param.6), channel_id=1, source_target_pairs={{0,2},{2,0},{4,6},{6,4},{8,10},{10,8},{12,14},{14,12},{16,18},{18,... | collective-permute-start | bytes 1544 | tf_op jit(solution)/shard_map/pair_mask/ppermute | solution.py:21
  0.5 43.5 %collective-permute-start = (bf16[2,256,1024]{2,1,0:T(8,128)(2,1)}, bf16[2,256,1024]{2,1,0:T(8,128)(2,1)S(1)}, u32[]{:S(2)}, u32[]{:S(2)}) collective-permute-start(bf16[2,256,1024]{2,1,0:T(8,128)(2,1)} %refs_5_.3), channel_id=1, source_target_pairs={{0,2},{2,0},{4,6},{6,4},{8,10},{10,8},{12,14},{14,12},{16,18},{18,... | collective-permute-start | bytes 3145736 | tf_op jit(solution)/shard_map/pair_q/ppermute | solution.py:21
  1.6 6.1 %copy-start.7 = (s32[4,32]{1,0:T(4,128)S(1)}, s32[4,32]{1,0:T(4,128)}, u32[]{:S(2)}) copy-start(s32[4,32]{1,0:T(4,128)} %param.6) | copy-start | bytes 1540
  5.0 113.8 %collective-permute-start.15 = (bf16[512,2048]{1,0:T(8,128)(2,1)}, bf16[512,2048]{1,0:T(8,128)(2,1)S(1)}, u32[]{:S(2)}, u32[]{:S(2)}) collective-permute-start(bf16[512,2048]{1,0:T(8,128)(2,1)} %shard_map.46.refs_2_), channel_id=1, source_target_pairs={{0,1},{1,0},{2,3},{3,2},{4,5},{5,4},{6,7},{7,6},{8,9},{9,8},{10,11... | collective-permute-start | bytes 6291464 | tf_op jit(solution)/shard_map/panel/ppermute | solution.py:27
  11.1 16.1 %collective-permute-start.7 = (bf16[2,2,256,256]{3,2,1,0:T(8,128)(2,1)}, bf16[2,2,256,256]{3,2,1,0:T(8,128)(2,1)}, u32[]{:S(2)}, u32[]{:S(2)}) collective-permute-start(bf16[2,2,256,256]{3,2,1,0:T(8,128)(2,1)} %get-tuple-element.16), channel_id=1, source_target_pairs={{0,8},{2,10},{4,12},{6,14},{8,16},{10,18},{12,20},{14,22},{16,24},... | collective-permute-start | bytes 1572872 | tf_op jit(solution)/shard_map/near0/ppermute | solution.py:21
  15.4 30.1 %collective-permute-start.2 = (bf16[2,2,256,512]{3,2,1,0:T(8,128)(2,1)}, bf16[2,2,256,512]{3,2,1,0:T(8,128)(2,1)}, u32[]{:S(2)}, u32[]{:S(2)}) collective-permute-start(bf16[2,2,256,512]{3,2,1,0:T(8,128)(2,1)} %get-tuple-element.14.refs_9_.refs_11_), channel_id=1, source_target_pairs={{0,4},{2,6},{8,12},{10,14},{16,20},{18,22},{24,28},{26,30},{1,5},{... | collective-permute-start | bytes 3145736 | tf_op jit(solution)/shard_map/ownx/ppermute | solution.py:21
  19.8 18.7 %collective-permute-start.3 = (bf16[2,2,256,256]{3,2,1,0:T(8,128)(2,1)}, bf16[2,2,256,256]{3,2,1,0:T(8,128)(2,1)}, u32[]{:S(2)}, u32[]{:S(2)}) collective-permute-start(bf16[2,2,256,256]{3,2,1,0:T(8,128)(2,1)} %get-tuple-element.15), channel_id=1, source_target_pairs={{0,8},{2,10},{4,12},{6,14},{8,16},{10,18},{12,20},{14,22},{16,24},... | collective-permute-start | bytes 1572872 | tf_op jit(solution)/shard_map/near1/ppermute | solution.py:21
  27.2 22.5 %collective-permute-start.8 = (bf16[2,2,256,256]{3,2,1,0:T(8,128)(2,1)}, bf16[2,2,256,256]{3,2,1,0:T(8,128)(2,1)}, u32[]{:S(2)}, u32[]{:S(2)}) collective-permute-start(bf16[2,2,256,256]{3,2,1,0:T(8,128)(2,1)} %collective-permute-done.7.refs_13_), channel_id=1, source_target_pairs={{0,8},{2,10},{4,12},{6,14},{8,16},{10,18},{12,20},{14,22},{16,24},... | collective-permute-start | bytes 1572872 | tf_op jit(solution)/shard_map/far0/ppermute | solution.py:21
  38.4 21.8 %collective-permute-start.4 = (bf16[2,2,256,256]{3,2,1,0:T(8,128)(2,1)}, bf16[2,2,256,256]{3,2,1,0:T(8,128)(2,1)}, u32[]{:S(2)}, u32[]{:S(2)}) collective-permute-start(bf16[2,2,256,256]{3,2,1,0:T(8,128)(2,1)} %collective-permute-done.3.refs_13_), channel_id=1, source_target_pairs={{0,8},{2,10},{4,12},{6,14},{8,16},{10,18},{12,20},{14,22},{16,24},... | collective-permute-start | bytes 1572872 | tf_op jit(solution)/shard_map/far1/ppermute | solution.py:21
  44.0 37.7 %copy-start.5 = (bf16[2,256,1024]{2,1,0:T(8,128)(2,1)}, bf16[2,256,1024]{2,1,0:T(8,128)(2,1)S(1)}, u32[]{:S(2)}) copy-start(bf16[2,256,1024]{2,1,0:T(8,128)(2,1)S(1)} %collective-permute-done.refs_3_.refs_7_) | copy-start | bytes 3145732
  44.0 18.1 %collective-permute-start.9 = (bf16[2,2,256,256]{3,2,1,0:T(8,128)(2,1)}, bf16[2,2,256,256]{3,2,1,0:T(8,128)(2,1)}, u32[]{:S(2)}, u32[]{:S(2)}) collective-permute-start(bf16[2,2,256,256]{3,2,1,0:T(8,128)(2,1)} %collective-permute-done.7.refs_13_), channel_id=1, source_target_pairs={{0,4},{2,6},{4,0},{6,2},{8,12},{10,14},{12,8},{14,10},{16,20},{18,... | collective-permute-start | bytes 1572872 | tf_op jit(solution)/shard_map/nearx0/ppermute | solution.py:21
  45.6 54.2 %collective-permute-start.5 = (bf16[2,2,256,256]{3,2,1,0:T(8,128)(2,1)}, bf16[2,2,256,256]{3,2,1,0:T(8,128)(2,1)S(1)}, u32[]{:S(2)}, u32[]{:S(2)}) collective-permute-start(bf16[2,2,256,256]{3,2,1,0:T(8,128)(2,1)} %collective-permute-done.3.refs_13_), channel_id=1, source_target_pairs={{0,4},{2,6},{4,0},{6,2},{8,12},{10,14},{12,8},{14,10},{16,20},{18,... | collective-permute-start | bytes 1572872 | tf_op jit(solution)/shard_map/nearx1/ppermute | solution.py:21
  49.7 32.0 %collective-permute-start.10 = (bf16[2,2,256,256]{3,2,1,0:T(8,128)(2,1)}, bf16[2,2,256,256]{3,2,1,0:T(8,128)(2,1)}, u32[]{:S(2)}, u32[]{:S(2)}) collective-permute-start(bf16[2,2,256,256]{3,2,1,0:T(8,128)(2,1)} %collective-permute-done.8.refs_14_), channel_id=1, source_target_pairs={{4,0},{6,2},{12,8},{14,10},{20,16},{22,18},{28,24},{30,26},{5,1},{... | collective-permute-start | bytes 1572872 | tf_op jit(solution)/shard_map/farx0/ppermute | solution.py:21
  60.2 39.5 %collective-permute-start.6 = (bf16[2,2,256,256]{3,2,1,0:T(8,128)(2,1)}, bf16[2,2,256,256]{3,2,1,0:T(8,128)(2,1)}, u32[]{:S(2)}, u32[]{:S(2)}) collective-permute-start(bf16[2,2,256,256]{3,2,1,0:T(8,128)(2,1)} %collective-permute-done.4.refs_14_), channel_id=1, source_target_pairs={{4,0},{6,2},{12,8},{14,10},{20,16},{22,18},{28,24},{30,26},{5,1},{... | collective-permute-start | bytes 1572872 | tf_op jit(solution)/shard_map/farx1/ppermute | solution.py:21
  99.7 0.8 copy-start.6
  118.8 1.3 copy-start
  120.2 0.9 copy-start.2
  120.2 2.0 %copy-start.8 = (bf16[2,256,256]{2,1,0:T(8,128)(2,1)S(1)}, bf16[2,256,256]{2,1,0:T(8,128)(2,1)}, u32[]{:S(2)}) copy-start(bf16[2,256,256]{2,1,0:T(8,128)(2,1)} %get-tuple-element.18) | copy-start | bytes 786436
  120.2 5.2 %copy-start.3 = (bf16[2,256,256]{2,1,0:T(8,128)(2,1)S(1)}, bf16[2,256,256]{2,1,0:T(8,128)(2,1)}, u32[]{:S(2)}) copy-start(bf16[2,256,256]{2,1,0:T(8,128)(2,1)} %get-tuple-element.19.refs_2_) | copy-start | bytes 786436
  120.2 13.9 %copy-start.4 = (s32[3]{0:T(128)S(1)}, s32[3]{0:T(128)}, u32[]{:S(2)}) copy-start(s32[3]{0:T(128)} %pad_add_fusion.2.info.refs_0_) | copy-start | bytes 40
  120.2 13.9 %collective-permute-start.16 = (bf16[512,2048]{1,0:T(8,128)(2,1)}, bf16[512,2048]{1,0:T(8,128)(2,1)S(1)}, u32[]{:S(2)}, u32[]{:S(2)}) collective-permute-start(bf16[512,2048]{1,0:T(8,128)(2,1)} %shard_map.50.refs_9_.refs_5_), channel_id=1, source_target_pairs={{0,2},{2,0},{4,6},{6,4},{8,10},{10,8},{12,14},{14,12},{16,18},{18,... | collective-permute-start | bytes 6291464 | tf_op jit(solution)/shard_map/panel_pair/ppermute | solution.py:21
  120.3 5.1 %collective-permute-start.17 = (bf16[2,256,256]{2,1,0:T(8,128)(2,1)}, bf16[2,256,256]{2,1,0:T(8,128)(2,1)S(1)}, u32[]{:S(2)}, u32[]{:S(2)}) collective-permute-start(bf16[2,256,256]{2,1,0:T(8,128)(2,1)} %get-tuple-element.22), channel_id=1, source_target_pairs={{0,2},{2,0},{4,6},{6,4},{8,10},{10,8},{12,14},{14,12},{16,18},{18,... | collective-permute-start | bytes 786440 | tf_op jit(solution)/shard_map/pair0/ppermute | solution.py:21
  121.1 9.2 %collective-permute-start.18 = (bf16[2,256,256]{2,1,0:T(8,128)(2,1)S(1)}, bf16[2,256,256]{2,1,0:T(8,128)(2,1)S(1)}, u32[]{:S(2)}, u32[]{:S(2)}) collective-permute-start(bf16[2,256,256]{2,1,0:T(8,128)(2,1)S(1)} %copy-done.2), channel_id=1, source_target_pairs={{0,1},{1,0},{2,3},{3,2},{4,5},{5,4},{6,7},{7,6},{8,9},{9,8},{10,11... | collective-permute-start | bytes 786440 | tf_op jit(solution)/shard_map/same0/ppermute | solution.py:27
  121.6 12.5 %collective-permute-start.19 = (bf16[2,256,256]{2,1,0:T(8,128)(2,1)}, bf16[2,256,256]{2,1,0:T(8,128)(2,1)S(1)}, u32[]{:S(2)}, u32[]{:S(2)}) collective-permute-start(bf16[2,256,256]{2,1,0:T(8,128)(2,1)} %get-tuple-element.22), channel_id=1, source_target_pairs={{0,3},{1,2},{2,1},{3,0},{4,7},{5,6},{6,5},{7,4},{8,11},{9,10},{10,... | collective-permute-start | bytes 786440 | tf_op jit(solution)/shard_map/cross0/ppermute | solution.py:27
  122.2 19.2 %collective-permute-start.12 = (bf16[2,256,256]{2,1,0:T(8,128)(2,1)S(1)}, bf16[2,256,256]{2,1,0:T(8,128)(2,1)S(1)}, u32[]{:S(2)}, u32[]{:S(2)}) collective-permute-start(bf16[2,256,256]{2,1,0:T(8,128)(2,1)S(1)} %copy-done.8), channel_id=1, source_target_pairs={{0,2},{2,0},{4,6},{6,4},{8,10},{10,8},{12,14},{14,12},{16,18},{18,... | collective-permute-start | bytes 786440 | tf_op jit(solution)/shard_map/pair1/ppermute | solution.py:21
  125.4 16.2 %collective-permute-start.13 = (bf16[2,256,256]{2,1,0:T(8,128)(2,1)S(1)}, bf16[2,256,256]{2,1,0:T(8,128)(2,1)S(1)}, u32[]{:S(2)}, u32[]{:S(2)}) collective-permute-start(bf16[2,256,256]{2,1,0:T(8,128)(2,1)S(1)} %copy-done.3), channel_id=1, source_target_pairs={{0,1},{1,0},{2,3},{3,2},{4,5},{5,4},{6,7},{7,6},{8,9},{9,8},{10,11... | collective-permute-start | bytes 786440 | tf_op jit(solution)/shard_map/same1/ppermute | solution.py:27
  130.3 14.3 %collective-permute-start.14 = (bf16[2,256,256]{2,1,0:T(8,128)(2,1)S(1)}, bf16[2,256,256]{2,1,0:T(8,128)(2,1)S(1)}, u32[]{:S(2)}, u32[]{:S(2)}) collective-permute-start(bf16[2,256,256]{2,1,0:T(8,128)(2,1)S(1)} %copy-done.8), channel_id=1, source_target_pairs={{0,3},{1,2},{2,1},{3,0},{4,7},{5,6},{6,5},{7,4},{8,11},{9,10},{10,... | collective-permute-start | bytes 786440 | tf_op jit(solution)/shard_map/cross1/ppermute | solution.py:27
  134.1 1.6 %copy-start.1 = (bf16[512,2048]{1,0:T(8,128)(2,1)S(1)}, bf16[512,2048]{1,0:T(8,128)(2,1)}, u32[]{:S(2)}) copy-start(bf16[512,2048]{1,0:T(8,128)(2,1)} %shard_map.50.refs_9_.refs_5_) | copy-start | bytes 6291460

commit v6 on v5

--- a/solution.py
+++ b/solution.py
@@ -174,34 +174,38 @@
             2, tokens, HD)
 
     shift_lane = 2 * rows
+    ones = jnp.ones((HD, HD), jnp.bfloat16)
+    squares = lambda x: jnp.dot(x * x, ones, preferred_element_type=jnp.float32)
     jobs = [(head, tile) for head in range(count) for tile in range(2)]
     low_sum = None
-    for head, tile in jobs:
-        query, key, bias, value = operands(head, tile)
-        wide = query.astype(jnp.float32)
+    for head in range(count):
         longest = None
-        for k in key:
-            k = k.astype(jnp.float32)
-            size = jnp.max(jnp.sum(k * k, axis=1, keepdims=True), axis=0, keepdims=True)
+        for k in range(span // step + 1):
+            size = squares(keys[head, k * step:(k + 1) * step, :])
             longest = size if longest is None else jnp.maximum(longest, size)
-        bound = jnp.sqrt(jnp.sum(wide * wide, axis=1, keepdims=True) * longest)
-        extra = jnp.where(lane == shift_lane, -bound, hot).astype(jnp.bfloat16)
-        query = jnp.concatenate([query, extra], 1)
-        parts = []
-        for k in range(tiles):
-            scores = lax.dot_general(
-                query, jnp.concatenate([key[k], bias[k]], 1), contract,
-                preferred_element_type=jnp.float32,
-            )
-            parts.append(jnp.exp2(scores * SCALE).astype(jnp.bfloat16))
-        expo = jnp.concatenate(parts, 1)
-        value = jnp.concatenate(value, 0)
-        value = jnp.concatenate([value, jnp.ones_like(value)], 1)
-        total = jnp.dot(expo, value, preferred_element_type=jnp.float32)
-        sums = total[:, HD:]
-        store(head, tile, total[:, :HD] / sums)
-        smallest = jnp.min(sums.reshape(-1, 8, HD), axis=0)
-        low_sum = smallest if low_sum is None else jnp.minimum(low_sum, smallest)
+        for tile in range(2):
+            longest = jnp.maximum(longest, squares(views[4 * head + 2 * tile + 1][0, 0]))
+        longest = jnp.max(longest, axis=0, keepdims=True) * 1.03
+        for tile in range(2):
+            query, key, bias, value = operands(head, tile)
+            bound = jnp.sqrt(squares(query) * longest)
+            extra = jnp.where(lane == shift_lane, -bound, hot).astype(jnp.bfloat16)
+            query = jnp.concatenate([query, extra], 1)
+            parts = []
+            for k in range(tiles):
+                scores = lax.dot_general(
+                    query, jnp.concatenate([key[k], bias[k]], 1), contract,
+                    preferred_element_type=jnp.float32,
+                )
+                parts.append(jnp.exp2(scores * SCALE).astype(jnp.bfloat16))
+            expo = jnp.concatenate(parts, 1)
+            value = jnp.concatenate(value, 0)
+            value = jnp.concatenate([value, jnp.ones_like(value)], 1)
+            total = jnp.dot(expo, value, preferred_element_type=jnp.float32)
+            sums = total[:, HD:]
+            store(head, tile, total[:, :HD] / sums)
+            smallest = jnp.min(sums.reshape(-1, 8, HD), axis=0)
+            low_sum = smallest if low_sum is None else jnp.minimum(low_sum, smallest)
     least[...] = low_sum
 
     @pl.when(jnp.logical_not(jnp.min(least[...]) > 2.0 ** -40))
@@ -369,25 +373,35 @@
 
     pair_shape = lambda heads: jax.ShapeDtypeStruct((2, 2, tokens, heads * HD), bf16)
     held = lambda heads: (2, tokens, heads * HD)
-    sizes = [heads_half] + [len(part) for part in parts]
-    whole, *own = copies(
-        info, [keys_values, got, *panels], [pair_shape(size) for size in sizes],
+    first, = copies(
+        info, [keys_values, got, *panels], [pair_shape(len(parts[0]))], [held(len(parts[0]))] * 2,
+        lambda core, place, ins, outs: join(core, ins, [(0, outs[0])]),
+    )
+    sizes = [heads_half] + [len(part) for part in parts[1:]]
+    whole, *rest = copies(
+        info, [keys_values, got, first], [pair_shape(size) for size in sizes],
         [held(size) for size in sizes] * 2,
         lambda core, place, ins, outs: join(
-            core, ins, [(0, outs[0])] + [(p[0], out) for p, out in zip(parts, outs[1:])]),
-    )
+            core, ins, [(0, outs[0])] + [(p[0], out) for p, out in zip(parts[1:], outs[1:])]),
+    )
+    own = [first] + rest
 
     sames = [
         moved_both(panel, n, f, lambda i, k: (i, (k + r) % f), "panel")
         for r, panel in enumerate(panels, 1)
     ]
 
+    low = moved(whole, n, upper, "ownx")
     blocks = []
     for k, mine in enumerate(own):
         one = moved(mine, n, ahead, f"near{k}")
+        swap = moved(one, n, across, f"nearx{k}")
+        if k:
+            one, = gated([one], blocks[0][2], blocks[0][1])
         two = moved(one, n, ahead, f"far{k}")
-        blocks.append((one, two, moved(one, n, across, f"nearx{k}"), moved(two, n, lower, f"farx{k}")))
-    low = moved(whole, n, upper, "ownx")
+        if k:
+            two, = gated([two], swap, blocks[0][3], low)
+        blocks.append((one, two, swap, moved(two, n, lower, f"farx{k}")))
     mask_there = moved(block_mask, n, pair, "pair_mask")
     table = jnp.stack([
         mask_table(index * rows, rows, block_mask),
@@ -410,7 +424,7 @@
         acts[1].append(moved(give, n, pair, f"pair{k}"))
     others = []
     for same in sames:
-        same, = gated([same], ties[-1])
+        same, = gated([same], blocks[-1][3], ties[0])
         others += [same, moved(same, n, pair, "panel_pair")]
 
     weights = [out_weight, out_weight] + others

time: 151 us -> 152 us (level)
  Pallas kernels: 54.2 us -> 58.5 us
  waiting for transfers between devices: 55.8 us -> 54 us
    ppermute x5, waiting for transfers between devices: 11.5 us -> 5.43 us  [moved_both(): return lax.ppermute(array, ('ctx', 'fsdp'), pairs)]
    ppermute x15, waiting for transfers between devices: 44.3 us -> 48.6 us  [moved(): return lax.ppermute(array, 'ctx', pairs)]
    pallas_call x2 -> x3, Pallas kernels: 6.89 us -> 9.24 us  [copies(): pl.pallas_call(kernel, grid_spec=pltpu.PrefetchScalarGridSpec(num_scalar_...]
    ppermute x15, starting transfers between devices: 29.8 us -> 27.8 us  [moved(): return lax.ppermute(array, 'ctx', pairs)]
    pallas_call x2, Pallas kernels: 36.3 us -> 37.9 us  [attend(): pl.pallas_call(lambda *refs: attend_kernel(tokens, count, *refs), grid_sp...]
  transfers between devices with their start and end apart: 20 -> 20, of which waited for: 10 -> 7; matrix products, arithmetic and copies ran while one was open for 1% -> 1% of each run, Pallas kernels for 33% -> 35%
where the time goes in v6:
time: 152 us; the launch traced here: 151 us
  Pallas kernels  58.5 us (38%)
  waiting for transfers between devices  54 us (36%)
  starting transfers between devices  33.3 us (22%)
  local copies, waits for them, and re-layouts  3.63 us (2%)
  other arithmetic  1.62 us (1%)
    ppermute x15, waiting for transfers between devices, moved(): return lax.ppermute(array, 'ctx', pairs)  48.6 us
    pallas_call x2, Pallas kernels, attend(): pl.pallas_call(lambda *refs: attend_kernel(tokens, count, *refs), grid_sp...  37.9 us
    ppermute x15, starting transfers between devices, moved(): return lax.ppermute(array, 'ctx', pairs)  27.8 us
    pallas_call x2, Pallas kernels, project(): pl.pallas_call(lambda *refs: project_kernel(len(flat), len(used), before...  11.4 us
    pallas_call x3, Pallas kernels, copies(): pl.pallas_call(kernel, grid_spec=pltpu.PrefetchScalarGridSpec(num_scalar_...  9.24 us
    ppermute x5, starting transfers between devices, moved_both(): return lax.ppermute(array, ('ctx', 'fsdp'), pairs)  5.45 us
    ppermute x5, waiting for transfers between devices, moved_both(): return lax.ppermute(array, ('ctx', 'fsdp'), pairs)  5.43 us
    unnamed x18, local copies, waits for them, and re-layouts  3.44 us
  transfers between devices with their start and end apart: 20, of which 7 were waited for; matrix products, arithmetic and copies ran while one was open for 1% of the time, Pallas kernels for 35%

profile of v6, /device:TPU:0, one launch (start us, length us, event | category | flops | bytes accessed | tf_op | source)
XLA Modules:
  0.0 151.3 jit_solution(13729953928327671224)
XLA Ops:
  0.0 0.5 collective-permute-start.1
  0.5 0.1 collective-permute-start.11
  0.5 0.6 pad_add_fusion.2.info.refs_0_
  1.1 3.3 %shard_map.46.refs_2_ = bf16[512,2048]{1,0:T(8,128)(2,1)} custom-call(s32[3]{0:T(128)} %pad_add_fusion.2.info.refs_0_, bf16[1024,4096]{1,0:T(8,128)(2,1)} %refs_4_.1), custom_call_target="tpu_custom_call" | custom-call | bytes 1048576 | tf_op jit(solution)/shard_map/pallas_call | solution.py:89
  4.5 3.0 %collective-permute-start.15 = (bf16[512,2048]{1,0:T(8,128)(2,1)}, bf16[512,2048]{1,0:T(8,128)(2,1)S(1)}, u32[]{:S(2)}, u32[]{:S(2)}) collective-permute-start(bf16[512,2048]{1,0:T(8,128)(2,1)} %shard_map.46.refs_2_), channel_id=1, source_target_pairs={{0,1},{1,0},{2,3},{3,2},{4,5},{5,4},{6,7},{7,6},{8,9},{9,8},{10,11... | collective-permute-start | bytes 6291464 | tf_op jit(solution)/shard_map/panel/ppermute | solution.py:27
  7.5 0.0 collective-permute-done.1.refs_1_.refs_4_.refs_8_
  7.5 2.7 %shard_map.47.refs_2_ = bf16[2,2,256,256]{3,2,1,0:T(8,128)(2,1)} custom-call(s32[3]{0:T(128)} %pad_add_fusion.2.info.refs_0_, bf16[2,2,256,1024]{3,2,1,0:T(8,128)(2,1)} %refs_6_.4, bf16[2,2,256,1024]{3,2,1,0:T(8,128)(2,1)} %collective-permute-done.1.refs_1_.refs_4_.refs_8_, bf16[512,2048]{1,0:T(8,128)(2,1)} %shard_map.46.refs_2_), custom_call_target="tpu_custom_call" | custom-call | bytes 262144 | tf_op jit(solution)/shard_map/pallas_call | solution.py:89
  10.2 0.0 copy-start.7
  10.2 4.3 %collective-permute-start.4 = (bf16[2,2,256,256]{3,2,1,0:T(8,128)(2,1)}, bf16[2,2,256,256]{3,2,1,0:T(8,128)(2,1)}, u32[]{:S(2)}, u32[]{:S(2)}) collective-permute-start(bf16[2,2,256,256]{3,2,1,0:T(8,128)(2,1)} %shard_map.47.refs_2_), channel_id=1, source_target_pairs={{0,8},{2,10},{4,12},{6,14},{8,16},{10,18},{12,20},{14,22},{16,24},... | collective-permute-start | bytes 1572872 | tf_op jit(solution)/shard_map/near0/ppermute | solution.py:21
  14.5 3.2 %shard_map.48 = (bf16[2,2,256,512]{3,2,1,0:T(8,128)(2,1)}, bf16[2,2,256,256]{3,2,1,0:T(8,128)(2,1)}) custom-call(s32[3]{0:T(128)} %pad_add_fusion.2.info.refs_0_, bf16[2,2,256,1024]{3,2,1,0:T(8,128)(2,1)} %refs_6_.4, bf16[2,2,256,1024]{3,2,1,0:T(8,128)(2,1)} %collective-permute-done.1.refs_1_.refs_4_.refs_8_, bf16[2,2,256,256]{3,2,1,0:T(8,128)(2,1)} %shard_map.47.refs_2_), custom_call_target="tpu_custom_call" | custom-call | bytes 786432 | tf_op jit(solution)/shard_map/pallas_call | solution.py:89
  17.7 3.6 %collective-permute-start.3 = (bf16[2,2,256,256]{3,2,1,0:T(8,128)(2,1)}, bf16[2,2,256,256]{3,2,1,0:T(8,128)(2,1)}, u32[]{:S(2)}, u32[]{:S(2)}) collective-permute-start(bf16[2,2,256,256]{3,2,1,0:T(8,128)(2,1)} %get-tuple-element.13), channel_id=1, source_target_pairs={{0,8},{2,10},{4,12},{6,14},{8,16},{10,18},{12,20},{14,22},{16,24},... | collective-permute-start | bytes 1572872 | tf_op jit(solution)/shard_map/near1/ppermute | solution.py:21
  21.3 0.1 fusion.4
  21.4 3.4 %collective-permute-start.2 = (bf16[2,2,256,512]{3,2,1,0:T(8,128)(2,1)}, bf16[2,2,256,512]{3,2,1,0:T(8,128)(2,1)S(1)}, u32[]{:S(2)}, u32[]{:S(2)}) collective-permute-start(bf16[2,2,256,512]{3,2,1,0:T(8,128)(2,1)} %get-tuple-element.12.refs_9_.refs_11_), channel_id=1, source_target_pairs={{0,4},{2,6},{8,12},{10,14},{16,20},{18,22},{24,28},{26,30},{1,5},{... | collective-permute-start | bytes 3145736 | tf_op jit(solution)/shard_map/ownx/ppermute | solution.py:21
  24.8 1.5 %collective-permute-done.4.refs_13_ = bf16[2,2,256,256]{3,2,1,0:T(8,128)(2,1)} collective-permute-done((bf16[2,2,256,256]{3,2,1,0:T(8,128)(2,1)}, bf16[2,2,256,256]{3,2,1,0:T(8,128)(2,1)}, u32[]{:S(2)}, u32[]{:S(2)}) %collective-permute-start.4) | collective-permute-done | bytes 524320 | tf_op jit(solution)/shard_map/near0/ppermute | solution.py:21
  26.4 5.2 %collective-permute-start.6 = (bf16[2,2,256,256]{3,2,1,0:T(8,128)(2,1)}, bf16[2,2,256,256]{3,2,1,0:T(8,128)(2,1)}, u32[]{:S(2)}, u32[]{:S(2)}) collective-permute-start(bf16[2,2,256,256]{3,2,1,0:T(8,128)(2,1)} %collective-permute-done.4.refs_13_), channel_id=1, source_target_pairs={{0,8},{2,10},{4,12},{6,14},{8,16},{10,18},{12,20},{14,22},{16,24},... | collective-permute-start | bytes 1572872 | tf_op jit(solution)/shard_map/far0/ppermute | solution.py:21
  31.6 1.5 collective-permute-start.5
  33.1 4.5 %collective-permute-done.3.refs_0_ = bf16[2,2,256,256]{3,2,1,0:T(8,128)(2,1)} collective-permute-done((bf16[2,2,256,256]{3,2,1,0:T(8,128)(2,1)}, bf16[2,2,256,256]{3,2,1,0:T(8,128)(2,1)}, u32[]{:S(2)}, u32[]{:S(2)}) %collective-permute-start.3) | collective-permute-done | bytes 524320 | tf_op jit(solution)/shard_map/near1/ppermute | solution.py:21
  37.6 1.5 collective-permute-start.8
  39.1 0.1 fusion.2
  39.3 8.3 %collective-permute-done.6.refs_2_.refs_14_ = bf16[2,2,256,256]{3,2,1,0:T(8,128)(2,1)} collective-permute-done((bf16[2,2,256,256]{3,2,1,0:T(8,128)(2,1)}, bf16[2,2,256,256]{3,2,1,0:T(8,128)(2,1)}, u32[]{:S(2)}, u32[]{:S(2)}) %collective-permute-start.6) | collective-permute-done | bytes 524320 | tf_op jit(solution)/shard_map/far0/ppermute | solution.py:21
  47.6 12.3 %collective-permute-done.5.refs_1_.refs_15_ = bf16[2,2,256,256]{3,2,1,0:T(8,128)(2,1)} collective-permute-done((bf16[2,2,256,256]{3,2,1,0:T(8,128)(2,1)}, bf16[2,2,256,256]{3,2,1,0:T(8,128)(2,1)}, u32[]{:S(2)}, u32[]{:S(2)}) %collective-permute-start.5) | collective-permute-done | bytes 524320 | tf_op jit(solution)/shard_map/nearx0/ppermute | solution.py:21
  59.9 9.4 %collective-permute-done.8.refs_1_.refs_15_ = bf16[2,2,256,256]{3,2,1,0:T(8,128)(2,1)} collective-permute-done((bf16[2,2,256,256]{3,2,1,0:T(8,128)(2,1)}, bf16[2,2,256,256]{3,2,1,0:T(8,128)(2,1)}, u32[]{:S(2)}, u32[]{:S(2)}) %collective-permute-start.8) | collective-permute-done | bytes 524320 | tf_op jit(solution)/shard_map/nearx1/ppermute | solution.py:21
  69.3 3.4 %collective-permute-start.7 = (bf16[2,2,256,256]{3,2,1,0:T(8,128)(2,1)}, bf16[2,2,256,256]{3,2,1,0:T(8,128)(2,1)}, u32[]{:S(2)}, u32[]{:S(2)}) collective-permute-start(bf16[2,2,256,256]{3,2,1,0:T(8,128)(2,1)} %shard_map.49.refs_13_), channel_id=1, source_target_pairs={{0,8},{2,10},{4,12},{6,14},{8,16},{10,18},{12,20},{14,22},{16,24},... | collective-permute-start | bytes 1572872 | tf_op jit(solution)/shard_map/far1/ppermute | solution.py:21
  72.7 1.3 collective-permute-start.9
  74.0 0.1 broadcast_and_fusion.3
  74.1 0.1 pad_add_fusion
  74.1 0.1 copy.11
  74.2 0.1 copy.12
  74.4 12.4 %collective-permute-done.9.refs_2_.refs_16_ = bf16[2,2,256,256]{3,2,1,0:T(8,128)(2,1)} collective-permute-done((bf16[2,2,256,256]{3,2,1,0:T(8,128)(2,1)}, bf16[2,2,256,256]{3,2,1,0:T(8,128)(2,1)}, u32[]{:S(2)}, u32[]{:S(2)}) %collective-permute-start.9) | collective-permute-done | bytes 524320 | tf_op jit(solution)/shard_map/farx0/ppermute | solution.py:21
  86.8 1.3 collective-permute-start.10
  88.1 0.6 pad_maximum_fusion.refs_17_.refs_18_
  88.8 18.8 %shard_map.51 = (bf16[2,256,256]{2,1,0:T(8,128)(2,1)}, bf16[2,256,256]{2,1,0:T(8,128)(2,1)}, f32[8,128]{1,0:T(8,128)}) custom-call(s32[3]{0:T(128)} %pad_add_fusion.2.info.refs_0_, bf16[2,256,1024]{2,1,0:T(8,128)(2,1)} %refs_5_.3, bf16[2,2,256,1024]{3,2,1,0:T(8,128)(2,1)} %refs_6_.4, bf16[2,256,1024]{2,1,0:T(8,128)(2,1)} %collective-permute-done.refs_3_.refs_7_, ...), custom_call_target="tpu_custom_call" | custom-call | flops 41943040 | bytes 131072 | tf_op jit(solution)/shard_map/pallas_call | solution.py:246
  107.6 0.0 copy-start
  107.6 1.3 copy-done
  108.9 0.2 copy-done.6
  109.1 0.9 copy-done.2
  110.1 0.5 collective-permute-start.18
  110.6 0.4 collective-permute-start.19
  111.0 1.2 collective-permute-start.17
  112.2 19.1 %shard_map.52 = (bf16[2,256,256]{2,1,0:T(8,128)(2,1)}, bf16[2,256,256]{2,1,0:T(8,128)(2,1)}, f32[8,128]{1,0:T(8,128)}) custom-call(s32[3]{0:T(128)} %pad_add_fusion.2.info.refs_0_, bf16[2,256,1024]{2,1,0:T(8,128)(2,1)} %refs_5_.3, bf16[2,2,256,1024]{3,2,1,0:T(8,128)(2,1)} %refs_6_.4, bf16[2,256,1024]{2,1,0:T(8,128)(2,1)} %collective-permute-done.refs_3_.refs_7_, ...), custom_call_target="tpu_custom_call" | custom-call | flops 41943040 | bytes 131072 | tf_op jit(solution)/shard_map/pallas_call | solution.py:246
  131.3 0.1 collective-permute-start.14
  131.4 0.6 collective-permute-start.12
  132.1 1.4 collective-permute-start.13
  133.5 0.0 collective-permute-done.17.refs_3_
  133.5 1.0 copy-done.3
  134.4 5.8 %shard_map.54.refs_7_ = f32[2,256,2048]{2,1,0:T(8,128)S(1)} custom-call(s32[3]{0:T(128)S(1)} %copy-done.4, bf16[2,256,256]{2,1,0:T(8,128)(2,1)S(1)} %copy-done.2, bf16[2,256,256]{2,1,0:T(8,128)(2,1)S(1)} %copy-done.3, bf16[2,256,256]{2,1,0:T(8,128)(2,1)S(1)} %collective-permute-done.17.refs_3_, bf16[2,256,256]{2,1,0:T(8,128)(2,1)S(1)} %collective-permute-done.18.refs_4_, ...), custom_call_target="tpu_custom_call" | custom-call | flops 335544320 | bytes 655360 | tf_op jit(solution)/shard_map/pallas_call | solution.py:310
  140.3 5.4 %collective-permute-done.13.refs_2_ = bf16[2,256,256]{2,1,0:T(8,128)(2,1)S(1)} collective-permute-done((bf16[2,256,256]{2,1,0:T(8,128)(2,1)}, bf16[2,256,256]{2,1,0:T(8,128)(2,1)S(1)}, u32[]{:S(2)}, u32[]{:S(2)}) %collective-permute-start.13) | collective-permute-done | bytes 262176 | tf_op jit(solution)/shard_map/same1/ppermute | solution.py:27
  145.7 5.5 %shard_map.55 = bf16[2,256,2048]{2,1,0:T(8,128)(2,1)} custom-call(s32[3]{0:T(128)S(1)} %copy-done.4, bf16[2,256,256]{2,1,0:T(8,128)(2,1)S(1)} %collective-permute-done.12.refs_1_, bf16[2,256,256]{2,1,0:T(8,128)(2,1)S(1)} %collective-permute-done.13.refs_2_, bf16[2,256,256]{2,1,0:T(8,128)(2,1)S(1)} %collective-permute-done.14.refs_3_, ...), custom_call_target="tpu_custom_call" | custom-call | flops 201326592 | bytes 393216 | tf_op jit(solution)/shard_map/pallas_call | solution.py:310
  (37 shorter events, 0.1 us)
Async XLA Ops:
  0.0 7.5 %collective-permute-start.1 = (bf16[2,2,256,1024]{3,2,1,0:T(8,128)(2,1)}, bf16[2,2,256,1024]{3,2,1,0:T(8,128)(2,1)}, u32[]{:S(2)}, u32[]{:S(2)}) collective-permute-start(bf16[2,2,256,1024]{3,2,1,0:T(8,128)(2,1)} %refs_6_.4), channel_id=1, source_target_pairs={{0,2},{2,0},{4,6},{6,4},{8,10},{10,8},{12,14},{14,12},{16,18},{18,... | collective-permute-start | bytes 6291464 | tf_op jit(solution)/shard_map/pair_kv/ppermute | solution.py:21
  0.5 31.1 %collective-permute-start.11 = (s32[4,32]{1,0:T(4,128)}, s32[4,32]{1,0:T(4,128)S(1)}, u32[]{:S(2)}, u32[]{:S(2)}) collective-permute-start(s32[4,32]{1,0:T(4,128)} %param.6), channel_id=1, source_target_pairs={{0,2},{2,0},{4,6},{6,4},{8,10},{10,8},{12,14},{14,12},{16,18},{18,... | collective-permute-start | bytes 1544 | tf_op jit(solution)/shard_map/pair_mask/ppermute | solution.py:21
  4.5 103.1 %collective-permute-start.15 = (bf16[512,2048]{1,0:T(8,128)(2,1)}, bf16[512,2048]{1,0:T(8,128)(2,1)S(1)}, u32[]{:S(2)}, u32[]{:S(2)}) collective-permute-start(bf16[512,2048]{1,0:T(8,128)(2,1)} %shard_map.46.refs_2_), channel_id=1, source_target_pairs={{0,1},{1,0},{2,3},{3,2},{4,5},{5,4},{6,7},{7,6},{8,9},{9,8},{10,11... | collective-permute-start | bytes 6291464 | tf_op jit(solution)/shard_map/panel/ppermute | solution.py:27
  10.2 11.1 %copy-start.7 = (s32[4,32]{1,0:T(4,128)S(1)}, s32[4,32]{1,0:T(4,128)}, u32[]{:S(2)}) copy-start(s32[4,32]{1,0:T(4,128)} %param.6) | copy-start | bytes 1540
  10.2 16.1 %collective-permute-start.4 = (bf16[2,2,256,256]{3,2,1,0:T(8,128)(2,1)}, bf16[2,2,256,256]{3,2,1,0:T(8,128)(2,1)}, u32[]{:S(2)}, u32[]{:S(2)}) collective-permute-start(bf16[2,2,256,256]{3,2,1,0:T(8,128)(2,1)} %shard_map.47.refs_2_), channel_id=1, source_target_pairs={{0,8},{2,10},{4,12},{6,14},{8,16},{10,18},{12,20},{14,22},{16,24},... | collective-permute-start | bytes 1572872 | tf_op jit(solution)/shard_map/near0/ppermute | solution.py:21
  17.7 19.9 %collective-permute-start.3 = (bf16[2,2,256,256]{3,2,1,0:T(8,128)(2,1)}, bf16[2,2,256,256]{3,2,1,0:T(8,128)(2,1)}, u32[]{:S(2)}, u32[]{:S(2)}) collective-permute-start(bf16[2,2,256,256]{3,2,1,0:T(8,128)(2,1)} %get-tuple-element.13), channel_id=1, source_target_pairs={{0,8},{2,10},{4,12},{6,14},{8,16},{10,18},{12,20},{14,22},{16,24},... | collective-permute-start | bytes 1572872 | tf_op jit(solution)/shard_map/near1/ppermute | solution.py:21
  21.4 53.0 %collective-permute-start.2 = (bf16[2,2,256,512]{3,2,1,0:T(8,128)(2,1)}, bf16[2,2,256,512]{3,2,1,0:T(8,128)(2,1)S(1)}, u32[]{:S(2)}, u32[]{:S(2)}) collective-permute-start(bf16[2,2,256,512]{3,2,1,0:T(8,128)(2,1)} %get-tuple-element.12.refs_9_.refs_11_), channel_id=1, source_target_pairs={{0,4},{2,6},{8,12},{10,14},{16,20},{18,22},{24,28},{26,30},{1,5},{... | collective-permute-start | bytes 3145736 | tf_op jit(solution)/shard_map/ownx/ppermute | solution.py:21
  26.4 21.2 %collective-permute-start.6 = (bf16[2,2,256,256]{3,2,1,0:T(8,128)(2,1)}, bf16[2,2,256,256]{3,2,1,0:T(8,128)(2,1)}, u32[]{:S(2)}, u32[]{:S(2)}) collective-permute-start(bf16[2,2,256,256]{3,2,1,0:T(8,128)(2,1)} %collective-permute-done.4.refs_13_), channel_id=1, source_target_pairs={{0,8},{2,10},{4,12},{6,14},{8,16},{10,18},{12,20},{14,22},{16,24},... | collective-permute-start | bytes 1572872 | tf_op jit(solution)/shard_map/far0/ppermute | solution.py:21
  31.6 28.3 %collective-permute-start.5 = (bf16[2,2,256,256]{3,2,1,0:T(8,128)(2,1)}, bf16[2,2,256,256]{3,2,1,0:T(8,128)(2,1)}, u32[]{:S(2)}, u32[]{:S(2)}) collective-permute-start(bf16[2,2,256,256]{3,2,1,0:T(8,128)(2,1)} %collective-permute-done.4.refs_13_), channel_id=1, source_target_pairs={{0,4},{2,6},{4,0},{6,2},{8,12},{10,14},{12,8},{14,10},{16,20},{18,... | collective-permute-start | bytes 1572872 | tf_op jit(solution)/shard_map/nearx0/ppermute | solution.py:21
  37.6 31.7 %collective-permute-start.8 = (bf16[2,2,256,256]{3,2,1,0:T(8,128)(2,1)}, bf16[2,2,256,256]{3,2,1,0:T(8,128)(2,1)}, u32[]{:S(2)}, u32[]{:S(2)}) collective-permute-start(bf16[2,2,256,256]{3,2,1,0:T(8,128)(2,1)} %collective-permute-done.3.refs_0_), channel_id=1, source_target_pairs={{0,4},{2,6},{4,0},{6,2},{8,12},{10,14},{12,8},{14,10},{16,20},{18,... | collective-permute-start | bytes 1572872 | tf_op jit(solution)/shard_map/nearx1/ppermute | solution.py:21
  47.6 41.2 %collective-permute-start = (bf16[2,256,1024]{2,1,0:T(8,128)(2,1)}, bf16[2,256,1024]{2,1,0:T(8,128)(2,1)}, u32[]{:S(2)}, u32[]{:S(2)}) collective-permute-start(bf16[2,256,1024]{2,1,0:T(8,128)(2,1)} %refs_5_.3), channel_id=1, source_target_pairs={{0,2},{2,0},{4,6},{6,4},{8,10},{10,8},{12,14},{14,12},{16,18},{18,... | collective-permute-start | bytes 3145736 | tf_op jit(solution)/shard_map/pair_q/ppermute | solution.py:21
  69.3 17.5 %collective-permute-start.7 = (bf16[2,2,256,256]{3,2,1,0:T(8,128)(2,1)}, bf16[2,2,256,256]{3,2,1,0:T(8,128)(2,1)}, u32[]{:S(2)}, u32[]{:S(2)}) collective-permute-start(bf16[2,2,256,256]{3,2,1,0:T(8,128)(2,1)} %shard_map.49.refs_13_), channel_id=1, source_target_pairs={{0,8},{2,10},{4,12},{6,14},{8,16},{10,18},{12,20},{14,22},{16,24},... | collective-permute-start | bytes 1572872 | tf_op jit(solution)/shard_map/far1/ppermute | solution.py:21
  72.7 14.1 %collective-permute-start.9 = (bf16[2,2,256,256]{3,2,1,0:T(8,128)(2,1)}, bf16[2,2,256,256]{3,2,1,0:T(8,128)(2,1)}, u32[]{:S(2)}, u32[]{:S(2)}) collective-permute-start(bf16[2,2,256,256]{3,2,1,0:T(8,128)(2,1)} %collective-permute-done.6.refs_2_.refs_14_), channel_id=1, source_target_pairs={{4,0},{6,2},{12,8},{14,10},{20,16},{22,18},{28,24},{30,26},{5,1},{... | collective-permute-start | bytes 1572872 | tf_op jit(solution)/shard_map/farx0/ppermute | solution.py:21
  74.4 12.5 %copy-start.5 = (bf16[2,2,256,512]{3,2,1,0:T(8,128)(2,1)}, bf16[2,2,256,512]{3,2,1,0:T(8,128)(2,1)S(1)}, u32[]{:S(2)}) copy-start(bf16[2,2,256,512]{3,2,1,0:T(8,128)(2,1)S(1)} %collective-permute-done.2.refs_3_.refs_10_.refs_12_) | copy-start | bytes 3145732
  86.8 20.8 %collective-permute-start.10 = (bf16[2,2,256,256]{3,2,1,0:T(8,128)(2,1)}, bf16[2,2,256,256]{3,2,1,0:T(8,128)(2,1)S(1)}, u32[]{:S(2)}, u32[]{:S(2)}) collective-permute-start(bf16[2,2,256,256]{3,2,1,0:T(8,128)(2,1)} %shard_map.50.refs_14_), channel_id=1, source_target_pairs={{4,0},{6,2},{12,8},{14,10},{20,16},{22,18},{28,24},{30,26},{5,1},{... | collective-permute-start | bytes 1572872 | tf_op jit(solution)/shard_map/farx1/ppermute | solution.py:21
  107.6 1.3 copy-start
  107.6 1.5 %copy-start.6 = (bf16[2,2,256,256]{3,2,1,0:T(8,128)(2,1)}, bf16[2,2,256,256]{3,2,1,0:T(8,128)(2,1)S(1)}, u32[]{:S(2)}) copy-start(bf16[2,2,256,256]{3,2,1,0:T(8,128)(2,1)S(1)} %collective-permute-done.10.refs_16_.refs_1_) | copy-start | bytes 1572868
  109.1 0.9 copy-start.2
  109.1 1.5 copy-start.8
  109.1 24.3 %collective-permute-start.16 = (bf16[512,2048]{1,0:T(8,128)(2,1)}, bf16[512,2048]{1,0:T(8,128)(2,1)}, u32[]{:S(2)}, u32[]{:S(2)}) collective-permute-start(bf16[512,2048]{1,0:T(8,128)(2,1)} %shard_map.53.refs_9_.refs_5_), channel_id=1, source_target_pairs={{0,2},{2,0},{4,6},{6,4},{8,10},{10,8},{12,14},{14,12},{16,18},{18,... | collective-permute-start | bytes 6291464 | tf_op jit(solution)/shard_map/panel_pair/ppermute | solution.py:21
  110.1 21.4 %collective-permute-start.18 = (bf16[2,256,256]{2,1,0:T(8,128)(2,1)S(1)}, bf16[2,256,256]{2,1,0:T(8,128)(2,1)S(1)}, u32[]{:S(2)}, u32[]{:S(2)}) collective-permute-start(bf16[2,256,256]{2,1,0:T(8,128)(2,1)S(1)} %copy-done.2), channel_id=1, source_target_pairs={{0,1},{1,0},{2,3},{3,2},{4,5},{5,4},{6,7},{7,6},{8,9},{9,8},{10,11... | collective-permute-start | bytes 786440 | tf_op jit(solution)/shard_map/same0/ppermute | solution.py:27
  110.6 22.9 %copy-start.1 = (bf16[512,2048]{1,0:T(8,128)(2,1)S(1)}, bf16[512,2048]{1,0:T(8,128)(2,1)}, u32[]{:S(2)}) copy-start(bf16[512,2048]{1,0:T(8,128)(2,1)} %shard_map.53.refs_9_.refs_5_) | copy-start | bytes 6291460
  110.6 22.9 %copy-start.4 = (s32[3]{0:T(128)S(1)}, s32[3]{0:T(128)}, u32[]{:S(2)}) copy-start(s32[3]{0:T(128)} %pad_add_fusion.2.info.refs_0_) | copy-start | bytes 40
  110.6 21.5 %collective-permute-start.19 = (bf16[2,256,256]{2,1,0:T(8,128)(2,1)S(1)}, bf16[2,256,256]{2,1,0:T(8,128)(2,1)S(1)}, u32[]{:S(2)}, u32[]{:S(2)}) collective-permute-start(bf16[2,256,256]{2,1,0:T(8,128)(2,1)S(1)} %copy-done.8), channel_id=1, source_target_pairs={{0,3},{1,2},{2,1},{3,0},{4,7},{5,6},{6,5},{7,4},{8,11},{9,10},{10,... | collective-permute-start | bytes 786440 | tf_op jit(solution)/shard_map/cross0/ppermute | solution.py:27
  111.0 22.5 %collective-permute-start.17 = (bf16[2,256,256]{2,1,0:T(8,128)(2,1)S(1)}, bf16[2,256,256]{2,1,0:T(8,128)(2,1)S(1)}, u32[]{:S(2)}, u32[]{:S(2)}) collective-permute-start(bf16[2,256,256]{2,1,0:T(8,128)(2,1)S(1)} %copy-done.8), channel_id=1, source_target_pairs={{0,2},{2,0},{4,6},{6,4},{8,10},{10,8},{12,14},{14,12},{16,18},{18,... | collective-permute-start | bytes 786440 | tf_op jit(solution)/shard_map/pair0/ppermute | solution.py:21
  131.3 9.0 %collective-permute-start.14 = (bf16[2,256,256]{2,1,0:T(8,128)(2,1)}, bf16[2,256,256]{2,1,0:T(8,128)(2,1)S(1)}, u32[]{:S(2)}, u32[]{:S(2)}) collective-permute-start(bf16[2,256,256]{2,1,0:T(8,128)(2,1)} %get-tuple-element.15), channel_id=1, source_target_pairs={{0,3},{1,2},{2,1},{3,0},{4,7},{5,6},{6,5},{7,4},{8,11},{9,10},{10,... | collective-permute-start | bytes 786440 | tf_op jit(solution)/shard_map/cross1/ppermute | solution.py:27
  131.4 8.9 %collective-permute-start.12 = (bf16[2,256,256]{2,1,0:T(8,128)(2,1)}, bf16[2,256,256]{2,1,0:T(8,128)(2,1)S(1)}, u32[]{:S(2)}, u32[]{:S(2)}) collective-permute-start(bf16[2,256,256]{2,1,0:T(8,128)(2,1)} %get-tuple-element.15), channel_id=1, source_target_pairs={{0,2},{2,0},{4,6},{6,4},{8,10},{10,8},{12,14},{14,12},{16,18},{18,... | collective-permute-start | bytes 786440 | tf_op jit(solution)/shard_map/pair1/ppermute | solution.py:21
  132.1 13.7 %collective-permute-start.13 = (bf16[2,256,256]{2,1,0:T(8,128)(2,1)}, bf16[2,256,256]{2,1,0:T(8,128)(2,1)S(1)}, u32[]{:S(2)}, u32[]{:S(2)}) collective-permute-start(bf16[2,256,256]{2,1,0:T(8,128)(2,1)} %get-tuple-element.16.refs_2_), channel_id=1, source_target_pairs={{0,1},{1,0},{2,3},{3,2},{4,5},{5,4},{6,7},{7,6},{8,9},{9,8},{10,11... | collective-permute-start | bytes 786440 | tf_op jit(solution)/shard_map/same1/ppermute | solution.py:27
  133.5 1.0 copy-start.3

commit v7 on v6

--- a/solution.py
+++ b/solution.py
@@ -60,7 +60,9 @@
     )
     table = jnp.where(allowed, 0.0, MASKED).astype(jnp.float32)
     table = jnp.concatenate([table, jnp.ones((count + rows, 1), jnp.float32)], 1)
-    return jnp.pad(table, ((0, 0), (0, HD - table.shape[1])))
+    table = jnp.pad(table, ((0, 0), (0, 16 - table.shape[1]))).astype(jnp.bfloat16)
+    table = jnp.repeat(table.reshape(-1, rows, 16).transpose(0, 2, 1), BLK, axis=2)
+    return table
 
 
 def copies(info, sources, outs, shapes, plan):
@@ -105,159 +107,128 @@
     )(info, *sources)
 
 
-def attend_kernel(tokens, count, info, *refs):
+def attend_kernel(tokens, info, *refs):
     core, side = info[0], info[1]
-    ins, refs = refs[:4 * count + 2 * count + 4], refs[-7:]
-    views, pairs, blocks = ins[:4 * count], ins[4 * count:6 * count], ins[6 * count:]
+    views, pairs, blocks, refs = refs[:4], refs[4:6], refs[6:10], refs[-7:]
+    own, low = pairs
+    one, two, swap, far = blocks
     table, mine, give, tie, keys, values, least = refs
     tie[...] = jnp.zeros_like(tie)
     rows = tokens // BLK
-    span = WINB * BLK + tokens
+    slots = WINB * BLK // tokens + 2
     back = WINB * BLK // (2 * tokens)
 
-    def place(head, ref, pair, lanes):
+    def place(ref, pair):
         for slot in range(2):
             half = core if slot == 0 else 1 - core
-            at = pl.multiple_of(pair * 2 * tokens + half * tokens, tokens)
-            keys[head, pl.ds(at, tokens), :] = ref[slot, 0, :, lanes]
-            values[head, pl.ds(at, tokens), :] = ref[slot, 1, :, lanes]
-
-    one, two, swap, far = blocks
-    for head in range(count):
-        lanes = slice(head * HD, (head + 1) * HD)
-        place(head, two, 0, lanes)
-        place(head, one, 2, lanes)
-        place(head, swap, jnp.where(side == 0, 3, 1), lanes)
-        place(head, pairs[2 * head], back, slice(None))
+            keys[pair * 2 + half] = ref[slot, 0].T
+            values[pair * 2 + half] = ref[slot, 1]
+
+    place(two, 0)
+    place(one, 2)
+    place(swap, jnp.where(side == 0, 3, 1))
+    place(own, back)
 
     @pl.when(side == 0)
     def _():
-        for head in range(count):
-            place(head, far, 1, slice(head * HD, (head + 1) * HD))
+        place(far, 1)
 
     @pl.when(side != 0)
     def _():
-        for head in range(count):
-            place(head, pairs[2 * head + 1], 3, slice(None))
+        place(low, 3)
+
+    for tile in range(2):
+        keys[slots + tile] = views[2 * tile + 1][0, 0].T
 
     spot = lax.broadcasted_iota(jnp.int32, (2 * tokens, HD), 0) // BLK
     lane = lax.broadcasted_iota(jnp.int32, (2 * tokens, HD), 1)
     hot = jnp.where(spot == lane, 1.0, 0.0)
-    contract = (((1,), (1,)), ((), ()))
-    step = tokens
-    tiles = (span + tokens) // step
-
-    def operands(head, tile):
+    rest = jnp.zeros((HD - table.shape[2], tokens), jnp.bfloat16)
+
+    def operands(tile, k):
         half = core if tile == 0 else 1 - core
-        q_ref, n_ref = views[4 * head + 2 * tile:4 * head + 2 * tile + 2]
-        query = q_ref[...].reshape(2 * tokens, HD)
-        key, value = [], []
-        for k in range(tiles):
-            at = pl.multiple_of((half + k) * tokens, tokens)
-            if k == tiles - 1:
-                key.append(n_ref[0, 0])
-                value.append(n_ref[1, 0])
-            else:
-                key.append(keys[head, pl.ds(at, step), :])
-                value.append(values[head, pl.ds(at, step), :])
-        bias = [
-            jnp.broadcast_to(
-                table[tile, k * rows:(k + 1) * rows][:, None, :], (rows, BLK, HD)
-            ).reshape(step, HD).astype(jnp.bfloat16)
-            for k in range(tiles)
-        ]
-        return query, key, bias, value
-
-    def store(head, tile, out):
-        lanes = slice(head * HD, (head + 1) * HD)
-        (mine if tile == 0 else give)[:, :, lanes] = out.astype(jnp.bfloat16).reshape(
-            2, tokens, HD)
+        if k == slots - 1:
+            key, value = keys[slots + tile], views[2 * tile + 1][1, 0]
+        else:
+            key, value = keys[half + k], values[half + k]
+        return (jnp.concatenate([key, table[tile, k], rest], 0),
+                jnp.concatenate([value, jnp.ones_like(value)], 1))
+
+    def store(tile, out):
+        (mine if tile == 0 else give)[...] = out.astype(jnp.bfloat16).reshape(2, tokens, HD)
 
     shift_lane = 2 * rows
-    ones = jnp.ones((HD, HD), jnp.bfloat16)
-    squares = lambda x: jnp.dot(x * x, ones, preferred_element_type=jnp.float32)
-    jobs = [(head, tile) for head in range(count) for tile in range(2)]
+    ones = jnp.ones((16, HD), jnp.bfloat16)
+    longest = None
+    for k in range(slots + 2):
+        key = keys[k]
+        size = jnp.dot(ones, key * key, preferred_element_type=jnp.float32)
+        longest = size if longest is None else jnp.maximum(longest, size)
+    longest = jnp.max(longest, axis=1, keepdims=True)[0:1] * 1.03
     low_sum = None
-    for head in range(count):
-        longest = None
-        for k in range(span // step + 1):
-            size = squares(keys[head, k * step:(k + 1) * step, :])
-            longest = size if longest is None else jnp.maximum(longest, size)
-        for tile in range(2):
-            longest = jnp.maximum(longest, squares(views[4 * head + 2 * tile + 1][0, 0]))
-        longest = jnp.max(longest, axis=0, keepdims=True) * 1.03
-        for tile in range(2):
-            query, key, bias, value = operands(head, tile)
-            bound = jnp.sqrt(squares(query) * longest)
-            extra = jnp.where(lane == shift_lane, -bound, hot).astype(jnp.bfloat16)
-            query = jnp.concatenate([query, extra], 1)
-            parts = []
-            for k in range(tiles):
-                scores = lax.dot_general(
-                    query, jnp.concatenate([key[k], bias[k]], 1), contract,
-                    preferred_element_type=jnp.float32,
-                )
-                parts.append(jnp.exp2(scores * SCALE).astype(jnp.bfloat16))
-            expo = jnp.concatenate(parts, 1)
-            value = jnp.concatenate(value, 0)
-            value = jnp.concatenate([value, jnp.ones_like(value)], 1)
-            total = jnp.dot(expo, value, preferred_element_type=jnp.float32)
-            sums = total[:, HD:]
-            store(head, tile, total[:, :HD] / sums)
-            smallest = jnp.min(sums.reshape(-1, 8, HD), axis=0)
-            low_sum = smallest if low_sum is None else jnp.minimum(low_sum, smallest)
+    for tile in range(2):
+        query = views[2 * tile][...].reshape(2 * tokens, HD)
+        size = jnp.dot(query * query, jnp.ones((HD, HD), jnp.bfloat16),
+                       preferred_element_type=jnp.float32)
+        bound = jnp.sqrt(size * longest)
+        extra = jnp.where(lane == shift_lane, -bound, hot).astype(jnp.bfloat16)
+        query = jnp.concatenate([query, extra], 1)
+        parts, value = [], []
+        for k in range(slots):
+            key, val = operands(tile, k)
+            scores = jnp.dot(query, key, preferred_element_type=jnp.float32)
+            parts.append(jnp.exp2(scores * SCALE).astype(jnp.bfloat16))
+            value.append(val)
+        total = jnp.dot(jnp.concatenate(parts, 1), jnp.concatenate(value, 0),
+                        preferred_element_type=jnp.float32)
+        sums = total[:, HD:]
+        store(tile, total[:, :HD] / sums)
+        smallest = jnp.min(sums.reshape(-1, 8, HD), axis=0)
+        low_sum = smallest if low_sum is None else jnp.minimum(low_sum, smallest)
     least[...] = low_sum
 
     @pl.when(jnp.logical_not(jnp.min(least[...]) > 2.0 ** -40))
     def _():
-        for head, tile in jobs:
-            query, key, bias, value = operands(head, tile)
+        for tile in range(2):
+            query = views[2 * tile][...].reshape(2 * tokens, HD)
             query = jnp.concatenate([query, hot.astype(jnp.bfloat16)], 1)
-            key = jnp.concatenate(
-                [jnp.concatenate(key, 0), jnp.concatenate(bias, 0)], 1)
-            scores = lax.dot_general(query, key, contract, preferred_element_type=jnp.float32)
+            pieces = [operands(tile, k) for k in range(slots)]
+            scores = jnp.concatenate(
+                [jnp.dot(query, key, preferred_element_type=jnp.float32) for key, _ in pieces], 1)
             top = jnp.max(scores, axis=1, keepdims=True)
             expo = jnp.exp2((scores - top) * SCALE).astype(jnp.bfloat16)
-            value = jnp.concatenate(value, 0)
-            value = jnp.concatenate([value, jnp.ones_like(value)], 1)
-            total = jnp.dot(expo, value, preferred_element_type=jnp.float32)
-            store(head, tile, total[:, :HD] / total[:, HD:])
+            total = jnp.dot(expo, jnp.concatenate([value for _, value in pieces], 0),
+                            preferred_element_type=jnp.float32)
+            store(tile, total[:, :HD] / total[:, HD:])
 
 
 def attend(info, queries, keys_values, there, got, own, low, blocks, table, part, heads_half, after):
     tokens = queries.shape[1]
-    span = WINB * BLK + 2 * tokens
-    count = len(part)
-    wide = count * HD
-    views, view_specs, pairs, pair_specs = [], [], [], []
-    for head in part:
-        here = lambda s, info, head=head: (0, 0, info[0] * heads_half + head)
-        noisy = lambda s, info, head=head: (0, 1, 0, info[0] * heads_half + head)
-        views += [queries, keys_values, there, got]
-        view_specs += [
-            pl.BlockSpec((2, tokens, HD), here), pl.BlockSpec((2, 1, tokens, HD), noisy)
-        ] * 2
-        pairs += [own, low]
-        pair_specs += [
-            pl.BlockSpec((2, 2, tokens, HD), lambda s, info, head=head: (0, 0, 0, head))] * 2
-    out_spec = pl.BlockSpec((2, tokens, wide), lambda s, info: (0, 0, 0))
-    out = jax.ShapeDtypeStruct((2, tokens, wide), jnp.bfloat16)
-    work = count * 2 * 2 * tokens * span
+    slots = WINB * BLK // tokens + 2
+    count, first = len(part), part[0]
+    here = lambda h, info: (0, 0, info[0] * heads_half + first + h)
+    noisy = lambda h, info: (0, 1, 0, info[0] * heads_half + first + h)
+    query_spec = pl.BlockSpec((2, tokens, HD), here)
+    noisy_spec = pl.BlockSpec((2, 1, tokens, HD), noisy)
+    whole = pl.BlockSpec((2, 2, tokens, HD), lambda h, info: (0, 0, 0, first + h))
+    chunk = pl.BlockSpec((2, 2, tokens, HD), lambda h, info: (0, 0, 0, h))
+    out_spec = pl.BlockSpec((2, tokens, HD), lambda h, info: (0, 0, h))
+    out = jax.ShapeDtypeStruct((2, tokens, count * HD), jnp.bfloat16)
+    work = count * 2 * 2 * tokens * slots * tokens
     return pl.pallas_call(
-        lambda *refs: attend_kernel(tokens, count, *refs),
+        lambda *refs: attend_kernel(tokens, *refs),
         grid_spec=pltpu.PrefetchScalarGridSpec(
             num_scalar_prefetch=1,
-            grid=(1,),
+            grid=(count,),
             in_specs=[
-                *view_specs, *pair_specs,
-                *[pl.BlockSpec((2, 2, tokens, wide), lambda s, info: (0, 0, 0, 0))] * 4,
+                query_spec, noisy_spec, query_spec, noisy_spec, whole, whole, *[chunk] * 4,
                 *[pl.BlockSpec(memory_space=pl.ANY)] * len(after),
-                pl.BlockSpec(table.shape, lambda s, info: (0, 0, 0)),
+                pl.BlockSpec(table.shape, lambda h, info: (0, 0, 0, 0)),
             ],
-            out_specs=[out_spec, out_spec, pl.BlockSpec((8, HD), lambda s, info: (0, 0))],
+            out_specs=[out_spec, out_spec, pl.BlockSpec((8, HD), lambda h, info: (0, 0))],
             scratch_shapes=[
-                pltpu.VMEM((count, span, HD), jnp.bfloat16),
-                pltpu.VMEM((count, span, HD), jnp.bfloat16),
+                pltpu.VMEM((slots + 2, HD, tokens), jnp.bfloat16),
+                pltpu.VMEM((slots, tokens, HD), jnp.bfloat16),
                 pltpu.VMEM((8, HD), jnp.float32),
             ],
         ),
@@ -266,7 +237,7 @@
         cost_estimate=pl.CostEstimate(
             flops=work * 8, bytes_accessed=count * 64 * 1024, transcendentals=0
         ),
-    )(info, *views, *pairs, *blocks, *after, table)
+    )(info, queries, keys_values, there, got, own, low, *blocks, *after, table)
 
 
 def project_kernel(count, groups, add, info, *refs):
@@ -391,7 +362,7 @@
         for r, panel in enumerate(panels, 1)
     ]
 
-    low = moved(whole, n, upper, "ownx")
+
     blocks = []
     for k, mine in enumerate(own):
         one = moved(mine, n, ahead, f"near{k}")
@@ -400,8 +371,11 @@
             one, = gated([one], blocks[0][2], blocks[0][1])
         two = moved(one, n, ahead, f"far{k}")
         if k:
-            two, = gated([two], swap, blocks[0][3], low)
+            two, = gated([two], swap, blocks[0][3])
         blocks.append((one, two, swap, moved(two, n, lower, f"farx{k}")))
+        if k == 0:
+            spare, = gated([whole], swap)
+            low = moved(spare, n, upper, "ownx")
     mask_there = moved(block_mask, n, pair, "pair_mask")
     table = jnp.stack([
         mask_table(index * rows, rows, block_mask),
@@ -413,7 +387,7 @@
     for k, part in enumerate(parts):
         after = []
         mine, give, tie = attend(
-            info, queries, keys_values, there, got, whole, low, blocks[k], table,
+            info, queries, keys_values, there, got, spare, low, blocks[k], table,
             part, heads_half, after + ties[-1:],
         )
         ties.append(tie)

time: 152 us -> 146 us (0.961)
  waiting for transfers between devices: 54 us -> 44.7 us
  Pallas kernels: 58.5 us -> 60.7 us
    ppermute x15, waiting for transfers between devices: 48.6 us -> 39.3 us  [moved(): return lax.ppermute(array, 'ctx', pairs)]
    pallas_call x2, Pallas kernels: 37.9 us -> 40.1 us  [attend(): pl.pallas_call(lambda *refs: attend_kernel(tokens, *refs), grid_spec=pltp...]
    unnamed x18 -> x23, local copies, waits for them, and re-layouts: 3.44 us -> 3.24 us
  transfers between devices with their start and end apart: 20 -> 20, of which waited for: 7 -> 7; matrix products, arithmetic and copies ran while one was open for 1% -> 2% of each run, Pallas kernels for 35% -> 38%
where the time goes in v7:
time: 146 us; the launch traced here: 145 us
  Pallas kernels  60.7 us (42%)
  waiting for transfers between devices  44.7 us (31%)
  starting transfers between devices  33.8 us (23%)
  local copies, waits for them, and re-layouts  4.54 us (3%)
    pallas_call x2, Pallas kernels, attend(): pl.pallas_call(lambda *refs: attend_kernel(tokens, *refs), grid_spec=pltp...  40.1 us
    ppermute x15, waiting for transfers between devices, moved(): return lax.ppermute(array, 'ctx', pairs)  39.3 us
    ppermute x15, starting transfers between devices, moved(): return lax.ppermute(array, 'ctx', pairs)  28.3 us
    pallas_call x2, Pallas kernels, project(): pl.pallas_call(lambda *refs: project_kernel(len(flat), len(used), before...  11.4 us
    pallas_call x3, Pallas kernels, copies(): pl.pallas_call(kernel, grid_spec=pltpu.PrefetchScalarGridSpec(num_scalar_...  9.25 us
    ppermute x5, starting transfers between devices, moved_both(): return lax.ppermute(array, ('ctx', 'fsdp'), pairs)  5.53 us
    ppermute x5, waiting for transfers between devices, moved_both(): return lax.ppermute(array, ('ctx', 'fsdp'), pairs)  5.43 us
    unnamed x23, local copies, waits for them, and re-layouts  3.24 us
  transfers between devices with their start and end apart: 20, of which 7 were waited for; matrix products, arithmetic and copies ran while one was open for 2% of the time, Pallas kernels for 38%

profile of v7, /device:TPU:0, one launch (start us, length us, event | category | flops | bytes accessed | tf_op | source)
XLA Modules:
  0.0 145.1 jit_solution(6476360474173199957)
XLA Ops:
  0.0 0.5 collective-permute-start.1
  0.5 0.6 pad_add_fusion.2.info.refs_0_
  1.1 3.3 %shard_map.46.refs_2_ = bf16[512,2048]{1,0:T(8,128)(2,1)} custom-call(s32[3]{0:T(128)} %pad_add_fusion.2.info.refs_0_, bf16[1024,4096]{1,0:T(8,128)(2,1)} %refs_4_.1), custom_call_target="tpu_custom_call" | custom-call | bytes 1048576 | tf_op jit(solution)/shard_map/pallas_call | solution.py:91
  4.5 3.0 %collective-permute-start.15 = (bf16[512,2048]{1,0:T(8,128)(2,1)}, bf16[512,2048]{1,0:T(8,128)(2,1)S(1)}, u32[]{:S(2)}, u32[]{:S(2)}) collective-permute-start(bf16[512,2048]{1,0:T(8,128)(2,1)} %shard_map.46.refs_2_), channel_id=1, source_target_pairs={{0,1},{1,0},{2,3},{3,2},{4,5},{5,4},{6,7},{7,6},{8,9},{9,8},{10,11... | collective-permute-start | bytes 6291464 | tf_op jit(solution)/shard_map/panel/ppermute | solution.py:27
  7.5 2.7 %shard_map.47.refs_2_ = bf16[2,2,256,256]{3,2,1,0:T(8,128)(2,1)} custom-call(s32[3]{0:T(128)} %pad_add_fusion.2.info.refs_0_, bf16[2,2,256,1024]{3,2,1,0:T(8,128)(2,1)} %refs_2_.3, bf16[2,2,256,1024]{3,2,1,0:T(8,128)(2,1)} %collective-permute-done.1.refs_1_.refs_4_, bf16[512,2048]{1,0:T(8,128)(2,1)} %shard_map.46.refs_2_), custom_call_target="tpu_custom_call" | custom-call | bytes 262144 | tf_op jit(solution)/shard_map/pallas_call | solution.py:91
  10.3 4.4 %collective-permute-start.2 = (bf16[2,2,256,256]{3,2,1,0:T(8,128)(2,1)}, bf16[2,2,256,256]{3,2,1,0:T(8,128)(2,1)}, u32[]{:S(2)}, u32[]{:S(2)}) collective-permute-start(bf16[2,2,256,256]{3,2,1,0:T(8,128)(2,1)} %shard_map.47.refs_2_), channel_id=1, source_target_pairs={{0,8},{2,10},{4,12},{6,14},{8,16},{10,18},{12,20},{14,22},{16,24},... | collective-permute-start | bytes 1572872 | tf_op jit(solution)/shard_map/near0/ppermute | solution.py:21
  14.7 3.2 %shard_map.48 = (bf16[2,2,256,512]{3,2,1,0:T(8,128)(2,1)}, bf16[2,2,256,256]{3,2,1,0:T(8,128)(2,1)}) custom-call(s32[3]{0:T(128)} %pad_add_fusion.2.info.refs_0_, bf16[2,2,256,1024]{3,2,1,0:T(8,128)(2,1)} %refs_2_.3, bf16[2,2,256,1024]{3,2,1,0:T(8,128)(2,1)} %collective-permute-done.1.refs_1_.refs_4_, bf16[2,2,256,256]{3,2,1,0:T(8,128)(2,1)} %shard_map.47.refs_2_), custom_call_target="tpu_custom_call" | custom-call | bytes 786432 | tf_op jit(solution)/shard_map/pallas_call | solution.py:91
  17.9 2.7 %collective-permute-start.5 = (bf16[2,2,256,256]{3,2,1,0:T(8,128)(2,1)}, bf16[2,2,256,256]{3,2,1,0:T(8,128)(2,1)S(1)}, u32[]{:S(2)}, u32[]{:S(2)}) collective-permute-start(bf16[2,2,256,256]{3,2,1,0:T(8,128)(2,1)} %get-tuple-element.13), channel_id=1, source_target_pairs={{0,8},{2,10},{4,12},{6,14},{8,16},{10,18},{12,20},{14,22},{16,24},... | collective-permute-start | bytes 1572872 | tf_op jit(solution)/shard_map/near1/ppermute | solution.py:21
  20.6 0.1 fusion.6
  20.7 5.8 %collective-permute-done.2.refs_7_ = bf16[2,2,256,256]{3,2,1,0:T(8,128)(2,1)} collective-permute-done((bf16[2,2,256,256]{3,2,1,0:T(8,128)(2,1)}, bf16[2,2,256,256]{3,2,1,0:T(8,128)(2,1)}, u32[]{:S(2)}, u32[]{:S(2)}) %collective-permute-start.2) | collective-permute-done | bytes 524320 | tf_op jit(solution)/shard_map/near0/ppermute | solution.py:21
  26.5 5.2 %collective-permute-start.6 = (bf16[2,2,256,256]{3,2,1,0:T(8,128)(2,1)}, bf16[2,2,256,256]{3,2,1,0:T(8,128)(2,1)}, u32[]{:S(2)}, u32[]{:S(2)}) collective-permute-start(bf16[2,2,256,256]{3,2,1,0:T(8,128)(2,1)} %collective-permute-done.2.refs_7_), channel_id=1, source_target_pairs={{0,8},{2,10},{4,12},{6,14},{8,16},{10,18},{12,20},{14,22},{16,24},... | collective-permute-start | bytes 1572872 | tf_op jit(solution)/shard_map/far0/ppermute | solution.py:21
  31.7 1.5 %collective-permute-start.3 = (bf16[2,2,256,256]{3,2,1,0:T(8,128)(2,1)}, bf16[2,2,256,256]{3,2,1,0:T(8,128)(2,1)S(1)}, u32[]{:S(2)}, u32[]{:S(2)}) collective-permute-start(bf16[2,2,256,256]{3,2,1,0:T(8,128)(2,1)} %collective-permute-done.2.refs_7_), channel_id=1, source_target_pairs={{0,4},{2,6},{4,0},{6,2},{8,12},{10,14},{12,8},{14,10},{16,20},{18,... | collective-permute-start | bytes 1572872 | tf_op jit(solution)/shard_map/nearx0/ppermute | solution.py:21
  33.2 4.6 %collective-permute-done.5.refs_0_ = bf16[2,2,256,256]{3,2,1,0:T(8,128)(2,1)S(1)} collective-permute-done((bf16[2,2,256,256]{3,2,1,0:T(8,128)(2,1)}, bf16[2,2,256,256]{3,2,1,0:T(8,128)(2,1)S(1)}, u32[]{:S(2)}, u32[]{:S(2)}) %collective-permute-start.5) | collective-permute-done | bytes 524320 | tf_op jit(solution)/shard_map/near1/ppermute | solution.py:21
  37.8 1.5 %collective-permute-start.8 = (bf16[2,2,256,256]{3,2,1,0:T(8,128)(2,1)S(1)}, bf16[2,2,256,256]{3,2,1,0:T(8,128)(2,1)}, u32[]{:S(2)}, u32[]{:S(2)}) collective-permute-start(bf16[2,2,256,256]{3,2,1,0:T(8,128)(2,1)S(1)} %collective-permute-done.5.refs_0_), channel_id=1, source_target_pairs={{0,4},{2,6},{4,0},{6,2},{8,12},{10,14},{12,8},{14,10},{16,20},{18,... | collective-permute-start | bytes 1572872 | tf_op jit(solution)/shard_map/nearx1/ppermute | solution.py:21
  39.3 0.1 collective-permute-start
  39.4 0.1 fusion.3
  39.5 8.2 %collective-permute-done.6.refs_2_.refs_8_ = bf16[2,2,256,256]{3,2,1,0:T(8,128)(2,1)} collective-permute-done((bf16[2,2,256,256]{3,2,1,0:T(8,128)(2,1)}, bf16[2,2,256,256]{3,2,1,0:T(8,128)(2,1)}, u32[]{:S(2)}, u32[]{:S(2)}) %collective-permute-start.6) | collective-permute-done | bytes 524320 | tf_op jit(solution)/shard_map/far0/ppermute | solution.py:21
  47.7 6.6 %collective-permute-done.8.refs_1_.refs_9_ = bf16[2,2,256,256]{3,2,1,0:T(8,128)(2,1)} collective-permute-done((bf16[2,2,256,256]{3,2,1,0:T(8,128)(2,1)S(1)}, bf16[2,2,256,256]{3,2,1,0:T(8,128)(2,1)}, u32[]{:S(2)}, u32[]{:S(2)}) %collective-permute-start.8) | collective-permute-done | bytes 524320 | tf_op jit(solution)/shard_map/nearx1/ppermute | solution.py:21
  54.4 3.6 %collective-permute-start.7 = (bf16[2,2,256,256]{3,2,1,0:T(8,128)(2,1)}, bf16[2,2,256,256]{3,2,1,0:T(8,128)(2,1)}, u32[]{:S(2)}, u32[]{:S(2)}) collective-permute-start(bf16[2,2,256,256]{3,2,1,0:T(8,128)(2,1)} %shard_map.50.refs_7_), channel_id=1, source_target_pairs={{0,8},{2,10},{4,12},{6,14},{8,16},{10,18},{12,20},{14,22},{16,24},... | collective-permute-start | bytes 1572872 | tf_op jit(solution)/shard_map/far1/ppermute | solution.py:21
  58.0 4.4 %collective-permute-start.4 = (bf16[2,2,256,512]{3,2,1,0:T(8,128)(2,1)}, bf16[2,2,256,512]{3,2,1,0:T(8,128)(2,1)}, u32[]{:S(2)}, u32[]{:S(2)}) collective-permute-start(bf16[2,2,256,512]{3,2,1,0:T(8,128)(2,1)} %shard_map.49.refs_5_), channel_id=1, source_target_pairs={{0,4},{2,6},{8,12},{10,14},{16,20},{18,22},{24,28},{26,30},{1,5},{... | collective-permute-start | bytes 3145736 | tf_op jit(solution)/shard_map/ownx/ppermute | solution.py:21
  62.4 1.3 collective-permute-start.9
  63.6 0.1 broadcast_and_fusion.1
  63.7 0.1 pad_add_fusion.1
  63.8 0.1 copy.18
  63.9 0.1 copy.16
  64.0 0.2 copy.17
  64.2 10.3 %collective-permute-done.9.refs_2_.refs_10_ = bf16[2,2,256,256]{3,2,1,0:T(8,128)(2,1)} collective-permute-done((bf16[2,2,256,256]{3,2,1,0:T(8,128)(2,1)}, bf16[2,2,256,256]{3,2,1,0:T(8,128)(2,1)}, u32[]{:S(2)}, u32[]{:S(2)}) %collective-permute-start.9) | collective-permute-done | bytes 524320 | tf_op jit(solution)/shard_map/farx0/ppermute | solution.py:21
  74.4 1.3 collective-permute-start.10
  75.8 0.2 copy.19
  75.9 0.2 broadcast_in_dim.17
  76.2 0.2 stack_reshape.7
  76.3 0.2 broadcast_in_dim.16
  76.6 0.2 stack_reshape.6
  76.8 3.8 %collective-permute-done.4.refs_6_ = bf16[2,2,256,512]{3,2,1,0:T(8,128)(2,1)} collective-permute-done((bf16[2,2,256,512]{3,2,1,0:T(8,128)(2,1)}, bf16[2,2,256,512]{3,2,1,0:T(8,128)(2,1)}, u32[]{:S(2)}, u32[]{:S(2)}) %collective-permute-start.4) | collective-permute-done | bytes 1048608 | tf_op jit(solution)/shard_map/ownx/ppermute | solution.py:21
  80.6 19.9 %shard_map.52 = (bf16[2,256,256]{2,1,0:T(8,128)(2,1)}, bf16[2,256,256]{2,1,0:T(8,128)(2,1)}, f32[8,128]{1,0:T(8,128)}) custom-call(s32[3]{0:T(128)} %pad_add_fusion.2.info.refs_0_, bf16[2,256,1024]{2,1,0:T(8,128)(2,1)} %refs_1_.3, bf16[2,2,256,1024]{3,2,1,0:T(8,128)(2,1)} %refs_2_.3, bf16[2,256,1024]{2,1,0:T(8,128)(2,1)} %collective-permute-done.refs_3_, ...), custom_call_target="tpu_custom_call" | custom-call | flops 41943040 | bytes 131072 | tf_op jit(solution)/shard_map/pallas_call | solution.py:218
  100.6 1.3 copy-done
  101.9 0.9 copy-done.2
  102.8 0.5 collective-permute-start.18
  103.3 0.4 collective-permute-start.19
  103.7 1.2 collective-permute-start.17
  105.0 20.1 %shard_map.53 = (bf16[2,256,256]{2,1,0:T(8,128)(2,1)}, bf16[2,256,256]{2,1,0:T(8,128)(2,1)}, f32[8,128]{1,0:T(8,128)}) custom-call(s32[3]{0:T(128)} %pad_add_fusion.2.info.refs_0_, bf16[2,256,1024]{2,1,0:T(8,128)(2,1)} %refs_1_.3, bf16[2,2,256,1024]{3,2,1,0:T(8,128)(2,1)} %refs_2_.3, bf16[2,256,1024]{2,1,0:T(8,128)(2,1)} %collective-permute-done.refs_3_, ...), custom_call_target="tpu_custom_call" | custom-call | flops 41943040 | bytes 131072 | tf_op jit(solution)/shard_map/pallas_call | solution.py:218
  125.1 0.2 collective-permute-start.14
  125.3 0.6 collective-permute-start.12
  125.9 1.4 collective-permute-start.13
  127.4 1.0 copy-done.3
  128.3 5.8 %shard_map.55.refs_7_ = f32[2,256,2048]{2,1,0:T(8,128)S(1)} custom-call(s32[3]{0:T(128)S(1)} %copy-done.4, bf16[2,256,256]{2,1,0:T(8,128)(2,1)S(1)} %copy-done.2, bf16[2,256,256]{2,1,0:T(8,128)(2,1)S(1)} %copy-done.3, bf16[2,256,256]{2,1,0:T(8,128)(2,1)S(1)} %collective-permute-done.17.refs_3_, bf16[2,256,256]{2,1,0:T(8,128)(2,1)S(1)} %collective-permute-done.18.refs_4_, ...), custom_call_target="tpu_custom_call" | custom-call | flops 335544320 | bytes 655360 | tf_op jit(solution)/shard_map/pallas_call | solution.py:281
  134.2 5.4 %collective-permute-done.13.refs_2_ = bf16[2,256,256]{2,1,0:T(8,128)(2,1)S(1)} collective-permute-done((bf16[2,256,256]{2,1,0:T(8,128)(2,1)}, bf16[2,256,256]{2,1,0:T(8,128)(2,1)S(1)}, u32[]{:S(2)}, u32[]{:S(2)}) %collective-permute-start.13) | collective-permute-done | bytes 262176 | tf_op jit(solution)/shard_map/same1/ppermute | solution.py:27
  139.6 5.5 %shard_map.56 = bf16[2,256,2048]{2,1,0:T(8,128)(2,1)} custom-call(s32[3]{0:T(128)S(1)} %copy-done.4, bf16[2,256,256]{2,1,0:T(8,128)(2,1)S(1)} %collective-permute-done.12.refs_1_, bf16[2,256,256]{2,1,0:T(8,128)(2,1)S(1)} %collective-permute-done.13.refs_2_, bf16[2,256,256]{2,1,0:T(8,128)(2,1)S(1)} %collective-permute-done.14.refs_3_, ...), custom_call_target="tpu_custom_call" | custom-call | flops 201326592 | bytes 393216 | tf_op jit(solution)/shard_map/pallas_call | solution.py:281
  (49 shorter events, 0.2 us)
Async XLA Ops:
  0.0 7.5 %collective-permute-start.1 = (bf16[2,2,256,1024]{3,2,1,0:T(8,128)(2,1)}, bf16[2,2,256,1024]{3,2,1,0:T(8,128)(2,1)}, u32[]{:S(2)}, u32[]{:S(2)}) collective-permute-start(bf16[2,2,256,1024]{3,2,1,0:T(8,128)(2,1)} %refs_2_.3), channel_id=1, source_target_pairs={{0,2},{2,0},{4,6},{6,4},{8,10},{10,8},{12,14},{14,12},{16,18},{18,... | collective-permute-start | bytes 6291464 | tf_op jit(solution)/shard_map/pair_kv/ppermute | solution.py:21
  0.5 38.8 %collective-permute-start.11 = (s32[4,32]{1,0:T(4,128)}, s32[4,32]{1,0:T(4,128)S(1)}, u32[]{:S(2)}, u32[]{:S(2)}) collective-permute-start(s32[4,32]{1,0:T(4,128)} %param.6), channel_id=1, source_target_pairs={{0,2},{2,0},{4,6},{6,4},{8,10},{10,8},{12,14},{14,12},{16,18},{18,... | collective-permute-start | bytes 1544 | tf_op jit(solution)/shard_map/pair_mask/ppermute | solution.py:21
  4.5 96.1 %collective-permute-start.15 = (bf16[512,2048]{1,0:T(8,128)(2,1)}, bf16[512,2048]{1,0:T(8,128)(2,1)S(1)}, u32[]{:S(2)}, u32[]{:S(2)}) collective-permute-start(bf16[512,2048]{1,0:T(8,128)(2,1)} %shard_map.46.refs_2_), channel_id=1, source_target_pairs={{0,1},{1,0},{2,3},{3,2},{4,5},{5,4},{6,7},{7,6},{8,9},{9,8},{10,11... | collective-permute-start | bytes 6291464 | tf_op jit(solution)/shard_map/panel/ppermute | solution.py:27
  10.2 10.4 %copy-start.9 = (s32[4,32]{1,0:T(4,128)S(1)}, s32[4,32]{1,0:T(4,128)}, u32[]{:S(2)}) copy-start(s32[4,32]{1,0:T(4,128)} %param.6) | copy-start | bytes 1540
  10.2 29.0 %copy-start.6 = (bf16[2,256,1024]{2,1,0:T(8,128)(2,1)S(1)}, bf16[2,256,1024]{2,1,0:T(8,128)(2,1)}, u32[]{:S(2)}) copy-start(bf16[2,256,1024]{2,1,0:T(8,128)(2,1)} %refs_1_.3) | copy-start | bytes 3145732
  10.3 16.3 %collective-permute-start.2 = (bf16[2,2,256,256]{3,2,1,0:T(8,128)(2,1)}, bf16[2,2,256,256]{3,2,1,0:T(8,128)(2,1)}, u32[]{:S(2)}, u32[]{:S(2)}) collective-permute-start(bf16[2,2,256,256]{3,2,1,0:T(8,128)(2,1)} %shard_map.47.refs_2_), channel_id=1, source_target_pairs={{0,8},{2,10},{4,12},{6,14},{8,16},{10,18},{12,20},{14,22},{16,24},... | collective-permute-start | bytes 1572872 | tf_op jit(solution)/shard_map/near0/ppermute | solution.py:21
  17.9 19.9 %collective-permute-start.5 = (bf16[2,2,256,256]{3,2,1,0:T(8,128)(2,1)}, bf16[2,2,256,256]{3,2,1,0:T(8,128)(2,1)S(1)}, u32[]{:S(2)}, u32[]{:S(2)}) collective-permute-start(bf16[2,2,256,256]{3,2,1,0:T(8,128)(2,1)} %get-tuple-element.13), channel_id=1, source_target_pairs={{0,8},{2,10},{4,12},{6,14},{8,16},{10,18},{12,20},{14,22},{16,24},... | collective-permute-start | bytes 1572872 | tf_op jit(solution)/shard_map/near1/ppermute | solution.py:21
  26.5 21.2 %collective-permute-start.6 = (bf16[2,2,256,256]{3,2,1,0:T(8,128)(2,1)}, bf16[2,2,256,256]{3,2,1,0:T(8,128)(2,1)}, u32[]{:S(2)}, u32[]{:S(2)}) collective-permute-start(bf16[2,2,256,256]{3,2,1,0:T(8,128)(2,1)} %collective-permute-done.2.refs_7_), channel_id=1, source_target_pairs={{0,8},{2,10},{4,12},{6,14},{8,16},{10,18},{12,20},{14,22},{16,24},... | collective-permute-start | bytes 1572872 | tf_op jit(solution)/shard_map/far0/ppermute | solution.py:21
  31.7 16.0 %collective-permute-start.3 = (bf16[2,2,256,256]{3,2,1,0:T(8,128)(2,1)}, bf16[2,2,256,256]{3,2,1,0:T(8,128)(2,1)S(1)}, u32[]{:S(2)}, u32[]{:S(2)}) collective-permute-start(bf16[2,2,256,256]{3,2,1,0:T(8,128)(2,1)} %collective-permute-done.2.refs_7_), channel_id=1, source_target_pairs={{0,4},{2,6},{4,0},{6,2},{8,12},{10,14},{12,8},{14,10},{16,20},{18,... | collective-permute-start | bytes 1572872 | tf_op jit(solution)/shard_map/nearx0/ppermute | solution.py:21
  37.8 10.0 %copy-start.7 = (bf16[2,2,256,256]{3,2,1,0:T(8,128)(2,1)}, bf16[2,2,256,256]{3,2,1,0:T(8,128)(2,1)S(1)}, u32[]{:S(2)}) copy-start(bf16[2,2,256,256]{3,2,1,0:T(8,128)(2,1)S(1)} %collective-permute-done.5.refs_0_) | copy-start | bytes 1572868
  37.8 16.6 %collective-permute-start.8 = (bf16[2,2,256,256]{3,2,1,0:T(8,128)(2,1)S(1)}, bf16[2,2,256,256]{3,2,1,0:T(8,128)(2,1)}, u32[]{:S(2)}, u32[]{:S(2)}) collective-permute-start(bf16[2,2,256,256]{3,2,1,0:T(8,128)(2,1)S(1)} %collective-permute-done.5.refs_0_), channel_id=1, source_target_pairs={{0,4},{2,6},{4,0},{6,2},{8,12},{10,14},{12,8},{14,10},{16,20},{18,... | collective-permute-start | bytes 1572872 | tf_op jit(solution)/shard_map/nearx1/ppermute | solution.py:21
  39.3 37.5 %collective-permute-start = (bf16[2,256,1024]{2,1,0:T(8,128)(2,1)S(1)}, bf16[2,256,1024]{2,1,0:T(8,128)(2,1)}, u32[]{:S(2)}, u32[]{:S(2)}) collective-permute-start(bf16[2,256,1024]{2,1,0:T(8,128)(2,1)S(1)} %copy-done.6), channel_id=1, source_target_pairs={{0,2},{2,0},{4,6},{6,4},{8,10},{10,8},{12,14},{14,12},{16,18},{18,... | collective-permute-start | bytes 3145736 | tf_op jit(solution)/shard_map/pair_q/ppermute | solution.py:21
  47.7 6.6 %copy-start.5 = (bf16[2,2,256,256]{3,2,1,0:T(8,128)(2,1)}, bf16[2,2,256,256]{3,2,1,0:T(8,128)(2,1)S(1)}, u32[]{:S(2)}) copy-start(bf16[2,2,256,256]{3,2,1,0:T(8,128)(2,1)S(1)} %collective-permute-done.3.refs_1_.refs_9_) | copy-start | bytes 1572868
  54.4 20.1 %collective-permute-start.7 = (bf16[2,2,256,256]{3,2,1,0:T(8,128)(2,1)}, bf16[2,2,256,256]{3,2,1,0:T(8,128)(2,1)}, u32[]{:S(2)}, u32[]{:S(2)}) collective-permute-start(bf16[2,2,256,256]{3,2,1,0:T(8,128)(2,1)} %shard_map.50.refs_7_), channel_id=1, source_target_pairs={{0,8},{2,10},{4,12},{6,14},{8,16},{10,18},{12,20},{14,22},{16,24},... | collective-permute-start | bytes 1572872 | tf_op jit(solution)/shard_map/far1/ppermute | solution.py:21
  58.0 22.6 %collective-permute-start.4 = (bf16[2,2,256,512]{3,2,1,0:T(8,128)(2,1)}, bf16[2,2,256,512]{3,2,1,0:T(8,128)(2,1)}, u32[]{:S(2)}, u32[]{:S(2)}) collective-permute-start(bf16[2,2,256,512]{3,2,1,0:T(8,128)(2,1)} %shard_map.49.refs_5_), channel_id=1, source_target_pairs={{0,4},{2,6},{8,12},{10,14},{16,20},{18,22},{24,28},{26,30},{1,5},{... | collective-permute-start | bytes 3145736 | tf_op jit(solution)/shard_map/ownx/ppermute | solution.py:21
  62.4 12.1 %collective-permute-start.9 = (bf16[2,2,256,256]{3,2,1,0:T(8,128)(2,1)}, bf16[2,2,256,256]{3,2,1,0:T(8,128)(2,1)}, u32[]{:S(2)}, u32[]{:S(2)}) collective-permute-start(bf16[2,2,256,256]{3,2,1,0:T(8,128)(2,1)} %collective-permute-done.6.refs_2_.refs_8_), channel_id=1, source_target_pairs={{4,0},{6,2},{12,8},{14,10},{20,16},{22,18},{28,24},{30,26},{5,1},{... | collective-permute-start | bytes 1572872 | tf_op jit(solution)/shard_map/farx0/ppermute | solution.py:21
  74.4 26.1 %collective-permute-start.10 = (bf16[2,2,256,256]{3,2,1,0:T(8,128)(2,1)}, bf16[2,2,256,256]{3,2,1,0:T(8,128)(2,1)}, u32[]{:S(2)}, u32[]{:S(2)}) collective-permute-start(bf16[2,2,256,256]{3,2,1,0:T(8,128)(2,1)} %shard_map.51.refs_8_), channel_id=1, source_target_pairs={{4,0},{6,2},{12,8},{14,10},{20,16},{22,18},{28,24},{30,26},{5,1},{... | collective-permute-start | bytes 1572872 | tf_op jit(solution)/shard_map/farx1/ppermute | solution.py:21
  76.8 3.8 %copy-start.8 = (bf16[2,10,16,256]{3,2,1,0:T(8,128)(2,1)}, bf16[2,10,16,256]{3,2,1,0:T(8,128)(2,1)S(1)}, u32[]{:S(2)}) copy-start(bf16[2,10,16,256]{3,2,1,0:T(8,128)(2,1)S(1)} %constant_dynamic-update-slice_fusion.refs_11_.refs_12_) | copy-start | bytes 491524
  100.5 1.3 copy-start
  101.9 0.9 copy-start.2
  101.9 1.5 copy-start.10
  101.9 25.5 %collective-permute-start.16 = (bf16[512,2048]{1,0:T(8,128)(2,1)}, bf16[512,2048]{1,0:T(8,128)(2,1)}, u32[]{:S(2)}, u32[]{:S(2)}) collective-permute-start(bf16[512,2048]{1,0:T(8,128)(2,1)} %shard_map.54.refs_9_.refs_5_), channel_id=1, source_target_pairs={{0,2},{2,0},{4,6},{6,4},{8,10},{10,8},{12,14},{14,12},{16,18},{18,... | collective-permute-start | bytes 6291464 | tf_op jit(solution)/shard_map/panel_pair/ppermute | solution.py:21
  102.8 22.5 %collective-permute-start.18 = (bf16[2,256,256]{2,1,0:T(8,128)(2,1)S(1)}, bf16[2,256,256]{2,1,0:T(8,128)(2,1)S(1)}, u32[]{:S(2)}, u32[]{:S(2)}) collective-permute-start(bf16[2,256,256]{2,1,0:T(8,128)(2,1)S(1)} %copy-done.2), channel_id=1, source_target_pairs={{0,1},{1,0},{2,3},{3,2},{4,5},{5,4},{6,7},{7,6},{8,9},{9,8},{10,11... | collective-permute-start | bytes 786440 | tf_op jit(solution)/shard_map/same0/ppermute | solution.py:27
  103.3 24.0 %copy-start.1 = (bf16[512,2048]{1,0:T(8,128)(2,1)S(1)}, bf16[512,2048]{1,0:T(8,128)(2,1)}, u32[]{:S(2)}) copy-start(bf16[512,2048]{1,0:T(8,128)(2,1)} %shard_map.54.refs_9_.refs_5_) | copy-start | bytes 6291460
  103.3 24.0 %copy-start.4 = (s32[3]{0:T(128)S(1)}, s32[3]{0:T(128)}, u32[]{:S(2)}) copy-start(s32[3]{0:T(128)} %pad_add_fusion.2.info.refs_0_) | copy-start | bytes 40
  103.3 22.6 %collective-permute-start.19 = (bf16[2,256,256]{2,1,0:T(8,128)(2,1)S(1)}, bf16[2,256,256]{2,1,0:T(8,128)(2,1)S(1)}, u32[]{:S(2)}, u32[]{:S(2)}) collective-permute-start(bf16[2,256,256]{2,1,0:T(8,128)(2,1)S(1)} %copy-done.10), channel_id=1, source_target_pairs={{0,3},{1,2},{2,1},{3,0},{4,7},{5,6},{6,5},{7,4},{8,11},{9,10},{10,... | collective-permute-start | bytes 786440 | tf_op jit(solution)/shard_map/cross0/ppermute | solution.py:27
  103.7 23.6 %collective-permute-start.17 = (bf16[2,256,256]{2,1,0:T(8,128)(2,1)S(1)}, bf16[2,256,256]{2,1,0:T(8,128)(2,1)S(1)}, u32[]{:S(2)}, u32[]{:S(2)}) collective-permute-start(bf16[2,256,256]{2,1,0:T(8,128)(2,1)S(1)} %copy-done.10), channel_id=1, source_target_pairs={{0,2},{2,0},{4,6},{6,4},{8,10},{10,8},{12,14},{14,12},{16,18},{18,... | collective-permute-start | bytes 786440 | tf_op jit(solution)/shard_map/pair0/ppermute | solution.py:21
  125.1 9.1 %collective-permute-start.14 = (bf16[2,256,256]{2,1,0:T(8,128)(2,1)}, bf16[2,256,256]{2,1,0:T(8,128)(2,1)S(1)}, u32[]{:S(2)}, u32[]{:S(2)}) collective-permute-start(bf16[2,256,256]{2,1,0:T(8,128)(2,1)} %get-tuple-element.15), channel_id=1, source_target_pairs={{0,3},{1,2},{2,1},{3,0},{4,7},{5,6},{6,5},{7,4},{8,11},{9,10},{10,... | collective-permute-start | bytes 786440 | tf_op jit(solution)/shard_map/cross1/ppermute | solution.py:27
  125.3 8.9 %collective-permute-start.12 = (bf16[2,256,256]{2,1,0:T(8,128)(2,1)}, bf16[2,256,256]{2,1,0:T(8,128)(2,1)S(1)}, u32[]{:S(2)}, u32[]{:S(2)}) collective-permute-start(bf16[2,256,256]{2,1,0:T(8,128)(2,1)} %get-tuple-element.15), channel_id=1, source_target_pairs={{0,2},{2,0},{4,6},{6,4},{8,10},{10,8},{12,14},{14,12},{16,18},{18,... | collective-permute-start | bytes 786440 | tf_op jit(solution)/shard_map/pair1/ppermute | solution.py:21
  125.9 13.7 %collective-permute-start.13 = (bf16[2,256,256]{2,1,0:T(8,128)(2,1)}, bf16[2,256,256]{2,1,0:T(8,128)(2,1)S(1)}, u32[]{:S(2)}, u32[]{:S(2)}) collective-permute-start(bf16[2,256,256]{2,1,0:T(8,128)(2,1)} %get-tuple-element.16.refs_2_), channel_id=1, source_target_pairs={{0,1},{1,0},{2,3},{3,2},{4,5},{5,4},{6,7},{7,6},{8,9},{9,8},{10,11... | collective-permute-start | bytes 786440 | tf_op jit(solution)/shard_map/same1/ppermute | solution.py:27
  127.3 1.0 copy-start.3

commit v8 on v7

--- a/solution.py
+++ b/solution.py
@@ -165,22 +165,37 @@
         size = jnp.dot(ones, key * key, preferred_element_type=jnp.float32)
         longest = size if longest is None else jnp.maximum(longest, size)
     longest = jnp.max(longest, axis=1, keepdims=True)[0:1] * 1.03
-    low_sum = None
+    queries = []
     for tile in range(2):
         query = views[2 * tile][...].reshape(2 * tokens, HD)
         size = jnp.dot(query * query, jnp.ones((HD, HD), jnp.bfloat16),
                        preferred_element_type=jnp.float32)
         bound = jnp.sqrt(size * longest)
         extra = jnp.where(lane == shift_lane, -bound, hot).astype(jnp.bfloat16)
-        query = jnp.concatenate([query, extra], 1)
-        parts, value = [], []
-        for k in range(slots):
-            key, val = operands(tile, k)
-            scores = jnp.dot(query, key, preferred_element_type=jnp.float32)
-            parts.append(jnp.exp2(scores * SCALE).astype(jnp.bfloat16))
-            value.append(val)
-        total = jnp.dot(jnp.concatenate(parts, 1), jnp.concatenate(value, 0),
-                        preferred_element_type=jnp.float32)
+        queries.append(jnp.concatenate([query, extra], 1))
+
+    steps = [(tile, k) for tile in range(2) for k in range(0, slots, 2)]
+    totals = [None, None]
+
+    def scores_of(tile, k):
+        key = jnp.concatenate([operands(tile, j)[0] for j in range(k, min(k + 2, slots))], 1)
+        return jnp.dot(queries[tile], key, preferred_element_type=jnp.float32)
+
+    def add(tile, k, expo):
+        value = jnp.concatenate([operands(tile, j)[1] for j in range(k, min(k + 2, slots))], 0)
+        part = jnp.dot(expo, value, preferred_element_type=jnp.float32)
+        totals[tile] = part if totals[tile] is None else totals[tile] + part
+
+    scores, last = scores_of(*steps[0]), None
+    for at, step in enumerate(steps):
+        upcoming = scores_of(*steps[at + 1]) if at + 1 < len(steps) else None
+        if last is not None:
+            add(*last)
+        last = (*step, jnp.exp2(scores * SCALE).astype(jnp.bfloat16))
+        scores = upcoming
+    add(*last)
+    low_sum = None
+    for tile, total in enumerate(totals):
         sums = total[:, HD:]
         store(tile, total[:, :HD] / sums)
         smallest = jnp.min(sums.reshape(-1, 8, HD), axis=0)
@@ -210,7 +225,6 @@
     noisy = lambda h, info: (0, 1, 0, info[0] * heads_half + first + h)
     query_spec = pl.BlockSpec((2, tokens, HD), here)
     noisy_spec = pl.BlockSpec((2, 1, tokens, HD), noisy)
-    whole = pl.BlockSpec((2, 2, tokens, HD), lambda h, info: (0, 0, 0, first + h))
     chunk = pl.BlockSpec((2, 2, tokens, HD), lambda h, info: (0, 0, 0, h))
     out_spec = pl.BlockSpec((2, tokens, HD), lambda h, info: (0, 0, h))
     out = jax.ShapeDtypeStruct((2, tokens, count * HD), jnp.bfloat16)
@@ -221,7 +235,7 @@
             num_scalar_prefetch=1,
             grid=(count,),
             in_specs=[
-                query_spec, noisy_spec, query_spec, noisy_spec, whole, whole, *[chunk] * 4,
+                query_spec, noisy_spec, query_spec, noisy_spec, *[chunk] * 6,
                 *[pl.BlockSpec(memory_space=pl.ANY)] * len(after),
                 pl.BlockSpec(table.shape, lambda h, info: (0, 0, 0, 0)),
             ],
@@ -284,7 +298,7 @@
             num_scalar_prefetch=1, grid=(steps,), in_specs=specs, out_specs=spec
         ),
         out_shape=jax.ShapeDtypeStruct((2, tokens, features), dtype),
-        compiler_params=pltpu.CompilerParams(vmem_limit_bytes=40 * 1024 * 1024),
+        compiler_params=pltpu.CompilerParams(vmem_limit_bytes=VMEM),
         cost_estimate=pl.CostEstimate(
             flops=2 * 2 * tokens * depth * features // 8,
             bytes_accessed=2 * depth * features // 8,
@@ -348,34 +362,39 @@
         info, [keys_values, got, *panels], [pair_shape(len(parts[0]))], [held(len(parts[0]))] * 2,
         lambda core, place, ins, outs: join(core, ins, [(0, outs[0])]),
     )
-    sizes = [heads_half] + [len(part) for part in parts[1:]]
-    whole, *rest = copies(
-        info, [keys_values, got, first], [pair_shape(size) for size in sizes],
-        [held(size) for size in sizes] * 2,
-        lambda core, place, ins, outs: join(
-            core, ins, [(0, outs[0])] + [(p[0], out) for p, out in zip(parts[1:], outs[1:])]),
-    )
-    own = [first] + rest
+    rest = []
+    if len(parts) > 1:
+        sizes = [len(part) for part in parts[1:]]
+        rest = copies(
+            info, [keys_values, got, first], [pair_shape(size) for size in sizes],
+            [held(size) for size in sizes] * 2,
+            lambda core, place, ins, outs: join(
+                core, ins, [(p[0], out) for p, out in zip(parts[1:], outs)]),
+        )
+    own = [first] + list(rest)
 
     sames = [
         moved_both(panel, n, f, lambda i, k: (i, (k + r) % f), "panel")
         for r, panel in enumerate(panels, 1)
     ]
 
-
     blocks = []
+    lows = []
     for k, mine in enumerate(own):
         one = moved(mine, n, ahead, f"near{k}")
         swap = moved(one, n, across, f"nearx{k}")
         if k:
-            one, = gated([one], blocks[0][2], blocks[0][1])
+            one, = gated([one], *blocks[-1][1:3])
         two = moved(one, n, ahead, f"far{k}")
         if k:
-            two, = gated([two], swap, blocks[0][3])
+            own[k - 1], = gated([own[k - 1]], swap)
+            lows.append(moved(own[k - 1], n, upper, f"ownx{k - 1}"))
+            two, = gated([two], swap, blocks[-1][3], lows[-1])
         blocks.append((one, two, swap, moved(two, n, lower, f"farx{k}")))
-        if k == 0:
-            spare, = gated([whole], swap)
-            low = moved(spare, n, upper, "ownx")
+    if lows:
+        own[-1], = gated([own[-1]], lows[-1])
+    lows.append(moved(own[-1], n, upper, f"ownx{len(own) - 1}"))
+
     mask_there = moved(block_mask, n, pair, "pair_mask")
     table = jnp.stack([
         mask_table(index * rows, rows, block_mask),
@@ -387,7 +406,7 @@
     for k, part in enumerate(parts):
         after = []
         mine, give, tie = attend(
-            info, queries, keys_values, there, got, spare, low, blocks[k], table,
+            info, queries, keys_values, there, got, own[k], lows[k], blocks[k], table,
             part, heads_half, after + ties[-1:],
         )
         ties.append(tie)
@@ -398,7 +417,7 @@
         acts[1].append(moved(give, n, pair, f"pair{k}"))
     others = []
     for same in sames:
-        same, = gated([same], blocks[-1][3], ties[0])
+        same, = gated([same], blocks[-1][3], ties[0], lows[-1])
         others += [same, moved(same, n, pair, "panel_pair")]
 
     weights = [out_weight, out_weight] + others

time: 146 us -> 145 us (level)
  waiting for transfers between devices: 44.7 us -> 28.5 us
  local copies, waits for them, and re-layouts: 4.54 us -> 12 us
  starting transfers between devices: 33.8 us -> 38.1 us
  Pallas kernels: 60.7 us -> 64.7 us
    ppermute x15 -> x16, waiting for transfers between devices: 39.3 us -> 26.3 us  [moved(): return lax.ppermute(array, 'ctx', pairs)]
    unnamed x23 -> x45, local copies, waits for them, and re-layouts: 3.24 us -> 10.7 us
    ppermute x15 -> x16, starting transfers between devices: 28.3 us -> 32.5 us  [moved(): return lax.ppermute(array, 'ctx', pairs)]
    pallas_call x2, Pallas kernels: 11.4 us -> 14.9 us  [project(): pl.pallas_call(lambda *refs: project_kernel(len(flat), len(used), before...]
    ppermute x5, waiting for transfers between devices: 5.43 us -> 2.22 us  [moved_both(): return lax.ppermute(array, ('ctx', 'fsdp'), pairs)]
  transfers between devices with their start and end apart: 20 -> 21, of which waited for: 7 -> 6; matrix products, arithmetic and copies ran while one was open for 2% -> 2% of each run, Pallas kernels for 38% -> 40%
where the time goes in v8:
time: 145 us
  Pallas kernels  64.7 us (45%)
  starting transfers between devices  38.1 us (26%)
  waiting for transfers between devices  28.5 us (20%)
  local copies, waits for them, and re-layouts  12 us (8%)
    pallas_call x2, Pallas kernels, attend(): pl.pallas_call(lambda *refs: attend_kernel(tokens, *refs), grid_spec=pltp...  40.9 us
    ppermute x16, starting transfers between devices, moved(): return lax.ppermute(array, 'ctx', pairs)  32.5 us
    ppermute x16, waiting for transfers between devices, moved(): return lax.ppermute(array, 'ctx', pairs)  26.3 us
    pallas_call x2, Pallas kernels, project(): pl.pallas_call(lambda *refs: project_kernel(len(flat), len(used), before...  14.9 us
    unnamed x45, local copies, waits for them, and re-layouts  10.7 us
    pallas_call x3, Pallas kernels, copies(): pl.pallas_call(kernel, grid_spec=pltpu.PrefetchScalarGridSpec(num_scalar_...  8.89 us
    ppermute x5, starting transfers between devices, moved_both(): return lax.ppermute(array, ('ctx', 'fsdp'), pairs)  5.64 us
  transfers between devices with their start and end apart: 21, of which 6 were waited for; matrix products, arithmetic and copies ran while one was open for 2% of the time, Pallas kernels for 40%

profile of v8, /device:TPU:0, one launch (start us, length us, event | category | flops | bytes accessed | tf_op | source)
XLA Modules:
  0.0 144.7 jit_solution(17873978942258664282)
XLA Ops:
  0.0 0.5 collective-permute-start.1
  0.5 0.6 pad_add_fusion.2.info.refs_0_
  1.1 3.4 %shard_map.46.refs_2_ = bf16[512,2048]{1,0:T(8,128)(2,1)} custom-call(s32[3]{0:T(128)} %pad_add_fusion.2.info.refs_0_, bf16[1024,4096]{1,0:T(8,128)(2,1)} %refs_4_.1), custom_call_target="tpu_custom_call" | custom-call | bytes 1048576 | tf_op jit(solution)/shard_map/pallas_call | solution.py:91
  4.5 3.0 %collective-permute-start.16 = (bf16[512,2048]{1,0:T(8,128)(2,1)}, bf16[512,2048]{1,0:T(8,128)(2,1)}, u32[]{:S(2)}, u32[]{:S(2)}) collective-permute-start(bf16[512,2048]{1,0:T(8,128)(2,1)} %shard_map.46.refs_2_), channel_id=1, source_target_pairs={{0,1},{1,0},{2,3},{3,2},{4,5},{5,4},{6,7},{7,6},{8,9},{9,8},{10,11... | collective-permute-start | bytes 6291464 | tf_op jit(solution)/shard_map/panel/ppermute | solution.py:27
  7.5 1.3 copy-done
  8.8 2.7 %shard_map.47.refs_2_.refs_0_ = bf16[2,2,256,256]{3,2,1,0:T(8,128)(2,1)} custom-call(s32[3]{0:T(128)} %pad_add_fusion.2.info.refs_0_, bf16[2,2,256,1024]{3,2,1,0:T(8,128)(2,1)} %refs_2_.3, bf16[2,2,256,1024]{3,2,1,0:T(8,128)(2,1)} %copy-done, bf16[512,2048]{1,0:T(8,128)(2,1)} %shard_map.46.refs_2_), custom_call_target="tpu_custom_call" | custom-call | bytes 262144 | tf_op jit(solution)/shard_map/pallas_call | solution.py:91
  11.6 3.6 %collective-permute-start.6 = (bf16[2,2,256,256]{3,2,1,0:T(8,128)(2,1)}, bf16[2,2,256,256]{3,2,1,0:T(8,128)(2,1)S(1)}, u32[]{:S(2)}, u32[]{:S(2)}) collective-permute-start(bf16[2,2,256,256]{3,2,1,0:T(8,128)(2,1)} %shard_map.47.refs_2_.refs_0_), channel_id=1, source_target_pairs={{0,8},{2,10},{4,12},{6,14},{8,16},{10,18},{12,20},{14,22},{16,24},... | collective-permute-start | bytes 1572872 | tf_op jit(solution)/shard_map/near0/ppermute | solution.py:21
  15.2 2.8 %shard_map.48.refs_0_ = bf16[2,2,256,256]{3,2,1,0:T(8,128)(2,1)} custom-call(s32[3]{0:T(128)} %pad_add_fusion.2.info.refs_0_, bf16[2,2,256,1024]{3,2,1,0:T(8,128)(2,1)} %refs_2_.3, bf16[2,2,256,1024]{3,2,1,0:T(8,128)(2,1)} %copy-done, bf16[2,2,256,256]{3,2,1,0:T(8,128)(2,1)} %shard_map.47.refs_2_.refs_0_), custom_call_target="tpu_custom_call" | custom-call | bytes 262144 | tf_op jit(solution)/shard_map/pallas_call | solution.py:91
  18.0 3.5 %collective-permute-start.2 = (bf16[2,2,256,256]{3,2,1,0:T(8,128)(2,1)}, bf16[2,2,256,256]{3,2,1,0:T(8,128)(2,1)S(1)}, u32[]{:S(2)}, u32[]{:S(2)}) collective-permute-start(bf16[2,2,256,256]{3,2,1,0:T(8,128)(2,1)} %shard_map.48.refs_0_), channel_id=1, source_target_pairs={{0,8},{2,10},{4,12},{6,14},{8,16},{10,18},{12,20},{14,22},{16,24},... | collective-permute-start | bytes 1572872 | tf_op jit(solution)/shard_map/near1/ppermute | solution.py:21
  21.6 6.2 %collective-permute-done.6.refs_7_ = bf16[2,2,256,256]{3,2,1,0:T(8,128)(2,1)S(1)} collective-permute-done((bf16[2,2,256,256]{3,2,1,0:T(8,128)(2,1)}, bf16[2,2,256,256]{3,2,1,0:T(8,128)(2,1)S(1)}, u32[]{:S(2)}, u32[]{:S(2)}) %collective-permute-start.6) | collective-permute-done | bytes 524320 | tf_op jit(solution)/shard_map/near0/ppermute | solution.py:21
  27.9 1.5 %collective-permute-start.8 = (bf16[2,2,256,256]{3,2,1,0:T(8,128)(2,1)S(1)}, bf16[2,2,256,256]{3,2,1,0:T(8,128)(2,1)S(1)}, u32[]{:S(2)}, u32[]{:S(2)}) collective-permute-start(bf16[2,2,256,256]{3,2,1,0:T(8,128)(2,1)S(1)} %collective-permute-done.6.refs_7_), channel_id=1, source_target_pairs={{0,4},{2,6},{4,0},{6,2},{8,12},{10,14},{12,8},{14,10},{16,20},{18,... | collective-permute-start | bytes 1572872 | tf_op jit(solution)/shard_map/nearx0/ppermute | solution.py:21
  29.4 4.3 %collective-permute-start.7 = (bf16[2,2,256,256]{3,2,1,0:T(8,128)(2,1)S(1)}, bf16[2,2,256,256]{3,2,1,0:T(8,128)(2,1)S(1)}, u32[]{:S(2)}, u32[]{:S(2)}) collective-permute-start(bf16[2,2,256,256]{3,2,1,0:T(8,128)(2,1)S(1)} %collective-permute-done.6.refs_7_), channel_id=1, source_target_pairs={{0,8},{2,10},{4,12},{6,14},{8,16},{10,18},{12,20},{14,22},{16,24},... | collective-permute-start | bytes 1572872 | tf_op jit(solution)/shard_map/far0/ppermute | solution.py:21
  33.7 5.4 %collective-permute-done.2.refs_0_ = bf16[2,2,256,256]{3,2,1,0:T(8,128)(2,1)S(1)} collective-permute-done((bf16[2,2,256,256]{3,2,1,0:T(8,128)(2,1)}, bf16[2,2,256,256]{3,2,1,0:T(8,128)(2,1)S(1)}, u32[]{:S(2)}, u32[]{:S(2)}) %collective-permute-start.2) | collective-permute-done | bytes 524320 | tf_op jit(solution)/shard_map/near1/ppermute | solution.py:21
  39.1 1.5 %collective-permute-start.3 = (bf16[2,2,256,256]{3,2,1,0:T(8,128)(2,1)S(1)}, bf16[2,2,256,256]{3,2,1,0:T(8,128)(2,1)S(1)}, u32[]{:S(2)}, u32[]{:S(2)}) collective-permute-start(bf16[2,2,256,256]{3,2,1,0:T(8,128)(2,1)S(1)} %collective-permute-done.2.refs_0_), channel_id=1, source_target_pairs={{0,4},{2,6},{4,0},{6,2},{8,12},{10,14},{12,8},{14,10},{16,20},{18,... | collective-permute-start | bytes 1572872 | tf_op jit(solution)/shard_map/nearx1/ppermute | solution.py:21
  40.8 9.6 %collective-permute-done.3.refs_1_.refs_9_ = bf16[2,2,256,256]{3,2,1,0:T(8,128)(2,1)S(1)} collective-permute-done((bf16[2,2,256,256]{3,2,1,0:T(8,128)(2,1)S(1)}, bf16[2,2,256,256]{3,2,1,0:T(8,128)(2,1)S(1)}, u32[]{:S(2)}, u32[]{:S(2)}) %collective-permute-start.3) | collective-permute-done | bytes 524320 | tf_op jit(solution)/shard_map/nearx1/ppermute | solution.py:21
  50.5 0.8 copy-done.2
  51.3 3.4 %collective-permute-start.4 = (bf16[2,2,256,256]{3,2,1,0:T(8,128)(2,1)}, bf16[2,2,256,256]{3,2,1,0:T(8,128)(2,1)S(1)}, u32[]{:S(2)}, u32[]{:S(2)}) collective-permute-start(bf16[2,2,256,256]{3,2,1,0:T(8,128)(2,1)} %shard_map.49.refs_5_), channel_id=1, source_target_pairs={{0,4},{2,6},{8,12},{10,14},{16,20},{18,22},{24,28},{26,30},{1,5},{... | collective-permute-start | bytes 1572872 | tf_op jit(solution)/shard_map/ownx0/ppermute | solution.py:21
  54.7 0.8 copy-done.8
  55.5 0.8 copy-done.9
  56.3 5.2 %collective-permute-start.9 = (bf16[2,2,256,256]{3,2,1,0:T(8,128)(2,1)}, bf16[2,2,256,256]{3,2,1,0:T(8,128)(2,1)}, u32[]{:S(2)}, u32[]{:S(2)}) collective-permute-start(bf16[2,2,256,256]{3,2,1,0:T(8,128)(2,1)} %shard_map.51.refs_7_), channel_id=1, source_target_pairs={{0,8},{2,10},{4,12},{6,14},{8,16},{10,18},{12,20},{14,22},{16,24},... | collective-permute-start | bytes 1572872 | tf_op jit(solution)/shard_map/far1/ppermute | solution.py:21
  61.5 1.3 collective-permute-start.10
  63.3 0.8 copy-done.3
  64.1 4.6 %collective-permute-start.5 = (bf16[2,2,256,256]{3,2,1,0:T(8,128)(2,1)}, bf16[2,2,256,256]{3,2,1,0:T(8,128)(2,1)S(1)}, u32[]{:S(2)}, u32[]{:S(2)}) collective-permute-start(bf16[2,2,256,256]{3,2,1,0:T(8,128)(2,1)} %shard_map.50.refs_5_), channel_id=1, source_target_pairs={{0,4},{2,6},{8,12},{10,14},{16,20},{18,22},{24,28},{26,30},{1,5},{... | collective-permute-start | bytes 1572872 | tf_op jit(solution)/shard_map/ownx1/ppermute | solution.py:21
  68.9 4.8 %collective-permute-done.10.refs_2_.refs_10_ = bf16[2,2,256,256]{3,2,1,0:T(8,128)(2,1)S(1)} collective-permute-done((bf16[2,2,256,256]{3,2,1,0:T(8,128)(2,1)}, bf16[2,2,256,256]{3,2,1,0:T(8,128)(2,1)S(1)}, u32[]{:S(2)}, u32[]{:S(2)}) %collective-permute-start.10) | collective-permute-done | bytes 524320 | tf_op jit(solution)/shard_map/farx0/ppermute | solution.py:21
  73.7 0.8 copy-done.5
  74.5 1.3 collective-permute-start.11
  76.0 0.2 broadcast_in_dim.17
  76.2 0.2 stack_reshape.7
  76.4 0.2 broadcast_in_dim.16
  76.6 0.2 stack_reshape.6
  76.9 0.6 copy-done.11
  77.5 20.3 %shard_map.53 = (bf16[2,256,256]{2,1,0:T(8,128)(2,1)}, bf16[2,256,256]{2,1,0:T(8,128)(2,1)}, f32[8,128]{1,0:T(8,128)}) custom-call(s32[3]{0:T(128)} %pad_add_fusion.2.info.refs_0_, bf16[2,256,1024]{2,1,0:T(8,128)(2,1)} %refs_1_.3, bf16[2,2,256,1024]{3,2,1,0:T(8,128)(2,1)} %refs_2_.3, bf16[2,256,1024]{2,1,0:T(8,128)(2,1)} %collective-permute-done.refs_3_, ...), custom_call_target="tpu_custom_call" | custom-call | flops 41943040 | bytes 131072 | tf_op jit(solution)/shard_map/pallas_call | solution.py:232
  97.9 0.8 copy-done.6
  98.6 0.2 copy-done.7
  98.8 0.9 copy-done.13
  99.8 0.5 collective-permute-start.19
  100.3 0.4 collective-permute-start.20
  100.7 1.2 collective-permute-start.18
  101.9 20.6 %shard_map.54 = (bf16[2,256,256]{2,1,0:T(8,128)(2,1)}, bf16[2,256,256]{2,1,0:T(8,128)(2,1)}, f32[8,128]{1,0:T(8,128)}) custom-call(s32[3]{0:T(128)} %pad_add_fusion.2.info.refs_0_, bf16[2,256,1024]{2,1,0:T(8,128)(2,1)} %refs_1_.3, bf16[2,2,256,1024]{3,2,1,0:T(8,128)(2,1)} %refs_2_.3, bf16[2,256,1024]{2,1,0:T(8,128)(2,1)} %collective-permute-done.refs_3_, ...), custom_call_target="tpu_custom_call" | custom-call | flops 41943040 | bytes 131072 | tf_op jit(solution)/shard_map/pallas_call | solution.py:232
  122.5 0.2 collective-permute-start.15
  122.7 0.5 collective-permute-start.13
  123.2 1.5 %collective-permute-start.14 = (bf16[2,256,256]{2,1,0:T(8,128)(2,1)}, bf16[2,256,256]{2,1,0:T(8,128)(2,1)S(1)}, u32[]{:S(2)}, u32[]{:S(2)}) collective-permute-start(bf16[2,256,256]{2,1,0:T(8,128)(2,1)} %get-tuple-element.12.refs_2_), channel_id=1, source_target_pairs={{0,1},{1,0},{2,3},{3,2},{4,5},{5,4},{6,7},{7,6},{8,9},{9,8},{10,11... | collective-permute-start | bytes 786440 | tf_op jit(solution)/shard_map/same1/ppermute | solution.py:27
  124.8 0.7 copy-done.16
  125.4 1.4 copy-done.1
  126.8 7.9 %shard_map.56.refs_7_ = f32[2,256,2048]{2,1,0:T(8,128)} custom-call(s32[3]{0:T(128)} %pad_add_fusion.2.info.refs_0_, bf16[2,256,256]{2,1,0:T(8,128)(2,1)} %get-tuple-element.13.refs_1_, bf16[2,256,256]{2,1,0:T(8,128)(2,1)} %get-tuple-element.12.refs_2_, bf16[2,256,256]{2,1,0:T(8,128)(2,1)} %copy-done.16, bf16[2,256,256]{2,1,0:T(8,128)(2,1)} %copy-done.14, ...), custom_call_target="tpu_custom_call" | custom-call | flops 335544320 | bytes 655360 | tf_op jit(solution)/shard_map/pallas_call | solution.py:295
  134.8 2.2 %collective-permute-done.14.refs_2_ = bf16[2,256,256]{2,1,0:T(8,128)(2,1)S(1)} collective-permute-done((bf16[2,256,256]{2,1,0:T(8,128)(2,1)}, bf16[2,256,256]{2,1,0:T(8,128)(2,1)S(1)}, u32[]{:S(2)}, u32[]{:S(2)}) %collective-permute-start.14) | collective-permute-done | bytes 262176 | tf_op jit(solution)/shard_map/same1/ppermute | solution.py:27
  137.0 0.7 copy-done.19
  137.7 6.9 %shard_map.57 = bf16[2,256,2048]{2,1,0:T(8,128)(2,1)} custom-call(s32[3]{0:T(128)} %pad_add_fusion.2.info.refs_0_, bf16[2,256,256]{2,1,0:T(8,128)(2,1)} %copy-done.18, bf16[2,256,256]{2,1,0:T(8,128)(2,1)} %copy-done.19, bf16[2,256,256]{2,1,0:T(8,128)(2,1)} %copy-done.17, bf16[1024,4096]{1,0:T(8,128)(2,1)} %refs_4_.1, ...), custom_call_target="tpu_custom_call" | custom-call | flops 201326592 | bytes 393216 | tf_op jit(solution)/shard_map/pallas_call | solution.py:295
  (74 shorter events, 1.3 us)
Async XLA Ops:
  0.0 7.5 %collective-permute-start.1 = (bf16[2,2,256,1024]{3,2,1,0:T(8,128)(2,1)}, bf16[2,2,256,1024]{3,2,1,0:T(8,128)(2,1)S(1)}, u32[]{:S(2)}, u32[]{:S(2)}) collective-permute-start(bf16[2,2,256,1024]{3,2,1,0:T(8,128)(2,1)} %refs_2_.3), channel_id=1, source_target_pairs={{0,2},{2,0},{4,6},{6,4},{8,10},{10,8},{12,14},{14,12},{16,18},{18,... | collective-permute-start | bytes 6291464 | tf_op jit(solution)/shard_map/pair_kv/ppermute | solution.py:21
  0.5 40.2 %collective-permute-start.12 = (s32[4,32]{1,0:T(4,128)}, s32[4,32]{1,0:T(4,128)S(1)}, u32[]{:S(2)}, u32[]{:S(2)}) collective-permute-start(s32[4,32]{1,0:T(4,128)} %param.6), channel_id=1, source_target_pairs={{0,2},{2,0},{4,6},{6,4},{8,10},{10,8},{12,14},{14,12},{16,18},{18,... | collective-permute-start | bytes 1544 | tf_op jit(solution)/shard_map/pair_mask/ppermute | solution.py:21
  4.5 93.3 %collective-permute-start.16 = (bf16[512,2048]{1,0:T(8,128)(2,1)}, bf16[512,2048]{1,0:T(8,128)(2,1)}, u32[]{:S(2)}, u32[]{:S(2)}) collective-permute-start(bf16[512,2048]{1,0:T(8,128)(2,1)} %shard_map.46.refs_2_), channel_id=1, source_target_pairs={{0,1},{1,0},{2,3},{3,2},{4,5},{5,4},{6,7},{7,6},{8,9},{9,8},{10,11... | collective-permute-start | bytes 6291464 | tf_op jit(solution)/shard_map/panel/ppermute | solution.py:27
  7.5 1.3 copy-start
  11.6 10.0 %copy-start.20 = (s32[4,32]{1,0:T(4,128)S(1)}, s32[4,32]{1,0:T(4,128)}, u32[]{:S(2)}) copy-start(s32[4,32]{1,0:T(4,128)} %param.6) | copy-start | bytes 1540
  11.6 29.0 %copy-start.4 = (bf16[2,256,1024]{2,1,0:T(8,128)(2,1)S(1)}, bf16[2,256,1024]{2,1,0:T(8,128)(2,1)}, u32[]{:S(2)}) copy-start(bf16[2,256,1024]{2,1,0:T(8,128)(2,1)} %refs_1_.3) | copy-start | bytes 3145732
  11.6 16.3 %collective-permute-start.6 = (bf16[2,2,256,256]{3,2,1,0:T(8,128)(2,1)}, bf16[2,2,256,256]{3,2,1,0:T(8,128)(2,1)S(1)}, u32[]{:S(2)}, u32[]{:S(2)}) collective-permute-start(bf16[2,2,256,256]{3,2,1,0:T(8,128)(2,1)} %shard_map.47.refs_2_.refs_0_), channel_id=1, source_target_pairs={{0,8},{2,10},{4,12},{6,14},{8,16},{10,18},{12,20},{14,22},{16,24},... | collective-permute-start | bytes 1572872 | tf_op jit(solution)/shard_map/near0/ppermute | solution.py:21
  18.0 21.1 %collective-permute-start.2 = (bf16[2,2,256,256]{3,2,1,0:T(8,128)(2,1)}, bf16[2,2,256,256]{3,2,1,0:T(8,128)(2,1)S(1)}, u32[]{:S(2)}, u32[]{:S(2)}) collective-permute-start(bf16[2,2,256,256]{3,2,1,0:T(8,128)(2,1)} %shard_map.48.refs_0_), channel_id=1, source_target_pairs={{0,8},{2,10},{4,12},{6,14},{8,16},{10,18},{12,20},{14,22},{16,24},... | collective-permute-start | bytes 1572872 | tf_op jit(solution)/shard_map/near1/ppermute | solution.py:21
  27.9 49.0 %copy-start.12 = (bf16[2,2,256,256]{3,2,1,0:T(8,128)(2,1)}, bf16[2,2,256,256]{3,2,1,0:T(8,128)(2,1)S(1)}, u32[]{:S(2)}) copy-start(bf16[2,2,256,256]{3,2,1,0:T(8,128)(2,1)S(1)} %collective-permute-done.6.refs_7_) | copy-start | bytes 1572868
  27.9 26.8 %collective-permute-start.8 = (bf16[2,2,256,256]{3,2,1,0:T(8,128)(2,1)S(1)}, bf16[2,2,256,256]{3,2,1,0:T(8,128)(2,1)S(1)}, u32[]{:S(2)}, u32[]{:S(2)}) collective-permute-start(bf16[2,2,256,256]{3,2,1,0:T(8,128)(2,1)S(1)} %collective-permute-done.6.refs_7_), channel_id=1, source_target_pairs={{0,4},{2,6},{4,0},{6,2},{8,12},{10,14},{12,8},{14,10},{16,20},{18,... | collective-permute-start | bytes 1572872 | tf_op jit(solution)/shard_map/nearx0/ppermute | solution.py:21
  29.4 25.4 %collective-permute-start.7 = (bf16[2,2,256,256]{3,2,1,0:T(8,128)(2,1)S(1)}, bf16[2,2,256,256]{3,2,1,0:T(8,128)(2,1)S(1)}, u32[]{:S(2)}, u32[]{:S(2)}) collective-permute-start(bf16[2,2,256,256]{3,2,1,0:T(8,128)(2,1)S(1)} %collective-permute-done.6.refs_7_), channel_id=1, source_target_pairs={{0,8},{2,10},{4,12},{6,14},{8,16},{10,18},{12,20},{14,22},{16,24},... | collective-permute-start | bytes 1572872 | tf_op jit(solution)/shard_map/far0/ppermute | solution.py:21
  39.1 15.6 %copy-start.10 = (bf16[2,2,256,256]{3,2,1,0:T(8,128)(2,1)}, bf16[2,2,256,256]{3,2,1,0:T(8,128)(2,1)S(1)}, u32[]{:S(2)}) copy-start(bf16[2,2,256,256]{3,2,1,0:T(8,128)(2,1)S(1)} %collective-permute-done.2.refs_0_) | copy-start | bytes 1572868
  39.1 11.4 %collective-permute-start.3 = (bf16[2,2,256,256]{3,2,1,0:T(8,128)(2,1)S(1)}, bf16[2,2,256,256]{3,2,1,0:T(8,128)(2,1)S(1)}, u32[]{:S(2)}, u32[]{:S(2)}) collective-permute-start(bf16[2,2,256,256]{3,2,1,0:T(8,128)(2,1)S(1)} %collective-permute-done.2.refs_0_), channel_id=1, source_target_pairs={{0,4},{2,6},{4,0},{6,2},{8,12},{10,14},{12,8},{14,10},{16,20},{18,... | collective-permute-start | bytes 1572872 | tf_op jit(solution)/shard_map/nearx1/ppermute | solution.py:21
  40.6 36.2 %collective-permute-start = (bf16[2,256,1024]{2,1,0:T(8,128)(2,1)S(1)}, bf16[2,256,1024]{2,1,0:T(8,128)(2,1)}, u32[]{:S(2)}, u32[]{:S(2)}) collective-permute-start(bf16[2,256,1024]{2,1,0:T(8,128)(2,1)S(1)} %copy-done.4), channel_id=1, source_target_pairs={{0,2},{2,0},{4,6},{6,4},{8,10},{10,8},{12,14},{14,12},{16,18},{18,... | collective-permute-start | bytes 3145736 | tf_op jit(solution)/shard_map/pair_q/ppermute | solution.py:21
  50.5 0.8 copy-start.2
  51.3 12.0 %collective-permute-start.4 = (bf16[2,2,256,256]{3,2,1,0:T(8,128)(2,1)}, bf16[2,2,256,256]{3,2,1,0:T(8,128)(2,1)S(1)}, u32[]{:S(2)}, u32[]{:S(2)}) collective-permute-start(bf16[2,2,256,256]{3,2,1,0:T(8,128)(2,1)} %shard_map.49.refs_5_), channel_id=1, source_target_pairs={{0,4},{2,6},{8,12},{10,14},{16,20},{18,22},{24,28},{26,30},{1,5},{... | collective-permute-start | bytes 1572872 | tf_op jit(solution)/shard_map/ownx0/ppermute | solution.py:21
  54.7 0.8 copy-start.8
  55.5 0.8 copy-start.9
  56.3 12.6 %collective-permute-start.9 = (bf16[2,2,256,256]{3,2,1,0:T(8,128)(2,1)}, bf16[2,2,256,256]{3,2,1,0:T(8,128)(2,1)}, u32[]{:S(2)}, u32[]{:S(2)}) collective-permute-start(bf16[2,2,256,256]{3,2,1,0:T(8,128)(2,1)} %shard_map.51.refs_7_), channel_id=1, source_target_pairs={{0,8},{2,10},{4,12},{6,14},{8,16},{10,18},{12,20},{14,22},{16,24},... | collective-permute-start | bytes 1572872 | tf_op jit(solution)/shard_map/far1/ppermute | solution.py:21
  61.5 12.2 %collective-permute-start.10 = (bf16[2,2,256,256]{3,2,1,0:T(8,128)(2,1)}, bf16[2,2,256,256]{3,2,1,0:T(8,128)(2,1)S(1)}, u32[]{:S(2)}, u32[]{:S(2)}) collective-permute-start(bf16[2,2,256,256]{3,2,1,0:T(8,128)(2,1)} %copy-done.9), channel_id=1, source_target_pairs={{4,0},{6,2},{12,8},{14,10},{20,16},{22,18},{28,24},{30,26},{5,1},{... | collective-permute-start | bytes 1572872 | tf_op jit(solution)/shard_map/farx0/ppermute | solution.py:21
  63.3 0.8 copy-start.3
  64.1 33.7 %collective-permute-start.5 = (bf16[2,2,256,256]{3,2,1,0:T(8,128)(2,1)}, bf16[2,2,256,256]{3,2,1,0:T(8,128)(2,1)S(1)}, u32[]{:S(2)}, u32[]{:S(2)}) collective-permute-start(bf16[2,2,256,256]{3,2,1,0:T(8,128)(2,1)} %shard_map.50.refs_5_), channel_id=1, source_target_pairs={{0,4},{2,6},{8,12},{10,14},{16,20},{18,22},{24,28},{26,30},{1,5},{... | collective-permute-start | bytes 1572872 | tf_op jit(solution)/shard_map/ownx1/ppermute | solution.py:21
  73.7 0.8 copy-start.5
  74.5 23.3 %collective-permute-start.11 = (bf16[2,2,256,256]{3,2,1,0:T(8,128)(2,1)}, bf16[2,2,256,256]{3,2,1,0:T(8,128)(2,1)S(1)}, u32[]{:S(2)}, u32[]{:S(2)}) collective-permute-start(bf16[2,2,256,256]{3,2,1,0:T(8,128)(2,1)} %shard_map.52.refs_8_), channel_id=1, source_target_pairs={{4,0},{6,2},{12,8},{14,10},{20,16},{22,18},{28,24},{30,26},{5,1},{... | collective-permute-start | bytes 1572872 | tf_op jit(solution)/shard_map/farx1/ppermute | solution.py:21
  76.8 0.7 copy-start.11
  97.8 0.8 copy-start.6
  97.9 1.0 copy-start.7
  98.8 0.9 copy-start.13
  98.8 1.5 %copy-start.21 = (bf16[2,256,256]{2,1,0:T(8,128)(2,1)S(1)}, bf16[2,256,256]{2,1,0:T(8,128)(2,1)}, u32[]{:S(2)}) copy-start(bf16[2,256,256]{2,1,0:T(8,128)(2,1)} %get-tuple-element.14) | copy-start | bytes 786436
  98.8 25.9 %collective-permute-start.17 = (bf16[512,2048]{1,0:T(8,128)(2,1)}, bf16[512,2048]{1,0:T(8,128)(2,1)S(1)}, u32[]{:S(2)}, u32[]{:S(2)}) collective-permute-start(bf16[512,2048]{1,0:T(8,128)(2,1)} %shard_map.55.refs_9_.refs_5_), channel_id=1, source_target_pairs={{0,2},{2,0},{4,6},{6,4},{8,10},{10,8},{12,14},{14,12},{16,18},{18,... | collective-permute-start | bytes 6291464 | tf_op jit(solution)/shard_map/panel_pair/ppermute | solution.py:21
  99.8 22.9 %collective-permute-start.19 = (bf16[2,256,256]{2,1,0:T(8,128)(2,1)S(1)}, bf16[2,256,256]{2,1,0:T(8,128)(2,1)S(1)}, u32[]{:S(2)}, u32[]{:S(2)}) collective-permute-start(bf16[2,256,256]{2,1,0:T(8,128)(2,1)S(1)} %copy-done.13), channel_id=1, source_target_pairs={{0,1},{1,0},{2,3},{3,2},{4,5},{5,4},{6,7},{7,6},{8,9},{9,8},{10,11... | collective-permute-start | bytes 786440 | tf_op jit(solution)/shard_map/same0/ppermute | solution.py:27
  100.3 22.9 %collective-permute-start.20 = (bf16[2,256,256]{2,1,0:T(8,128)(2,1)S(1)}, bf16[2,256,256]{2,1,0:T(8,128)(2,1)S(1)}, u32[]{:S(2)}, u32[]{:S(2)}) collective-permute-start(bf16[2,256,256]{2,1,0:T(8,128)(2,1)S(1)} %copy-done.21), channel_id=1, source_target_pairs={{0,3},{1,2},{2,1},{3,0},{4,7},{5,6},{6,5},{7,4},{8,11},{9,10},{10,... | collective-permute-start | bytes 786440 | tf_op jit(solution)/shard_map/cross0/ppermute | solution.py:27
  100.7 24.0 %collective-permute-start.18 = (bf16[2,256,256]{2,1,0:T(8,128)(2,1)S(1)}, bf16[2,256,256]{2,1,0:T(8,128)(2,1)S(1)}, u32[]{:S(2)}, u32[]{:S(2)}) collective-permute-start(bf16[2,256,256]{2,1,0:T(8,128)(2,1)S(1)} %copy-done.21), channel_id=1, source_target_pairs={{0,2},{2,0},{4,6},{6,4},{8,10},{10,8},{12,14},{14,12},{16,18},{18,... | collective-permute-start | bytes 786440 | tf_op jit(solution)/shard_map/pair0/ppermute | solution.py:21
  122.5 12.3 %collective-permute-start.15 = (bf16[2,256,256]{2,1,0:T(8,128)(2,1)}, bf16[2,256,256]{2,1,0:T(8,128)(2,1)S(1)}, u32[]{:S(2)}, u32[]{:S(2)}) collective-permute-start(bf16[2,256,256]{2,1,0:T(8,128)(2,1)} %get-tuple-element.11), channel_id=1, source_target_pairs={{0,3},{1,2},{2,1},{3,0},{4,7},{5,6},{6,5},{7,4},{8,11},{9,10},{10,... | collective-permute-start | bytes 786440 | tf_op jit(solution)/shard_map/cross1/ppermute | solution.py:27
  122.7 2.1 %copy-start.14 = (bf16[2,256,256]{2,1,0:T(8,128)(2,1)}, bf16[2,256,256]{2,1,0:T(8,128)(2,1)S(1)}, u32[]{:S(2)}) copy-start(bf16[2,256,256]{2,1,0:T(8,128)(2,1)S(1)} %collective-permute-done.19.refs_4_) | copy-start | bytes 786436
  122.7 12.1 %collective-permute-start.13 = (bf16[2,256,256]{2,1,0:T(8,128)(2,1)}, bf16[2,256,256]{2,1,0:T(8,128)(2,1)S(1)}, u32[]{:S(2)}, u32[]{:S(2)}) collective-permute-start(bf16[2,256,256]{2,1,0:T(8,128)(2,1)} %get-tuple-element.11), channel_id=1, source_target_pairs={{0,2},{2,0},{4,6},{6,4},{8,10},{10,8},{12,14},{14,12},{16,18},{18,... | collective-permute-start | bytes 786440 | tf_op jit(solution)/shard_map/pair1/ppermute | solution.py:21
  123.2 1.5 %copy-start.15 = (bf16[2,256,256]{2,1,0:T(8,128)(2,1)}, bf16[2,256,256]{2,1,0:T(8,128)(2,1)S(1)}, u32[]{:S(2)}) copy-start(bf16[2,256,256]{2,1,0:T(8,128)(2,1)S(1)} %collective-permute-done.20.refs_5_) | copy-start | bytes 786436
  123.2 13.8 %collective-permute-start.14 = (bf16[2,256,256]{2,1,0:T(8,128)(2,1)}, bf16[2,256,256]{2,1,0:T(8,128)(2,1)S(1)}, u32[]{:S(2)}, u32[]{:S(2)}) collective-permute-start(bf16[2,256,256]{2,1,0:T(8,128)(2,1)} %get-tuple-element.12.refs_2_), channel_id=1, source_target_pairs={{0,1},{1,0},{2,3},{3,2},{4,5},{5,4},{6,7},{7,6},{8,9},{9,8},{10,11... | collective-permute-start | bytes 786440 | tf_op jit(solution)/shard_map/same1/ppermute | solution.py:27
  124.7 0.7 copy-start.16
  125.4 1.4 copy-start.1
  134.8 2.2 %copy-start.17 = (bf16[2,256,256]{2,1,0:T(8,128)(2,1)}, bf16[2,256,256]{2,1,0:T(8,128)(2,1)S(1)}, u32[]{:S(2)}) copy-start(bf16[2,256,256]{2,1,0:T(8,128)(2,1)S(1)} %collective-permute-done.15.refs_3_) | copy-start | bytes 786436
  134.8 2.2 %copy-start.18 = (bf16[2,256,256]{2,1,0:T(8,128)(2,1)}, bf16[2,256,256]{2,1,0:T(8,128)(2,1)S(1)}, u32[]{:S(2)}) copy-start(bf16[2,256,256]{2,1,0:T(8,128)(2,1)S(1)} %collective-permute-done.13.refs_1_) | copy-start | bytes 786436
  137.0 0.7 copy-start.19

commit v9 on v8

--- a/solution.py
+++ b/solution.py
@@ -11,7 +11,7 @@
 BLK = 64
 WINB = 32
 MASKED = -1e30
-SCALE = math.log2(math.e) / math.sqrt(HD)
+SCALE = 1.0 / math.sqrt(HD)
 VMEM = 60 * 1024 * 1024
 
 
@@ -32,6 +32,7 @@
 
 
 def gated(arrays, *ties):
+    ties = [t[(0,) * (t.ndim - 2)][:8] for t in ties]
     some = pl.BlockSpec(memory_space=pl.ANY)
     return pl.pallas_call(
         lambda *refs: None,
@@ -39,7 +40,7 @@
         out_specs=[some] * len(arrays),
         out_shape=[jax.ShapeDtypeStruct(a.shape, a.dtype) for a in arrays],
         input_output_aliases={k: k for k in range(len(arrays))},
-        compiler_params=pltpu.CompilerParams(vmem_limit_bytes=VMEM),
+        compiler_params=pltpu.CompilerParams(vmem_limit_bytes=1024 * 1024),
         cost_estimate=pl.CostEstimate(flops=0, bytes_accessed=0, transcendentals=0),
     )(*arrays, *ties)
 
@@ -109,9 +110,7 @@
 
 def attend_kernel(tokens, info, *refs):
     core, side = info[0], info[1]
-    views, pairs, blocks, refs = refs[:4], refs[4:6], refs[6:10], refs[-7:]
-    own, low = pairs
-    one, two, swap, far = blocks
+    views, (own, one, two, swap, extra), refs = refs[:4], refs[4:9], refs[-7:]
     table, mine, give, tie, keys, values, least = refs
     tie[...] = jnp.zeros_like(tie)
     rows = tokens // BLK
@@ -121,22 +120,15 @@
     def place(ref, pair):
         for slot in range(2):
             half = core if slot == 0 else 1 - core
-            keys[pair * 2 + half] = ref[slot, 0].T
-            values[pair * 2 + half] = ref[slot, 1]
+            keys[pair * 2 + half] = ref[0, slot, 0].T
+            values[pair * 2 + half] = ref[0, slot, 1]
 
     place(two, 0)
     place(one, 2)
     place(swap, jnp.where(side == 0, 3, 1))
     place(own, back)
 
-    @pl.when(side == 0)
-    def _():
-        place(far, 1)
-
-    @pl.when(side != 0)
-    def _():
-        place(low, 3)
-
+    place(extra, jnp.where(side == 0, 1, 3))
     for tile in range(2):
         keys[slots + tile] = views[2 * tile + 1][0, 0].T
 
@@ -191,7 +183,7 @@
         upcoming = scores_of(*steps[at + 1]) if at + 1 < len(steps) else None
         if last is not None:
             add(*last)
-        last = (*step, jnp.exp2(scores * SCALE).astype(jnp.bfloat16))
+        last = (*step, jnp.exp(scores * SCALE).astype(jnp.bfloat16))
         scores = upcoming
     add(*last)
     low_sum = None
@@ -211,13 +203,13 @@
             scores = jnp.concatenate(
                 [jnp.dot(query, key, preferred_element_type=jnp.float32) for key, _ in pieces], 1)
             top = jnp.max(scores, axis=1, keepdims=True)
-            expo = jnp.exp2((scores - top) * SCALE).astype(jnp.bfloat16)
+            expo = jnp.exp((scores - top) * SCALE).astype(jnp.bfloat16)
             total = jnp.dot(expo, jnp.concatenate([value for _, value in pieces], 0),
                             preferred_element_type=jnp.float32)
             store(tile, total[:, :HD] / total[:, HD:])
 
 
-def attend(info, queries, keys_values, there, got, own, low, blocks, table, part, heads_half, after):
+def attend(info, queries, keys_values, there, got, own, blocks, table, part, heads_half, after):
     tokens = queries.shape[1]
     slots = WINB * BLK // tokens + 2
     count, first = len(part), part[0]
@@ -225,7 +217,7 @@
     noisy = lambda h, info: (0, 1, 0, info[0] * heads_half + first + h)
     query_spec = pl.BlockSpec((2, tokens, HD), here)
     noisy_spec = pl.BlockSpec((2, 1, tokens, HD), noisy)
-    chunk = pl.BlockSpec((2, 2, tokens, HD), lambda h, info: (0, 0, 0, h))
+    chunk = pl.BlockSpec((1, 2, 2, tokens, HD), lambda h, info: (h, 0, 0, 0, 0))
     out_spec = pl.BlockSpec((2, tokens, HD), lambda h, info: (0, 0, h))
     out = jax.ShapeDtypeStruct((2, tokens, count * HD), jnp.bfloat16)
     work = count * 2 * 2 * tokens * slots * tokens
@@ -235,7 +227,7 @@
             num_scalar_prefetch=1,
             grid=(count,),
             in_specs=[
-                query_spec, noisy_spec, query_spec, noisy_spec, *[chunk] * 6,
+                query_spec, noisy_spec, query_spec, noisy_spec, *[chunk] * 5,
                 *[pl.BlockSpec(memory_space=pl.ANY)] * len(after),
                 pl.BlockSpec(table.shape, lambda h, info: (0, 0, 0, 0)),
             ],
@@ -251,7 +243,7 @@
         cost_estimate=pl.CostEstimate(
             flops=work * 8, bytes_accessed=count * 64 * 1024, transcendentals=0
         ),
-    )(info, queries, keys_values, there, got, own, low, *blocks, *after, table)
+    )(info, queries, keys_values, there, got, own, *blocks, *after, table)
 
 
 def project_kernel(count, groups, add, info, *refs):
@@ -298,7 +290,7 @@
             num_scalar_prefetch=1, grid=(steps,), in_specs=specs, out_specs=spec
         ),
         out_shape=jax.ShapeDtypeStruct((2, tokens, features), dtype),
-        compiler_params=pltpu.CompilerParams(vmem_limit_bytes=VMEM),
+        compiler_params=pltpu.CompilerParams(vmem_limit_bytes=40 * 1024 * 1024),
         cost_estimate=pl.CostEstimate(
             flops=2 * 2 * tokens * depth * features // 8,
             bytes_accessed=2 * depth * features // 8,
@@ -351,12 +343,15 @@
         pieces = []
         for slot, source in enumerate(ins[:2]):
             for head_at, target in outs:
-                wide = target.shape[-1]
-                here = lanes(core * width + head_at * HD, wide)
-                pieces.append((source.at[:, 0, :, here], [(slice(None), target.at[slot])]))
+                heads = target.shape[0]
+                here = lanes(core * width + head_at * HD, heads * HD)
+                pieces.append((source.at[:, 0, :, here], [
+                    ((slice(None), slice(None), slice(h * HD, (h + 1) * HD)), target.at[h, slot])
+                    for h in range(heads)
+                ]))
         return pieces
 
-    pair_shape = lambda heads: jax.ShapeDtypeStruct((2, 2, tokens, heads * HD), bf16)
+    pair_shape = lambda heads: jax.ShapeDtypeStruct((heads, 2, 2, tokens, HD), bf16)
     held = lambda heads: (2, tokens, heads * HD)
     first, = copies(
         info, [keys_values, got, *panels], [pair_shape(len(parts[0]))], [held(len(parts[0]))] * 2,
@@ -378,8 +373,8 @@
         for r, panel in enumerate(panels, 1)
     ]
 
+
     blocks = []
-    lows = []
     for k, mine in enumerate(own):
         one = moved(mine, n, ahead, f"near{k}")
         swap = moved(one, n, across, f"nearx{k}")
@@ -387,13 +382,9 @@
             one, = gated([one], *blocks[-1][1:3])
         two = moved(one, n, ahead, f"far{k}")
         if k:
-            own[k - 1], = gated([own[k - 1]], swap)
-            lows.append(moved(own[k - 1], n, upper, f"ownx{k - 1}"))
-            two, = gated([two], swap, blocks[-1][3], lows[-1])
-        blocks.append((one, two, swap, moved(two, n, lower, f"farx{k}")))
-    if lows:
-        own[-1], = gated([own[-1]], lows[-1])
-    lows.append(moved(own[-1], n, upper, f"ownx{len(own) - 1}"))
+            two, = gated([two], swap, blocks[-1][3])
+        extra = moved(jnp.where(side == 0, mine, two), n, across, f"extra{k}")
+        blocks.append((one, two, swap, extra))
 
     mask_there = moved(block_mask, n, pair, "pair_mask")
     table = jnp.stack([
@@ -406,7 +397,7 @@
     for k, part in enumerate(parts):
         after = []
         mine, give, tie = attend(
-            info, queries, keys_values, there, got, own[k], lows[k], blocks[k], table,
+            info, queries, keys_values, there, got, own[k], blocks[k], table,
             part, heads_half, after + ties[-1:],
         )
         ties.append(tie)
@@ -417,7 +408,7 @@
         acts[1].append(moved(give, n, pair, f"pair{k}"))
     others = []
     for same in sames:
-        same, = gated([same], blocks[-1][3], ties[0], lows[-1])
+        same, = gated([same], blocks[-1][3], ties[0])
         others += [same, moved(same, n, pair, "panel_pair")]
 
     weights = [out_weight, out_weight] + others

time: 145 us -> 139 us (0.959)
  starting transfers between devices: 38.1 us -> 27.6 us
  waiting for transfers between devices: 28.5 us -> 36 us
  local copies, waits for them, and re-layouts: 12 us -> 8.73 us
  other arithmetic: 0.99 us -> 4.04 us
  Pallas kernels: 64.7 us -> 61.9 us
    ppermute x16 -> x14, starting transfers between devices: 32.5 us -> 22.4 us  [moved(): return lax.ppermute(array, 'ctx', pairs)]
    unnamed x45 -> x23, local copies, waits for them, and re-layouts: 10.7 us -> 4.06 us
    ppermute x16 -> x14, waiting for transfers between devices: 26.3 us -> 30.6 us  [moved(): return lax.ppermute(array, 'ctx', pairs)]
    pallas_call x2, Pallas kernels: 14.9 us -> 11.4 us  [project(): pl.pallas_call(lambda *refs: project_kernel(len(flat), len(used), before...]
    slice x0 -> x5, local copies, waits for them, and re-layouts: none -> 3.37 us  [gated(): ties = [t[(0,) * (t.ndim - 2)][:8] for t in ties]]
    ppermute x5, waiting for transfers between devices: 2.22 us -> 5.43 us  [moved_both(): return lax.ppermute(array, ('ctx', 'fsdp'), pairs)]
    select_n x0 -> x2, other arithmetic: none -> 3.02 us  [on_device(): extra = moved(jnp.where(side == 0, mine, two), n, across, f'extra{k}')]
  transfers between devices with their start and end apart: 21 -> 19, of which waited for: 6 -> 7; matrix products, arithmetic and copies ran while one was open for 2% -> 6% of each run, Pallas kernels for 40% -> 41%
where the time goes in v9:
time: 139 us; the launch traced here: 138 us
  Pallas kernels  61.9 us (45%)
  waiting for transfers between devices  36 us (26%)
  starting transfers between devices  27.6 us (20%)
  local copies, waits for them, and re-layouts  8.73 us (6%)
  other arithmetic  4.04 us (3%)
    pallas_call x2, Pallas kernels, attend(): pl.pallas_call(lambda *refs: attend_kernel(tokens, *refs), grid_spec=pltp...  41.4 us
    ppermute x14, waiting for transfers between devices, moved(): return lax.ppermute(array, 'ctx', pairs)  30.6 us
    ppermute x14, starting transfers between devices, moved(): return lax.ppermute(array, 'ctx', pairs)  22.4 us
    pallas_call x2, Pallas kernels, project(): pl.pallas_call(lambda *refs: project_kernel(len(flat), len(used), before...  11.4 us
    pallas_call x3, Pallas kernels, copies(): pl.pallas_call(kernel, grid_spec=pltpu.PrefetchScalarGridSpec(num_scalar_...  9.08 us
    ppermute x5, waiting for transfers between devices, moved_both(): return lax.ppermute(array, ('ctx', 'fsdp'), pairs)  5.43 us
    ppermute x5, starting transfers between devices, moved_both(): return lax.ppermute(array, ('ctx', 'fsdp'), pairs)  5.2 us
    unnamed x23, local copies, waits for them, and re-layouts  4.06 us
  transfers between devices with their start and end apart: 19, of which 7 were waited for; matrix products, arithmetic and copies ran while one was open for 6% of the time, Pallas kernels for 41%

profile of v9, /device:TPU:0, one launch (start us, length us, event | category | flops | bytes accessed | tf_op | source)
XLA Modules:
  0.0 138.5 jit_solution(13492428918847890724)
XLA Ops:
  0.0 0.5 collective-permute-start.1
  0.5 0.5 collective-permute-start
  1.0 0.6 pad_add_fusion.2.info.refs_0_
  1.6 3.5 %shard_map.46.refs_2_ = bf16[512,2048]{1,0:T(8,128)(2,1)} custom-call(s32[3]{0:T(128)} %pad_add_fusion.2.info.refs_0_, bf16[1024,4096]{1,0:T(8,128)(2,1)} %refs_4_.1), custom_call_target="tpu_custom_call" | custom-call | bytes 1048576 | tf_op jit(solution)/shard_map/pallas_call | solution.py:92
  5.1 2.6 %collective-permute-start.14 = (bf16[512,2048]{1,0:T(8,128)(2,1)}, bf16[512,2048]{1,0:T(8,128)(2,1)S(1)}, u32[]{:S(2)}, u32[]{:S(2)}) collective-permute-start(bf16[512,2048]{1,0:T(8,128)(2,1)} %shard_map.46.refs_2_), channel_id=1, source_target_pairs={{0,1},{1,0},{2,3},{3,2},{4,5},{5,4},{6,7},{7,6},{8,9},{9,8},{10,11... | collective-permute-start | bytes 6291464 | tf_op jit(solution)/shard_map/panel/ppermute | solution.py:27
  7.7 2.7 %shard_map.47.refs_2_.refs_5_ = bf16[2,2,2,256,128]{4,3,2,1,0:T(8,128)(2,1)} custom-call(s32[3]{0:T(128)} %pad_add_fusion.2.info.refs_0_, bf16[2,2,256,1024]{3,2,1,0:T(8,128)(2,1)} %refs_2_.3, bf16[2,2,256,1024]{3,2,1,0:T(8,128)(2,1)} %collective-permute-done.1.refs_1_.refs_4_, bf16[512,2048]{1,0:T(8,128)(2,1)} %shard_map.46.refs_2_), custom_call_target="tpu_custom_call" | custom-call | bytes 262144 | tf_op jit(solution)/shard_map/pallas_call | solution.py:92
  10.5 4.3 %collective-permute-start.3 = (bf16[2,2,2,256,128]{4,3,2,1,0:T(8,128)(2,1)}, bf16[2,2,2,256,128]{4,3,2,1,0:T(8,128)(2,1)}, u32[]{:S(2)}, u32[]{:S(2)}) collective-permute-start(bf16[2,2,2,256,128]{4,3,2,1,0:T(8,128)(2,1)} %shard_map.47.refs_2_.refs_5_), channel_id=1, source_target_pairs={{0,8},{2,10},{4,12},{6,14},{8,16},{10,18},{12,20},{14,22},{16,24},... | collective-permute-start | bytes 1572872 | tf_op jit(solution)/shard_map/near0/ppermute | solution.py:21
  14.9 2.9 %shard_map.48.refs_5_ = bf16[2,2,2,256,128]{4,3,2,1,0:T(8,128)(2,1)} custom-call(s32[3]{0:T(128)} %pad_add_fusion.2.info.refs_0_, bf16[2,2,256,1024]{3,2,1,0:T(8,128)(2,1)} %refs_2_.3, bf16[2,2,256,1024]{3,2,1,0:T(8,128)(2,1)} %collective-permute-done.1.refs_1_.refs_4_, bf16[2,2,2,256,128]{4,3,2,1,0:T(8,128)(2,1)} %shard_map.47.refs_2_.refs_5_), custom_call_target="tpu_custom_call" | custom-call | bytes 262144 | tf_op jit(solution)/shard_map/pallas_call | solution.py:92
  17.8 2.7 %collective-permute-start.2 = (bf16[2,2,2,256,128]{4,3,2,1,0:T(8,128)(2,1)}, bf16[2,2,2,256,128]{4,3,2,1,0:T(8,128)(2,1)S(1)}, u32[]{:S(2)}, u32[]{:S(2)}) collective-permute-start(bf16[2,2,2,256,128]{4,3,2,1,0:T(8,128)(2,1)} %shard_map.48.refs_5_), channel_id=1, source_target_pairs={{0,8},{2,10},{4,12},{6,14},{8,16},{10,18},{12,20},{14,22},{16,24},... | collective-permute-start | bytes 1572872 | tf_op jit(solution)/shard_map/near1/ppermute | solution.py:21
  20.6 6.0 %collective-permute-done.3.refs_6_ = bf16[2,2,2,256,128]{4,3,2,1,0:T(8,128)(2,1)} collective-permute-done((bf16[2,2,2,256,128]{4,3,2,1,0:T(8,128)(2,1)}, bf16[2,2,2,256,128]{4,3,2,1,0:T(8,128)(2,1)}, u32[]{:S(2)}, u32[]{:S(2)}) %collective-permute-start.3) | collective-permute-done | bytes 524320 | tf_op jit(solution)/shard_map/near0/ppermute | solution.py:21
  26.5 5.2 %collective-permute-start.4 = (bf16[2,2,2,256,128]{4,3,2,1,0:T(8,128)(2,1)}, bf16[2,2,2,256,128]{4,3,2,1,0:T(8,128)(2,1)}, u32[]{:S(2)}, u32[]{:S(2)}) collective-permute-start(bf16[2,2,2,256,128]{4,3,2,1,0:T(8,128)(2,1)} %collective-permute-done.3.refs_6_), channel_id=1, source_target_pairs={{0,8},{2,10},{4,12},{6,14},{8,16},{10,18},{12,20},{14,22},{16,24},... | collective-permute-start | bytes 1572872 | tf_op jit(solution)/shard_map/far0/ppermute | solution.py:21
  32.0 1.6 %collective-permute-start.5 = (bf16[2,2,2,256,128]{4,3,2,1,0:T(8,128)(2,1)}, bf16[2,2,2,256,128]{4,3,2,1,0:T(8,128)(2,1)}, u32[]{:S(2)}, u32[]{:S(2)}) collective-permute-start(bf16[2,2,2,256,128]{4,3,2,1,0:T(8,128)(2,1)} %collective-permute-done.3.refs_6_), channel_id=1, source_target_pairs={{0,4},{2,6},{4,0},{6,2},{8,12},{10,14},{12,8},{14,10},{16,20},{18,... | collective-permute-start | bytes 1572872 | tf_op jit(solution)/shard_map/nearx0/ppermute | solution.py:21
  33.7 4.1 %collective-permute-done.2.refs_0_ = bf16[2,2,2,256,128]{4,3,2,1,0:T(8,128)(2,1)S(1)} collective-permute-done((bf16[2,2,2,256,128]{4,3,2,1,0:T(8,128)(2,1)}, bf16[2,2,2,256,128]{4,3,2,1,0:T(8,128)(2,1)S(1)}, u32[]{:S(2)}, u32[]{:S(2)}) %collective-permute-start.2) | collective-permute-done | bytes 524320 | tf_op jit(solution)/shard_map/near1/ppermute | solution.py:21
  37.8 1.5 %collective-permute-start.7 = (bf16[2,2,2,256,128]{4,3,2,1,0:T(8,128)(2,1)S(1)}, bf16[2,2,2,256,128]{4,3,2,1,0:T(8,128)(2,1)S(1)}, u32[]{:S(2)}, u32[]{:S(2)}) collective-permute-start(bf16[2,2,2,256,128]{4,3,2,1,0:T(8,128)(2,1)S(1)} %collective-permute-done.2.refs_0_), channel_id=1, source_target_pairs={{0,4},{2,6},{4,0},{6,2},{8,12},{10,14},{12,8},{14,10},{16,20},{18,... | collective-permute-start | bytes 1572872 | tf_op jit(solution)/shard_map/nearx1/ppermute | solution.py:21
  39.3 9.0 %collective-permute-done.4.refs_7_ = bf16[2,2,2,256,128]{4,3,2,1,0:T(8,128)(2,1)} collective-permute-done((bf16[2,2,2,256,128]{4,3,2,1,0:T(8,128)(2,1)}, bf16[2,2,2,256,128]{4,3,2,1,0:T(8,128)(2,1)}, u32[]{:S(2)}, u32[]{:S(2)}) %collective-permute-start.4) | collective-permute-done | bytes 524320 | tf_op jit(solution)/shard_map/far0/ppermute | solution.py:21
  48.3 0.9 broadcast_select_fusion.1
  49.2 2.5 %collective-permute-start.8 = (bf16[2,2,2,256,128]{4,3,2,1,0:T(8,128)(2,1)}, bf16[2,2,2,256,128]{4,3,2,1,0:T(8,128)(2,1)}, u32[]{:S(2)}, u32[]{:S(2)}) collective-permute-start(bf16[2,2,2,256,128]{4,3,2,1,0:T(8,128)(2,1)} %broadcast_select_fusion.1), channel_id=1, source_target_pairs={{0,4},{2,6},{4,0},{6,2},{8,12},{10,14},{12,8},{14,10},{16,20},{18,... | collective-permute-start | bytes 1572872 | tf_op jit(solution)/shard_map/extra0/ppermute | solution.py:21
  51.7 0.7 slice_bitcast_fusion.4.refs_1_
  52.4 0.7 slice_bitcast_fusion.3.refs_2_
  53.0 5.3 %collective-permute-done.7.refs_8_ = bf16[2,2,2,256,128]{4,3,2,1,0:T(8,128)(2,1)S(1)} collective-permute-done((bf16[2,2,2,256,128]{4,3,2,1,0:T(8,128)(2,1)S(1)}, bf16[2,2,2,256,128]{4,3,2,1,0:T(8,128)(2,1)S(1)}, u32[]{:S(2)}, u32[]{:S(2)}) %collective-permute-start.7) | collective-permute-done | bytes 524320 | tf_op jit(solution)/shard_map/nearx1/ppermute | solution.py:21
  58.4 0.8 copy-done.8
  59.2 1.9 %collective-permute-start.6 = (bf16[2,2,2,256,128]{4,3,2,1,0:T(8,128)(2,1)S(1)}, bf16[2,2,2,256,128]{4,3,2,1,0:T(8,128)(2,1)S(1)}, u32[]{:S(2)}, u32[]{:S(2)}) collective-permute-start(bf16[2,2,2,256,128]{4,3,2,1,0:T(8,128)(2,1)S(1)} %shard_map.49.refs_6_), channel_id=1, source_target_pairs={{0,8},{2,10},{4,12},{6,14},{8,16},{10,18},{12,20},{14,22},{16,24},... | collective-permute-start | bytes 1572872 | tf_op jit(solution)/shard_map/far1/ppermute | solution.py:21
  61.1 0.2 copy.16
  61.3 0.7 slice_bitcast_fusion.2.refs_1_
  61.9 5.2 %collective-permute-done.8.refs_9_ = bf16[2,2,2,256,128]{4,3,2,1,0:T(8,128)(2,1)} collective-permute-done((bf16[2,2,2,256,128]{4,3,2,1,0:T(8,128)(2,1)}, bf16[2,2,2,256,128]{4,3,2,1,0:T(8,128)(2,1)}, u32[]{:S(2)}, u32[]{:S(2)}) %collective-permute-start.8) | collective-permute-done | bytes 524320 | tf_op jit(solution)/shard_map/extra0/ppermute | solution.py:21
  67.1 0.7 slice_bitcast_fusion.1.refs_2_
  67.8 0.9 collective-permute-done.6.refs_0_
  68.7 2.2 %broadcast_select_fusion = bf16[2,2,2,256,128]{4,3,2,1,0:T(8,128)(2,1)} fusion(bf16[2,2,2,256,128]{4,3,2,1,0:T(8,128)(2,1)} %shard_map.48.refs_5_, bf16[2,2,2,256,128]{4,3,2,1,0:T(8,128)(2,1)S(1)} %shard_map.50.refs_7_, pred[]{:T(512)S(6)} %eq.45), kind=kLoop, calls=%fused_computation | loop fusion | flops 262144 | bytes 1572865 | tf_op jit(solution)/shard_map/jit(_where)/select_n | solution.py:386
  71.1 0.2 broadcast_in_dim.17
  71.3 0.2 stack_reshape.7
  71.5 0.2 broadcast_in_dim.16
  71.7 0.2 stack_reshape.6
  71.9 0.6 copy-done.7
  72.6 20.6 %shard_map.51 = (bf16[2,256,256]{2,1,0:T(8,128)(2,1)}, bf16[2,256,256]{2,1,0:T(8,128)(2,1)}, f32[8,128]{1,0:T(8,128)}) custom-call(s32[3]{0:T(128)} %pad_add_fusion.2.info.refs_0_, bf16[2,256,1024]{2,1,0:T(8,128)(2,1)} %refs_1_.3, bf16[2,2,256,1024]{3,2,1,0:T(8,128)(2,1)} %refs_2_.3, bf16[2,256,1024]{2,1,0:T(8,128)(2,1)} %collective-permute-done.refs_3_, ...), custom_call_target="tpu_custom_call" | custom-call | flops 41943040 | bytes 131072 | tf_op jit(solution)/shard_map/pallas_call | solution.py:224
  93.2 0.7 slice_bitcast_fusion.refs_1_
  93.9 0.7 copy-done.5
  94.5 0.9 copy-done.2
  95.5 0.5 collective-permute-start.17
  96.0 0.4 collective-permute-start.18
  96.4 1.2 collective-permute-start.16
  97.6 20.8 %shard_map.52 = (bf16[2,256,256]{2,1,0:T(8,128)(2,1)}, bf16[2,256,256]{2,1,0:T(8,128)(2,1)}, f32[8,128]{1,0:T(8,128)}) custom-call(s32[3]{0:T(128)} %pad_add_fusion.2.info.refs_0_, bf16[2,256,1024]{2,1,0:T(8,128)(2,1)} %refs_1_.3, bf16[2,2,256,1024]{3,2,1,0:T(8,128)(2,1)} %refs_2_.3, bf16[2,256,1024]{2,1,0:T(8,128)(2,1)} %collective-permute-done.refs_3_, ...), custom_call_target="tpu_custom_call" | custom-call | flops 41943040 | bytes 131072 | tf_op jit(solution)/shard_map/pallas_call | solution.py:224
  118.5 0.2 collective-permute-start.13
  118.6 0.5 collective-permute-start.11
  119.1 1.5 %collective-permute-start.12 = (bf16[2,256,256]{2,1,0:T(8,128)(2,1)}, bf16[2,256,256]{2,1,0:T(8,128)(2,1)S(1)}, u32[]{:S(2)}, u32[]{:S(2)}) collective-permute-start(bf16[2,256,256]{2,1,0:T(8,128)(2,1)} %get-tuple-element.12.refs_2_), channel_id=1, source_target_pairs={{0,1},{1,0},{2,3},{3,2},{4,5},{5,4},{6,7},{7,6},{8,9},{9,8},{10,11... | collective-permute-start | bytes 786440 | tf_op jit(solution)/shard_map/same1/ppermute | solution.py:27
  120.7 1.0 copy-done.3
  121.6 5.9 %shard_map.54.refs_7_ = f32[2,256,2048]{2,1,0:T(8,128)S(1)} custom-call(s32[3]{0:T(128)S(1)} %copy-done.4, bf16[2,256,256]{2,1,0:T(8,128)(2,1)S(1)} %copy-done.2, bf16[2,256,256]{2,1,0:T(8,128)(2,1)S(1)} %copy-done.3, bf16[2,256,256]{2,1,0:T(8,128)(2,1)S(1)} %collective-permute-done.16.refs_3_, bf16[2,256,256]{2,1,0:T(8,128)(2,1)S(1)} %collective-permute-done.17.refs_4_, ...), custom_call_target="tpu_custom_call" | custom-call | flops 335544320 | bytes 655360 | tf_op jit(solution)/shard_map/pallas_call | solution.py:287
  127.5 5.4 %collective-permute-done.12.refs_2_ = bf16[2,256,256]{2,1,0:T(8,128)(2,1)S(1)} collective-permute-done((bf16[2,256,256]{2,1,0:T(8,128)(2,1)}, bf16[2,256,256]{2,1,0:T(8,128)(2,1)S(1)}, u32[]{:S(2)}, u32[]{:S(2)}) %collective-permute-start.12) | collective-permute-done | bytes 262176 | tf_op jit(solution)/shard_map/same1/ppermute | solution.py:27
  132.9 5.5 %shard_map.55 = bf16[2,256,2048]{2,1,0:T(8,128)(2,1)} custom-call(s32[3]{0:T(128)S(1)} %copy-done.4, bf16[2,256,256]{2,1,0:T(8,128)(2,1)S(1)} %collective-permute-done.11.refs_1_, bf16[2,256,256]{2,1,0:T(8,128)(2,1)S(1)} %collective-permute-done.12.refs_2_, bf16[2,256,256]{2,1,0:T(8,128)(2,1)S(1)} %collective-permute-done.13.refs_3_, ...), custom_call_target="tpu_custom_call" | custom-call | flops 201326592 | bytes 393216 | tf_op jit(solution)/shard_map/pallas_call | solution.py:287
  (53 shorter events, 0.9 us)
Async XLA Ops:
  0.0 7.7 %collective-permute-start.1 = (bf16[2,2,256,1024]{3,2,1,0:T(8,128)(2,1)}, bf16[2,2,256,1024]{3,2,1,0:T(8,128)(2,1)}, u32[]{:S(2)}, u32[]{:S(2)}) collective-permute-start(bf16[2,2,256,1024]{3,2,1,0:T(8,128)(2,1)} %refs_2_.3), channel_id=1, source_target_pairs={{0,2},{2,0},{4,6},{6,4},{8,10},{10,8},{12,14},{14,12},{16,18},{18,... | collective-permute-start | bytes 6291464 | tf_op jit(solution)/shard_map/pair_kv/ppermute | solution.py:21
  0.5 14.3 %collective-permute-start.10 = (s32[4,32]{1,0:T(4,128)}, s32[4,32]{1,0:T(4,128)S(1)}, u32[]{:S(2)}, u32[]{:S(2)}) collective-permute-start(s32[4,32]{1,0:T(4,128)} %param.6), channel_id=1, source_target_pairs={{0,2},{2,0},{4,6},{6,4},{8,10},{10,8},{12,14},{14,12},{16,18},{18,... | collective-permute-start | bytes 1544 | tf_op jit(solution)/shard_map/pair_mask/ppermute | solution.py:21
  0.5 71.4 %collective-permute-start = (bf16[2,256,1024]{2,1,0:T(8,128)(2,1)}, bf16[2,256,1024]{2,1,0:T(8,128)(2,1)}, u32[]{:S(2)}, u32[]{:S(2)}) collective-permute-start(bf16[2,256,1024]{2,1,0:T(8,128)(2,1)} %refs_1_.3), channel_id=1, source_target_pairs={{0,2},{2,0},{4,6},{6,4},{8,10},{10,8},{12,14},{14,12},{16,18},{18,... | collective-permute-start | bytes 3145736 | tf_op jit(solution)/shard_map/pair_q/ppermute | solution.py:21
  1.6 6.1 %copy-start.9 = (s32[4,32]{1,0:T(4,128)S(1)}, s32[4,32]{1,0:T(4,128)}, u32[]{:S(2)}) copy-start(s32[4,32]{1,0:T(4,128)} %param.6) | copy-start | bytes 1540
  5.1 88.8 %collective-permute-start.14 = (bf16[512,2048]{1,0:T(8,128)(2,1)}, bf16[512,2048]{1,0:T(8,128)(2,1)S(1)}, u32[]{:S(2)}, u32[]{:S(2)}) collective-permute-start(bf16[512,2048]{1,0:T(8,128)(2,1)} %shard_map.46.refs_2_), channel_id=1, source_target_pairs={{0,1},{1,0},{2,3},{3,2},{4,5},{5,4},{6,7},{7,6},{8,9},{9,8},{10,11... | collective-permute-start | bytes 6291464 | tf_op jit(solution)/shard_map/panel/ppermute | solution.py:27
  10.5 16.1 %collective-permute-start.3 = (bf16[2,2,2,256,128]{4,3,2,1,0:T(8,128)(2,1)}, bf16[2,2,2,256,128]{4,3,2,1,0:T(8,128)(2,1)}, u32[]{:S(2)}, u32[]{:S(2)}) collective-permute-start(bf16[2,2,2,256,128]{4,3,2,1,0:T(8,128)(2,1)} %shard_map.47.refs_2_.refs_5_), channel_id=1, source_target_pairs={{0,8},{2,10},{4,12},{6,14},{8,16},{10,18},{12,20},{14,22},{16,24},... | collective-permute-start | bytes 1572872 | tf_op jit(solution)/shard_map/near0/ppermute | solution.py:21
  14.9 33.4 %copy-start.6 = (bf16[2,2,2,256,128]{4,3,2,1,0:T(8,128)(2,1)S(1)}, bf16[2,2,2,256,128]{4,3,2,1,0:T(8,128)(2,1)}, u32[]{:S(2)}) copy-start(bf16[2,2,2,256,128]{4,3,2,1,0:T(8,128)(2,1)} %shard_map.47.refs_2_.refs_5_) | copy-start | bytes 1572868
  17.8 20.0 %collective-permute-start.2 = (bf16[2,2,2,256,128]{4,3,2,1,0:T(8,128)(2,1)}, bf16[2,2,2,256,128]{4,3,2,1,0:T(8,128)(2,1)S(1)}, u32[]{:S(2)}, u32[]{:S(2)}) collective-permute-start(bf16[2,2,2,256,128]{4,3,2,1,0:T(8,128)(2,1)} %shard_map.48.refs_5_), channel_id=1, source_target_pairs={{0,8},{2,10},{4,12},{6,14},{8,16},{10,18},{12,20},{14,22},{16,24},... | collective-permute-start | bytes 1572872 | tf_op jit(solution)/shard_map/near1/ppermute | solution.py:21
  26.5 21.8 %collective-permute-start.4 = (bf16[2,2,2,256,128]{4,3,2,1,0:T(8,128)(2,1)}, bf16[2,2,2,256,128]{4,3,2,1,0:T(8,128)(2,1)}, u32[]{:S(2)}, u32[]{:S(2)}) collective-permute-start(bf16[2,2,2,256,128]{4,3,2,1,0:T(8,128)(2,1)} %collective-permute-done.3.refs_6_), channel_id=1, source_target_pairs={{0,8},{2,10},{4,12},{6,14},{8,16},{10,18},{12,20},{14,22},{16,24},... | collective-permute-start | bytes 1572872 | tf_op jit(solution)/shard_map/far0/ppermute | solution.py:21
  32.0 20.4 %collective-permute-start.5 = (bf16[2,2,2,256,128]{4,3,2,1,0:T(8,128)(2,1)}, bf16[2,2,2,256,128]{4,3,2,1,0:T(8,128)(2,1)}, u32[]{:S(2)}, u32[]{:S(2)}) collective-permute-start(bf16[2,2,2,256,128]{4,3,2,1,0:T(8,128)(2,1)} %collective-permute-done.3.refs_6_), channel_id=1, source_target_pairs={{0,4},{2,6},{4,0},{6,2},{8,12},{10,14},{12,8},{14,10},{16,20},{18,... | collective-permute-start | bytes 1572872 | tf_op jit(solution)/shard_map/nearx0/ppermute | solution.py:21
  37.8 20.6 %collective-permute-start.7 = (bf16[2,2,2,256,128]{4,3,2,1,0:T(8,128)(2,1)S(1)}, bf16[2,2,2,256,128]{4,3,2,1,0:T(8,128)(2,1)S(1)}, u32[]{:S(2)}, u32[]{:S(2)}) collective-permute-start(bf16[2,2,2,256,128]{4,3,2,1,0:T(8,128)(2,1)S(1)} %collective-permute-done.2.refs_0_), channel_id=1, source_target_pairs={{0,4},{2,6},{4,0},{6,2},{8,12},{10,14},{12,8},{14,10},{16,20},{18,... | collective-permute-start | bytes 1572872 | tf_op jit(solution)/shard_map/nearx1/ppermute | solution.py:21
  49.2 17.9 %collective-permute-start.8 = (bf16[2,2,2,256,128]{4,3,2,1,0:T(8,128)(2,1)}, bf16[2,2,2,256,128]{4,3,2,1,0:T(8,128)(2,1)}, u32[]{:S(2)}, u32[]{:S(2)}) collective-permute-start(bf16[2,2,2,256,128]{4,3,2,1,0:T(8,128)(2,1)} %broadcast_select_fusion.1), channel_id=1, source_target_pairs={{0,4},{2,6},{4,0},{6,2},{8,12},{10,14},{12,8},{14,10},{16,20},{18,... | collective-permute-start | bytes 1572872 | tf_op jit(solution)/shard_map/extra0/ppermute | solution.py:21
  58.4 0.8 copy-start.8
  59.2 34.0 %copy-start.1 = (bf16[2,2,2,256,128]{4,3,2,1,0:T(8,128)(2,1)}, bf16[2,2,2,256,128]{4,3,2,1,0:T(8,128)(2,1)S(1)}, u32[]{:S(2)}) copy-start(bf16[2,2,2,256,128]{4,3,2,1,0:T(8,128)(2,1)S(1)} %shard_map.49.refs_6_) | copy-start | bytes 1572868
  59.2 9.5 %collective-permute-start.6 = (bf16[2,2,2,256,128]{4,3,2,1,0:T(8,128)(2,1)S(1)}, bf16[2,2,2,256,128]{4,3,2,1,0:T(8,128)(2,1)S(1)}, u32[]{:S(2)}, u32[]{:S(2)}) collective-permute-start(bf16[2,2,2,256,128]{4,3,2,1,0:T(8,128)(2,1)S(1)} %shard_map.49.refs_6_), channel_id=1, source_target_pairs={{0,8},{2,10},{4,12},{6,14},{8,16},{10,18},{12,20},{14,22},{16,24},... | collective-permute-start | bytes 1572872 | tf_op jit(solution)/shard_map/far1/ppermute | solution.py:21
  68.7 24.5 %copy-start = (bf16[2,2,2,256,128]{4,3,2,1,0:T(8,128)(2,1)}, bf16[2,2,2,256,128]{4,3,2,1,0:T(8,128)(2,1)S(1)}, u32[]{:S(2)}) copy-start(bf16[2,2,2,256,128]{4,3,2,1,0:T(8,128)(2,1)S(1)} %shard_map.50.refs_7_) | copy-start | bytes 1572868
  70.9 22.3 %collective-permute-start.9 = (bf16[2,2,2,256,128]{4,3,2,1,0:T(8,128)(2,1)}, bf16[2,2,2,256,128]{4,3,2,1,0:T(8,128)(2,1)}, u32[]{:S(2)}, u32[]{:S(2)}) collective-permute-start(bf16[2,2,2,256,128]{4,3,2,1,0:T(8,128)(2,1)} %broadcast_select_fusion), channel_id=1, source_target_pairs={{0,4},{2,6},{4,0},{6,2},{8,12},{10,14},{12,8},{14,10},{16,20},{18,... | collective-permute-start | bytes 1572872 | tf_op jit(solution)/shard_map/extra1/ppermute | solution.py:21
  71.9 0.7 copy-start.7
  93.9 0.7 copy-start.5
  94.5 0.9 copy-start.2
  94.5 1.5 %copy-start.10 = (bf16[2,256,256]{2,1,0:T(8,128)(2,1)S(1)}, bf16[2,256,256]{2,1,0:T(8,128)(2,1)}, u32[]{:S(2)}) copy-start(bf16[2,256,256]{2,1,0:T(8,128)(2,1)} %get-tuple-element.14) | copy-start | bytes 786436
  94.5 26.1 %collective-permute-start.15 = (bf16[512,2048]{1,0:T(8,128)(2,1)S(1)}, bf16[512,2048]{1,0:T(8,128)(2,1)}, u32[]{:S(2)}, u32[]{:S(2)}) collective-permute-start(bf16[512,2048]{1,0:T(8,128)(2,1)S(1)} %shard_map.53.refs_9_.refs_5_), channel_id=1, source_target_pairs={{0,2},{2,0},{4,6},{6,4},{8,10},{10,8},{12,14},{14,12},{16,18},{18,... | collective-permute-start | bytes 6291464 | tf_op jit(solution)/shard_map/panel_pair/ppermute | solution.py:21
  95.5 23.1 %collective-permute-start.17 = (bf16[2,256,256]{2,1,0:T(8,128)(2,1)S(1)}, bf16[2,256,256]{2,1,0:T(8,128)(2,1)S(1)}, u32[]{:S(2)}, u32[]{:S(2)}) collective-permute-start(bf16[2,256,256]{2,1,0:T(8,128)(2,1)S(1)} %copy-done.2), channel_id=1, source_target_pairs={{0,1},{1,0},{2,3},{3,2},{4,5},{5,4},{6,7},{7,6},{8,9},{9,8},{10,11... | collective-permute-start | bytes 786440 | tf_op jit(solution)/shard_map/same0/ppermute | solution.py:27
  96.0 24.7 %copy-start.4 = (s32[3]{0:T(128)S(1)}, s32[3]{0:T(128)}, u32[]{:S(2)}) copy-start(s32[3]{0:T(128)} %pad_add_fusion.2.info.refs_0_) | copy-start | bytes 40
  96.0 23.1 %collective-permute-start.18 = (bf16[2,256,256]{2,1,0:T(8,128)(2,1)S(1)}, bf16[2,256,256]{2,1,0:T(8,128)(2,1)S(1)}, u32[]{:S(2)}, u32[]{:S(2)}) collective-permute-start(bf16[2,256,256]{2,1,0:T(8,128)(2,1)S(1)} %copy-done.10), channel_id=1, source_target_pairs={{0,3},{1,2},{2,1},{3,0},{4,7},{5,6},{6,5},{7,4},{8,11},{9,10},{10,... | collective-permute-start | bytes 786440 | tf_op jit(solution)/shard_map/cross0/ppermute | solution.py:27
  96.4 24.3 %collective-permute-start.16 = (bf16[2,256,256]{2,1,0:T(8,128)(2,1)S(1)}, bf16[2,256,256]{2,1,0:T(8,128)(2,1)S(1)}, u32[]{:S(2)}, u32[]{:S(2)}) collective-permute-start(bf16[2,256,256]{2,1,0:T(8,128)(2,1)S(1)} %copy-done.10), channel_id=1, source_target_pairs={{0,2},{2,0},{4,6},{6,4},{8,10},{10,8},{12,14},{14,12},{16,18},{18,... | collective-permute-start | bytes 786440 | tf_op jit(solution)/shard_map/pair0/ppermute | solution.py:21
  118.5 9.1 %collective-permute-start.13 = (bf16[2,256,256]{2,1,0:T(8,128)(2,1)}, bf16[2,256,256]{2,1,0:T(8,128)(2,1)S(1)}, u32[]{:S(2)}, u32[]{:S(2)}) collective-permute-start(bf16[2,256,256]{2,1,0:T(8,128)(2,1)} %get-tuple-element.11), channel_id=1, source_target_pairs={{0,3},{1,2},{2,1},{3,0},{4,7},{5,6},{6,5},{7,4},{8,11},{9,10},{10,... | collective-permute-start | bytes 786440 | tf_op jit(solution)/shard_map/cross1/ppermute | solution.py:27
  118.6 8.9 %collective-permute-start.11 = (bf16[2,256,256]{2,1,0:T(8,128)(2,1)}, bf16[2,256,256]{2,1,0:T(8,128)(2,1)S(1)}, u32[]{:S(2)}, u32[]{:S(2)}) collective-permute-start(bf16[2,256,256]{2,1,0:T(8,128)(2,1)} %get-tuple-element.11), channel_id=1, source_target_pairs={{0,2},{2,0},{4,6},{6,4},{8,10},{10,8},{12,14},{14,12},{16,18},{18,... | collective-permute-start | bytes 786440 | tf_op jit(solution)/shard_map/pair1/ppermute | solution.py:21
  119.1 13.8 %collective-permute-start.12 = (bf16[2,256,256]{2,1,0:T(8,128)(2,1)}, bf16[2,256,256]{2,1,0:T(8,128)(2,1)S(1)}, u32[]{:S(2)}, u32[]{:S(2)}) collective-permute-start(bf16[2,256,256]{2,1,0:T(8,128)(2,1)} %get-tuple-element.12.refs_2_), channel_id=1, source_target_pairs={{0,1},{1,0},{2,3},{3,2},{4,5},{5,4},{6,7},{7,6},{8,9},{9,8},{10,11... | collective-permute-start | bytes 786440 | tf_op jit(solution)/shard_map/same1/ppermute | solution.py:27
  120.7 1.0 copy-start.3

commit v10 on v9

--- a/solution.py
+++ b/solution.py
@@ -60,10 +60,7 @@
         [jnp.concatenate([clean, noisy], 1), jnp.concatenate([own_clean, own_noisy], 1)], 0
     )
     table = jnp.where(allowed, 0.0, MASKED).astype(jnp.float32)
-    table = jnp.concatenate([table, jnp.ones((count + rows, 1), jnp.float32)], 1)
-    table = jnp.pad(table, ((0, 0), (0, 16 - table.shape[1]))).astype(jnp.bfloat16)
-    table = jnp.repeat(table.reshape(-1, rows, 16).transpose(0, 2, 1), BLK, axis=2)
-    return table
+    return jnp.repeat(table.reshape(-1, rows, 2 * rows).transpose(0, 2, 1), BLK, axis=2)
 
 
 def copies(info, sources, outs, shapes, plan):
@@ -132,24 +129,15 @@
     for tile in range(2):
         keys[slots + tile] = views[2 * tile + 1][0, 0].T
 
-    spot = lax.broadcasted_iota(jnp.int32, (2 * tokens, HD), 0) // BLK
-    lane = lax.broadcasted_iota(jnp.int32, (2 * tokens, HD), 1)
-    hot = jnp.where(spot == lane, 1.0, 0.0)
-    rest = jnp.zeros((HD - table.shape[2], tokens), jnp.bfloat16)
-
     def operands(tile, k):
         half = core if tile == 0 else 1 - core
         if k == slots - 1:
-            key, value = keys[slots + tile], views[2 * tile + 1][1, 0]
-        else:
-            key, value = keys[half + k], values[half + k]
-        return (jnp.concatenate([key, table[tile, k], rest], 0),
-                jnp.concatenate([value, jnp.ones_like(value)], 1))
+            return keys[slots + tile], views[2 * tile + 1][1, 0]
+        return keys[half + k], values[half + k]
 
     def store(tile, out):
         (mine if tile == 0 else give)[...] = out.astype(jnp.bfloat16).reshape(2, tokens, HD)
 
-    shift_lane = 2 * rows
     ones = jnp.ones((16, HD), jnp.bfloat16)
     longest = None
     for k in range(slots + 2):
@@ -157,21 +145,28 @@
         size = jnp.dot(ones, key * key, preferred_element_type=jnp.float32)
         longest = size if longest is None else jnp.maximum(longest, size)
     longest = jnp.max(longest, axis=1, keepdims=True)[0:1] * 1.03
-    queries = []
+    queries, shifts = [], []
     for tile in range(2):
         query = views[2 * tile][...].reshape(2 * tokens, HD)
         size = jnp.dot(query * query, jnp.ones((HD, HD), jnp.bfloat16),
                        preferred_element_type=jnp.float32)
-        bound = jnp.sqrt(size * longest)
-        extra = jnp.where(lane == shift_lane, -bound, hot).astype(jnp.bfloat16)
-        queries.append(jnp.concatenate([query, extra], 1))
+        queries.append(query)
+        shifts.append((jnp.sqrt(size * longest) * SCALE)[:, 0:1])
 
     steps = [(tile, k) for tile in range(2) for k in range(0, slots, 2)]
-    totals = [None, None]
+    totals, sums = [None, None], [None, None]
 
     def scores_of(tile, k):
         key = jnp.concatenate([operands(tile, j)[0] for j in range(k, min(k + 2, slots))], 1)
-        return jnp.dot(queries[tile], key, preferred_element_type=jnp.float32)
+        scores = jnp.dot(queries[tile], key, preferred_element_type=jnp.float32)
+        bias = jnp.concatenate([table[tile, j] for j in range(k, min(k + 2, slots))], 1)
+        return scores, bias
+
+    def weights_of(tile, scores, bias, shift):
+        wide = scores.shape[1]
+        shifted = scores * SCALE - shift
+        shifted = shifted.reshape(2 * rows, BLK, wide) + bias[:, None, :]
+        return jnp.exp(shifted.reshape(2 * tokens, wide))
 
     def add(tile, k, expo):
         value = jnp.concatenate([operands(tile, j)[1] for j in range(k, min(k + 2, slots))], 0)
@@ -183,30 +178,35 @@
         upcoming = scores_of(*steps[at + 1]) if at + 1 < len(steps) else None
         if last is not None:
             add(*last)
-        last = (*step, jnp.exp(scores * SCALE).astype(jnp.bfloat16))
+        tile = step[0]
+        expo = weights_of(tile, *scores, shifts[tile])
+        for lanes in range(0, expo.shape[1], HD):
+            part = expo[:, lanes:lanes + HD]
+            sums[tile] = part if sums[tile] is None else sums[tile] + part
+        last = (*step, expo.astype(jnp.bfloat16))
         scores = upcoming
     add(*last)
     low_sum = None
     for tile, total in enumerate(totals):
-        sums = total[:, HD:]
-        store(tile, total[:, :HD] / sums)
-        smallest = jnp.min(sums.reshape(-1, 8, HD), axis=0)
+        whole = jnp.sum(sums[tile], axis=1, keepdims=True)
+        store(tile, total / whole)
+        smallest = jnp.min(whole, axis=0, keepdims=True)
         low_sum = smallest if low_sum is None else jnp.minimum(low_sum, smallest)
-    least[...] = low_sum
+    least[...] = jnp.broadcast_to(low_sum, least.shape)
 
     @pl.when(jnp.logical_not(jnp.min(least[...]) > 2.0 ** -40))
     def _():
         for tile in range(2):
-            query = views[2 * tile][...].reshape(2 * tokens, HD)
-            query = jnp.concatenate([query, hot.astype(jnp.bfloat16)], 1)
-            pieces = [operands(tile, k) for k in range(slots)]
-            scores = jnp.concatenate(
-                [jnp.dot(query, key, preferred_element_type=jnp.float32) for key, _ in pieces], 1)
-            top = jnp.max(scores, axis=1, keepdims=True)
-            expo = jnp.exp((scores - top) * SCALE).astype(jnp.bfloat16)
-            total = jnp.dot(expo, jnp.concatenate([value for _, value in pieces], 0),
-                            preferred_element_type=jnp.float32)
-            store(tile, total[:, :HD] / total[:, HD:])
+            runs = [scores_of(tile, k) for k in range(0, slots, 2)]
+            scores = jnp.concatenate([score for score, _ in runs], 1) * SCALE
+            bias = jnp.concatenate([bias for _, bias in runs], 1)
+            wide = scores.shape[1]
+            scores = (scores.reshape(2 * rows, BLK, wide) + bias[:, None, :]).reshape(
+                2 * tokens, wide)
+            expo = jnp.exp(scores - jnp.max(scores, axis=1, keepdims=True))
+            value = jnp.concatenate([operands(tile, k)[1] for k in range(slots)], 0)
+            total = jnp.dot(expo.astype(jnp.bfloat16), value, preferred_element_type=jnp.float32)
+            store(tile, total / jnp.sum(expo, axis=1, keepdims=True))
 
 
 def attend(info, queries, keys_values, there, got, own, blocks, table, part, heads_half, after):

time: 139 us -> 140 us (level)
  starting transfers between devices: 27.6 us -> 30.1 us
  other arithmetic: 4.04 us -> 2.11 us
  local copies, waits for them, and re-layouts: 8.73 us -> 7.1 us
  Pallas kernels: 61.9 us -> 63.4 us
    ppermute x14, starting transfers between devices: 22.4 us -> 25.4 us  [moved(): return lax.ppermute(array, 'ctx', pairs)]
    slice x5, local copies, waits for them, and re-layouts: 3.37 us -> 1.35 us  [gated(): ties = [t[(0,) * (t.ndim - 2)][:8] for t in ties]]
    select_n x2, other arithmetic: 3.02 us -> 1.09 us  [on_device(): extra = moved(jnp.where(side == 0, mine, two), n, across, f'extra{k}')]
    pallas_call x2, Pallas kernels: 41.4 us -> 43.1 us  [attend(): pl.pallas_call(lambda *refs: attend_kernel(tokens, *refs), grid_spec=pltp...]
    unnamed x23 -> x31, local copies, waits for them, and re-layouts: 4.06 us -> 4.72 us
  transfers between devices with their start and end apart: 19 -> 19, of which waited for: 7 -> 7; matrix products, arithmetic and copies ran while one was open for 6% -> 3% of each run, Pallas kernels for 41% -> 40%
where the time goes in v10:
time: 140 us; the launch traced here: 139 us
  Pallas kernels  63.4 us (45%)
  waiting for transfers between devices  36 us (26%)
  starting transfers between devices  30.1 us (22%)
  local copies, waits for them, and re-layouts  7.1 us (5%)
  other arithmetic  2.11 us (2%)
    pallas_call x2, Pallas kernels, attend(): pl.pallas_call(lambda *refs: attend_kernel(tokens, *refs), grid_spec=pltp...  43.1 us
    ppermute x14, waiting for transfers between devices, moved(): return lax.ppermute(array, 'ctx', pairs)  30.6 us
    ppermute x14, starting transfers between devices, moved(): return lax.ppermute(array, 'ctx', pairs)  25.4 us
    pallas_call x2, Pallas kernels, project(): pl.pallas_call(lambda *refs: project_kernel(len(flat), len(used), before...  11.4 us
    pallas_call x3, Pallas kernels, copies(): pl.pallas_call(kernel, grid_spec=pltpu.PrefetchScalarGridSpec(num_scalar_...  8.97 us
    ppermute x5, waiting for transfers between devices, moved_both(): return lax.ppermute(array, ('ctx', 'fsdp'), pairs)  5.43 us
    ppermute x5, starting transfers between devices, moved_both(): return lax.ppermute(array, ('ctx', 'fsdp'), pairs)  4.74 us
    unnamed x31, local copies, waits for them, and re-layouts  4.72 us
  transfers between devices with their start and end apart: 19, of which 7 were waited for; matrix products, arithmetic and copies ran while one was open for 3% of the time, Pallas kernels for 40%

profile of v10, /device:TPU:0, one launch (start us, length us, event | category | flops | bytes accessed | tf_op | source)
XLA Modules:
  0.0 139.0 jit_solution(1926489544112699629)
XLA Ops:
  0.0 0.5 collective-permute-start.1
  0.5 0.7 pad_add_fusion.2.info.refs_0_
  1.1 3.4 %shard_map.46.refs_2_ = bf16[512,2048]{1,0:T(8,128)(2,1)} custom-call(s32[3]{0:T(128)} %pad_add_fusion.2.info.refs_0_, bf16[1024,4096]{1,0:T(8,128)(2,1)} %refs_4_.1), custom_call_target="tpu_custom_call" | custom-call | bytes 1048576 | tf_op jit(solution)/shard_map/pallas_call | solution.py:89
  4.5 1.3 copy-done.6
  5.8 2.7 %shard_map.47.refs_2_.refs_5_ = bf16[2,2,2,256,128]{4,3,2,1,0:T(8,128)(2,1)} custom-call(s32[3]{0:T(128)} %pad_add_fusion.2.info.refs_0_, bf16[2,2,256,1024]{3,2,1,0:T(8,128)(2,1)} %refs_2_.3, bf16[2,2,256,1024]{3,2,1,0:T(8,128)(2,1)} %copy-done.6, bf16[512,2048]{1,0:T(8,128)(2,1)} %shard_map.46.refs_2_), custom_call_target="tpu_custom_call" | custom-call | bytes 262144 | tf_op jit(solution)/shard_map/pallas_call | solution.py:89
  8.6 5.6 %collective-permute-start.3 = (bf16[2,2,2,256,128]{4,3,2,1,0:T(8,128)(2,1)}, bf16[2,2,2,256,128]{4,3,2,1,0:T(8,128)(2,1)}, u32[]{:S(2)}, u32[]{:S(2)}) collective-permute-start(bf16[2,2,2,256,128]{4,3,2,1,0:T(8,128)(2,1)} %shard_map.47.refs_2_.refs_5_), channel_id=1, source_target_pairs={{0,8},{2,10},{4,12},{6,14},{8,16},{10,18},{12,20},{14,22},{16,24},... | collective-permute-start | bytes 1572872 | tf_op jit(solution)/shard_map/near0/ppermute | solution.py:21
  14.2 1.5 %collective-permute-start.14 = (bf16[512,2048]{1,0:T(8,128)(2,1)}, bf16[512,2048]{1,0:T(8,128)(2,1)S(1)}, u32[]{:S(2)}, u32[]{:S(2)}) collective-permute-start(bf16[512,2048]{1,0:T(8,128)(2,1)} %shard_map.46.refs_2_), channel_id=1, source_target_pairs={{0,1},{1,0},{2,3},{3,2},{4,5},{5,4},{6,7},{7,6},{8,9},{9,8},{10,11... | collective-permute-start | bytes 6291464 | tf_op jit(solution)/shard_map/panel/ppermute | solution.py:27
  15.7 0.5 collective-permute-start
  16.2 2.9 %shard_map.48.refs_5_ = bf16[2,2,2,256,128]{4,3,2,1,0:T(8,128)(2,1)} custom-call(s32[3]{0:T(128)} %pad_add_fusion.2.info.refs_0_, bf16[2,2,256,1024]{3,2,1,0:T(8,128)(2,1)} %refs_2_.3, bf16[2,2,256,1024]{3,2,1,0:T(8,128)(2,1)} %copy-done.6, bf16[2,2,2,256,128]{4,3,2,1,0:T(8,128)(2,1)} %shard_map.47.refs_2_.refs_5_), custom_call_target="tpu_custom_call" | custom-call | bytes 262144 | tf_op jit(solution)/shard_map/pallas_call | solution.py:89
  19.1 2.8 %collective-permute-start.2 = (bf16[2,2,2,256,128]{4,3,2,1,0:T(8,128)(2,1)}, bf16[2,2,2,256,128]{4,3,2,1,0:T(8,128)(2,1)S(1)}, u32[]{:S(2)}, u32[]{:S(2)}) collective-permute-start(bf16[2,2,2,256,128]{4,3,2,1,0:T(8,128)(2,1)} %shard_map.48.refs_5_), channel_id=1, source_target_pairs={{0,8},{2,10},{4,12},{6,14},{8,16},{10,18},{12,20},{14,22},{16,24},... | collective-permute-start | bytes 1572872 | tf_op jit(solution)/shard_map/near1/ppermute | solution.py:21
  21.9 4.1 %collective-permute-done.3.refs_6_ = bf16[2,2,2,256,128]{4,3,2,1,0:T(8,128)(2,1)} collective-permute-done((bf16[2,2,2,256,128]{4,3,2,1,0:T(8,128)(2,1)}, bf16[2,2,2,256,128]{4,3,2,1,0:T(8,128)(2,1)}, u32[]{:S(2)}, u32[]{:S(2)}) %collective-permute-start.3) | collective-permute-done | bytes 524320 | tf_op jit(solution)/shard_map/near0/ppermute | solution.py:21
  25.9 5.2 %collective-permute-start.4 = (bf16[2,2,2,256,128]{4,3,2,1,0:T(8,128)(2,1)}, bf16[2,2,2,256,128]{4,3,2,1,0:T(8,128)(2,1)}, u32[]{:S(2)}, u32[]{:S(2)}) collective-permute-start(bf16[2,2,2,256,128]{4,3,2,1,0:T(8,128)(2,1)} %collective-permute-done.3.refs_6_), channel_id=1, source_target_pairs={{0,8},{2,10},{4,12},{6,14},{8,16},{10,18},{12,20},{14,22},{16,24},... | collective-permute-start | bytes 1572872 | tf_op jit(solution)/shard_map/far0/ppermute | solution.py:21
  31.2 1.6 %collective-permute-start.5 = (bf16[2,2,2,256,128]{4,3,2,1,0:T(8,128)(2,1)}, bf16[2,2,2,256,128]{4,3,2,1,0:T(8,128)(2,1)S(1)}, u32[]{:S(2)}, u32[]{:S(2)}) collective-permute-start(bf16[2,2,2,256,128]{4,3,2,1,0:T(8,128)(2,1)} %collective-permute-done.3.refs_6_), channel_id=1, source_target_pairs={{0,4},{2,6},{4,0},{6,2},{8,12},{10,14},{12,8},{14,10},{16,20},{18,... | collective-permute-start | bytes 1572872 | tf_op jit(solution)/shard_map/nearx0/ppermute | solution.py:21
  32.8 4.4 %collective-permute-done.2.refs_0_ = bf16[2,2,2,256,128]{4,3,2,1,0:T(8,128)(2,1)S(1)} collective-permute-done((bf16[2,2,2,256,128]{4,3,2,1,0:T(8,128)(2,1)}, bf16[2,2,2,256,128]{4,3,2,1,0:T(8,128)(2,1)S(1)}, u32[]{:S(2)}, u32[]{:S(2)}) %collective-permute-start.2) | collective-permute-done | bytes 524320 | tf_op jit(solution)/shard_map/near1/ppermute | solution.py:21
  37.2 1.5 %collective-permute-start.7 = (bf16[2,2,2,256,128]{4,3,2,1,0:T(8,128)(2,1)S(1)}, bf16[2,2,2,256,128]{4,3,2,1,0:T(8,128)(2,1)S(1)}, u32[]{:S(2)}, u32[]{:S(2)}) collective-permute-start(bf16[2,2,2,256,128]{4,3,2,1,0:T(8,128)(2,1)S(1)} %collective-permute-done.2.refs_0_), channel_id=1, source_target_pairs={{0,4},{2,6},{4,0},{6,2},{8,12},{10,14},{12,8},{14,10},{16,20},{18,... | collective-permute-start | bytes 1572872 | tf_op jit(solution)/shard_map/nearx1/ppermute | solution.py:21
  38.7 9.0 %collective-permute-done.4.refs_7_ = bf16[2,2,2,256,128]{4,3,2,1,0:T(8,128)(2,1)} collective-permute-done((bf16[2,2,2,256,128]{4,3,2,1,0:T(8,128)(2,1)}, bf16[2,2,2,256,128]{4,3,2,1,0:T(8,128)(2,1)}, u32[]{:S(2)}, u32[]{:S(2)}) %collective-permute-start.4) | collective-permute-done | bytes 524320 | tf_op jit(solution)/shard_map/far0/ppermute | solution.py:21
  47.8 2.6 %collective-permute-start.8 = (bf16[2,2,2,256,128]{4,3,2,1,0:T(8,128)(2,1)S(1)}, bf16[2,2,2,256,128]{4,3,2,1,0:T(8,128)(2,1)S(1)}, u32[]{:S(2)}, u32[]{:S(2)}) collective-permute-start(bf16[2,2,2,256,128]{4,3,2,1,0:T(8,128)(2,1)S(1)} %broadcast_select_fusion.1), channel_id=1, source_target_pairs={{0,4},{2,6},{4,0},{6,2},{8,12},{10,14},{12,8},{14,10},{16,20},{18,... | collective-permute-start | bytes 1572872 | tf_op jit(solution)/shard_map/extra0/ppermute | solution.py:21
  50.4 0.7 slice_bitcast_fusion.4.refs_1_
  51.0 6.6 %collective-permute-done.7.refs_8_ = bf16[2,2,2,256,128]{4,3,2,1,0:T(8,128)(2,1)S(1)} collective-permute-done((bf16[2,2,2,256,128]{4,3,2,1,0:T(8,128)(2,1)S(1)}, bf16[2,2,2,256,128]{4,3,2,1,0:T(8,128)(2,1)S(1)}, u32[]{:S(2)}, u32[]{:S(2)}) %collective-permute-start.7) | collective-permute-done | bytes 524320 | tf_op jit(solution)/shard_map/nearx1/ppermute | solution.py:21
  57.6 2.6 %collective-permute-start.6 = (bf16[2,2,2,256,128]{4,3,2,1,0:T(8,128)(2,1)S(1)}, bf16[2,2,2,256,128]{4,3,2,1,0:T(8,128)(2,1)S(1)}, u32[]{:S(2)}, u32[]{:S(2)}) collective-permute-start(bf16[2,2,2,256,128]{4,3,2,1,0:T(8,128)(2,1)S(1)} %shard_map.49.refs_6_), channel_id=1, source_target_pairs={{0,8},{2,10},{4,12},{6,14},{8,16},{10,18},{12,20},{14,22},{16,24},... | collective-permute-start | bytes 1572872 | tf_op jit(solution)/shard_map/far1/ppermute | solution.py:21
  60.2 0.1 fusion.3
  60.4 5.8 %collective-permute-done.8.refs_9_ = bf16[2,2,2,256,128]{4,3,2,1,0:T(8,128)(2,1)S(1)} collective-permute-done((bf16[2,2,2,256,128]{4,3,2,1,0:T(8,128)(2,1)S(1)}, bf16[2,2,2,256,128]{4,3,2,1,0:T(8,128)(2,1)S(1)}, u32[]{:S(2)}, u32[]{:S(2)}) %collective-permute-start.8) | collective-permute-done | bytes 524320 | tf_op jit(solution)/shard_map/extra0/ppermute | solution.py:21
  66.2 0.7 collective-permute-done.6.refs_0_
  66.9 0.1 copy-done.12
  67.0 1.0 broadcast_select_fusion
  68.0 1.5 %collective-permute-start.9 = (bf16[2,2,2,256,128]{4,3,2,1,0:T(8,128)(2,1)}, bf16[2,2,2,256,128]{4,3,2,1,0:T(8,128)(2,1)}, u32[]{:S(2)}, u32[]{:S(2)}) collective-permute-start(bf16[2,2,2,256,128]{4,3,2,1,0:T(8,128)(2,1)} %broadcast_select_fusion), channel_id=1, source_target_pairs={{0,4},{2,6},{4,0},{6,2},{8,12},{10,14},{12,8},{14,10},{16,20},{18,... | collective-permute-start | bytes 1572872 | tf_op jit(solution)/shard_map/extra1/ppermute | solution.py:21
  69.7 0.1 copy.17
  69.8 0.1 copy.18
  70.0 0.1 copy.16
  70.1 0.1 broadcast_in_dim.16
  70.3 0.2 stack_reshape.6
  70.4 0.1 broadcast_in_dim.17
  70.6 0.2 stack_reshape.7
  70.8 0.7 copy-done.9
  71.4 21.5 %shard_map.51 = (bf16[2,256,256]{2,1,0:T(8,128)(2,1)}, bf16[2,256,256]{2,1,0:T(8,128)(2,1)}, f32[8,128]{1,0:T(8,128)}) custom-call(s32[3]{0:T(128)} %pad_add_fusion.2.info.refs_0_, bf16[2,256,1024]{2,1,0:T(8,128)(2,1)} %refs_1_.3, bf16[2,2,256,1024]{3,2,1,0:T(8,128)(2,1)} %refs_2_.3, bf16[2,256,1024]{2,1,0:T(8,128)(2,1)} %collective-permute-done.refs_3_, ...), custom_call_target="tpu_custom_call" | custom-call | flops 41943040 | bytes 131072 | tf_op jit(solution)/shard_map/pallas_call | solution.py:224
  92.9 0.7 slice_bitcast_fusion.refs_1_
  93.6 0.7 copy-done.5
  94.3 0.9 copy-done.2
  95.2 1.5 %collective-permute-start.17 = (bf16[2,256,256]{2,1,0:T(8,128)(2,1)S(1)}, bf16[2,256,256]{2,1,0:T(8,128)(2,1)S(1)}, u32[]{:S(2)}, u32[]{:S(2)}) collective-permute-start(bf16[2,256,256]{2,1,0:T(8,128)(2,1)S(1)} %copy-done.2), channel_id=1, source_target_pairs={{0,1},{1,0},{2,3},{3,2},{4,5},{5,4},{6,7},{7,6},{8,9},{9,8},{10,11... | collective-permute-start | bytes 786440 | tf_op jit(solution)/shard_map/same0/ppermute | solution.py:27
  96.7 0.6 collective-permute-start.16
  97.4 21.6 %shard_map.52 = (bf16[2,256,256]{2,1,0:T(8,128)(2,1)}, bf16[2,256,256]{2,1,0:T(8,128)(2,1)}, f32[8,128]{1,0:T(8,128)}) custom-call(s32[3]{0:T(128)} %pad_add_fusion.2.info.refs_0_, bf16[2,256,1024]{2,1,0:T(8,128)(2,1)} %refs_1_.3, bf16[2,2,256,1024]{3,2,1,0:T(8,128)(2,1)} %refs_2_.3, bf16[2,256,1024]{2,1,0:T(8,128)(2,1)} %collective-permute-done.refs_3_, ...), custom_call_target="tpu_custom_call" | custom-call | flops 41943040 | bytes 131072 | tf_op jit(solution)/shard_map/pallas_call | solution.py:224
  119.0 1.2 collective-permute-start.13
  120.2 0.5 collective-permute-start.11
  120.7 0.5 collective-permute-start.12
  121.2 1.0 copy-done.3
  122.2 5.8 %shard_map.54.refs_7_ = f32[2,256,2048]{2,1,0:T(8,128)S(1)} custom-call(s32[3]{0:T(128)S(1)} %copy-done.4, bf16[2,256,256]{2,1,0:T(8,128)(2,1)S(1)} %copy-done.2, bf16[2,256,256]{2,1,0:T(8,128)(2,1)S(1)} %copy-done.3, bf16[2,256,256]{2,1,0:T(8,128)(2,1)S(1)} %collective-permute-done.16.refs_3_, bf16[2,256,256]{2,1,0:T(8,128)(2,1)S(1)} %collective-permute-done.17.refs_4_, ...), custom_call_target="tpu_custom_call" | custom-call | flops 335544320 | bytes 655360 | tf_op jit(solution)/shard_map/pallas_call | solution.py:287
  128.1 5.4 %collective-permute-done.12.refs_2_ = bf16[2,256,256]{2,1,0:T(8,128)(2,1)S(1)} collective-permute-done((bf16[2,256,256]{2,1,0:T(8,128)(2,1)}, bf16[2,256,256]{2,1,0:T(8,128)(2,1)S(1)}, u32[]{:S(2)}, u32[]{:S(2)}) %collective-permute-start.12) | collective-permute-done | bytes 262176 | tf_op jit(solution)/shard_map/same1/ppermute | solution.py:27
  133.5 5.5 %shard_map.55 = bf16[2,256,2048]{2,1,0:T(8,128)(2,1)} custom-call(s32[3]{0:T(128)S(1)} %copy-done.4, bf16[2,256,256]{2,1,0:T(8,128)(2,1)S(1)} %collective-permute-done.11.refs_1_, bf16[2,256,256]{2,1,0:T(8,128)(2,1)S(1)} %collective-permute-done.12.refs_2_, bf16[2,256,256]{2,1,0:T(8,128)(2,1)S(1)} %collective-permute-done.13.refs_3_, ...), custom_call_target="tpu_custom_call" | custom-call | flops 201326592 | bytes 393216 | tf_op jit(solution)/shard_map/pallas_call | solution.py:287
  (57 shorter events, 0.5 us)
Async XLA Ops:
  0.0 4.5 %collective-permute-start.1 = (bf16[2,2,256,1024]{3,2,1,0:T(8,128)(2,1)}, bf16[2,2,256,1024]{3,2,1,0:T(8,128)(2,1)S(1)}, u32[]{:S(2)}, u32[]{:S(2)}) collective-permute-start(bf16[2,2,256,1024]{3,2,1,0:T(8,128)(2,1)} %refs_2_.3), channel_id=1, source_target_pairs={{0,2},{2,0},{4,6},{6,4},{8,10},{10,8},{12,14},{14,12},{16,18},{18,... | collective-permute-start | bytes 6291464 | tf_op jit(solution)/shard_map/pair_kv/ppermute | solution.py:21
  4.5 11.2 %copy-start.13 = (s32[4,32]{1,0:T(4,128)S(1)}, s32[4,32]{1,0:T(4,128)}, u32[]{:S(2)}) copy-start(s32[4,32]{1,0:T(4,128)} %param.6) | copy-start | bytes 1540
  4.5 1.3 copy-start.6
  8.6 17.4 %collective-permute-start.3 = (bf16[2,2,2,256,128]{4,3,2,1,0:T(8,128)(2,1)}, bf16[2,2,2,256,128]{4,3,2,1,0:T(8,128)(2,1)}, u32[]{:S(2)}, u32[]{:S(2)}) collective-permute-start(bf16[2,2,2,256,128]{4,3,2,1,0:T(8,128)(2,1)} %shard_map.47.refs_2_.refs_5_), channel_id=1, source_target_pairs={{0,8},{2,10},{4,12},{6,14},{8,16},{10,18},{12,20},{14,22},{16,24},... | collective-permute-start | bytes 1572872 | tf_op jit(solution)/shard_map/near0/ppermute | solution.py:21
  14.2 79.4 %collective-permute-start.14 = (bf16[512,2048]{1,0:T(8,128)(2,1)}, bf16[512,2048]{1,0:T(8,128)(2,1)S(1)}, u32[]{:S(2)}, u32[]{:S(2)}) collective-permute-start(bf16[512,2048]{1,0:T(8,128)(2,1)} %shard_map.46.refs_2_), channel_id=1, source_target_pairs={{0,1},{1,0},{2,3},{3,2},{4,5},{5,4},{6,7},{7,6},{8,9},{9,8},{10,11... | collective-permute-start | bytes 6291464 | tf_op jit(solution)/shard_map/panel/ppermute | solution.py:27
  15.7 15.5 %collective-permute-start.10 = (s32[4,32]{1,0:T(4,128)S(1)}, s32[4,32]{1,0:T(4,128)S(1)}, u32[]{:S(2)}, u32[]{:S(2)}) collective-permute-start(s32[4,32]{1,0:T(4,128)S(1)} %copy-done.13), channel_id=1, source_target_pairs={{0,2},{2,0},{4,6},{6,4},{8,10},{10,8},{12,14},{14,12},{16,18},{18,... | collective-permute-start | bytes 1544 | tf_op jit(solution)/shard_map/pair_mask/ppermute | solution.py:21
  15.7 55.1 %collective-permute-start = (bf16[2,256,1024]{2,1,0:T(8,128)(2,1)}, bf16[2,256,1024]{2,1,0:T(8,128)(2,1)}, u32[]{:S(2)}, u32[]{:S(2)}) collective-permute-start(bf16[2,256,1024]{2,1,0:T(8,128)(2,1)} %refs_1_.3), channel_id=1, source_target_pairs={{0,2},{2,0},{4,6},{6,4},{8,10},{10,8},{12,14},{14,12},{16,18},{18,... | collective-permute-start | bytes 3145736 | tf_op jit(solution)/shard_map/pair_q/ppermute | solution.py:21
  16.2 31.5 %copy-start.7 = (bf16[2,2,2,256,128]{4,3,2,1,0:T(8,128)(2,1)S(1)}, bf16[2,2,2,256,128]{4,3,2,1,0:T(8,128)(2,1)}, u32[]{:S(2)}) copy-start(bf16[2,2,2,256,128]{4,3,2,1,0:T(8,128)(2,1)} %shard_map.47.refs_2_.refs_5_) | copy-start | bytes 1572868
  19.1 18.1 %collective-permute-start.2 = (bf16[2,2,2,256,128]{4,3,2,1,0:T(8,128)(2,1)}, bf16[2,2,2,256,128]{4,3,2,1,0:T(8,128)(2,1)S(1)}, u32[]{:S(2)}, u32[]{:S(2)}) collective-permute-start(bf16[2,2,2,256,128]{4,3,2,1,0:T(8,128)(2,1)} %shard_map.48.refs_5_), channel_id=1, source_target_pairs={{0,8},{2,10},{4,12},{6,14},{8,16},{10,18},{12,20},{14,22},{16,24},... | collective-permute-start | bytes 1572872 | tf_op jit(solution)/shard_map/near1/ppermute | solution.py:21
  25.9 21.7 %collective-permute-start.4 = (bf16[2,2,2,256,128]{4,3,2,1,0:T(8,128)(2,1)}, bf16[2,2,2,256,128]{4,3,2,1,0:T(8,128)(2,1)}, u32[]{:S(2)}, u32[]{:S(2)}) collective-permute-start(bf16[2,2,2,256,128]{4,3,2,1,0:T(8,128)(2,1)} %collective-permute-done.3.refs_6_), channel_id=1, source_target_pairs={{0,8},{2,10},{4,12},{6,14},{8,16},{10,18},{12,20},{14,22},{16,24},... | collective-permute-start | bytes 1572872 | tf_op jit(solution)/shard_map/far0/ppermute | solution.py:21
  31.2 35.8 %copy-start.8 = (bf16[2,2,2,256,128]{4,3,2,1,0:T(8,128)(2,1)S(1)}, bf16[2,2,2,256,128]{4,3,2,1,0:T(8,128)(2,1)}, u32[]{:S(2)}) copy-start(bf16[2,2,2,256,128]{4,3,2,1,0:T(8,128)(2,1)} %shard_map.48.refs_5_) | copy-start | bytes 1572868
  31.2 19.8 %collective-permute-start.5 = (bf16[2,2,2,256,128]{4,3,2,1,0:T(8,128)(2,1)}, bf16[2,2,2,256,128]{4,3,2,1,0:T(8,128)(2,1)S(1)}, u32[]{:S(2)}, u32[]{:S(2)}) collective-permute-start(bf16[2,2,2,256,128]{4,3,2,1,0:T(8,128)(2,1)} %collective-permute-done.3.refs_6_), channel_id=1, source_target_pairs={{0,4},{2,6},{4,0},{6,2},{8,12},{10,14},{12,8},{14,10},{16,20},{18,... | collective-permute-start | bytes 1572872 | tf_op jit(solution)/shard_map/nearx0/ppermute | solution.py:21
  37.2 20.4 %collective-permute-start.7 = (bf16[2,2,2,256,128]{4,3,2,1,0:T(8,128)(2,1)S(1)}, bf16[2,2,2,256,128]{4,3,2,1,0:T(8,128)(2,1)S(1)}, u32[]{:S(2)}, u32[]{:S(2)}) collective-permute-start(bf16[2,2,2,256,128]{4,3,2,1,0:T(8,128)(2,1)S(1)} %collective-permute-done.2.refs_0_), channel_id=1, source_target_pairs={{0,4},{2,6},{4,0},{6,2},{8,12},{10,14},{12,8},{14,10},{16,20},{18,... | collective-permute-start | bytes 1572872 | tf_op jit(solution)/shard_map/nearx1/ppermute | solution.py:21
  47.8 18.4 %collective-permute-start.8 = (bf16[2,2,2,256,128]{4,3,2,1,0:T(8,128)(2,1)S(1)}, bf16[2,2,2,256,128]{4,3,2,1,0:T(8,128)(2,1)S(1)}, u32[]{:S(2)}, u32[]{:S(2)}) collective-permute-start(bf16[2,2,2,256,128]{4,3,2,1,0:T(8,128)(2,1)S(1)} %broadcast_select_fusion.1), channel_id=1, source_target_pairs={{0,4},{2,6},{4,0},{6,2},{8,12},{10,14},{12,8},{14,10},{16,20},{18,... | collective-permute-start | bytes 1572872 | tf_op jit(solution)/shard_map/extra0/ppermute | solution.py:21
  51.0 18.5 %copy-start.11 = (bf16[2,2,2,256,128]{4,3,2,1,0:T(8,128)(2,1)}, bf16[2,2,2,256,128]{4,3,2,1,0:T(8,128)(2,1)S(1)}, u32[]{:S(2)}) copy-start(bf16[2,2,2,256,128]{4,3,2,1,0:T(8,128)(2,1)S(1)} %collective-permute-done.5.refs_8_) | copy-start | bytes 1572868
  57.6 10.5 %copy-start.10 = (bf16[2,2,2,256,128]{4,3,2,1,0:T(8,128)(2,1)}, bf16[2,2,2,256,128]{4,3,2,1,0:T(8,128)(2,1)S(1)}, u32[]{:S(2)}) copy-start(bf16[2,2,2,256,128]{4,3,2,1,0:T(8,128)(2,1)S(1)} %collective-permute-done.7.refs_8_) | copy-start | bytes 1572868
  57.6 35.3 %copy-start.1 = (bf16[2,2,2,256,128]{4,3,2,1,0:T(8,128)(2,1)}, bf16[2,2,2,256,128]{4,3,2,1,0:T(8,128)(2,1)S(1)}, u32[]{:S(2)}) copy-start(bf16[2,2,2,256,128]{4,3,2,1,0:T(8,128)(2,1)S(1)} %shard_map.49.refs_6_) | copy-start | bytes 1572868
  57.6 9.3 %collective-permute-start.6 = (bf16[2,2,2,256,128]{4,3,2,1,0:T(8,128)(2,1)S(1)}, bf16[2,2,2,256,128]{4,3,2,1,0:T(8,128)(2,1)S(1)}, u32[]{:S(2)}, u32[]{:S(2)}) collective-permute-start(bf16[2,2,2,256,128]{4,3,2,1,0:T(8,128)(2,1)S(1)} %shard_map.49.refs_6_), channel_id=1, source_target_pairs={{0,8},{2,10},{4,12},{6,14},{8,16},{10,18},{12,20},{14,22},{16,24},... | collective-permute-start | bytes 1572872 | tf_op jit(solution)/shard_map/far1/ppermute | solution.py:21
  66.1 0.8 copy-start.12
  67.0 25.9 %copy-start = (bf16[2,2,2,256,128]{4,3,2,1,0:T(8,128)(2,1)}, bf16[2,2,2,256,128]{4,3,2,1,0:T(8,128)(2,1)S(1)}, u32[]{:S(2)}) copy-start(bf16[2,2,2,256,128]{4,3,2,1,0:T(8,128)(2,1)S(1)} %shard_map.50.refs_7_) | copy-start | bytes 1572868
  68.0 24.9 %collective-permute-start.9 = (bf16[2,2,2,256,128]{4,3,2,1,0:T(8,128)(2,1)}, bf16[2,2,2,256,128]{4,3,2,1,0:T(8,128)(2,1)}, u32[]{:S(2)}, u32[]{:S(2)}) collective-permute-start(bf16[2,2,2,256,128]{4,3,2,1,0:T(8,128)(2,1)} %broadcast_select_fusion), channel_id=1, source_target_pairs={{0,4},{2,6},{4,0},{6,2},{8,12},{10,14},{12,8},{14,10},{16,20},{18,... | collective-permute-start | bytes 1572872 | tf_op jit(solution)/shard_map/extra1/ppermute | solution.py:21
  70.8 0.7 copy-start.9
  93.6 0.7 copy-start.5
  94.3 0.9 copy-start.2
  94.3 2.5 %copy-start.14 = (bf16[2,256,256]{2,1,0:T(8,128)(2,1)S(1)}, bf16[2,256,256]{2,1,0:T(8,128)(2,1)}, u32[]{:S(2)}) copy-start(bf16[2,256,256]{2,1,0:T(8,128)(2,1)} %get-tuple-element.14) | copy-start | bytes 786436
  94.3 27.0 %collective-permute-start.15 = (bf16[512,2048]{1,0:T(8,128)(2,1)S(1)}, bf16[512,2048]{1,0:T(8,128)(2,1)}, u32[]{:S(2)}, u32[]{:S(2)}) collective-permute-start(bf16[512,2048]{1,0:T(8,128)(2,1)S(1)} %shard_map.53.refs_9_.refs_5_), channel_id=1, source_target_pairs={{0,2},{2,0},{4,6},{6,4},{8,10},{10,8},{12,14},{14,12},{16,18},{18,... | collective-permute-start | bytes 6291464 | tf_op jit(solution)/shard_map/panel_pair/ppermute | solution.py:21
  95.2 25.0 %collective-permute-start.17 = (bf16[2,256,256]{2,1,0:T(8,128)(2,1)S(1)}, bf16[2,256,256]{2,1,0:T(8,128)(2,1)S(1)}, u32[]{:S(2)}, u32[]{:S(2)}) collective-permute-start(bf16[2,256,256]{2,1,0:T(8,128)(2,1)S(1)} %copy-done.2), channel_id=1, source_target_pairs={{0,1},{1,0},{2,3},{3,2},{4,5},{5,4},{6,7},{7,6},{8,9},{9,8},{10,11... | collective-permute-start | bytes 786440 | tf_op jit(solution)/shard_map/same0/ppermute | solution.py:27
  96.7 24.5 %copy-start.4 = (s32[3]{0:T(128)S(1)}, s32[3]{0:T(128)}, u32[]{:S(2)}) copy-start(s32[3]{0:T(128)} %pad_add_fusion.2.info.refs_0_) | copy-start | bytes 40
  96.7 24.0 %collective-permute-start.18 = (bf16[2,256,256]{2,1,0:T(8,128)(2,1)S(1)}, bf16[2,256,256]{2,1,0:T(8,128)(2,1)S(1)}, u32[]{:S(2)}, u32[]{:S(2)}) collective-permute-start(bf16[2,256,256]{2,1,0:T(8,128)(2,1)S(1)} %copy-done.14), channel_id=1, source_target_pairs={{0,3},{1,2},{2,1},{3,0},{4,7},{5,6},{6,5},{7,4},{8,11},{9,10},{10,... | collective-permute-start | bytes 786440 | tf_op jit(solution)/shard_map/cross0/ppermute | solution.py:27
  96.7 24.5 %collective-permute-start.16 = (bf16[2,256,256]{2,1,0:T(8,128)(2,1)S(1)}, bf16[2,256,256]{2,1,0:T(8,128)(2,1)S(1)}, u32[]{:S(2)}, u32[]{:S(2)}) collective-permute-start(bf16[2,256,256]{2,1,0:T(8,128)(2,1)S(1)} %copy-done.14), channel_id=1, source_target_pairs={{0,2},{2,0},{4,6},{6,4},{8,10},{10,8},{12,14},{14,12},{16,18},{18,... | collective-permute-start | bytes 786440 | tf_op jit(solution)/shard_map/pair0/ppermute | solution.py:21
  119.0 9.1 %collective-permute-start.13 = (bf16[2,256,256]{2,1,0:T(8,128)(2,1)}, bf16[2,256,256]{2,1,0:T(8,128)(2,1)S(1)}, u32[]{:S(2)}, u32[]{:S(2)}) collective-permute-start(bf16[2,256,256]{2,1,0:T(8,128)(2,1)} %get-tuple-element.11), channel_id=1, source_target_pairs={{0,3},{1,2},{2,1},{3,0},{4,7},{5,6},{6,5},{7,4},{8,11},{9,10},{10,... | collective-permute-start | bytes 786440 | tf_op jit(solution)/shard_map/cross1/ppermute | solution.py:27
  120.2 7.9 %collective-permute-start.11 = (bf16[2,256,256]{2,1,0:T(8,128)(2,1)}, bf16[2,256,256]{2,1,0:T(8,128)(2,1)S(1)}, u32[]{:S(2)}, u32[]{:S(2)}) collective-permute-start(bf16[2,256,256]{2,1,0:T(8,128)(2,1)} %get-tuple-element.11), channel_id=1, source_target_pairs={{0,2},{2,0},{4,6},{6,4},{8,10},{10,8},{12,14},{14,12},{16,18},{18,... | collective-permute-start | bytes 786440 | tf_op jit(solution)/shard_map/pair1/ppermute | solution.py:21
  120.7 12.8 %collective-permute-start.12 = (bf16[2,256,256]{2,1,0:T(8,128)(2,1)}, bf16[2,256,256]{2,1,0:T(8,128)(2,1)S(1)}, u32[]{:S(2)}, u32[]{:S(2)}) collective-permute-start(bf16[2,256,256]{2,1,0:T(8,128)(2,1)} %get-tuple-element.12.refs_2_), channel_id=1, source_target_pairs={{0,1},{1,0},{2,3},{3,2},{4,5},{5,4},{6,7},{7,6},{8,9},{9,8},{10,11... | collective-permute-start | bytes 786440 | tf_op jit(solution)/shard_map/same1/ppermute | solution.py:27
  121.2 1.0 copy-start.3

commit v11 on v9

--- a/solution.py
+++ b/solution.py
@@ -13,6 +13,7 @@
 MASKED = -1e30
 SCALE = 1.0 / math.sqrt(HD)
 VMEM = 60 * 1024 * 1024
+GRID = 1.5 * 2.0 ** 21
 
 
 def moved(array, n, go, name):
@@ -108,6 +109,14 @@
     )(info, *sources)
 
 
+def exponentials(x):
+    high = (x + GRID) - GRID
+    low = ((x - high) * math.log(2.0)).astype(jnp.bfloat16)
+    low = low + low * low * jnp.bfloat16(0.5)
+    expo = jnp.exp2(high.astype(jnp.bfloat16))
+    return expo + expo * low
+
+
 def attend_kernel(tokens, info, *refs):
     core, side = info[0], info[1]
     views, (own, one, two, swap, extra), refs = refs[:4], refs[4:9], refs[-7:]
@@ -183,7 +192,7 @@
         upcoming = scores_of(*steps[at + 1]) if at + 1 < len(steps) else None
         if last is not None:
             add(*last)
-        last = (*step, jnp.exp(scores * SCALE).astype(jnp.bfloat16))
+        last = (*step, exponentials(scores * (SCALE * math.log2(math.e))))
         scores = upcoming
     add(*last)
     low_sum = None

time: 139 us -> 141 us (1.014)
  Pallas kernels: 61.9 us -> 63.4 us
    pallas_call x2, Pallas kernels: 41.4 us -> 43 us  [attend(): pl.pallas_call(lambda *refs: attend_kernel(tokens, *refs), grid_spec=pltp...]
where the time goes in v11:
time: 141 us; the launch traced here: 140 us
  Pallas kernels  63.4 us (45%)
  waiting for transfers between devices  36 us (26%)
  starting transfers between devices  27.6 us (20%)
  local copies, waits for them, and re-layouts  8.73 us (6%)
  other arithmetic  4.04 us (3%)
    pallas_call x2, Pallas kernels, attend(): pl.pallas_call(lambda *refs: attend_kernel(tokens, *refs), grid_spec=pltp...  43 us
    ppermute x14, waiting for transfers between devices, moved(): return lax.ppermute(array, 'ctx', pairs)  30.6 us
    ppermute x14, starting transfers between devices, moved(): return lax.ppermute(array, 'ctx', pairs)  22.4 us
    pallas_call x2, Pallas kernels, project(): pl.pallas_call(lambda *refs: project_kernel(len(flat), len(used), before...  11.4 us
    pallas_call x3, Pallas kernels, copies(): pl.pallas_call(kernel, grid_spec=pltpu.PrefetchScalarGridSpec(num_scalar_...  9.08 us
    ppermute x5, waiting for transfers between devices, moved_both(): return lax.ppermute(array, ('ctx', 'fsdp'), pairs)  5.43 us
    ppermute x5, starting transfers between devices, moved_both(): return lax.ppermute(array, ('ctx', 'fsdp'), pairs)  5.2 us
    unnamed x23, local copies, waits for them, and re-layouts  4.06 us
  transfers between devices with their start and end apart: 19, of which 7 were waited for; matrix products, arithmetic and copies ran while one was open for 6% of the time, Pallas kernels for 41%

profile of v11, /device:TPU:0, one launch (start us, length us, event | category | flops | bytes accessed | tf_op | source)
XLA Modules:
  0.0 140.0 jit_solution(2769818234281834666)
XLA Ops:
  0.0 0.5 collective-permute-start.1
  0.5 0.5 collective-permute-start
  1.0 0.6 pad_add_fusion.2.info.refs_0_
  1.6 3.5 %shard_map.46.refs_2_ = bf16[512,2048]{1,0:T(8,128)(2,1)} custom-call(s32[3]{0:T(128)} %pad_add_fusion.2.info.refs_0_, bf16[1024,4096]{1,0:T(8,128)(2,1)} %refs_4_.1), custom_call_target="tpu_custom_call" | custom-call | bytes 1048576 | tf_op jit(solution)/shard_map/pallas_call | solution.py:93
  5.1 2.6 %collective-permute-start.14 = (bf16[512,2048]{1,0:T(8,128)(2,1)}, bf16[512,2048]{1,0:T(8,128)(2,1)S(1)}, u32[]{:S(2)}, u32[]{:S(2)}) collective-permute-start(bf16[512,2048]{1,0:T(8,128)(2,1)} %shard_map.46.refs_2_), channel_id=1, source_target_pairs={{0,1},{1,0},{2,3},{3,2},{4,5},{5,4},{6,7},{7,6},{8,9},{9,8},{10,11... | collective-permute-start | bytes 6291464 | tf_op jit(solution)/shard_map/panel/ppermute | solution.py:28
  7.7 2.7 %shard_map.47.refs_2_.refs_5_ = bf16[2,2,2,256,128]{4,3,2,1,0:T(8,128)(2,1)} custom-call(s32[3]{0:T(128)} %pad_add_fusion.2.info.refs_0_, bf16[2,2,256,1024]{3,2,1,0:T(8,128)(2,1)} %refs_2_.3, bf16[2,2,256,1024]{3,2,1,0:T(8,128)(2,1)} %collective-permute-done.1.refs_1_.refs_4_, bf16[512,2048]{1,0:T(8,128)(2,1)} %shard_map.46.refs_2_), custom_call_target="tpu_custom_call" | custom-call | bytes 262144 | tf_op jit(solution)/shard_map/pallas_call | solution.py:93
  10.5 4.3 %collective-permute-start.3 = (bf16[2,2,2,256,128]{4,3,2,1,0:T(8,128)(2,1)}, bf16[2,2,2,256,128]{4,3,2,1,0:T(8,128)(2,1)}, u32[]{:S(2)}, u32[]{:S(2)}) collective-permute-start(bf16[2,2,2,256,128]{4,3,2,1,0:T(8,128)(2,1)} %shard_map.47.refs_2_.refs_5_), channel_id=1, source_target_pairs={{0,8},{2,10},{4,12},{6,14},{8,16},{10,18},{12,20},{14,22},{16,24},... | collective-permute-start | bytes 1572872 | tf_op jit(solution)/shard_map/near0/ppermute | solution.py:22
  14.9 2.9 %shard_map.48.refs_5_ = bf16[2,2,2,256,128]{4,3,2,1,0:T(8,128)(2,1)} custom-call(s32[3]{0:T(128)} %pad_add_fusion.2.info.refs_0_, bf16[2,2,256,1024]{3,2,1,0:T(8,128)(2,1)} %refs_2_.3, bf16[2,2,256,1024]{3,2,1,0:T(8,128)(2,1)} %collective-permute-done.1.refs_1_.refs_4_, bf16[2,2,2,256,128]{4,3,2,1,0:T(8,128)(2,1)} %shard_map.47.refs_2_.refs_5_), custom_call_target="tpu_custom_call" | custom-call | bytes 262144 | tf_op jit(solution)/shard_map/pallas_call | solution.py:93
  17.8 2.7 %collective-permute-start.2 = (bf16[2,2,2,256,128]{4,3,2,1,0:T(8,128)(2,1)}, bf16[2,2,2,256,128]{4,3,2,1,0:T(8,128)(2,1)S(1)}, u32[]{:S(2)}, u32[]{:S(2)}) collective-permute-start(bf16[2,2,2,256,128]{4,3,2,1,0:T(8,128)(2,1)} %shard_map.48.refs_5_), channel_id=1, source_target_pairs={{0,8},{2,10},{4,12},{6,14},{8,16},{10,18},{12,20},{14,22},{16,24},... | collective-permute-start | bytes 1572872 | tf_op jit(solution)/shard_map/near1/ppermute | solution.py:22
  20.6 6.0 %collective-permute-done.3.refs_6_ = bf16[2,2,2,256,128]{4,3,2,1,0:T(8,128)(2,1)} collective-permute-done((bf16[2,2,2,256,128]{4,3,2,1,0:T(8,128)(2,1)}, bf16[2,2,2,256,128]{4,3,2,1,0:T(8,128)(2,1)}, u32[]{:S(2)}, u32[]{:S(2)}) %collective-permute-start.3) | collective-permute-done | bytes 524320 | tf_op jit(solution)/shard_map/near0/ppermute | solution.py:22
  26.5 5.2 %collective-permute-start.4 = (bf16[2,2,2,256,128]{4,3,2,1,0:T(8,128)(2,1)}, bf16[2,2,2,256,128]{4,3,2,1,0:T(8,128)(2,1)}, u32[]{:S(2)}, u32[]{:S(2)}) collective-permute-start(bf16[2,2,2,256,128]{4,3,2,1,0:T(8,128)(2,1)} %collective-permute-done.3.refs_6_), channel_id=1, source_target_pairs={{0,8},{2,10},{4,12},{6,14},{8,16},{10,18},{12,20},{14,22},{16,24},... | collective-permute-start | bytes 1572872 | tf_op jit(solution)/shard_map/far0/ppermute | solution.py:22
  32.0 1.6 %collective-permute-start.5 = (bf16[2,2,2,256,128]{4,3,2,1,0:T(8,128)(2,1)}, bf16[2,2,2,256,128]{4,3,2,1,0:T(8,128)(2,1)}, u32[]{:S(2)}, u32[]{:S(2)}) collective-permute-start(bf16[2,2,2,256,128]{4,3,2,1,0:T(8,128)(2,1)} %collective-permute-done.3.refs_6_), channel_id=1, source_target_pairs={{0,4},{2,6},{4,0},{6,2},{8,12},{10,14},{12,8},{14,10},{16,20},{18,... | collective-permute-start | bytes 1572872 | tf_op jit(solution)/shard_map/nearx0/ppermute | solution.py:22
  33.7 4.1 %collective-permute-done.2.refs_0_ = bf16[2,2,2,256,128]{4,3,2,1,0:T(8,128)(2,1)S(1)} collective-permute-done((bf16[2,2,2,256,128]{4,3,2,1,0:T(8,128)(2,1)}, bf16[2,2,2,256,128]{4,3,2,1,0:T(8,128)(2,1)S(1)}, u32[]{:S(2)}, u32[]{:S(2)}) %collective-permute-start.2) | collective-permute-done | bytes 524320 | tf_op jit(solution)/shard_map/near1/ppermute | solution.py:22
  37.8 1.5 %collective-permute-start.7 = (bf16[2,2,2,256,128]{4,3,2,1,0:T(8,128)(2,1)S(1)}, bf16[2,2,2,256,128]{4,3,2,1,0:T(8,128)(2,1)S(1)}, u32[]{:S(2)}, u32[]{:S(2)}) collective-permute-start(bf16[2,2,2,256,128]{4,3,2,1,0:T(8,128)(2,1)S(1)} %collective-permute-done.2.refs_0_), channel_id=1, source_target_pairs={{0,4},{2,6},{4,0},{6,2},{8,12},{10,14},{12,8},{14,10},{16,20},{18,... | collective-permute-start | bytes 1572872 | tf_op jit(solution)/shard_map/nearx1/ppermute | solution.py:22
  39.3 9.0 %collective-permute-done.4.refs_7_ = bf16[2,2,2,256,128]{4,3,2,1,0:T(8,128)(2,1)} collective-permute-done((bf16[2,2,2,256,128]{4,3,2,1,0:T(8,128)(2,1)}, bf16[2,2,2,256,128]{4,3,2,1,0:T(8,128)(2,1)}, u32[]{:S(2)}, u32[]{:S(2)}) %collective-permute-start.4) | collective-permute-done | bytes 524320 | tf_op jit(solution)/shard_map/far0/ppermute | solution.py:22
  48.3 0.9 broadcast_select_fusion.1
  49.2 2.5 %collective-permute-start.8 = (bf16[2,2,2,256,128]{4,3,2,1,0:T(8,128)(2,1)}, bf16[2,2,2,256,128]{4,3,2,1,0:T(8,128)(2,1)}, u32[]{:S(2)}, u32[]{:S(2)}) collective-permute-start(bf16[2,2,2,256,128]{4,3,2,1,0:T(8,128)(2,1)} %broadcast_select_fusion.1), channel_id=1, source_target_pairs={{0,4},{2,6},{4,0},{6,2},{8,12},{10,14},{12,8},{14,10},{16,20},{18,... | collective-permute-start | bytes 1572872 | tf_op jit(solution)/shard_map/extra0/ppermute | solution.py:22
  51.7 0.7 slice_bitcast_fusion.4.refs_1_
  52.4 0.7 slice_bitcast_fusion.3.refs_2_
  53.0 5.3 %collective-permute-done.7.refs_8_ = bf16[2,2,2,256,128]{4,3,2,1,0:T(8,128)(2,1)S(1)} collective-permute-done((bf16[2,2,2,256,128]{4,3,2,1,0:T(8,128)(2,1)S(1)}, bf16[2,2,2,256,128]{4,3,2,1,0:T(8,128)(2,1)S(1)}, u32[]{:S(2)}, u32[]{:S(2)}) %collective-permute-start.7) | collective-permute-done | bytes 524320 | tf_op jit(solution)/shard_map/nearx1/ppermute | solution.py:22
  58.4 0.8 copy-done.8
  59.2 1.9 %collective-permute-start.6 = (bf16[2,2,2,256,128]{4,3,2,1,0:T(8,128)(2,1)S(1)}, bf16[2,2,2,256,128]{4,3,2,1,0:T(8,128)(2,1)S(1)}, u32[]{:S(2)}, u32[]{:S(2)}) collective-permute-start(bf16[2,2,2,256,128]{4,3,2,1,0:T(8,128)(2,1)S(1)} %shard_map.49.refs_6_), channel_id=1, source_target_pairs={{0,8},{2,10},{4,12},{6,14},{8,16},{10,18},{12,20},{14,22},{16,24},... | collective-permute-start | bytes 1572872 | tf_op jit(solution)/shard_map/far1/ppermute | solution.py:22
  61.1 0.2 copy.16
  61.3 0.7 slice_bitcast_fusion.2.refs_1_
  61.9 5.2 %collective-permute-done.8.refs_9_ = bf16[2,2,2,256,128]{4,3,2,1,0:T(8,128)(2,1)} collective-permute-done((bf16[2,2,2,256,128]{4,3,2,1,0:T(8,128)(2,1)}, bf16[2,2,2,256,128]{4,3,2,1,0:T(8,128)(2,1)}, u32[]{:S(2)}, u32[]{:S(2)}) %collective-permute-start.8) | collective-permute-done | bytes 524320 | tf_op jit(solution)/shard_map/extra0/ppermute | solution.py:22
  67.1 0.7 slice_bitcast_fusion.1.refs_2_
  67.8 0.9 collective-permute-done.6.refs_0_
  68.7 2.2 %broadcast_select_fusion = bf16[2,2,2,256,128]{4,3,2,1,0:T(8,128)(2,1)} fusion(bf16[2,2,2,256,128]{4,3,2,1,0:T(8,128)(2,1)} %shard_map.48.refs_5_, bf16[2,2,2,256,128]{4,3,2,1,0:T(8,128)(2,1)S(1)} %shard_map.50.refs_7_, pred[]{:T(512)S(6)} %eq.45), kind=kLoop, calls=%fused_computation | loop fusion | flops 262144 | bytes 1572865 | tf_op jit(solution)/shard_map/jit(_where)/select_n | solution.py:395
  71.1 0.2 broadcast_in_dim.17
  71.3 0.2 stack_reshape.7
  71.5 0.2 broadcast_in_dim.16
  71.7 0.2 stack_reshape.6
  71.9 0.6 copy-done.7
  72.6 21.4 %shard_map.51 = (bf16[2,256,256]{2,1,0:T(8,128)(2,1)}, bf16[2,256,256]{2,1,0:T(8,128)(2,1)}, f32[8,128]{1,0:T(8,128)}) custom-call(s32[3]{0:T(128)} %pad_add_fusion.2.info.refs_0_, bf16[2,256,1024]{2,1,0:T(8,128)(2,1)} %refs_1_.3, bf16[2,2,256,1024]{3,2,1,0:T(8,128)(2,1)} %refs_2_.3, bf16[2,256,1024]{2,1,0:T(8,128)(2,1)} %collective-permute-done.refs_3_, ...), custom_call_target="tpu_custom_call" | custom-call | flops 41943040 | bytes 131072 | tf_op jit(solution)/shard_map/pallas_call | solution.py:233
  94.0 0.7 slice_bitcast_fusion.refs_1_
  94.6 0.7 copy-done.5
  95.3 0.9 copy-done.2
  96.3 0.5 collective-permute-start.17
  96.8 0.4 collective-permute-start.18
  97.2 1.2 collective-permute-start.16
  98.4 21.6 %shard_map.52 = (bf16[2,256,256]{2,1,0:T(8,128)(2,1)}, bf16[2,256,256]{2,1,0:T(8,128)(2,1)}, f32[8,128]{1,0:T(8,128)}) custom-call(s32[3]{0:T(128)} %pad_add_fusion.2.info.refs_0_, bf16[2,256,1024]{2,1,0:T(8,128)(2,1)} %refs_1_.3, bf16[2,2,256,1024]{3,2,1,0:T(8,128)(2,1)} %refs_2_.3, bf16[2,256,1024]{2,1,0:T(8,128)(2,1)} %collective-permute-done.refs_3_, ...), custom_call_target="tpu_custom_call" | custom-call | flops 41943040 | bytes 131072 | tf_op jit(solution)/shard_map/pallas_call | solution.py:233
  120.0 0.2 collective-permute-start.13
  120.2 0.5 collective-permute-start.11
  120.7 1.5 %collective-permute-start.12 = (bf16[2,256,256]{2,1,0:T(8,128)(2,1)}, bf16[2,256,256]{2,1,0:T(8,128)(2,1)S(1)}, u32[]{:S(2)}, u32[]{:S(2)}) collective-permute-start(bf16[2,256,256]{2,1,0:T(8,128)(2,1)} %get-tuple-element.12.refs_2_), channel_id=1, source_target_pairs={{0,1},{1,0},{2,3},{3,2},{4,5},{5,4},{6,7},{7,6},{8,9},{9,8},{10,11... | collective-permute-start | bytes 786440 | tf_op jit(solution)/shard_map/same1/ppermute | solution.py:28
  122.2 1.0 copy-done.3
  123.2 5.9 %shard_map.54.refs_7_ = f32[2,256,2048]{2,1,0:T(8,128)S(1)} custom-call(s32[3]{0:T(128)S(1)} %copy-done.4, bf16[2,256,256]{2,1,0:T(8,128)(2,1)S(1)} %copy-done.2, bf16[2,256,256]{2,1,0:T(8,128)(2,1)S(1)} %copy-done.3, bf16[2,256,256]{2,1,0:T(8,128)(2,1)S(1)} %collective-permute-done.16.refs_3_, bf16[2,256,256]{2,1,0:T(8,128)(2,1)S(1)} %collective-permute-done.17.refs_4_, ...), custom_call_target="tpu_custom_call" | custom-call | flops 335544320 | bytes 655360 | tf_op jit(solution)/shard_map/pallas_call | solution.py:296
  129.1 5.4 %collective-permute-done.12.refs_2_ = bf16[2,256,256]{2,1,0:T(8,128)(2,1)S(1)} collective-permute-done((bf16[2,256,256]{2,1,0:T(8,128)(2,1)}, bf16[2,256,256]{2,1,0:T(8,128)(2,1)S(1)}, u32[]{:S(2)}, u32[]{:S(2)}) %collective-permute-start.12) | collective-permute-done | bytes 262176 | tf_op jit(solution)/shard_map/same1/ppermute | solution.py:28
  134.5 5.5 %shard_map.55 = bf16[2,256,2048]{2,1,0:T(8,128)(2,1)} custom-call(s32[3]{0:T(128)S(1)} %copy-done.4, bf16[2,256,256]{2,1,0:T(8,128)(2,1)S(1)} %collective-permute-done.11.refs_1_, bf16[2,256,256]{2,1,0:T(8,128)(2,1)S(1)} %collective-permute-done.12.refs_2_, bf16[2,256,256]{2,1,0:T(8,128)(2,1)S(1)} %collective-permute-done.13.refs_3_, ...), custom_call_target="tpu_custom_call" | custom-call | flops 201326592 | bytes 393216 | tf_op jit(solution)/shard_map/pallas_call | solution.py:296
  (53 shorter events, 0.9 us)
Async XLA Ops:
  0.0 7.7 %collective-permute-start.1 = (bf16[2,2,256,1024]{3,2,1,0:T(8,128)(2,1)}, bf16[2,2,256,1024]{3,2,1,0:T(8,128)(2,1)}, u32[]{:S(2)}, u32[]{:S(2)}) collective-permute-start(bf16[2,2,256,1024]{3,2,1,0:T(8,128)(2,1)} %refs_2_.3), channel_id=1, source_target_pairs={{0,2},{2,0},{4,6},{6,4},{8,10},{10,8},{12,14},{14,12},{16,18},{18,... | collective-permute-start | bytes 6291464 | tf_op jit(solution)/shard_map/pair_kv/ppermute | solution.py:22
  0.5 14.3 %collective-permute-start.10 = (s32[4,32]{1,0:T(4,128)}, s32[4,32]{1,0:T(4,128)S(1)}, u32[]{:S(2)}, u32[]{:S(2)}) collective-permute-start(s32[4,32]{1,0:T(4,128)} %param.6), channel_id=1, source_target_pairs={{0,2},{2,0},{4,6},{6,4},{8,10},{10,8},{12,14},{14,12},{16,18},{18,... | collective-permute-start | bytes 1544 | tf_op jit(solution)/shard_map/pair_mask/ppermute | solution.py:22
  0.5 71.4 %collective-permute-start = (bf16[2,256,1024]{2,1,0:T(8,128)(2,1)}, bf16[2,256,1024]{2,1,0:T(8,128)(2,1)}, u32[]{:S(2)}, u32[]{:S(2)}) collective-permute-start(bf16[2,256,1024]{2,1,0:T(8,128)(2,1)} %refs_1_.3), channel_id=1, source_target_pairs={{0,2},{2,0},{4,6},{6,4},{8,10},{10,8},{12,14},{14,12},{16,18},{18,... | collective-permute-start | bytes 3145736 | tf_op jit(solution)/shard_map/pair_q/ppermute | solution.py:22
  1.6 6.1 %copy-start.9 = (s32[4,32]{1,0:T(4,128)S(1)}, s32[4,32]{1,0:T(4,128)}, u32[]{:S(2)}) copy-start(s32[4,32]{1,0:T(4,128)} %param.6) | copy-start | bytes 1540
  5.1 89.6 %collective-permute-start.14 = (bf16[512,2048]{1,0:T(8,128)(2,1)}, bf16[512,2048]{1,0:T(8,128)(2,1)S(1)}, u32[]{:S(2)}, u32[]{:S(2)}) collective-permute-start(bf16[512,2048]{1,0:T(8,128)(2,1)} %shard_map.46.refs_2_), channel_id=1, source_target_pairs={{0,1},{1,0},{2,3},{3,2},{4,5},{5,4},{6,7},{7,6},{8,9},{9,8},{10,11... | collective-permute-start | bytes 6291464 | tf_op jit(solution)/shard_map/panel/ppermute | solution.py:28
  10.5 16.1 %collective-permute-start.3 = (bf16[2,2,2,256,128]{4,3,2,1,0:T(8,128)(2,1)}, bf16[2,2,2,256,128]{4,3,2,1,0:T(8,128)(2,1)}, u32[]{:S(2)}, u32[]{:S(2)}) collective-permute-start(bf16[2,2,2,256,128]{4,3,2,1,0:T(8,128)(2,1)} %shard_map.47.refs_2_.refs_5_), channel_id=1, source_target_pairs={{0,8},{2,10},{4,12},{6,14},{8,16},{10,18},{12,20},{14,22},{16,24},... | collective-permute-start | bytes 1572872 | tf_op jit(solution)/shard_map/near0/ppermute | solution.py:22
  14.9 33.4 %copy-start.6 = (bf16[2,2,2,256,128]{4,3,2,1,0:T(8,128)(2,1)S(1)}, bf16[2,2,2,256,128]{4,3,2,1,0:T(8,128)(2,1)}, u32[]{:S(2)}) copy-start(bf16[2,2,2,256,128]{4,3,2,1,0:T(8,128)(2,1)} %shard_map.47.refs_2_.refs_5_) | copy-start | bytes 1572868
  17.8 20.0 %collective-permute-start.2 = (bf16[2,2,2,256,128]{4,3,2,1,0:T(8,128)(2,1)}, bf16[2,2,2,256,128]{4,3,2,1,0:T(8,128)(2,1)S(1)}, u32[]{:S(2)}, u32[]{:S(2)}) collective-permute-start(bf16[2,2,2,256,128]{4,3,2,1,0:T(8,128)(2,1)} %shard_map.48.refs_5_), channel_id=1, source_target_pairs={{0,8},{2,10},{4,12},{6,14},{8,16},{10,18},{12,20},{14,22},{16,24},... | collective-permute-start | bytes 1572872 | tf_op jit(solution)/shard_map/near1/ppermute | solution.py:22
  26.5 21.8 %collective-permute-start.4 = (bf16[2,2,2,256,128]{4,3,2,1,0:T(8,128)(2,1)}, bf16[2,2,2,256,128]{4,3,2,1,0:T(8,128)(2,1)}, u32[]{:S(2)}, u32[]{:S(2)}) collective-permute-start(bf16[2,2,2,256,128]{4,3,2,1,0:T(8,128)(2,1)} %collective-permute-done.3.refs_6_), channel_id=1, source_target_pairs={{0,8},{2,10},{4,12},{6,14},{8,16},{10,18},{12,20},{14,22},{16,24},... | collective-permute-start | bytes 1572872 | tf_op jit(solution)/shard_map/far0/ppermute | solution.py:22
  32.0 20.4 %collective-permute-start.5 = (bf16[2,2,2,256,128]{4,3,2,1,0:T(8,128)(2,1)}, bf16[2,2,2,256,128]{4,3,2,1,0:T(8,128)(2,1)}, u32[]{:S(2)}, u32[]{:S(2)}) collective-permute-start(bf16[2,2,2,256,128]{4,3,2,1,0:T(8,128)(2,1)} %collective-permute-done.3.refs_6_), channel_id=1, source_target_pairs={{0,4},{2,6},{4,0},{6,2},{8,12},{10,14},{12,8},{14,10},{16,20},{18,... | collective-permute-start | bytes 1572872 | tf_op jit(solution)/shard_map/nearx0/ppermute | solution.py:22
  37.8 20.6 %collective-permute-start.7 = (bf16[2,2,2,256,128]{4,3,2,1,0:T(8,128)(2,1)S(1)}, bf16[2,2,2,256,128]{4,3,2,1,0:T(8,128)(2,1)S(1)}, u32[]{:S(2)}, u32[]{:S(2)}) collective-permute-start(bf16[2,2,2,256,128]{4,3,2,1,0:T(8,128)(2,1)S(1)} %collective-permute-done.2.refs_0_), channel_id=1, source_target_pairs={{0,4},{2,6},{4,0},{6,2},{8,12},{10,14},{12,8},{14,10},{16,20},{18,... | collective-permute-start | bytes 1572872 | tf_op jit(solution)/shard_map/nearx1/ppermute | solution.py:22
  49.2 17.9 %collective-permute-start.8 = (bf16[2,2,2,256,128]{4,3,2,1,0:T(8,128)(2,1)}, bf16[2,2,2,256,128]{4,3,2,1,0:T(8,128)(2,1)}, u32[]{:S(2)}, u32[]{:S(2)}) collective-permute-start(bf16[2,2,2,256,128]{4,3,2,1,0:T(8,128)(2,1)} %broadcast_select_fusion.1), channel_id=1, source_target_pairs={{0,4},{2,6},{4,0},{6,2},{8,12},{10,14},{12,8},{14,10},{16,20},{18,... | collective-permute-start | bytes 1572872 | tf_op jit(solution)/shard_map/extra0/ppermute | solution.py:22
  58.4 0.8 copy-start.8
  59.2 34.8 %copy-start.1 = (bf16[2,2,2,256,128]{4,3,2,1,0:T(8,128)(2,1)}, bf16[2,2,2,256,128]{4,3,2,1,0:T(8,128)(2,1)S(1)}, u32[]{:S(2)}) copy-start(bf16[2,2,2,256,128]{4,3,2,1,0:T(8,128)(2,1)S(1)} %shard_map.49.refs_6_) | copy-start | bytes 1572868
  59.2 9.5 %collective-permute-start.6 = (bf16[2,2,2,256,128]{4,3,2,1,0:T(8,128)(2,1)S(1)}, bf16[2,2,2,256,128]{4,3,2,1,0:T(8,128)(2,1)S(1)}, u32[]{:S(2)}, u32[]{:S(2)}) collective-permute-start(bf16[2,2,2,256,128]{4,3,2,1,0:T(8,128)(2,1)S(1)} %shard_map.49.refs_6_), channel_id=1, source_target_pairs={{0,8},{2,10},{4,12},{6,14},{8,16},{10,18},{12,20},{14,22},{16,24},... | collective-permute-start | bytes 1572872 | tf_op jit(solution)/shard_map/far1/ppermute | solution.py:22
  68.7 25.2 %copy-start = (bf16[2,2,2,256,128]{4,3,2,1,0:T(8,128)(2,1)}, bf16[2,2,2,256,128]{4,3,2,1,0:T(8,128)(2,1)S(1)}, u32[]{:S(2)}) copy-start(bf16[2,2,2,256,128]{4,3,2,1,0:T(8,128)(2,1)S(1)} %shard_map.50.refs_7_) | copy-start | bytes 1572868
  70.9 23.1 %collective-permute-start.9 = (bf16[2,2,2,256,128]{4,3,2,1,0:T(8,128)(2,1)}, bf16[2,2,2,256,128]{4,3,2,1,0:T(8,128)(2,1)}, u32[]{:S(2)}, u32[]{:S(2)}) collective-permute-start(bf16[2,2,2,256,128]{4,3,2,1,0:T(8,128)(2,1)} %broadcast_select_fusion), channel_id=1, source_target_pairs={{0,4},{2,6},{4,0},{6,2},{8,12},{10,14},{12,8},{14,10},{16,20},{18,... | collective-permute-start | bytes 1572872 | tf_op jit(solution)/shard_map/extra1/ppermute | solution.py:22
  71.9 0.7 copy-start.7
  94.6 0.7 copy-start.5
  95.3 0.9 copy-start.2
  95.3 1.5 %copy-start.10 = (bf16[2,256,256]{2,1,0:T(8,128)(2,1)S(1)}, bf16[2,256,256]{2,1,0:T(8,128)(2,1)}, u32[]{:S(2)}) copy-start(bf16[2,256,256]{2,1,0:T(8,128)(2,1)} %get-tuple-element.14) | copy-start | bytes 786436
  95.3 26.9 %collective-permute-start.15 = (bf16[512,2048]{1,0:T(8,128)(2,1)S(1)}, bf16[512,2048]{1,0:T(8,128)(2,1)}, u32[]{:S(2)}, u32[]{:S(2)}) collective-permute-start(bf16[512,2048]{1,0:T(8,128)(2,1)S(1)} %shard_map.53.refs_9_.refs_5_), channel_id=1, source_target_pairs={{0,2},{2,0},{4,6},{6,4},{8,10},{10,8},{12,14},{14,12},{16,18},{18,... | collective-permute-start | bytes 6291464 | tf_op jit(solution)/shard_map/panel_pair/ppermute | solution.py:22
  96.3 23.9 %collective-permute-start.17 = (bf16[2,256,256]{2,1,0:T(8,128)(2,1)S(1)}, bf16[2,256,256]{2,1,0:T(8,128)(2,1)S(1)}, u32[]{:S(2)}, u32[]{:S(2)}) collective-permute-start(bf16[2,256,256]{2,1,0:T(8,128)(2,1)S(1)} %copy-done.2), channel_id=1, source_target_pairs={{0,1},{1,0},{2,3},{3,2},{4,5},{5,4},{6,7},{7,6},{8,9},{9,8},{10,11... | collective-permute-start | bytes 786440 | tf_op jit(solution)/shard_map/same0/ppermute | solution.py:28
  96.8 25.5 %copy-start.4 = (s32[3]{0:T(128)S(1)}, s32[3]{0:T(128)}, u32[]{:S(2)}) copy-start(s32[3]{0:T(128)} %pad_add_fusion.2.info.refs_0_) | copy-start | bytes 40
  96.8 23.9 %collective-permute-start.18 = (bf16[2,256,256]{2,1,0:T(8,128)(2,1)S(1)}, bf16[2,256,256]{2,1,0:T(8,128)(2,1)S(1)}, u32[]{:S(2)}, u32[]{:S(2)}) collective-permute-start(bf16[2,256,256]{2,1,0:T(8,128)(2,1)S(1)} %copy-done.10), channel_id=1, source_target_pairs={{0,3},{1,2},{2,1},{3,0},{4,7},{5,6},{6,5},{7,4},{8,11},{9,10},{10,... | collective-permute-start | bytes 786440 | tf_op jit(solution)/shard_map/cross0/ppermute | solution.py:28
  97.2 25.0 %collective-permute-start.16 = (bf16[2,256,256]{2,1,0:T(8,128)(2,1)S(1)}, bf16[2,256,256]{2,1,0:T(8,128)(2,1)S(1)}, u32[]{:S(2)}, u32[]{:S(2)}) collective-permute-start(bf16[2,256,256]{2,1,0:T(8,128)(2,1)S(1)} %copy-done.10), channel_id=1, source_target_pairs={{0,2},{2,0},{4,6},{6,4},{8,10},{10,8},{12,14},{14,12},{16,18},{18,... | collective-permute-start | bytes 786440 | tf_op jit(solution)/shard_map/pair0/ppermute | solution.py:22
  120.0 9.1 %collective-permute-start.13 = (bf16[2,256,256]{2,1,0:T(8,128)(2,1)}, bf16[2,256,256]{2,1,0:T(8,128)(2,1)S(1)}, u32[]{:S(2)}, u32[]{:S(2)}) collective-permute-start(bf16[2,256,256]{2,1,0:T(8,128)(2,1)} %get-tuple-element.11), channel_id=1, source_target_pairs={{0,3},{1,2},{2,1},{3,0},{4,7},{5,6},{6,5},{7,4},{8,11},{9,10},{10,... | collective-permute-start | bytes 786440 | tf_op jit(solution)/shard_map/cross1/ppermute | solution.py:28
  120.2 8.9 %collective-permute-start.11 = (bf16[2,256,256]{2,1,0:T(8,128)(2,1)}, bf16[2,256,256]{2,1,0:T(8,128)(2,1)S(1)}, u32[]{:S(2)}, u32[]{:S(2)}) collective-permute-start(bf16[2,256,256]{2,1,0:T(8,128)(2,1)} %get-tuple-element.11), channel_id=1, source_target_pairs={{0,2},{2,0},{4,6},{6,4},{8,10},{10,8},{12,14},{14,12},{16,18},{18,... | collective-permute-start | bytes 786440 | tf_op jit(solution)/shard_map/pair1/ppermute | solution.py:22
  120.7 13.8 %collective-permute-start.12 = (bf16[2,256,256]{2,1,0:T(8,128)(2,1)}, bf16[2,256,256]{2,1,0:T(8,128)(2,1)S(1)}, u32[]{:S(2)}, u32[]{:S(2)}) collective-permute-start(bf16[2,256,256]{2,1,0:T(8,128)(2,1)} %get-tuple-element.12.refs_2_), channel_id=1, source_target_pairs={{0,1},{1,0},{2,3},{3,2},{4,5},{5,4},{6,7},{7,6},{8,9},{9,8},{10,11... | collective-permute-start | bytes 786440 | tf_op jit(solution)/shard_map/same1/ppermute | solution.py:28
  122.2 1.0 copy-start.3

commit v12 on v10

--- a/solution.py
+++ b/solution.py
@@ -63,7 +63,7 @@
     return jnp.repeat(table.reshape(-1, rows, 2 * rows).transpose(0, 2, 1), BLK, axis=2)
 
 
-def copies(info, sources, outs, shapes, plan):
+def copies(info, sources, outs, shapes, plan, limit=8 * 1024 * 1024):
     total = sum(math.prod(o.shape) for o in outs)
 
     def kernel(info, *refs):
@@ -100,7 +100,7 @@
             ],
         ),
         out_shape=[jax.ShapeDtypeStruct(o.shape, o.dtype) for o in outs],
-        compiler_params=pltpu.CompilerParams(vmem_limit_bytes=VMEM),
+        compiler_params=pltpu.CompilerParams(vmem_limit_bytes=limit),
         cost_estimate=pl.CostEstimate(flops=0, bytes_accessed=total, transcendentals=0),
     )(info, *sources)
 
@@ -153,25 +153,36 @@
         queries.append(query)
         shifts.append((jnp.sqrt(size * longest) * SCALE)[:, 0:1])
 
-    steps = [(tile, k) for tile in range(2) for k in range(0, slots, 2)]
+    steps = [(tile, k) for tile in range(2) for k in (*range(0, slots - 1, 2), slots - 1)]
     totals, sums = [None, None], [None, None]
 
-    def scores_of(tile, k):
-        key = jnp.concatenate([operands(tile, j)[0] for j in range(k, min(k + 2, slots))], 1)
-        scores = jnp.dot(queries[tile], key, preferred_element_type=jnp.float32)
-        bias = jnp.concatenate([table[tile, j] for j in range(k, min(k + 2, slots))], 1)
-        return scores, bias
-
-    def weights_of(tile, scores, bias, shift):
-        wide = scores.shape[1]
-        shifted = scores * SCALE - shift
-        shifted = shifted.reshape(2 * rows, BLK, wide) + bias[:, None, :]
-        return jnp.exp(shifted.reshape(2 * tokens, wide))
+    def runs_of(k):
+        return range(k, k + 1 if k == slots - 1 else min(k + 2, slots - 1))
+
+    def scores_of(tile, k, everyone=False):
+        key = jnp.concatenate([operands(tile, j)[0] for j in runs_of(k)], 1)
+        bias = jnp.concatenate([table[tile, j] for j in runs_of(k)], 1)
+        query = queries[tile]
+        if k == slots - 1 and not everyone:
+            query, bias = query[tokens:], bias[rows:]
+        return jnp.dot(query, key, preferred_element_type=jnp.float32), bias
+
+    def weights_of(scores, bias, shift):
+        count, wide = scores.shape
+        shifted = scores * SCALE - shift[2 * tokens - count:]
+        shifted = shifted.reshape(count // BLK, BLK, wide) + bias[:, None, :]
+        return jnp.exp(shifted.reshape(count, wide))
+
+    def plus(total, part):
+        if total is None or total.shape == part.shape:
+            return part if total is None else total + part
+        half = part.shape[0]
+        return jnp.concatenate([total[:-half], total[-half:] + part], 0)
 
     def add(tile, k, expo):
-        value = jnp.concatenate([operands(tile, j)[1] for j in range(k, min(k + 2, slots))], 0)
-        part = jnp.dot(expo, value, preferred_element_type=jnp.float32)
-        totals[tile] = part if totals[tile] is None else totals[tile] + part
+        value = jnp.concatenate([operands(tile, j)[1] for j in runs_of(k)], 0)
+        totals[tile] = plus(
+            totals[tile], jnp.dot(expo, value, preferred_element_type=jnp.float32))
 
     scores, last = scores_of(*steps[0]), None
     for at, step in enumerate(steps):
@@ -179,10 +190,9 @@
         if last is not None:
             add(*last)
         tile = step[0]
-        expo = weights_of(tile, *scores, shifts[tile])
+        expo = weights_of(*scores, shifts[tile])
         for lanes in range(0, expo.shape[1], HD):
-            part = expo[:, lanes:lanes + HD]
-            sums[tile] = part if sums[tile] is None else sums[tile] + part
+            sums[tile] = plus(sums[tile], expo[:, lanes:lanes + HD])
         last = (*step, expo.astype(jnp.bfloat16))
         scores = upcoming
     add(*last)
@@ -197,7 +207,7 @@
     @pl.when(jnp.logical_not(jnp.min(least[...]) > 2.0 ** -40))
     def _():
         for tile in range(2):
-            runs = [scores_of(tile, k) for k in range(0, slots, 2)]
+            runs = [scores_of(tile, k, True) for t, k in steps if t == tile]
             scores = jnp.concatenate([score for score, _ in runs], 1) * SCALE
             bias = jnp.concatenate([bias for _, bias in runs], 1)
             wide = scores.shape[1]
@@ -336,7 +346,7 @@
     cuts = 4 if f == 2 else 1
     panels = copies(
         info, [out_weight], [jax.ShapeDtypeStruct((width, features), bf16)] * (f - 1),
-        [(width // cuts, features)] * (cuts * (f - 1)), cut_panels,
+        [(width // cuts, features)] * (cuts * (f - 1)), cut_panels, VMEM,
     )
 
     def join(core, ins, outs):
@@ -412,12 +422,17 @@
         others += [same, moved(same, n, pair, "panel_pair")]
 
     weights = [out_weight, out_weight] + others
-    early, late = [], []
+    stages = [[], [], []]
     for g in range(2 * f):
         for k, (part, act) in enumerate(zip(parts, acts[g])):
-            (late if g and k == len(parts) - 1 else early).append((g, part[0], act))
-    before = project(info, early, weights, features, jnp.float32)
-    return project(info, late, weights, features, jnp.bfloat16, before)
+            late = k == len(parts) - 1 and g > 0
+            stages[(1 if g % 2 else 2) if late else 0].append((g, part[0], act))
+    total = None
+    stages = [stage for stage in stages if stage]
+    for k, stage in enumerate(stages):
+        dtype = jnp.bfloat16 if k == len(stages) - 1 else jnp.float32
+        total = project(info, stage, weights, features, dtype, total)
+    return total
 
 
 def solution(mesh):

time: 140 us -> 138 us (0.986)
  Pallas kernels: 63.4 us -> 66.4 us
  local copies, waits for them, and re-layouts: 7.1 us -> 4.99 us
  waiting for transfers between devices: 36 us -> 34.2 us
    ppermute x5, waiting for transfers between devices: 5.43 us -> 1.29 us  [moved_both(): return lax.ppermute(array, ('ctx', 'fsdp'), pairs)]
    pallas_call x2 -> x3, Pallas kernels: 11.4 us -> 14.6 us  [project(): pl.pallas_call(lambda *refs: project_kernel(len(flat), len(used), before...]
    ppermute x14, waiting for transfers between devices: 30.6 us -> 32.9 us  [moved(): return lax.ppermute(array, 'ctx', pairs)]
    pallas_call x3, Pallas kernels: 8.97 us -> 7.27 us  [copies(): pl.pallas_call(kernel, grid_spec=pltpu.PrefetchScalarGridSpec(num_scalar_...]
    unnamed x31 -> x35, local copies, waits for them, and re-layouts: 4.72 us -> 3.28 us
    pallas_call x2, Pallas kernels: 43.1 us -> 44.5 us  [attend(): pl.pallas_call(lambda *refs: attend_kernel(tokens, *refs), grid_spec=pltp...]
  transfers between devices with their start and end apart: 19 -> 19, of which waited for: 7 -> 7; matrix products, arithmetic and copies ran while one was open for 3% -> 3% of each run, Pallas kernels for 40% -> 44%
where the time goes in v12:
time: 138 us; the launch traced here: 137 us
  Pallas kernels  66.4 us (48%)
  waiting for transfers between devices  34.2 us (25%)
  starting transfers between devices  29.3 us (21%)
  local copies, waits for them, and re-layouts  4.99 us (4%)
  other arithmetic  2.02 us (1%)
    pallas_call x2, Pallas kernels, attend(): pl.pallas_call(lambda *refs: attend_kernel(tokens, *refs), grid_spec=pltp...  44.5 us
    ppermute x14, waiting for transfers between devices, moved(): return lax.ppermute(array, 'ctx', pairs)  32.9 us
    ppermute x14, starting transfers between devices, moved(): return lax.ppermute(array, 'ctx', pairs)  24.6 us
    pallas_call x3, Pallas kernels, project(): pl.pallas_call(lambda *refs: project_kernel(len(flat), len(used), before...  14.6 us
    pallas_call x3, Pallas kernels, copies(): pl.pallas_call(kernel, grid_spec=pltpu.PrefetchScalarGridSpec(num_scalar_...  7.27 us
    ppermute x5, starting transfers between devices, moved_both(): return lax.ppermute(array, ('ctx', 'fsdp'), pairs)  4.74 us
    unnamed x35, local copies, waits for them, and re-layouts  3.28 us
  transfers between devices with their start and end apart: 19, of which 7 were waited for; matrix products, arithmetic and copies ran while one was open for 3% of the time, Pallas kernels for 44%

profile of v12, /device:TPU:0, one launch (start us, length us, event | category | flops | bytes accessed | tf_op | source)
XLA Modules:
  0.0 137.2 jit_solution(16549255080426512452)
XLA Ops:
  0.0 0.5 collective-permute-start.1
  0.5 0.7 pad_add_fusion.2.info.refs_0_
  1.1 3.5 %shard_map.46.refs_2_ = bf16[512,2048]{1,0:T(8,128)(2,1)} custom-call(s32[3]{0:T(128)} %pad_add_fusion.2.info.refs_0_, bf16[1024,4096]{1,0:T(8,128)(2,1)} %refs_3_.1), custom_call_target="tpu_custom_call" | custom-call | bytes 1048576 | tf_op jit(solution)/shard_map/pallas_call | solution.py:89
  4.6 1.9 %shard_map.47.refs_2_.refs_5_ = bf16[2,2,2,256,128]{4,3,2,1,0:T(8,128)(2,1)S(1)} custom-call(s32[3]{0:T(128)S(1)} %copy-done.7, bf16[2,2,256,1024]{3,2,1,0:T(8,128)(2,1)S(1)} %copy-done, bf16[2,2,256,1024]{3,2,1,0:T(8,128)(2,1)} %collective-permute-done.1.refs_1_.refs_4_, bf16[512,2048]{1,0:T(8,128)(2,1)} %shard_map.46.refs_2_), custom_call_target="tpu_custom_call" | custom-call | bytes 262144 | tf_op jit(solution)/shard_map/pallas_call | solution.py:89
  6.6 5.7 %collective-permute-start.3 = (bf16[2,2,2,256,128]{4,3,2,1,0:T(8,128)(2,1)S(1)}, bf16[2,2,2,256,128]{4,3,2,1,0:T(8,128)(2,1)}, u32[]{:S(2)}, u32[]{:S(2)}) collective-permute-start(bf16[2,2,2,256,128]{4,3,2,1,0:T(8,128)(2,1)S(1)} %shard_map.47.refs_2_.refs_5_), channel_id=1, source_target_pairs={{0,8},{2,10},{4,12},{6,14},{8,16},{10,18},{12,20},{14,22},{16,24},... | collective-permute-start | bytes 1572872 | tf_op jit(solution)/shard_map/near0/ppermute | solution.py:21
  12.2 1.5 %collective-permute-start.12 = (bf16[512,2048]{1,0:T(8,128)(2,1)}, bf16[512,2048]{1,0:T(8,128)(2,1)}, u32[]{:S(2)}, u32[]{:S(2)}) collective-permute-start(bf16[512,2048]{1,0:T(8,128)(2,1)} %shard_map.46.refs_2_), channel_id=1, source_target_pairs={{0,1},{1,0},{2,3},{3,2},{4,5},{5,4},{6,7},{7,6},{8,9},{9,8},{10,11... | collective-permute-start | bytes 6291464 | tf_op jit(solution)/shard_map/panel/ppermute | solution.py:27
  13.7 0.5 collective-permute-start
  14.3 1.9 %shard_map.48.refs_5_ = bf16[2,2,2,256,128]{4,3,2,1,0:T(8,128)(2,1)S(1)} custom-call(s32[3]{0:T(128)S(1)} %copy-done.7, bf16[2,2,256,1024]{3,2,1,0:T(8,128)(2,1)S(1)} %copy-done, bf16[2,2,256,1024]{3,2,1,0:T(8,128)(2,1)} %collective-permute-done.1.refs_1_.refs_4_, bf16[2,2,2,256,128]{4,3,2,1,0:T(8,128)(2,1)S(1)} %shard_map.47.refs_2_.refs_5_), custom_call_target="tpu_custom_call" | custom-call | bytes 262144 | tf_op jit(solution)/shard_map/pallas_call | solution.py:89
  16.2 2.7 %collective-permute-start.2 = (bf16[2,2,2,256,128]{4,3,2,1,0:T(8,128)(2,1)S(1)}, bf16[2,2,2,256,128]{4,3,2,1,0:T(8,128)(2,1)S(1)}, u32[]{:S(2)}, u32[]{:S(2)}) collective-permute-start(bf16[2,2,2,256,128]{4,3,2,1,0:T(8,128)(2,1)S(1)} %shard_map.48.refs_5_), channel_id=1, source_target_pairs={{0,8},{2,10},{4,12},{6,14},{8,16},{10,18},{12,20},{14,22},{16,24},... | collective-permute-start | bytes 1572872 | tf_op jit(solution)/shard_map/near1/ppermute | solution.py:21
  18.9 4.7 %collective-permute-done.3.refs_6_ = bf16[2,2,2,256,128]{4,3,2,1,0:T(8,128)(2,1)} collective-permute-done((bf16[2,2,2,256,128]{4,3,2,1,0:T(8,128)(2,1)S(1)}, bf16[2,2,2,256,128]{4,3,2,1,0:T(8,128)(2,1)}, u32[]{:S(2)}, u32[]{:S(2)}) %collective-permute-start.3) | collective-permute-done | bytes 524320 | tf_op jit(solution)/shard_map/near0/ppermute | solution.py:21
  23.6 4.5 %collective-permute-start.4 = (bf16[2,2,2,256,128]{4,3,2,1,0:T(8,128)(2,1)}, bf16[2,2,2,256,128]{4,3,2,1,0:T(8,128)(2,1)S(1)}, u32[]{:S(2)}, u32[]{:S(2)}) collective-permute-start(bf16[2,2,2,256,128]{4,3,2,1,0:T(8,128)(2,1)} %collective-permute-done.3.refs_6_), channel_id=1, source_target_pairs={{0,8},{2,10},{4,12},{6,14},{8,16},{10,18},{12,20},{14,22},{16,24},... | collective-permute-start | bytes 1572872 | tf_op jit(solution)/shard_map/far0/ppermute | solution.py:21
  28.2 1.6 %collective-permute-start.5 = (bf16[2,2,2,256,128]{4,3,2,1,0:T(8,128)(2,1)}, bf16[2,2,2,256,128]{4,3,2,1,0:T(8,128)(2,1)S(1)}, u32[]{:S(2)}, u32[]{:S(2)}) collective-permute-start(bf16[2,2,2,256,128]{4,3,2,1,0:T(8,128)(2,1)} %collective-permute-done.3.refs_6_), channel_id=1, source_target_pairs={{0,4},{2,6},{4,0},{6,2},{8,12},{10,14},{12,8},{14,10},{16,20},{18,... | collective-permute-start | bytes 1572872 | tf_op jit(solution)/shard_map/nearx0/ppermute | solution.py:21
  29.8 5.1 %collective-permute-done.2.refs_0_ = bf16[2,2,2,256,128]{4,3,2,1,0:T(8,128)(2,1)S(1)} collective-permute-done((bf16[2,2,2,256,128]{4,3,2,1,0:T(8,128)(2,1)S(1)}, bf16[2,2,2,256,128]{4,3,2,1,0:T(8,128)(2,1)S(1)}, u32[]{:S(2)}, u32[]{:S(2)}) %collective-permute-start.2) | collective-permute-done | bytes 524320 | tf_op jit(solution)/shard_map/near1/ppermute | solution.py:21
  34.9 1.5 %collective-permute-start.7 = (bf16[2,2,2,256,128]{4,3,2,1,0:T(8,128)(2,1)S(1)}, bf16[2,2,2,256,128]{4,3,2,1,0:T(8,128)(2,1)S(1)}, u32[]{:S(2)}, u32[]{:S(2)}) collective-permute-start(bf16[2,2,2,256,128]{4,3,2,1,0:T(8,128)(2,1)S(1)} %collective-permute-done.2.refs_0_), channel_id=1, source_target_pairs={{0,4},{2,6},{4,0},{6,2},{8,12},{10,14},{12,8},{14,10},{16,20},{18,... | collective-permute-start | bytes 1572872 | tf_op jit(solution)/shard_map/nearx1/ppermute | solution.py:21
  36.4 9.1 %collective-permute-done.4.refs_7_ = bf16[2,2,2,256,128]{4,3,2,1,0:T(8,128)(2,1)S(1)} collective-permute-done((bf16[2,2,2,256,128]{4,3,2,1,0:T(8,128)(2,1)}, bf16[2,2,2,256,128]{4,3,2,1,0:T(8,128)(2,1)S(1)}, u32[]{:S(2)}, u32[]{:S(2)}) %collective-permute-start.4) | collective-permute-done | bytes 524320 | tf_op jit(solution)/shard_map/far0/ppermute | solution.py:21
  45.5 1.6 %collective-permute-start.8 = (bf16[2,2,2,256,128]{4,3,2,1,0:T(8,128)(2,1)S(1)}, bf16[2,2,2,256,128]{4,3,2,1,0:T(8,128)(2,1)S(1)}, u32[]{:S(2)}, u32[]{:S(2)}) collective-permute-start(bf16[2,2,2,256,128]{4,3,2,1,0:T(8,128)(2,1)S(1)} %broadcast_select_fusion.1), channel_id=1, source_target_pairs={{0,4},{2,6},{4,0},{6,2},{8,12},{10,14},{12,8},{14,10},{16,20},{18,... | collective-permute-start | bytes 1572872 | tf_op jit(solution)/shard_map/extra0/ppermute | solution.py:21
  47.1 7.5 %collective-permute-done.7.refs_8_ = bf16[2,2,2,256,128]{4,3,2,1,0:T(8,128)(2,1)S(1)} collective-permute-done((bf16[2,2,2,256,128]{4,3,2,1,0:T(8,128)(2,1)S(1)}, bf16[2,2,2,256,128]{4,3,2,1,0:T(8,128)(2,1)S(1)}, u32[]{:S(2)}, u32[]{:S(2)}) %collective-permute-start.7) | collective-permute-done | bytes 524320 | tf_op jit(solution)/shard_map/nearx1/ppermute | solution.py:21
  54.6 3.5 %collective-permute-start.6 = (bf16[2,2,2,256,128]{4,3,2,1,0:T(8,128)(2,1)S(1)}, bf16[2,2,2,256,128]{4,3,2,1,0:T(8,128)(2,1)S(1)}, u32[]{:S(2)}, u32[]{:S(2)}) collective-permute-start(bf16[2,2,2,256,128]{4,3,2,1,0:T(8,128)(2,1)S(1)} %shard_map.49.refs_6_), channel_id=1, source_target_pairs={{0,8},{2,10},{4,12},{6,14},{8,16},{10,18},{12,20},{14,22},{16,24},... | collective-permute-start | bytes 1572872 | tf_op jit(solution)/shard_map/far1/ppermute | solution.py:21
  58.1 0.1 fusion.3
  58.2 4.9 %collective-permute-done.8.refs_9_ = bf16[2,2,2,256,128]{4,3,2,1,0:T(8,128)(2,1)S(1)} collective-permute-done((bf16[2,2,2,256,128]{4,3,2,1,0:T(8,128)(2,1)S(1)}, bf16[2,2,2,256,128]{4,3,2,1,0:T(8,128)(2,1)S(1)}, u32[]{:S(2)}, u32[]{:S(2)}) %collective-permute-start.8) | collective-permute-done | bytes 524320 | tf_op jit(solution)/shard_map/extra0/ppermute | solution.py:21
  63.1 1.6 %collective-permute-done.6.refs_0_ = bf16[2,2,2,256,128]{4,3,2,1,0:T(8,128)(2,1)S(1)} collective-permute-done((bf16[2,2,2,256,128]{4,3,2,1,0:T(8,128)(2,1)S(1)}, bf16[2,2,2,256,128]{4,3,2,1,0:T(8,128)(2,1)S(1)}, u32[]{:S(2)}, u32[]{:S(2)}) %collective-permute-start.6) | collective-permute-done | bytes 524320 | tf_op jit(solution)/shard_map/far1/ppermute | solution.py:21
  64.8 0.9 broadcast_select_fusion
  65.7 1.5 %collective-permute-start.9 = (bf16[2,2,2,256,128]{4,3,2,1,0:T(8,128)(2,1)}, bf16[2,2,2,256,128]{4,3,2,1,0:T(8,128)(2,1)}, u32[]{:S(2)}, u32[]{:S(2)}) collective-permute-start(bf16[2,2,2,256,128]{4,3,2,1,0:T(8,128)(2,1)} %broadcast_select_fusion), channel_id=1, source_target_pairs={{0,4},{2,6},{4,0},{6,2},{8,12},{10,14},{12,8},{14,10},{16,20},{18,... | collective-permute-start | bytes 1572872 | tf_op jit(solution)/shard_map/extra1/ppermute | solution.py:21
  67.3 0.1 fusion.4
  67.3 0.1 copy.17
  67.4 0.1 copy.18
  67.6 0.1 copy.15
  67.6 0.1 copy.16
  67.8 0.1 broadcast_in_dim.16
  67.9 0.2 stack_reshape.6
  68.1 0.1 broadcast_in_dim.17
  68.2 0.2 stack_reshape.7
  68.4 0.6 copy-done.11
  69.1 22.2 %shard_map.51 = (bf16[2,256,256]{2,1,0:T(8,128)(2,1)}, bf16[2,256,256]{2,1,0:T(8,128)(2,1)}, f32[8,128]{1,0:T(8,128)}) custom-call(s32[3]{0:T(128)} %pad_add_fusion.2.info.refs_0_, bf16[2,256,1024]{2,1,0:T(8,128)(2,1)} %refs_1_.3, bf16[2,2,256,1024]{3,2,1,0:T(8,128)(2,1)} %refs_2_.3, bf16[2,256,1024]{2,1,0:T(8,128)(2,1)} %collective-permute-done.refs_3_, ...), custom_call_target="tpu_custom_call" | custom-call | flops 41943040 | bytes 131072 | tf_op jit(solution)/shard_map/pallas_call | solution.py:234
  91.3 0.7 slice_bitcast_fusion.refs_1_
  91.9 0.7 copy-done.9
  92.6 0.9 copy-done.5
  93.6 1.5 %collective-permute-start.17 = (bf16[2,256,256]{2,1,0:T(8,128)(2,1)S(1)}, bf16[2,256,256]{2,1,0:T(8,128)(2,1)S(1)}, u32[]{:S(2)}, u32[]{:S(2)}) collective-permute-start(bf16[2,256,256]{2,1,0:T(8,128)(2,1)S(1)} %copy-done.5), channel_id=1, source_target_pairs={{0,1},{1,0},{2,3},{3,2},{4,5},{5,4},{6,7},{7,6},{8,9},{9,8},{10,11... | collective-permute-start | bytes 786440 | tf_op jit(solution)/shard_map/same0/ppermute | solution.py:27
  95.1 0.6 collective-permute-start.16
  95.7 22.3 %shard_map.52 = (bf16[2,256,256]{2,1,0:T(8,128)(2,1)}, bf16[2,256,256]{2,1,0:T(8,128)(2,1)}, f32[8,128]{1,0:T(8,128)}) custom-call(s32[3]{0:T(128)} %pad_add_fusion.2.info.refs_0_, bf16[2,256,1024]{2,1,0:T(8,128)(2,1)} %refs_1_.3, bf16[2,2,256,1024]{3,2,1,0:T(8,128)(2,1)} %refs_2_.3, bf16[2,256,1024]{2,1,0:T(8,128)(2,1)} %collective-permute-done.refs_3_, ...), custom_call_target="tpu_custom_call" | custom-call | flops 41943040 | bytes 131072 | tf_op jit(solution)/shard_map/pallas_call | solution.py:234
  118.1 1.2 collective-permute-start.14
  119.3 0.5 collective-permute-start.13
  119.8 0.5 collective-permute-start.11
  120.3 1.0 copy-done.6
  121.3 5.8 %shard_map.54.refs_5_ = f32[2,256,2048]{2,1,0:T(8,128)S(1)} custom-call(s32[3]{0:T(128)S(1)} %copy-done.8, bf16[2,256,256]{2,1,0:T(8,128)(2,1)S(1)} %copy-done.5, bf16[2,256,256]{2,1,0:T(8,128)(2,1)S(1)} %copy-done.6, bf16[2,256,256]{2,1,0:T(8,128)(2,1)S(1)} %collective-permute-done.16.refs_3_, bf16[2,256,256]{2,1,0:T(8,128)(2,1)S(1)} %collective-permute-done.17.refs_4_, ...), custom_call_target="tpu_custom_call" | custom-call | flops 335544320 | bytes 655360 | tf_op jit(solution)/shard_map/pallas_call | solution.py:297
  127.1 4.1 %shard_map.55.refs_3_ = f32[2,256,2048]{2,1,0:T(8,128)S(1)} custom-call(s32[3]{0:T(128)S(1)} %copy-done.8, bf16[2,256,256]{2,1,0:T(8,128)(2,1)S(1)} %collective-permute-done.13.refs_1_, bf16[2,256,256]{2,1,0:T(8,128)(2,1)S(1)} %collective-permute-done.14.refs_2_, bf16[1024,4096]{1,0:T(8,128)(2,1)} %refs_3_.1, ...), custom_call_target="tpu_custom_call" | custom-call | flops 134217728 | bytes 262144 | tf_op jit(solution)/shard_map/pallas_call | solution.py:297
  131.3 1.3 collective-permute-done.11.refs_1_
  132.6 4.6 %shard_map.56 = bf16[2,256,2048]{2,1,0:T(8,128)(2,1)} custom-call(s32[3]{0:T(128)S(1)} %copy-done.8, bf16[2,256,256]{2,1,0:T(8,128)(2,1)S(1)} %collective-permute-done.11.refs_1_, bf16[512,2048]{1,0:T(8,128)(2,1)} %shard_map.53.refs_9_.refs_2_, f32[2,256,2048]{2,1,0:T(8,128)S(1)} %shard_map.55.refs_3_), custom_call_target="tpu_custom_call" | custom-call | flops 67108864 | bytes 131072 | tf_op jit(solution)/shard_map/pallas_call | solution.py:297
  (62 shorter events, 0.4 us)
Async XLA Ops:
  0.0 4.6 %collective-permute-start.1 = (bf16[2,2,256,1024]{3,2,1,0:T(8,128)(2,1)}, bf16[2,2,256,1024]{3,2,1,0:T(8,128)(2,1)}, u32[]{:S(2)}, u32[]{:S(2)}) collective-permute-start(bf16[2,2,256,1024]{3,2,1,0:T(8,128)(2,1)} %refs_2_.3), channel_id=1, source_target_pairs={{0,2},{2,0},{4,6},{6,4},{8,10},{10,8},{12,14},{14,12},{16,18},{18,... | collective-permute-start | bytes 6291464 | tf_op jit(solution)/shard_map/pair_kv/ppermute | solution.py:21
  1.1 3.5 %copy-start = (bf16[2,2,256,1024]{3,2,1,0:T(8,128)(2,1)S(1)}, bf16[2,2,256,1024]{3,2,1,0:T(8,128)(2,1)}, u32[]{:S(2)}) copy-start(bf16[2,2,256,1024]{3,2,1,0:T(8,128)(2,1)} %refs_2_.3) | copy-start | bytes 6291460
  1.1 3.5 %copy-start.7 = (s32[3]{0:T(128)S(1)}, s32[3]{0:T(128)}, u32[]{:S(2)}) copy-start(s32[3]{0:T(128)} %pad_add_fusion.2.info.refs_0_) | copy-start | bytes 40
  4.6 9.1 %copy-start.15 = (s32[4,32]{1,0:T(4,128)S(1)}, s32[4,32]{1,0:T(4,128)}, u32[]{:S(2)}) copy-start(s32[4,32]{1,0:T(4,128)} %param.6) | copy-start | bytes 1540
  6.5 38.9 %copy-start.1 = (bf16[2,2,2,256,128]{4,3,2,1,0:T(8,128)(2,1)}, bf16[2,2,2,256,128]{4,3,2,1,0:T(8,128)(2,1)S(1)}, u32[]{:S(2)}) copy-start(bf16[2,2,2,256,128]{4,3,2,1,0:T(8,128)(2,1)S(1)} %shard_map.47.refs_2_.refs_5_) | copy-start | bytes 1572868
  6.6 17.1 %collective-permute-start.3 = (bf16[2,2,2,256,128]{4,3,2,1,0:T(8,128)(2,1)S(1)}, bf16[2,2,2,256,128]{4,3,2,1,0:T(8,128)(2,1)}, u32[]{:S(2)}, u32[]{:S(2)}) collective-permute-start(bf16[2,2,2,256,128]{4,3,2,1,0:T(8,128)(2,1)S(1)} %shard_map.47.refs_2_.refs_5_), channel_id=1, source_target_pairs={{0,8},{2,10},{4,12},{6,14},{8,16},{10,18},{12,20},{14,22},{16,24},... | collective-permute-start | bytes 1572872 | tf_op jit(solution)/shard_map/near0/ppermute | solution.py:21
  12.2 79.7 %collective-permute-start.12 = (bf16[512,2048]{1,0:T(8,128)(2,1)}, bf16[512,2048]{1,0:T(8,128)(2,1)}, u32[]{:S(2)}, u32[]{:S(2)}) collective-permute-start(bf16[512,2048]{1,0:T(8,128)(2,1)} %shard_map.46.refs_2_), channel_id=1, source_target_pairs={{0,1},{1,0},{2,3},{3,2},{4,5},{5,4},{6,7},{7,6},{8,9},{9,8},{10,11... | collective-permute-start | bytes 6291464 | tf_op jit(solution)/shard_map/panel/ppermute | solution.py:27
  13.7 14.5 %collective-permute-start.10 = (s32[4,32]{1,0:T(4,128)S(1)}, s32[4,32]{1,0:T(4,128)S(1)}, u32[]{:S(2)}, u32[]{:S(2)}) collective-permute-start(s32[4,32]{1,0:T(4,128)S(1)} %copy-done.15), channel_id=1, source_target_pairs={{0,2},{2,0},{4,6},{6,4},{8,10},{10,8},{12,14},{14,12},{16,18},{18,... | collective-permute-start | bytes 1544 | tf_op jit(solution)/shard_map/pair_mask/ppermute | solution.py:21
  13.7 54.7 %collective-permute-start = (bf16[2,256,1024]{2,1,0:T(8,128)(2,1)}, bf16[2,256,1024]{2,1,0:T(8,128)(2,1)}, u32[]{:S(2)}, u32[]{:S(2)}) collective-permute-start(bf16[2,256,1024]{2,1,0:T(8,128)(2,1)} %refs_1_.3), channel_id=1, source_target_pairs={{0,2},{2,0},{4,6},{6,4},{8,10},{10,8},{12,14},{14,12},{16,18},{18,... | collective-permute-start | bytes 3145736 | tf_op jit(solution)/shard_map/pair_q/ppermute | solution.py:21
  16.2 49.5 %copy-start.3 = (bf16[2,2,2,256,128]{4,3,2,1,0:T(8,128)(2,1)}, bf16[2,2,2,256,128]{4,3,2,1,0:T(8,128)(2,1)S(1)}, u32[]{:S(2)}) copy-start(bf16[2,2,2,256,128]{4,3,2,1,0:T(8,128)(2,1)S(1)} %shard_map.48.refs_5_) | copy-start | bytes 1572868
  16.2 18.7 %collective-permute-start.2 = (bf16[2,2,2,256,128]{4,3,2,1,0:T(8,128)(2,1)S(1)}, bf16[2,2,2,256,128]{4,3,2,1,0:T(8,128)(2,1)S(1)}, u32[]{:S(2)}, u32[]{:S(2)}) collective-permute-start(bf16[2,2,2,256,128]{4,3,2,1,0:T(8,128)(2,1)S(1)} %shard_map.48.refs_5_), channel_id=1, source_target_pairs={{0,8},{2,10},{4,12},{6,14},{8,16},{10,18},{12,20},{14,22},{16,24},... | collective-permute-start | bytes 1572872 | tf_op jit(solution)/shard_map/near1/ppermute | solution.py:21
  23.6 21.8 %collective-permute-start.4 = (bf16[2,2,2,256,128]{4,3,2,1,0:T(8,128)(2,1)}, bf16[2,2,2,256,128]{4,3,2,1,0:T(8,128)(2,1)S(1)}, u32[]{:S(2)}, u32[]{:S(2)}) collective-permute-start(bf16[2,2,2,256,128]{4,3,2,1,0:T(8,128)(2,1)} %collective-permute-done.3.refs_6_), channel_id=1, source_target_pairs={{0,8},{2,10},{4,12},{6,14},{8,16},{10,18},{12,20},{14,22},{16,24},... | collective-permute-start | bytes 1572872 | tf_op jit(solution)/shard_map/far0/ppermute | solution.py:21
  28.2 18.9 %collective-permute-start.5 = (bf16[2,2,2,256,128]{4,3,2,1,0:T(8,128)(2,1)}, bf16[2,2,2,256,128]{4,3,2,1,0:T(8,128)(2,1)S(1)}, u32[]{:S(2)}, u32[]{:S(2)}) collective-permute-start(bf16[2,2,2,256,128]{4,3,2,1,0:T(8,128)(2,1)} %collective-permute-done.3.refs_6_), channel_id=1, source_target_pairs={{0,4},{2,6},{4,0},{6,2},{8,12},{10,14},{12,8},{14,10},{16,20},{18,... | collective-permute-start | bytes 1572872 | tf_op jit(solution)/shard_map/nearx0/ppermute | solution.py:21
  34.9 19.7 %collective-permute-start.7 = (bf16[2,2,2,256,128]{4,3,2,1,0:T(8,128)(2,1)S(1)}, bf16[2,2,2,256,128]{4,3,2,1,0:T(8,128)(2,1)S(1)}, u32[]{:S(2)}, u32[]{:S(2)}) collective-permute-start(bf16[2,2,2,256,128]{4,3,2,1,0:T(8,128)(2,1)S(1)} %collective-permute-done.2.refs_0_), channel_id=1, source_target_pairs={{0,4},{2,6},{4,0},{6,2},{8,12},{10,14},{12,8},{14,10},{16,20},{18,... | collective-permute-start | bytes 1572872 | tf_op jit(solution)/shard_map/nearx1/ppermute | solution.py:21
  45.5 20.2 %copy-start.10 = (bf16[2,2,2,256,128]{4,3,2,1,0:T(8,128)(2,1)}, bf16[2,2,2,256,128]{4,3,2,1,0:T(8,128)(2,1)S(1)}, u32[]{:S(2)}) copy-start(bf16[2,2,2,256,128]{4,3,2,1,0:T(8,128)(2,1)S(1)} %collective-permute-done.4.refs_7_) | copy-start | bytes 1572868
  45.5 17.6 %collective-permute-start.8 = (bf16[2,2,2,256,128]{4,3,2,1,0:T(8,128)(2,1)S(1)}, bf16[2,2,2,256,128]{4,3,2,1,0:T(8,128)(2,1)S(1)}, u32[]{:S(2)}, u32[]{:S(2)}) collective-permute-start(bf16[2,2,2,256,128]{4,3,2,1,0:T(8,128)(2,1)S(1)} %broadcast_select_fusion.1), channel_id=1, source_target_pairs={{0,4},{2,6},{4,0},{6,2},{8,12},{10,14},{12,8},{14,10},{16,20},{18,... | collective-permute-start | bytes 1572872 | tf_op jit(solution)/shard_map/extra0/ppermute | solution.py:21
  47.1 7.5 %copy-start.13 = (bf16[2,2,2,256,128]{4,3,2,1,0:T(8,128)(2,1)}, bf16[2,2,2,256,128]{4,3,2,1,0:T(8,128)(2,1)S(1)}, u32[]{:S(2)}) copy-start(bf16[2,2,2,256,128]{4,3,2,1,0:T(8,128)(2,1)S(1)} %collective-permute-done.5.refs_8_) | copy-start | bytes 1572868
  54.6 12.6 %copy-start.12 = (bf16[2,2,2,256,128]{4,3,2,1,0:T(8,128)(2,1)}, bf16[2,2,2,256,128]{4,3,2,1,0:T(8,128)(2,1)S(1)}, u32[]{:S(2)}) copy-start(bf16[2,2,2,256,128]{4,3,2,1,0:T(8,128)(2,1)S(1)} %collective-permute-done.7.refs_8_) | copy-start | bytes 1572868
  54.6 36.6 %copy-start.4 = (bf16[2,2,2,256,128]{4,3,2,1,0:T(8,128)(2,1)}, bf16[2,2,2,256,128]{4,3,2,1,0:T(8,128)(2,1)S(1)}, u32[]{:S(2)}) copy-start(bf16[2,2,2,256,128]{4,3,2,1,0:T(8,128)(2,1)S(1)} %shard_map.49.refs_6_) | copy-start | bytes 1572868
  54.6 10.1 %collective-permute-start.6 = (bf16[2,2,2,256,128]{4,3,2,1,0:T(8,128)(2,1)S(1)}, bf16[2,2,2,256,128]{4,3,2,1,0:T(8,128)(2,1)S(1)}, u32[]{:S(2)}, u32[]{:S(2)}) collective-permute-start(bf16[2,2,2,256,128]{4,3,2,1,0:T(8,128)(2,1)S(1)} %shard_map.49.refs_6_), channel_id=1, source_target_pairs={{0,8},{2,10},{4,12},{6,14},{8,16},{10,18},{12,20},{14,22},{16,24},... | collective-permute-start | bytes 1572872 | tf_op jit(solution)/shard_map/far1/ppermute | solution.py:21
  63.1 5.1 %copy-start.14 = (bf16[2,2,2,256,128]{4,3,2,1,0:T(8,128)(2,1)}, bf16[2,2,2,256,128]{4,3,2,1,0:T(8,128)(2,1)S(1)}, u32[]{:S(2)}) copy-start(bf16[2,2,2,256,128]{4,3,2,1,0:T(8,128)(2,1)S(1)} %collective-permute-done.8.refs_9_) | copy-start | bytes 1572868
  64.8 26.5 %copy-start.2 = (bf16[2,2,2,256,128]{4,3,2,1,0:T(8,128)(2,1)}, bf16[2,2,2,256,128]{4,3,2,1,0:T(8,128)(2,1)S(1)}, u32[]{:S(2)}) copy-start(bf16[2,2,2,256,128]{4,3,2,1,0:T(8,128)(2,1)S(1)} %shard_map.50.refs_7_) | copy-start | bytes 1572868
  65.7 25.6 %collective-permute-start.9 = (bf16[2,2,2,256,128]{4,3,2,1,0:T(8,128)(2,1)}, bf16[2,2,2,256,128]{4,3,2,1,0:T(8,128)(2,1)}, u32[]{:S(2)}, u32[]{:S(2)}) collective-permute-start(bf16[2,2,2,256,128]{4,3,2,1,0:T(8,128)(2,1)} %broadcast_select_fusion), channel_id=1, source_target_pairs={{0,4},{2,6},{4,0},{6,2},{8,12},{10,14},{12,8},{14,10},{16,20},{18,... | collective-permute-start | bytes 1572872 | tf_op jit(solution)/shard_map/extra1/ppermute | solution.py:21
  68.4 0.7 copy-start.11
  91.9 0.7 copy-start.9
  92.6 0.9 copy-start.5
  92.6 2.5 %copy-start.16 = (bf16[2,256,256]{2,1,0:T(8,128)(2,1)S(1)}, bf16[2,256,256]{2,1,0:T(8,128)(2,1)}, u32[]{:S(2)}) copy-start(bf16[2,256,256]{2,1,0:T(8,128)(2,1)} %get-tuple-element.14) | copy-start | bytes 786436
  92.6 27.6 %collective-permute-start.15 = (bf16[512,2048]{1,0:T(8,128)(2,1)}, bf16[512,2048]{1,0:T(8,128)(2,1)S(1)}, u32[]{:S(2)}, u32[]{:S(2)}) collective-permute-start(bf16[512,2048]{1,0:T(8,128)(2,1)} %shard_map.53.refs_9_.refs_2_), channel_id=1, source_target_pairs={{0,2},{2,0},{4,6},{6,4},{8,10},{10,8},{12,14},{14,12},{16,18},{18,... | collective-permute-start | bytes 6291464 | tf_op jit(solution)/shard_map/panel_pair/ppermute | solution.py:21
  93.6 25.7 %collective-permute-start.17 = (bf16[2,256,256]{2,1,0:T(8,128)(2,1)S(1)}, bf16[2,256,256]{2,1,0:T(8,128)(2,1)S(1)}, u32[]{:S(2)}, u32[]{:S(2)}) collective-permute-start(bf16[2,256,256]{2,1,0:T(8,128)(2,1)S(1)} %copy-done.5), channel_id=1, source_target_pairs={{0,1},{1,0},{2,3},{3,2},{4,5},{5,4},{6,7},{7,6},{8,9},{9,8},{10,11... | collective-permute-start | bytes 786440 | tf_op jit(solution)/shard_map/same0/ppermute | solution.py:27
  95.1 25.2 %copy-start.8 = (s32[3]{0:T(128)S(1)}, s32[3]{0:T(128)}, u32[]{:S(2)}) copy-start(s32[3]{0:T(128)} %pad_add_fusion.2.info.refs_0_) | copy-start | bytes 40
  95.1 24.7 %collective-permute-start.18 = (bf16[2,256,256]{2,1,0:T(8,128)(2,1)S(1)}, bf16[2,256,256]{2,1,0:T(8,128)(2,1)S(1)}, u32[]{:S(2)}, u32[]{:S(2)}) collective-permute-start(bf16[2,256,256]{2,1,0:T(8,128)(2,1)S(1)} %copy-done.16), channel_id=1, source_target_pairs={{0,3},{1,2},{2,1},{3,0},{4,7},{5,6},{6,5},{7,4},{8,11},{9,10},{10,... | collective-permute-start | bytes 786440 | tf_op jit(solution)/shard_map/cross0/ppermute | solution.py:27
  95.1 25.2 %collective-permute-start.16 = (bf16[2,256,256]{2,1,0:T(8,128)(2,1)S(1)}, bf16[2,256,256]{2,1,0:T(8,128)(2,1)S(1)}, u32[]{:S(2)}, u32[]{:S(2)}) collective-permute-start(bf16[2,256,256]{2,1,0:T(8,128)(2,1)S(1)} %copy-done.16), channel_id=1, source_target_pairs={{0,2},{2,0},{4,6},{6,4},{8,10},{10,8},{12,14},{14,12},{16,18},{18,... | collective-permute-start | bytes 786440 | tf_op jit(solution)/shard_map/pair0/ppermute | solution.py:21
  118.1 9.0 %collective-permute-start.14 = (bf16[2,256,256]{2,1,0:T(8,128)(2,1)}, bf16[2,256,256]{2,1,0:T(8,128)(2,1)S(1)}, u32[]{:S(2)}, u32[]{:S(2)}) collective-permute-start(bf16[2,256,256]{2,1,0:T(8,128)(2,1)} %get-tuple-element.12), channel_id=1, source_target_pairs={{0,3},{1,2},{2,1},{3,0},{4,7},{5,6},{6,5},{7,4},{8,11},{9,10},{10,... | collective-permute-start | bytes 786440 | tf_op jit(solution)/shard_map/cross1/ppermute | solution.py:27
  119.3 7.9 %collective-permute-start.13 = (bf16[2,256,256]{2,1,0:T(8,128)(2,1)}, bf16[2,256,256]{2,1,0:T(8,128)(2,1)S(1)}, u32[]{:S(2)}, u32[]{:S(2)}) collective-permute-start(bf16[2,256,256]{2,1,0:T(8,128)(2,1)} %get-tuple-element.12), channel_id=1, source_target_pairs={{0,2},{2,0},{4,6},{6,4},{8,10},{10,8},{12,14},{14,12},{16,18},{18,... | collective-permute-start | bytes 786440 | tf_op jit(solution)/shard_map/pair1/ppermute | solution.py:21
  119.8 12.8 %collective-permute-start.11 = (bf16[2,256,256]{2,1,0:T(8,128)(2,1)}, bf16[2,256,256]{2,1,0:T(8,128)(2,1)S(1)}, u32[]{:S(2)}, u32[]{:S(2)}) collective-permute-start(bf16[2,256,256]{2,1,0:T(8,128)(2,1)} %get-tuple-element.11.refs_2_), channel_id=1, source_target_pairs={{0,1},{1,0},{2,3},{3,2},{4,5},{5,4},{6,7},{7,6},{8,9},{9,8},{10,11... | collective-permute-start | bytes 786440 | tf_op jit(solution)/shard_map/same1/ppermute | solution.py:27
  120.3 1.0 copy-start.6

commit v13 on v10

--- a/solution.py
+++ b/solution.py
@@ -63,7 +63,7 @@
     return jnp.repeat(table.reshape(-1, rows, 2 * rows).transpose(0, 2, 1), BLK, axis=2)
 
 
-def copies(info, sources, outs, shapes, plan):
+def copies(info, sources, outs, shapes, plan, limit=8 * 1024 * 1024):
     total = sum(math.prod(o.shape) for o in outs)
 
     def kernel(info, *refs):
@@ -100,7 +100,7 @@
             ],
         ),
         out_shape=[jax.ShapeDtypeStruct(o.shape, o.dtype) for o in outs],
-        compiler_params=pltpu.CompilerParams(vmem_limit_bytes=VMEM),
+        compiler_params=pltpu.CompilerParams(vmem_limit_bytes=limit),
         cost_estimate=pl.CostEstimate(flops=0, bytes_accessed=total, transcendentals=0),
     )(info, *sources)
 
@@ -259,7 +259,7 @@
 
 def project(info, pieces, weights, features, dtype, before=None):
     tokens = pieces[0][2].shape[1]
-    tile = min(512, features)
+    tile = min(512 if before is None else 256, features)
     steps = features // tile
     half = weights[0].shape[0] // 2
     used, specs = [], []
@@ -336,7 +336,7 @@
     cuts = 4 if f == 2 else 1
     panels = copies(
         info, [out_weight], [jax.ShapeDtypeStruct((width, features), bf16)] * (f - 1),
-        [(width // cuts, features)] * (cuts * (f - 1)), cut_panels,
+        [(width // cuts, features)] * (cuts * (f - 1)), cut_panels, VMEM,
     )
 
     def join(core, ins, outs):
@@ -378,11 +378,8 @@
     for k, mine in enumerate(own):
         one = moved(mine, n, ahead, f"near{k}")
         swap = moved(one, n, across, f"nearx{k}")
-        if k:
-            one, = gated([one], *blocks[-1][1:3])
         two = moved(one, n, ahead, f"far{k}")
-        if k:
-            two, = gated([two], swap, blocks[-1][3])
+        two, = gated([two], swap, *[block[3] for block in blocks])
         extra = moved(jnp.where(side == 0, mine, two), n, across, f"extra{k}")
         blocks.append((one, two, swap, extra))
 
@@ -412,12 +409,17 @@
         others += [same, moved(same, n, pair, "panel_pair")]
 
     weights = [out_weight, out_weight] + others
-    early, late = [], []
+    stages = [[], [], []]
     for g in range(2 * f):
         for k, (part, act) in enumerate(zip(parts, acts[g])):
-            (late if g and k == len(parts) - 1 else early).append((g, part[0], act))
-    before = project(info, early, weights, features, jnp.float32)
-    return project(info, late, weights, features, jnp.bfloat16, before)
+            late = k == len(parts) - 1 and g > 0
+            stages[(1 if g % 2 else 2) if late else 0].append((g, part[0], act))
+    total = None
+    stages = [stage for stage in stages if stage]
+    for k, stage in enumerate(stages):
+        dtype = jnp.bfloat16 if k == len(stages) - 1 else jnp.float32
+        total = project(info, stage, weights, features, dtype, total)
+    return total
 
 
 def solution(mesh):

time: 140 us -> 135 us (0.964)
  waiting for transfers between devices: 36 us -> 29.7 us
  Pallas kernels: 63.4 us -> 69 us
  local copies, waits for them, and re-layouts: 7.1 us -> 4.33 us
    pallas_call x2 -> x3, Pallas kernels: 11.4 us -> 18.6 us  [project(): pl.pallas_call(lambda *refs: project_kernel(len(flat), len(used), before...]
    ppermute x5, waiting for transfers between devices: 5.43 us -> 0.01 us  [moved_both(): return lax.ppermute(array, ('ctx', 'fsdp'), pairs)]
    pallas_call x3, Pallas kernels: 8.97 us -> 7.27 us  [copies(): pl.pallas_call(kernel, grid_spec=pltpu.PrefetchScalarGridSpec(num_scalar_...]
    unnamed x31 -> x37, local copies, waits for them, and re-layouts: 4.72 us -> 3.29 us
  transfers between devices with their start and end apart: 19 -> 19, of which waited for: 7 -> 6; matrix products, arithmetic and copies ran while one was open for 3% -> 2% of each run, Pallas kernels for 40% -> 45%
where the time goes in v13:
time: 135 us; the launch traced here: 134 us
  Pallas kernels  69 us (51%)
  waiting for transfers between devices  29.7 us (22%)
  starting transfers between devices  29.1 us (22%)
  local copies, waits for them, and re-layouts  4.33 us (3%)
  other arithmetic  1.97 us (1%)
    pallas_call x2, Pallas kernels, attend(): pl.pallas_call(lambda *refs: attend_kernel(tokens, *refs), grid_spec=pltp...  43.1 us
    ppermute x14, waiting for transfers between devices, moved(): return lax.ppermute(array, 'ctx', pairs)  29.7 us
    ppermute x14, starting transfers between devices, moved(): return lax.ppermute(array, 'ctx', pairs)  24.4 us
    pallas_call x3, Pallas kernels, project(): pl.pallas_call(lambda *refs: project_kernel(len(flat), len(used), before...  18.6 us
    pallas_call x3, Pallas kernels, copies(): pl.pallas_call(kernel, grid_spec=pltpu.PrefetchScalarGridSpec(num_scalar_...  7.27 us
    ppermute x5, starting transfers between devices, moved_both(): return lax.ppermute(array, ('ctx', 'fsdp'), pairs)  4.72 us
    unnamed x37, local copies, waits for them, and re-layouts  3.29 us
  transfers between devices with their start and end apart: 19, of which 6 were waited for; matrix products, arithmetic and copies ran while one was open for 2% of the time, Pallas kernels for 45%

profile of v13, /device:TPU:0, one launch (start us, length us, event | category | flops | bytes accessed | tf_op | source)
XLA Modules:
  0.0 134.4 jit_solution(66200099901214391)
XLA Ops:
  0.0 0.5 collective-permute-start.1
  0.5 0.6 pad_add_fusion.2.info.refs_0_
  1.1 3.5 %shard_map.46.refs_2_ = bf16[512,2048]{1,0:T(8,128)(2,1)} custom-call(s32[3]{0:T(128)} %pad_add_fusion.2.info.refs_0_, bf16[1024,4096]{1,0:T(8,128)(2,1)} %refs_3_.1), custom_call_target="tpu_custom_call" | custom-call | bytes 1048576 | tf_op jit(solution)/shard_map/pallas_call | solution.py:89
  4.6 1.9 %shard_map.47.refs_2_.refs_5_ = bf16[2,2,2,256,128]{4,3,2,1,0:T(8,128)(2,1)S(1)} custom-call(s32[3]{0:T(128)S(1)} %copy-done.7, bf16[2,2,256,1024]{3,2,1,0:T(8,128)(2,1)S(1)} %copy-done, bf16[2,2,256,1024]{3,2,1,0:T(8,128)(2,1)} %collective-permute-done.1.refs_1_.refs_4_, bf16[512,2048]{1,0:T(8,128)(2,1)} %shard_map.46.refs_2_), custom_call_target="tpu_custom_call" | custom-call | bytes 262144 | tf_op jit(solution)/shard_map/pallas_call | solution.py:89
  6.5 5.7 %collective-permute-start.5 = (bf16[2,2,2,256,128]{4,3,2,1,0:T(8,128)(2,1)S(1)}, bf16[2,2,2,256,128]{4,3,2,1,0:T(8,128)(2,1)}, u32[]{:S(2)}, u32[]{:S(2)}) collective-permute-start(bf16[2,2,2,256,128]{4,3,2,1,0:T(8,128)(2,1)S(1)} %shard_map.47.refs_2_.refs_5_), channel_id=1, source_target_pairs={{0,8},{2,10},{4,12},{6,14},{8,16},{10,18},{12,20},{14,22},{16,24},... | collective-permute-start | bytes 1572872 | tf_op jit(solution)/shard_map/near0/ppermute | solution.py:21
  12.2 1.5 %collective-permute-start.12 = (bf16[512,2048]{1,0:T(8,128)(2,1)}, bf16[512,2048]{1,0:T(8,128)(2,1)}, u32[]{:S(2)}, u32[]{:S(2)}) collective-permute-start(bf16[512,2048]{1,0:T(8,128)(2,1)} %shard_map.46.refs_2_), channel_id=1, source_target_pairs={{0,1},{1,0},{2,3},{3,2},{4,5},{5,4},{6,7},{7,6},{8,9},{9,8},{10,11... | collective-permute-start | bytes 6291464 | tf_op jit(solution)/shard_map/panel/ppermute | solution.py:27
  13.8 1.9 %shard_map.48.refs_5_ = bf16[2,2,2,256,128]{4,3,2,1,0:T(8,128)(2,1)S(1)} custom-call(s32[3]{0:T(128)S(1)} %copy-done.7, bf16[2,2,256,1024]{3,2,1,0:T(8,128)(2,1)S(1)} %copy-done, bf16[2,2,256,1024]{3,2,1,0:T(8,128)(2,1)} %collective-permute-done.1.refs_1_.refs_4_, bf16[2,2,2,256,128]{4,3,2,1,0:T(8,128)(2,1)S(1)} %shard_map.47.refs_2_.refs_5_), custom_call_target="tpu_custom_call" | custom-call | bytes 262144 | tf_op jit(solution)/shard_map/pallas_call | solution.py:89
  15.7 2.7 %collective-permute-start.2 = (bf16[2,2,2,256,128]{4,3,2,1,0:T(8,128)(2,1)S(1)}, bf16[2,2,2,256,128]{4,3,2,1,0:T(8,128)(2,1)S(1)}, u32[]{:S(2)}, u32[]{:S(2)}) collective-permute-start(bf16[2,2,2,256,128]{4,3,2,1,0:T(8,128)(2,1)S(1)} %shard_map.48.refs_5_), channel_id=1, source_target_pairs={{0,8},{2,10},{4,12},{6,14},{8,16},{10,18},{12,20},{14,22},{16,24},... | collective-permute-start | bytes 1572872 | tf_op jit(solution)/shard_map/near1/ppermute | solution.py:21
  18.4 5.2 %collective-permute-done.5.refs_6_ = bf16[2,2,2,256,128]{4,3,2,1,0:T(8,128)(2,1)} collective-permute-done((bf16[2,2,2,256,128]{4,3,2,1,0:T(8,128)(2,1)S(1)}, bf16[2,2,2,256,128]{4,3,2,1,0:T(8,128)(2,1)}, u32[]{:S(2)}, u32[]{:S(2)}) %collective-permute-start.5) | collective-permute-done | bytes 524320 | tf_op jit(solution)/shard_map/near0/ppermute | solution.py:21
  23.6 1.5 %collective-permute-start.7 = (bf16[2,2,2,256,128]{4,3,2,1,0:T(8,128)(2,1)}, bf16[2,2,2,256,128]{4,3,2,1,0:T(8,128)(2,1)S(1)}, u32[]{:S(2)}, u32[]{:S(2)}) collective-permute-start(bf16[2,2,2,256,128]{4,3,2,1,0:T(8,128)(2,1)} %collective-permute-done.5.refs_6_), channel_id=1, source_target_pairs={{0,4},{2,6},{4,0},{6,2},{8,12},{10,14},{12,8},{14,10},{16,20},{18,... | collective-permute-start | bytes 1572872 | tf_op jit(solution)/shard_map/nearx0/ppermute | solution.py:21
  25.1 4.5 %collective-permute-start.6 = (bf16[2,2,2,256,128]{4,3,2,1,0:T(8,128)(2,1)}, bf16[2,2,2,256,128]{4,3,2,1,0:T(8,128)(2,1)S(1)}, u32[]{:S(2)}, u32[]{:S(2)}) collective-permute-start(bf16[2,2,2,256,128]{4,3,2,1,0:T(8,128)(2,1)} %collective-permute-done.5.refs_6_), channel_id=1, source_target_pairs={{0,8},{2,10},{4,12},{6,14},{8,16},{10,18},{12,20},{14,22},{16,24},... | collective-permute-start | bytes 1572872 | tf_op jit(solution)/shard_map/far0/ppermute | solution.py:21
  29.7 0.1 fusion.6
  29.7 5.1 %collective-permute-done.2.refs_6_ = bf16[2,2,2,256,128]{4,3,2,1,0:T(8,128)(2,1)S(1)} collective-permute-done((bf16[2,2,2,256,128]{4,3,2,1,0:T(8,128)(2,1)S(1)}, bf16[2,2,2,256,128]{4,3,2,1,0:T(8,128)(2,1)S(1)}, u32[]{:S(2)}, u32[]{:S(2)}) %collective-permute-start.2) | collective-permute-done | bytes 524320 | tf_op jit(solution)/shard_map/near1/ppermute | solution.py:21
  34.9 1.3 collective-permute-done.7.refs_8_
  36.2 1.5 %collective-permute-start.4 = (bf16[2,2,2,256,128]{4,3,2,1,0:T(8,128)(2,1)S(1)}, bf16[2,2,2,256,128]{4,3,2,1,0:T(8,128)(2,1)S(1)}, u32[]{:S(2)}, u32[]{:S(2)}) collective-permute-start(bf16[2,2,2,256,128]{4,3,2,1,0:T(8,128)(2,1)S(1)} %collective-permute-done.2.refs_6_), channel_id=1, source_target_pairs={{0,4},{2,6},{4,0},{6,2},{8,12},{10,14},{12,8},{14,10},{16,20},{18,... | collective-permute-start | bytes 1572872 | tf_op jit(solution)/shard_map/nearx1/ppermute | solution.py:21
  37.7 7.7 %collective-permute-done.6.refs_0_ = bf16[2,2,2,256,128]{4,3,2,1,0:T(8,128)(2,1)S(1)} collective-permute-done((bf16[2,2,2,256,128]{4,3,2,1,0:T(8,128)(2,1)}, bf16[2,2,2,256,128]{4,3,2,1,0:T(8,128)(2,1)S(1)}, u32[]{:S(2)}, u32[]{:S(2)}) %collective-permute-start.6) | collective-permute-done | bytes 524320 | tf_op jit(solution)/shard_map/far0/ppermute | solution.py:21
  45.5 1.6 %collective-permute-start.8 = (bf16[2,2,2,256,128]{4,3,2,1,0:T(8,128)(2,1)S(1)}, bf16[2,2,2,256,128]{4,3,2,1,0:T(8,128)(2,1)S(1)}, u32[]{:S(2)}, u32[]{:S(2)}) collective-permute-start(bf16[2,2,2,256,128]{4,3,2,1,0:T(8,128)(2,1)S(1)} %broadcast_select_fusion.1), channel_id=1, source_target_pairs={{0,4},{2,6},{4,0},{6,2},{8,12},{10,14},{12,8},{14,10},{16,20},{18,... | collective-permute-start | bytes 1572872 | tf_op jit(solution)/shard_map/extra0/ppermute | solution.py:21
  47.0 4.3 %collective-permute-start.3 = (bf16[2,2,2,256,128]{4,3,2,1,0:T(8,128)(2,1)S(1)}, bf16[2,2,2,256,128]{4,3,2,1,0:T(8,128)(2,1)S(1)}, u32[]{:S(2)}, u32[]{:S(2)}) collective-permute-start(bf16[2,2,2,256,128]{4,3,2,1,0:T(8,128)(2,1)S(1)} %collective-permute-done.2.refs_6_), channel_id=1, source_target_pairs={{0,8},{2,10},{4,12},{6,14},{8,16},{10,18},{12,20},{14,22},{16,24},... | collective-permute-start | bytes 1572872 | tf_op jit(solution)/shard_map/far1/ppermute | solution.py:21
  51.4 0.1 fusion.3
  51.5 8.9 %collective-permute-done.8.refs_9_ = bf16[2,2,2,256,128]{4,3,2,1,0:T(8,128)(2,1)S(1)} collective-permute-done((bf16[2,2,2,256,128]{4,3,2,1,0:T(8,128)(2,1)S(1)}, bf16[2,2,2,256,128]{4,3,2,1,0:T(8,128)(2,1)S(1)}, u32[]{:S(2)}, u32[]{:S(2)}) %collective-permute-start.8) | collective-permute-done | bytes 524320 | tf_op jit(solution)/shard_map/extra0/ppermute | solution.py:21
  60.5 1.3 collective-permute-done.3.refs_0_
  61.8 0.9 broadcast_select_fusion
  62.7 1.0 collective-permute-start.9
  63.7 0.1 broadcast_and_fusion.1
  63.8 0.1 fusion.4
  63.9 0.1 copy.17
  64.0 0.1 copy.18
  64.1 0.1 copy.15
  64.2 0.1 copy.16
  64.3 0.1 broadcast_in_dim.16
  64.5 0.2 stack_reshape.6
  64.6 0.1 broadcast_in_dim.17
  64.8 0.2 stack_reshape.7
  65.0 0.6 copy-done.10
  65.6 21.4 %shard_map.51 = (bf16[2,256,256]{2,1,0:T(8,128)(2,1)}, bf16[2,256,256]{2,1,0:T(8,128)(2,1)}, f32[8,128]{1,0:T(8,128)}) custom-call(s32[3]{0:T(128)} %pad_add_fusion.2.info.refs_0_, bf16[2,256,1024]{2,1,0:T(8,128)(2,1)} %refs_1_.3, bf16[2,2,256,1024]{3,2,1,0:T(8,128)(2,1)} %refs_2_.3, bf16[2,256,1024]{2,1,0:T(8,128)(2,1)} %collective-permute-done.refs_3_, ...), custom_call_target="tpu_custom_call" | custom-call | flops 41943040 | bytes 131072 | tf_op jit(solution)/shard_map/pallas_call | solution.py:224
  87.1 0.7 copy-done.9
  87.8 0.1 copy-done.13
  87.9 0.8 copy-done.5
  88.7 1.5 %collective-permute-start.17 = (bf16[2,256,256]{2,1,0:T(8,128)(2,1)S(1)}, bf16[2,256,256]{2,1,0:T(8,128)(2,1)S(1)}, u32[]{:S(2)}, u32[]{:S(2)}) collective-permute-start(bf16[2,256,256]{2,1,0:T(8,128)(2,1)S(1)} %copy-done.5), channel_id=1, source_target_pairs={{0,1},{1,0},{2,3},{3,2},{4,5},{5,4},{6,7},{7,6},{8,9},{9,8},{10,11... | collective-permute-start | bytes 786440 | tf_op jit(solution)/shard_map/same0/ppermute | solution.py:27
  90.3 0.6 collective-permute-start.16
  90.9 21.6 %shard_map.52 = (bf16[2,256,256]{2,1,0:T(8,128)(2,1)}, bf16[2,256,256]{2,1,0:T(8,128)(2,1)}, f32[8,128]{1,0:T(8,128)}) custom-call(s32[3]{0:T(128)} %pad_add_fusion.2.info.refs_0_, bf16[2,256,1024]{2,1,0:T(8,128)(2,1)} %refs_1_.3, bf16[2,2,256,1024]{3,2,1,0:T(8,128)(2,1)} %refs_2_.3, bf16[2,256,1024]{2,1,0:T(8,128)(2,1)} %collective-permute-done.refs_3_, ...), custom_call_target="tpu_custom_call" | custom-call | flops 41943040 | bytes 131072 | tf_op jit(solution)/shard_map/pallas_call | solution.py:224
  112.5 1.2 collective-permute-start.14
  113.7 0.5 collective-permute-start.13
  114.2 0.5 collective-permute-start.11
  114.8 1.0 copy-done.6
  115.7 5.8 %shard_map.54.refs_5_ = f32[2,256,2048]{2,1,0:T(8,128)S(1)} custom-call(s32[3]{0:T(128)S(1)} %copy-done.8, bf16[2,256,256]{2,1,0:T(8,128)(2,1)S(1)} %copy-done.5, bf16[2,256,256]{2,1,0:T(8,128)(2,1)S(1)} %copy-done.6, bf16[2,256,256]{2,1,0:T(8,128)(2,1)S(1)} %collective-permute-done.16.refs_3_, bf16[2,256,256]{2,1,0:T(8,128)(2,1)S(1)} %collective-permute-done.17.refs_4_, ...), custom_call_target="tpu_custom_call" | custom-call | flops 335544320 | bytes 655360 | tf_op jit(solution)/shard_map/pallas_call | solution.py:287
  121.6 6.0 %shard_map.55.refs_3_ = f32[2,256,2048]{2,1,0:T(8,128)S(1)} custom-call(s32[3]{0:T(128)S(1)} %copy-done.8, bf16[2,256,256]{2,1,0:T(8,128)(2,1)S(1)} %collective-permute-done.13.refs_1_, bf16[2,256,256]{2,1,0:T(8,128)(2,1)S(1)} %collective-permute-done.14.refs_2_, bf16[1024,4096]{1,0:T(8,128)(2,1)} %refs_3_.1, ...), custom_call_target="tpu_custom_call" | custom-call | flops 134217728 | bytes 262144 | tf_op jit(solution)/shard_map/pallas_call | solution.py:287
  127.6 6.8 %shard_map.56 = bf16[2,256,2048]{2,1,0:T(8,128)(2,1)} custom-call(s32[3]{0:T(128)S(1)} %copy-done.8, bf16[2,256,256]{2,1,0:T(8,128)(2,1)S(1)} %collective-permute-done.11.refs_1_, bf16[512,2048]{1,0:T(8,128)(2,1)} %shard_map.53.refs_9_.refs_2_, f32[2,256,2048]{2,1,0:T(8,128)S(1)} %shard_map.55.refs_3_), custom_call_target="tpu_custom_call" | custom-call | flops 67108864 | bytes 131072 | tf_op jit(solution)/shard_map/pallas_call | solution.py:287
  (63 shorter events, 0.2 us)
Async XLA Ops:
  0.0 4.6 %collective-permute-start.1 = (bf16[2,2,256,1024]{3,2,1,0:T(8,128)(2,1)}, bf16[2,2,256,1024]{3,2,1,0:T(8,128)(2,1)}, u32[]{:S(2)}, u32[]{:S(2)}) collective-permute-start(bf16[2,2,256,1024]{3,2,1,0:T(8,128)(2,1)} %refs_2_.3), channel_id=1, source_target_pairs={{0,2},{2,0},{4,6},{6,4},{8,10},{10,8},{12,14},{14,12},{16,18},{18,... | collective-permute-start | bytes 6291464 | tf_op jit(solution)/shard_map/pair_kv/ppermute | solution.py:21
  1.1 3.5 %copy-start = (bf16[2,2,256,1024]{3,2,1,0:T(8,128)(2,1)S(1)}, bf16[2,2,256,1024]{3,2,1,0:T(8,128)(2,1)}, u32[]{:S(2)}) copy-start(bf16[2,2,256,1024]{3,2,1,0:T(8,128)(2,1)} %refs_2_.3) | copy-start | bytes 6291460
  1.1 3.5 %copy-start.7 = (s32[3]{0:T(128)S(1)}, s32[3]{0:T(128)}, u32[]{:S(2)}) copy-start(s32[3]{0:T(128)} %pad_add_fusion.2.info.refs_0_) | copy-start | bytes 40
  4.5 9.2 %copy-start.16 = (s32[4,32]{1,0:T(4,128)S(1)}, s32[4,32]{1,0:T(4,128)}, u32[]{:S(2)}) copy-start(s32[4,32]{1,0:T(4,128)} %param.6) | copy-start | bytes 1540
  6.5 38.9 %copy-start.1 = (bf16[2,2,2,256,128]{4,3,2,1,0:T(8,128)(2,1)}, bf16[2,2,2,256,128]{4,3,2,1,0:T(8,128)(2,1)S(1)}, u32[]{:S(2)}) copy-start(bf16[2,2,2,256,128]{4,3,2,1,0:T(8,128)(2,1)S(1)} %shard_map.47.refs_2_.refs_5_) | copy-start | bytes 1572868
  6.5 17.1 %collective-permute-start.5 = (bf16[2,2,2,256,128]{4,3,2,1,0:T(8,128)(2,1)S(1)}, bf16[2,2,2,256,128]{4,3,2,1,0:T(8,128)(2,1)}, u32[]{:S(2)}, u32[]{:S(2)}) collective-permute-start(bf16[2,2,2,256,128]{4,3,2,1,0:T(8,128)(2,1)S(1)} %shard_map.47.refs_2_.refs_5_), channel_id=1, source_target_pairs={{0,8},{2,10},{4,12},{6,14},{8,16},{10,18},{12,20},{14,22},{16,24},... | collective-permute-start | bytes 1572872 | tf_op jit(solution)/shard_map/near0/ppermute | solution.py:21
  12.2 74.9 %collective-permute-start.12 = (bf16[512,2048]{1,0:T(8,128)(2,1)}, bf16[512,2048]{1,0:T(8,128)(2,1)}, u32[]{:S(2)}, u32[]{:S(2)}) collective-permute-start(bf16[512,2048]{1,0:T(8,128)(2,1)} %shard_map.46.refs_2_), channel_id=1, source_target_pairs={{0,1},{1,0},{2,3},{3,2},{4,5},{5,4},{6,7},{7,6},{8,9},{9,8},{10,11... | collective-permute-start | bytes 6291464 | tf_op jit(solution)/shard_map/panel/ppermute | solution.py:27
  13.7 33.3 %collective-permute-start.10 = (s32[4,32]{1,0:T(4,128)S(1)}, s32[4,32]{1,0:T(4,128)S(1)}, u32[]{:S(2)}, u32[]{:S(2)}) collective-permute-start(s32[4,32]{1,0:T(4,128)S(1)} %copy-done.16), channel_id=1, source_target_pairs={{0,2},{2,0},{4,6},{6,4},{8,10},{10,8},{12,14},{14,12},{16,18},{18,... | collective-permute-start | bytes 1544 | tf_op jit(solution)/shard_map/pair_mask/ppermute | solution.py:21
  15.7 47.1 %copy-start.4 = (bf16[2,2,2,256,128]{4,3,2,1,0:T(8,128)(2,1)}, bf16[2,2,2,256,128]{4,3,2,1,0:T(8,128)(2,1)S(1)}, u32[]{:S(2)}) copy-start(bf16[2,2,2,256,128]{4,3,2,1,0:T(8,128)(2,1)S(1)} %shard_map.48.refs_5_) | copy-start | bytes 1572868
  15.7 19.2 %collective-permute-start.2 = (bf16[2,2,2,256,128]{4,3,2,1,0:T(8,128)(2,1)S(1)}, bf16[2,2,2,256,128]{4,3,2,1,0:T(8,128)(2,1)S(1)}, u32[]{:S(2)}, u32[]{:S(2)}) collective-permute-start(bf16[2,2,2,256,128]{4,3,2,1,0:T(8,128)(2,1)S(1)} %shard_map.48.refs_5_), channel_id=1, source_target_pairs={{0,8},{2,10},{4,12},{6,14},{8,16},{10,18},{12,20},{14,22},{16,24},... | collective-permute-start | bytes 1572872 | tf_op jit(solution)/shard_map/near1/ppermute | solution.py:21
  23.6 12.5 %collective-permute-start.7 = (bf16[2,2,2,256,128]{4,3,2,1,0:T(8,128)(2,1)}, bf16[2,2,2,256,128]{4,3,2,1,0:T(8,128)(2,1)S(1)}, u32[]{:S(2)}, u32[]{:S(2)}) collective-permute-start(bf16[2,2,2,256,128]{4,3,2,1,0:T(8,128)(2,1)} %collective-permute-done.5.refs_6_), channel_id=1, source_target_pairs={{0,4},{2,6},{4,0},{6,2},{8,12},{10,14},{12,8},{14,10},{16,20},{18,... | collective-permute-start | bytes 1572872 | tf_op jit(solution)/shard_map/nearx0/ppermute | solution.py:21
  25.1 20.3 %collective-permute-start.6 = (bf16[2,2,2,256,128]{4,3,2,1,0:T(8,128)(2,1)}, bf16[2,2,2,256,128]{4,3,2,1,0:T(8,128)(2,1)S(1)}, u32[]{:S(2)}, u32[]{:S(2)}) collective-permute-start(bf16[2,2,2,256,128]{4,3,2,1,0:T(8,128)(2,1)} %collective-permute-done.5.refs_6_), channel_id=1, source_target_pairs={{0,8},{2,10},{4,12},{6,14},{8,16},{10,18},{12,20},{14,22},{16,24},... | collective-permute-start | bytes 1572872 | tf_op jit(solution)/shard_map/far0/ppermute | solution.py:21
  34.9 27.9 %copy-start.15 = (bf16[2,2,2,256,128]{4,3,2,1,0:T(8,128)(2,1)}, bf16[2,2,2,256,128]{4,3,2,1,0:T(8,128)(2,1)S(1)}, u32[]{:S(2)}) copy-start(bf16[2,2,2,256,128]{4,3,2,1,0:T(8,128)(2,1)S(1)} %collective-permute-done.2.refs_6_) | copy-start | bytes 1572868
  34.9 30.1 %collective-permute-start = (bf16[2,256,1024]{2,1,0:T(8,128)(2,1)}, bf16[2,256,1024]{2,1,0:T(8,128)(2,1)}, u32[]{:S(2)}, u32[]{:S(2)}) collective-permute-start(bf16[2,256,1024]{2,1,0:T(8,128)(2,1)} %refs_1_.3), channel_id=1, source_target_pairs={{0,2},{2,0},{4,6},{6,4},{8,10},{10,8},{12,14},{14,12},{16,18},{18,... | collective-permute-start | bytes 3145736 | tf_op jit(solution)/shard_map/pair_q/ppermute | solution.py:21
  36.2 10.9 %copy-start.12 = (bf16[2,2,2,256,128]{4,3,2,1,0:T(8,128)(2,1)}, bf16[2,2,2,256,128]{4,3,2,1,0:T(8,128)(2,1)S(1)}, u32[]{:S(2)}) copy-start(bf16[2,2,2,256,128]{4,3,2,1,0:T(8,128)(2,1)S(1)} %collective-permute-done.7.refs_8_) | copy-start | bytes 1572868
  36.2 15.3 %collective-permute-start.4 = (bf16[2,2,2,256,128]{4,3,2,1,0:T(8,128)(2,1)S(1)}, bf16[2,2,2,256,128]{4,3,2,1,0:T(8,128)(2,1)S(1)}, u32[]{:S(2)}, u32[]{:S(2)}) collective-permute-start(bf16[2,2,2,256,128]{4,3,2,1,0:T(8,128)(2,1)S(1)} %collective-permute-done.2.refs_6_), channel_id=1, source_target_pairs={{0,4},{2,6},{4,0},{6,2},{8,12},{10,14},{12,8},{14,10},{16,20},{18,... | collective-permute-start | bytes 1572872 | tf_op jit(solution)/shard_map/nearx1/ppermute | solution.py:21
  45.4 17.3 %copy-start.2 = (bf16[2,2,2,256,128]{4,3,2,1,0:T(8,128)(2,1)}, bf16[2,2,2,256,128]{4,3,2,1,0:T(8,128)(2,1)S(1)}, u32[]{:S(2)}) copy-start(bf16[2,2,2,256,128]{4,3,2,1,0:T(8,128)(2,1)S(1)} %shard_map.49.refs_7_) | copy-start | bytes 1572868
  45.5 15.0 %collective-permute-start.8 = (bf16[2,2,2,256,128]{4,3,2,1,0:T(8,128)(2,1)S(1)}, bf16[2,2,2,256,128]{4,3,2,1,0:T(8,128)(2,1)S(1)}, u32[]{:S(2)}, u32[]{:S(2)}) collective-permute-start(bf16[2,2,2,256,128]{4,3,2,1,0:T(8,128)(2,1)S(1)} %broadcast_select_fusion.1), channel_id=1, source_target_pairs={{0,4},{2,6},{4,0},{6,2},{8,12},{10,14},{12,8},{14,10},{16,20},{18,... | collective-permute-start | bytes 1572872 | tf_op jit(solution)/shard_map/extra0/ppermute | solution.py:21
  47.0 14.8 %collective-permute-start.3 = (bf16[2,2,2,256,128]{4,3,2,1,0:T(8,128)(2,1)S(1)}, bf16[2,2,2,256,128]{4,3,2,1,0:T(8,128)(2,1)S(1)}, u32[]{:S(2)}, u32[]{:S(2)}) collective-permute-start(bf16[2,2,2,256,128]{4,3,2,1,0:T(8,128)(2,1)S(1)} %collective-permute-done.2.refs_6_), channel_id=1, source_target_pairs={{0,8},{2,10},{4,12},{6,14},{8,16},{10,18},{12,20},{14,22},{16,24},... | collective-permute-start | bytes 1572872 | tf_op jit(solution)/shard_map/far1/ppermute | solution.py:21
  51.5 35.6 %copy-start.11 = (bf16[2,2,2,256,128]{4,3,2,1,0:T(8,128)(2,1)}, bf16[2,2,2,256,128]{4,3,2,1,0:T(8,128)(2,1)S(1)}, u32[]{:S(2)}) copy-start(bf16[2,2,2,256,128]{4,3,2,1,0:T(8,128)(2,1)S(1)} %collective-permute-done.4.refs_8_) | copy-start | bytes 1572868
  60.4 1.3 %copy-start.14 = (bf16[2,2,2,256,128]{4,3,2,1,0:T(8,128)(2,1)}, bf16[2,2,2,256,128]{4,3,2,1,0:T(8,128)(2,1)S(1)}, u32[]{:S(2)}) copy-start(bf16[2,2,2,256,128]{4,3,2,1,0:T(8,128)(2,1)S(1)} %collective-permute-done.8.refs_9_) | copy-start | bytes 1572868
  61.8 25.3 %copy-start.3 = (bf16[2,2,2,256,128]{4,3,2,1,0:T(8,128)(2,1)}, bf16[2,2,2,256,128]{4,3,2,1,0:T(8,128)(2,1)S(1)}, u32[]{:S(2)}) copy-start(bf16[2,2,2,256,128]{4,3,2,1,0:T(8,128)(2,1)S(1)} %shard_map.50.refs_7_) | copy-start | bytes 1572868
  62.7 24.3 %collective-permute-start.9 = (bf16[2,2,2,256,128]{4,3,2,1,0:T(8,128)(2,1)}, bf16[2,2,2,256,128]{4,3,2,1,0:T(8,128)(2,1)S(1)}, u32[]{:S(2)}, u32[]{:S(2)}) collective-permute-start(bf16[2,2,2,256,128]{4,3,2,1,0:T(8,128)(2,1)} %broadcast_select_fusion), channel_id=1, source_target_pairs={{0,4},{2,6},{4,0},{6,2},{8,12},{10,14},{12,8},{14,10},{16,20},{18,... | collective-permute-start | bytes 1572872 | tf_op jit(solution)/shard_map/extra1/ppermute | solution.py:21
  64.9 0.7 copy-start.10
  87.1 0.8 copy-start.13
  87.1 0.7 copy-start.9
  87.8 0.9 copy-start.5
  87.8 2.5 %copy-start.17 = (bf16[2,256,256]{2,1,0:T(8,128)(2,1)S(1)}, bf16[2,256,256]{2,1,0:T(8,128)(2,1)}, u32[]{:S(2)}) copy-start(bf16[2,256,256]{2,1,0:T(8,128)(2,1)} %get-tuple-element.14) | copy-start | bytes 786436
  87.9 26.8 %collective-permute-start.15 = (bf16[512,2048]{1,0:T(8,128)(2,1)}, bf16[512,2048]{1,0:T(8,128)(2,1)S(1)}, u32[]{:S(2)}, u32[]{:S(2)}) collective-permute-start(bf16[512,2048]{1,0:T(8,128)(2,1)} %shard_map.53.refs_9_.refs_2_), channel_id=1, source_target_pairs={{0,2},{2,0},{4,6},{6,4},{8,10},{10,8},{12,14},{14,12},{16,18},{18,... | collective-permute-start | bytes 6291464 | tf_op jit(solution)/shard_map/panel_pair/ppermute | solution.py:21
  88.7 25.0 %collective-permute-start.17 = (bf16[2,256,256]{2,1,0:T(8,128)(2,1)S(1)}, bf16[2,256,256]{2,1,0:T(8,128)(2,1)S(1)}, u32[]{:S(2)}, u32[]{:S(2)}) collective-permute-start(bf16[2,256,256]{2,1,0:T(8,128)(2,1)S(1)} %copy-done.5), channel_id=1, source_target_pairs={{0,1},{1,0},{2,3},{3,2},{4,5},{5,4},{6,7},{7,6},{8,9},{9,8},{10,11... | collective-permute-start | bytes 786440 | tf_op jit(solution)/shard_map/same0/ppermute | solution.py:27
  90.3 24.5 %copy-start.8 = (s32[3]{0:T(128)S(1)}, s32[3]{0:T(128)}, u32[]{:S(2)}) copy-start(s32[3]{0:T(128)} %pad_add_fusion.2.info.refs_0_) | copy-start | bytes 40
  90.3 24.0 %collective-permute-start.18 = (bf16[2,256,256]{2,1,0:T(8,128)(2,1)S(1)}, bf16[2,256,256]{2,1,0:T(8,128)(2,1)S(1)}, u32[]{:S(2)}, u32[]{:S(2)}) collective-permute-start(bf16[2,256,256]{2,1,0:T(8,128)(2,1)S(1)} %copy-done.17), channel_id=1, source_target_pairs={{0,3},{1,2},{2,1},{3,0},{4,7},{5,6},{6,5},{7,4},{8,11},{9,10},{10,... | collective-permute-start | bytes 786440 | tf_op jit(solution)/shard_map/cross0/ppermute | solution.py:27
  90.3 24.5 %collective-permute-start.16 = (bf16[2,256,256]{2,1,0:T(8,128)(2,1)S(1)}, bf16[2,256,256]{2,1,0:T(8,128)(2,1)S(1)}, u32[]{:S(2)}, u32[]{:S(2)}) collective-permute-start(bf16[2,256,256]{2,1,0:T(8,128)(2,1)S(1)} %copy-done.17), channel_id=1, source_target_pairs={{0,2},{2,0},{4,6},{6,4},{8,10},{10,8},{12,14},{14,12},{16,18},{18,... | collective-permute-start | bytes 786440 | tf_op jit(solution)/shard_map/pair0/ppermute | solution.py:21
  112.5 9.0 %collective-permute-start.14 = (bf16[2,256,256]{2,1,0:T(8,128)(2,1)}, bf16[2,256,256]{2,1,0:T(8,128)(2,1)S(1)}, u32[]{:S(2)}, u32[]{:S(2)}) collective-permute-start(bf16[2,256,256]{2,1,0:T(8,128)(2,1)} %get-tuple-element.12), channel_id=1, source_target_pairs={{0,3},{1,2},{2,1},{3,0},{4,7},{5,6},{6,5},{7,4},{8,11},{9,10},{10,... | collective-permute-start | bytes 786440 | tf_op jit(solution)/shard_map/cross1/ppermute | solution.py:27
  113.7 7.9 %collective-permute-start.13 = (bf16[2,256,256]{2,1,0:T(8,128)(2,1)}, bf16[2,256,256]{2,1,0:T(8,128)(2,1)S(1)}, u32[]{:S(2)}, u32[]{:S(2)}) collective-permute-start(bf16[2,256,256]{2,1,0:T(8,128)(2,1)} %get-tuple-element.12), channel_id=1, source_target_pairs={{0,2},{2,0},{4,6},{6,4},{8,10},{10,8},{12,14},{14,12},{16,18},{18,... | collective-permute-start | bytes 786440 | tf_op jit(solution)/shard_map/pair1/ppermute | solution.py:21
  114.2 13.4 %collective-permute-start.11 = (bf16[2,256,256]{2,1,0:T(8,128)(2,1)}, bf16[2,256,256]{2,1,0:T(8,128)(2,1)S(1)}, u32[]{:S(2)}, u32[]{:S(2)}) collective-permute-start(bf16[2,256,256]{2,1,0:T(8,128)(2,1)} %get-tuple-element.11.refs_2_), channel_id=1, source_target_pairs={{0,1},{1,0},{2,3},{3,2},{4,5},{5,4},{6,7},{7,6},{8,9},{9,8},{10,11... | collective-permute-start | bytes 786440 | tf_op jit(solution)/shard_map/same1/ppermute | solution.py:27
  114.8 1.0 copy-start.6

commit v14 on v13

--- a/solution.py
+++ b/solution.py
@@ -239,7 +239,7 @@
             ],
         ),
         out_shape=[out, out, jax.ShapeDtypeStruct((8, HD), jnp.float32)],
-        compiler_params=pltpu.CompilerParams(vmem_limit_bytes=VMEM),
+        compiler_params=pltpu.CompilerParams(vmem_limit_bytes=24 * 1024 * 1024),
         cost_estimate=pl.CostEstimate(
             flops=work * 8, bytes_accessed=count * 64 * 1024, transcendentals=0
         ),
@@ -259,7 +259,7 @@
 
 def project(info, pieces, weights, features, dtype, before=None):
     tokens = pieces[0][2].shape[1]
-    tile = min(512 if before is None else 256, features)
+    tile = min(512 if before is None else 1024, features)
     steps = features // tile
     half = weights[0].shape[0] // 2
     used, specs = [], []

time: 135 us -> 130 us (0.963)
  Pallas kernels: 69 us -> 61.3 us
  local copies, waits for them, and re-layouts: 4.33 us -> 7.1 us
    pallas_call x3, Pallas kernels: 18.6 us -> 12.7 us  [project(): pl.pallas_call(lambda *refs: project_kernel(len(flat), len(used), before...]
    ppermute x5, waiting for transfers between devices: 0.01 us -> 2.87 us  [moved_both(): return lax.ppermute(array, ('ctx', 'fsdp'), pairs)]
    ppermute x14, waiting for transfers between devices: 29.7 us -> 27.4 us  [moved(): return lax.ppermute(array, 'ctx', pairs)]
    unnamed x37 -> x31, local copies, waits for them, and re-layouts: 3.29 us -> 5.38 us
    pallas_call x2, Pallas kernels: 43.1 us -> 41.4 us  [attend(): pl.pallas_call(lambda *refs: attend_kernel(tokens, *refs), grid_spec=pltp...]
  transfers between devices with their start and end apart: 19 -> 19, of which waited for: 6 -> 8; matrix products, arithmetic and copies ran while one was open for 2% -> 3% of each run, Pallas kernels for 45% -> 43%
where the time goes in v14:
time: 130 us
  Pallas kernels  61.3 us (47%)
  waiting for transfers between devices  30.2 us (23%)
  starting transfers between devices  29 us (22%)
  local copies, waits for them, and re-layouts  7.1 us (5%)
  other arithmetic  1.95 us (2%)
    pallas_call x2, Pallas kernels, attend(): pl.pallas_call(lambda *refs: attend_kernel(tokens, *refs), grid_spec=pltp...  41.4 us
    ppermute x14, waiting for transfers between devices, moved(): return lax.ppermute(array, 'ctx', pairs)  27.4 us
    ppermute x14, starting transfers between devices, moved(): return lax.ppermute(array, 'ctx', pairs)  23.8 us
    pallas_call x3, Pallas kernels, project(): pl.pallas_call(lambda *refs: project_kernel(len(flat), len(used), before...  12.7 us
    pallas_call x3, Pallas kernels, copies(): pl.pallas_call(kernel, grid_spec=pltpu.PrefetchScalarGridSpec(num_scalar_...  7.27 us
    unnamed x31, local copies, waits for them, and re-layouts  5.38 us
    ppermute x5, starting transfers between devices, moved_both(): return lax.ppermute(array, ('ctx', 'fsdp'), pairs)  5.17 us
    ppermute x5, waiting for transfers between devices, moved_both(): return lax.ppermute(array, ('ctx', 'fsdp'), pairs)  2.87 us
  transfers between devices with their start and end apart: 19, of which 8 were waited for; matrix products, arithmetic and copies ran while one was open for 3% of the time, Pallas kernels for 43%

profile of v14, /device:TPU:0, one launch (start us, length us, event | category | flops | bytes accessed | tf_op | source)
XLA Modules:
  0.0 129.8 jit_solution(10121726737482463167)
XLA Ops:
  0.0 0.5 collective-permute-start.1
  0.5 0.7 pad_add_fusion.2.info.refs_0_
  1.1 3.5 %shard_map.46.refs_2_ = bf16[512,2048]{1,0:T(8,128)(2,1)} custom-call(s32[3]{0:T(128)} %pad_add_fusion.2.info.refs_0_, bf16[1024,4096]{1,0:T(8,128)(2,1)} %refs_3_.1), custom_call_target="tpu_custom_call" | custom-call | bytes 1048576 | tf_op jit(solution)/shard_map/pallas_call | solution.py:89
  4.6 1.9 %shard_map.47.refs_2_.refs_5_ = bf16[2,2,2,256,128]{4,3,2,1,0:T(8,128)(2,1)S(1)} custom-call(s32[3]{0:T(128)S(1)} %copy-done.13, bf16[2,2,256,1024]{3,2,1,0:T(8,128)(2,1)S(1)} %copy-done, bf16[2,2,256,1024]{3,2,1,0:T(8,128)(2,1)} %collective-permute-done.1.refs_1_.refs_4_, bf16[512,2048]{1,0:T(8,128)(2,1)} %shard_map.46.refs_2_), custom_call_target="tpu_custom_call" | custom-call | bytes 262144 | tf_op jit(solution)/shard_map/pallas_call | solution.py:89
  6.6 5.6 %collective-permute-start.5 = (bf16[2,2,2,256,128]{4,3,2,1,0:T(8,128)(2,1)S(1)}, bf16[2,2,2,256,128]{4,3,2,1,0:T(8,128)(2,1)}, u32[]{:S(2)}, u32[]{:S(2)}) collective-permute-start(bf16[2,2,2,256,128]{4,3,2,1,0:T(8,128)(2,1)S(1)} %shard_map.47.refs_2_.refs_5_), channel_id=1, source_target_pairs={{0,8},{2,10},{4,12},{6,14},{8,16},{10,18},{12,20},{14,22},{16,24},... | collective-permute-start | bytes 1572872 | tf_op jit(solution)/shard_map/near0/ppermute | solution.py:21
  12.2 1.5 %collective-permute-start.12 = (bf16[512,2048]{1,0:T(8,128)(2,1)}, bf16[512,2048]{1,0:T(8,128)(2,1)}, u32[]{:S(2)}, u32[]{:S(2)}) collective-permute-start(bf16[512,2048]{1,0:T(8,128)(2,1)} %shard_map.46.refs_2_), channel_id=1, source_target_pairs={{0,1},{1,0},{2,3},{3,2},{4,5},{5,4},{6,7},{7,6},{8,9},{9,8},{10,11... | collective-permute-start | bytes 6291464 | tf_op jit(solution)/shard_map/panel/ppermute | solution.py:27
  13.7 1.9 %shard_map.48.refs_5_ = bf16[2,2,2,256,128]{4,3,2,1,0:T(8,128)(2,1)S(1)} custom-call(s32[3]{0:T(128)S(1)} %copy-done.13, bf16[2,2,256,1024]{3,2,1,0:T(8,128)(2,1)S(1)} %copy-done, bf16[2,2,256,1024]{3,2,1,0:T(8,128)(2,1)} %collective-permute-done.1.refs_1_.refs_4_, bf16[2,2,2,256,128]{4,3,2,1,0:T(8,128)(2,1)S(1)} %shard_map.47.refs_2_.refs_5_), custom_call_target="tpu_custom_call" | custom-call | bytes 262144 | tf_op jit(solution)/shard_map/pallas_call | solution.py:89
  15.6 2.8 %collective-permute-start.2 = (bf16[2,2,2,256,128]{4,3,2,1,0:T(8,128)(2,1)S(1)}, bf16[2,2,2,256,128]{4,3,2,1,0:T(8,128)(2,1)S(1)}, u32[]{:S(2)}, u32[]{:S(2)}) collective-permute-start(bf16[2,2,2,256,128]{4,3,2,1,0:T(8,128)(2,1)S(1)} %shard_map.48.refs_5_), channel_id=1, source_target_pairs={{0,8},{2,10},{4,12},{6,14},{8,16},{10,18},{12,20},{14,22},{16,24},... | collective-permute-start | bytes 1572872 | tf_op jit(solution)/shard_map/near1/ppermute | solution.py:21
  18.4 5.2 %collective-permute-done.5.refs_6_ = bf16[2,2,2,256,128]{4,3,2,1,0:T(8,128)(2,1)} collective-permute-done((bf16[2,2,2,256,128]{4,3,2,1,0:T(8,128)(2,1)S(1)}, bf16[2,2,2,256,128]{4,3,2,1,0:T(8,128)(2,1)}, u32[]{:S(2)}, u32[]{:S(2)}) %collective-permute-start.5) | collective-permute-done | bytes 524320 | tf_op jit(solution)/shard_map/near0/ppermute | solution.py:21
  23.6 1.5 %collective-permute-start.7 = (bf16[2,2,2,256,128]{4,3,2,1,0:T(8,128)(2,1)}, bf16[2,2,2,256,128]{4,3,2,1,0:T(8,128)(2,1)S(1)}, u32[]{:S(2)}, u32[]{:S(2)}) collective-permute-start(bf16[2,2,2,256,128]{4,3,2,1,0:T(8,128)(2,1)} %collective-permute-done.5.refs_6_), channel_id=1, source_target_pairs={{0,4},{2,6},{4,0},{6,2},{8,12},{10,14},{12,8},{14,10},{16,20},{18,... | collective-permute-start | bytes 1572872 | tf_op jit(solution)/shard_map/nearx0/ppermute | solution.py:21
  25.1 4.5 %collective-permute-start.6 = (bf16[2,2,2,256,128]{4,3,2,1,0:T(8,128)(2,1)}, bf16[2,2,2,256,128]{4,3,2,1,0:T(8,128)(2,1)S(1)}, u32[]{:S(2)}, u32[]{:S(2)}) collective-permute-start(bf16[2,2,2,256,128]{4,3,2,1,0:T(8,128)(2,1)} %collective-permute-done.5.refs_6_), channel_id=1, source_target_pairs={{0,8},{2,10},{4,12},{6,14},{8,16},{10,18},{12,20},{14,22},{16,24},... | collective-permute-start | bytes 1572872 | tf_op jit(solution)/shard_map/far0/ppermute | solution.py:21
  29.7 5.1 %collective-permute-done.2.refs_6_ = bf16[2,2,2,256,128]{4,3,2,1,0:T(8,128)(2,1)S(1)} collective-permute-done((bf16[2,2,2,256,128]{4,3,2,1,0:T(8,128)(2,1)S(1)}, bf16[2,2,2,256,128]{4,3,2,1,0:T(8,128)(2,1)S(1)}, u32[]{:S(2)}, u32[]{:S(2)}) %collective-permute-start.2) | collective-permute-done | bytes 524320 | tf_op jit(solution)/shard_map/near1/ppermute | solution.py:21
  34.9 1.4 %collective-permute-done.7.refs_8_ = bf16[2,2,2,256,128]{4,3,2,1,0:T(8,128)(2,1)S(1)} collective-permute-done((bf16[2,2,2,256,128]{4,3,2,1,0:T(8,128)(2,1)}, bf16[2,2,2,256,128]{4,3,2,1,0:T(8,128)(2,1)S(1)}, u32[]{:S(2)}, u32[]{:S(2)}) %collective-permute-start.7) | collective-permute-done | bytes 524320 | tf_op jit(solution)/shard_map/nearx0/ppermute | solution.py:21
  36.3 1.5 %collective-permute-start.4 = (bf16[2,2,2,256,128]{4,3,2,1,0:T(8,128)(2,1)S(1)}, bf16[2,2,2,256,128]{4,3,2,1,0:T(8,128)(2,1)S(1)}, u32[]{:S(2)}, u32[]{:S(2)}) collective-permute-start(bf16[2,2,2,256,128]{4,3,2,1,0:T(8,128)(2,1)S(1)} %collective-permute-done.2.refs_6_), channel_id=1, source_target_pairs={{0,4},{2,6},{4,0},{6,2},{8,12},{10,14},{12,8},{14,10},{16,20},{18,... | collective-permute-start | bytes 1572872 | tf_op jit(solution)/shard_map/nearx1/ppermute | solution.py:21
  37.8 0.8 copy-done.7
  38.6 6.8 %collective-permute-done.6.refs_0_ = bf16[2,2,2,256,128]{4,3,2,1,0:T(8,128)(2,1)S(1)} collective-permute-done((bf16[2,2,2,256,128]{4,3,2,1,0:T(8,128)(2,1)}, bf16[2,2,2,256,128]{4,3,2,1,0:T(8,128)(2,1)S(1)}, u32[]{:S(2)}, u32[]{:S(2)}) %collective-permute-start.6) | collective-permute-done | bytes 524320 | tf_op jit(solution)/shard_map/far0/ppermute | solution.py:21
  45.5 1.6 %collective-permute-start.8 = (bf16[2,2,2,256,128]{4,3,2,1,0:T(8,128)(2,1)S(1)}, bf16[2,2,2,256,128]{4,3,2,1,0:T(8,128)(2,1)S(1)}, u32[]{:S(2)}, u32[]{:S(2)}) collective-permute-start(bf16[2,2,2,256,128]{4,3,2,1,0:T(8,128)(2,1)S(1)} %broadcast_select_fusion.1), channel_id=1, source_target_pairs={{0,4},{2,6},{4,0},{6,2},{8,12},{10,14},{12,8},{14,10},{16,20},{18,... | collective-permute-start | bytes 1572872 | tf_op jit(solution)/shard_map/extra0/ppermute | solution.py:21
  47.1 4.3 %collective-permute-start.3 = (bf16[2,2,2,256,128]{4,3,2,1,0:T(8,128)(2,1)S(1)}, bf16[2,2,2,256,128]{4,3,2,1,0:T(8,128)(2,1)S(1)}, u32[]{:S(2)}, u32[]{:S(2)}) collective-permute-start(bf16[2,2,2,256,128]{4,3,2,1,0:T(8,128)(2,1)S(1)} %collective-permute-done.2.refs_6_), channel_id=1, source_target_pairs={{0,8},{2,10},{4,12},{6,14},{8,16},{10,18},{12,20},{14,22},{16,24},... | collective-permute-start | bytes 1572872 | tf_op jit(solution)/shard_map/far1/ppermute | solution.py:21
  51.4 0.8 copy-done.11
  52.2 0.1 fusion.3
  52.3 8.1 %collective-permute-done.8.refs_9_ = bf16[2,2,2,256,128]{4,3,2,1,0:T(8,128)(2,1)S(1)} collective-permute-done((bf16[2,2,2,256,128]{4,3,2,1,0:T(8,128)(2,1)S(1)}, bf16[2,2,2,256,128]{4,3,2,1,0:T(8,128)(2,1)S(1)}, u32[]{:S(2)}, u32[]{:S(2)}) %collective-permute-start.8) | collective-permute-done | bytes 524320 | tf_op jit(solution)/shard_map/extra0/ppermute | solution.py:21
  60.4 0.8 copy-done.9
  61.2 0.7 collective-permute-done.3.refs_0_
  61.9 0.9 broadcast_select_fusion
  62.7 0.8 copy-done.1
  63.6 0.8 collective-permute-start.9
  64.7 0.1 copy.18
  64.9 0.1 copy.16
  65.0 0.1 broadcast_in_dim.16
  65.1 0.2 stack_reshape.6
  65.3 0.1 broadcast_in_dim.17
  65.5 0.2 stack_reshape.7
  65.7 1.0 copy-done.8
  66.7 1.0 copy-done.10
  67.7 20.3 %shard_map.51 = (bf16[2,256,256]{2,1,0:T(8,128)(2,1)S(1)}, bf16[2,256,256]{2,1,0:T(8,128)(2,1)S(1)}, f32[8,128]{1,0:T(8,128)S(1)}) custom-call(s32[3]{0:T(128)S(1)} %copy-done.13, bf16[2,256,1024]{2,1,0:T(8,128)(2,1)} %refs_1_.3, bf16[2,2,256,1024]{3,2,1,0:T(8,128)(2,1)S(1)} %copy-done, bf16[2,256,1024]{2,1,0:T(8,128)(2,1)} %collective-permute-done.refs_3_, ...), custom_call_target="tpu_custom_call" | custom-call | flops 41943040 | bytes 131072 | tf_op jit(solution)/shard_map/pallas_call | solution.py:224
  88.1 0.7 slice_bitcast_fusion.refs_1_
  88.8 1.6 %collective-permute-start.17 = (bf16[2,256,256]{2,1,0:T(8,128)(2,1)S(1)}, bf16[2,256,256]{2,1,0:T(8,128)(2,1)S(1)}, u32[]{:S(2)}, u32[]{:S(2)}) collective-permute-start(bf16[2,256,256]{2,1,0:T(8,128)(2,1)S(1)} %get-tuple-element.13.refs_1_), channel_id=1, source_target_pairs={{0,1},{1,0},{2,3},{3,2},{4,5},{5,4},{6,7},{7,6},{8,9},{9,8},{10,11... | collective-permute-start | bytes 786440 | tf_op jit(solution)/shard_map/same0/ppermute | solution.py:27
  90.4 0.3 collective-permute-start.18
  90.7 0.3 collective-permute-start.16
  91.1 21.1 %shard_map.52 = (bf16[2,256,256]{2,1,0:T(8,128)(2,1)S(1)}, bf16[2,256,256]{2,1,0:T(8,128)(2,1)S(1)}, f32[8,128]{1,0:T(8,128)}) custom-call(s32[3]{0:T(128)S(1)} %copy-done.13, bf16[2,256,1024]{2,1,0:T(8,128)(2,1)} %refs_1_.3, bf16[2,2,256,1024]{3,2,1,0:T(8,128)(2,1)S(1)} %copy-done, bf16[2,256,1024]{2,1,0:T(8,128)(2,1)} %collective-permute-done.refs_3_, ...), custom_call_target="tpu_custom_call" | custom-call | flops 41943040 | bytes 131072 | tf_op jit(solution)/shard_map/pallas_call | solution.py:224
  112.1 1.3 collective-permute-start.14
  113.4 0.4 collective-permute-start.13
  113.8 0.5 collective-permute-start.11
  114.3 5.8 %shard_map.54.refs_5_ = f32[2,256,2048]{2,1,0:T(8,128)S(1)} custom-call(s32[3]{0:T(128)S(1)} %copy-done.13, bf16[2,256,256]{2,1,0:T(8,128)(2,1)S(1)} %get-tuple-element.13.refs_1_, bf16[2,256,256]{2,1,0:T(8,128)(2,1)S(1)} %get-tuple-element.11.refs_2_, bf16[2,256,256]{2,1,0:T(8,128)(2,1)S(1)} %collective-permute-done.16.refs_3_, ...), custom_call_target="tpu_custom_call" | custom-call | flops 335544320 | bytes 655360 | tf_op jit(solution)/shard_map/pallas_call | solution.py:287
  120.1 0.3 collective-permute-done.14.refs_2_
  120.4 3.3 %shard_map.55.refs_3_ = f32[2,256,2048]{2,1,0:T(8,128)S(1)} custom-call(s32[3]{0:T(128)S(1)} %copy-done.13, bf16[2,256,256]{2,1,0:T(8,128)(2,1)S(1)} %collective-permute-done.13.refs_1_, bf16[2,256,256]{2,1,0:T(8,128)(2,1)S(1)} %collective-permute-done.14.refs_2_, bf16[1024,4096]{1,0:T(8,128)(2,1)} %refs_3_.1, ...), custom_call_target="tpu_custom_call" | custom-call | flops 134217728 | bytes 262144 | tf_op jit(solution)/shard_map/pallas_call | solution.py:287
  123.7 2.6 %collective-permute-done.11.refs_1_ = bf16[2,256,256]{2,1,0:T(8,128)(2,1)S(1)} collective-permute-done((bf16[2,256,256]{2,1,0:T(8,128)(2,1)S(1)}, bf16[2,256,256]{2,1,0:T(8,128)(2,1)S(1)}, u32[]{:S(2)}, u32[]{:S(2)}) %collective-permute-start.11) | collective-permute-done | bytes 262176 | tf_op jit(solution)/shard_map/same1/ppermute | solution.py:27
  126.4 3.5 %shard_map.56 = bf16[2,256,2048]{2,1,0:T(8,128)(2,1)} custom-call(s32[3]{0:T(128)S(1)} %copy-done.13, bf16[2,256,256]{2,1,0:T(8,128)(2,1)S(1)} %collective-permute-done.11.refs_1_, bf16[512,2048]{1,0:T(8,128)(2,1)} %shard_map.53.refs_9_.refs_2_, f32[2,256,2048]{2,1,0:T(8,128)S(1)} %shard_map.55.refs_3_), custom_call_target="tpu_custom_call" | custom-call | flops 67108864 | bytes 131072 | tf_op jit(solution)/shard_map/pallas_call | solution.py:287
  (57 shorter events, 0.6 us)
Async XLA Ops:
  0.0 4.6 %collective-permute-start.1 = (bf16[2,2,256,1024]{3,2,1,0:T(8,128)(2,1)}, bf16[2,2,256,1024]{3,2,1,0:T(8,128)(2,1)}, u32[]{:S(2)}, u32[]{:S(2)}) collective-permute-start(bf16[2,2,256,1024]{3,2,1,0:T(8,128)(2,1)} %refs_2_.3), channel_id=1, source_target_pairs={{0,2},{2,0},{4,6},{6,4},{8,10},{10,8},{12,14},{14,12},{16,18},{18,... | collective-permute-start | bytes 6291464 | tf_op jit(solution)/shard_map/pair_kv/ppermute | solution.py:21
  1.1 3.5 %copy-start = (bf16[2,2,256,1024]{3,2,1,0:T(8,128)(2,1)S(1)}, bf16[2,2,256,1024]{3,2,1,0:T(8,128)(2,1)}, u32[]{:S(2)}) copy-start(bf16[2,2,256,1024]{3,2,1,0:T(8,128)(2,1)} %refs_2_.3) | copy-start | bytes 6291460
  1.1 3.5 %copy-start.13 = (s32[3]{0:T(128)S(1)}, s32[3]{0:T(128)}, u32[]{:S(2)}) copy-start(s32[3]{0:T(128)} %pad_add_fusion.2.info.refs_0_) | copy-start | bytes 40
  4.6 9.1 %copy-start.14 = (s32[4,32]{1,0:T(4,128)S(1)}, s32[4,32]{1,0:T(4,128)}, u32[]{:S(2)}) copy-start(s32[4,32]{1,0:T(4,128)} %param.6) | copy-start | bytes 1540
  6.6 17.1 %collective-permute-start.5 = (bf16[2,2,2,256,128]{4,3,2,1,0:T(8,128)(2,1)S(1)}, bf16[2,2,2,256,128]{4,3,2,1,0:T(8,128)(2,1)}, u32[]{:S(2)}, u32[]{:S(2)}) collective-permute-start(bf16[2,2,2,256,128]{4,3,2,1,0:T(8,128)(2,1)S(1)} %shard_map.47.refs_2_.refs_5_), channel_id=1, source_target_pairs={{0,8},{2,10},{4,12},{6,14},{8,16},{10,18},{12,20},{14,22},{16,24},... | collective-permute-start | bytes 1572872 | tf_op jit(solution)/shard_map/near0/ppermute | solution.py:21
  12.2 76.6 %collective-permute-start.12 = (bf16[512,2048]{1,0:T(8,128)(2,1)}, bf16[512,2048]{1,0:T(8,128)(2,1)}, u32[]{:S(2)}, u32[]{:S(2)}) collective-permute-start(bf16[512,2048]{1,0:T(8,128)(2,1)} %shard_map.46.refs_2_), channel_id=1, source_target_pairs={{0,1},{1,0},{2,3},{3,2},{4,5},{5,4},{6,7},{7,6},{8,9},{9,8},{10,11... | collective-permute-start | bytes 6291464 | tf_op jit(solution)/shard_map/panel/ppermute | solution.py:27
  13.7 33.4 %collective-permute-start.10 = (s32[4,32]{1,0:T(4,128)S(1)}, s32[4,32]{1,0:T(4,128)S(1)}, u32[]{:S(2)}, u32[]{:S(2)}) collective-permute-start(s32[4,32]{1,0:T(4,128)S(1)} %copy-done.14), channel_id=1, source_target_pairs={{0,2},{2,0},{4,6},{6,4},{8,10},{10,8},{12,14},{14,12},{16,18},{18,... | collective-permute-start | bytes 1544 | tf_op jit(solution)/shard_map/pair_mask/ppermute | solution.py:21
  15.6 47.1 %copy-start.3 = (bf16[2,2,2,256,128]{4,3,2,1,0:T(8,128)(2,1)}, bf16[2,2,2,256,128]{4,3,2,1,0:T(8,128)(2,1)S(1)}, u32[]{:S(2)}) copy-start(bf16[2,2,2,256,128]{4,3,2,1,0:T(8,128)(2,1)S(1)} %shard_map.48.refs_5_) | copy-start | bytes 1572868
  15.6 19.2 %collective-permute-start.2 = (bf16[2,2,2,256,128]{4,3,2,1,0:T(8,128)(2,1)S(1)}, bf16[2,2,2,256,128]{4,3,2,1,0:T(8,128)(2,1)S(1)}, u32[]{:S(2)}, u32[]{:S(2)}) collective-permute-start(bf16[2,2,2,256,128]{4,3,2,1,0:T(8,128)(2,1)S(1)} %shard_map.48.refs_5_), channel_id=1, source_target_pairs={{0,8},{2,10},{4,12},{6,14},{8,16},{10,18},{12,20},{14,22},{16,24},... | collective-permute-start | bytes 1572872 | tf_op jit(solution)/shard_map/near1/ppermute | solution.py:21
  23.6 12.7 %collective-permute-start.7 = (bf16[2,2,2,256,128]{4,3,2,1,0:T(8,128)(2,1)}, bf16[2,2,2,256,128]{4,3,2,1,0:T(8,128)(2,1)S(1)}, u32[]{:S(2)}, u32[]{:S(2)}) collective-permute-start(bf16[2,2,2,256,128]{4,3,2,1,0:T(8,128)(2,1)} %collective-permute-done.5.refs_6_), channel_id=1, source_target_pairs={{0,4},{2,6},{4,0},{6,2},{8,12},{10,14},{12,8},{14,10},{16,20},{18,... | collective-permute-start | bytes 1572872 | tf_op jit(solution)/shard_map/nearx0/ppermute | solution.py:21
  25.1 20.3 %collective-permute-start.6 = (bf16[2,2,2,256,128]{4,3,2,1,0:T(8,128)(2,1)}, bf16[2,2,2,256,128]{4,3,2,1,0:T(8,128)(2,1)S(1)}, u32[]{:S(2)}, u32[]{:S(2)}) collective-permute-start(bf16[2,2,2,256,128]{4,3,2,1,0:T(8,128)(2,1)} %collective-permute-done.5.refs_6_), channel_id=1, source_target_pairs={{0,8},{2,10},{4,12},{6,14},{8,16},{10,18},{12,20},{14,22},{16,24},... | collective-permute-start | bytes 1572872 | tf_op jit(solution)/shard_map/far0/ppermute | solution.py:21
  34.9 30.8 %collective-permute-start = (bf16[2,256,1024]{2,1,0:T(8,128)(2,1)}, bf16[2,256,1024]{2,1,0:T(8,128)(2,1)}, u32[]{:S(2)}, u32[]{:S(2)}) collective-permute-start(bf16[2,256,1024]{2,1,0:T(8,128)(2,1)} %refs_1_.3), channel_id=1, source_target_pairs={{0,2},{2,0},{4,6},{6,4},{8,10},{10,8},{12,14},{14,12},{16,18},{18,... | collective-permute-start | bytes 3145736 | tf_op jit(solution)/shard_map/pair_q/ppermute | solution.py:21
  36.3 16.0 %collective-permute-start.4 = (bf16[2,2,2,256,128]{4,3,2,1,0:T(8,128)(2,1)S(1)}, bf16[2,2,2,256,128]{4,3,2,1,0:T(8,128)(2,1)S(1)}, u32[]{:S(2)}, u32[]{:S(2)}) collective-permute-start(bf16[2,2,2,256,128]{4,3,2,1,0:T(8,128)(2,1)S(1)} %collective-permute-done.2.refs_6_), channel_id=1, source_target_pairs={{0,4},{2,6},{4,0},{6,2},{8,12},{10,14},{12,8},{14,10},{16,20},{18,... | collective-permute-start | bytes 1572872 | tf_op jit(solution)/shard_map/nearx1/ppermute | solution.py:21
  37.8 0.8 copy-start.7
  45.5 14.9 %collective-permute-start.8 = (bf16[2,2,2,256,128]{4,3,2,1,0:T(8,128)(2,1)S(1)}, bf16[2,2,2,256,128]{4,3,2,1,0:T(8,128)(2,1)S(1)}, u32[]{:S(2)}, u32[]{:S(2)}) collective-permute-start(bf16[2,2,2,256,128]{4,3,2,1,0:T(8,128)(2,1)S(1)} %broadcast_select_fusion.1), channel_id=1, source_target_pairs={{0,4},{2,6},{4,0},{6,2},{8,12},{10,14},{12,8},{14,10},{16,20},{18,... | collective-permute-start | bytes 1572872 | tf_op jit(solution)/shard_map/extra0/ppermute | solution.py:21
  47.1 14.8 %collective-permute-start.3 = (bf16[2,2,2,256,128]{4,3,2,1,0:T(8,128)(2,1)S(1)}, bf16[2,2,2,256,128]{4,3,2,1,0:T(8,128)(2,1)S(1)}, u32[]{:S(2)}, u32[]{:S(2)}) collective-permute-start(bf16[2,2,2,256,128]{4,3,2,1,0:T(8,128)(2,1)S(1)} %collective-permute-done.2.refs_6_), channel_id=1, source_target_pairs={{0,8},{2,10},{4,12},{6,14},{8,16},{10,18},{12,20},{14,22},{16,24},... | collective-permute-start | bytes 1572872 | tf_op jit(solution)/shard_map/far1/ppermute | solution.py:21
  51.4 0.8 copy-start.11
  52.3 12.1 %copy-start.5 = (bf16[2,2,2,256,128]{4,3,2,1,0:T(8,128)(2,1)}, bf16[2,2,2,256,128]{4,3,2,1,0:T(8,128)(2,1)S(1)}, u32[]{:S(2)}) copy-start(bf16[2,2,2,256,128]{4,3,2,1,0:T(8,128)(2,1)S(1)} %collective-permute-done.4.refs_8_) | copy-start | bytes 1572868
  60.4 0.8 copy-start.9
  62.7 0.8 copy-start.1
  63.6 24.5 %collective-permute-start.9 = (bf16[2,2,2,256,128]{4,3,2,1,0:T(8,128)(2,1)}, bf16[2,2,2,256,128]{4,3,2,1,0:T(8,128)(2,1)}, u32[]{:S(2)}, u32[]{:S(2)}) collective-permute-start(bf16[2,2,2,256,128]{4,3,2,1,0:T(8,128)(2,1)} %broadcast_select_fusion), channel_id=1, source_target_pairs={{0,4},{2,6},{4,0},{6,2},{8,12},{10,14},{12,8},{14,10},{16,20},{18,... | collective-permute-start | bytes 1572872 | tf_op jit(solution)/shard_map/extra1/ppermute | solution.py:21
  65.7 1.0 copy-start.8
  66.7 1.0 copy-start.10
  88.7 2.3 %copy-start.2 = (bf16[2,2,2,256,128]{4,3,2,1,0:T(8,128)(2,1)S(1)}, bf16[2,2,2,256,128]{4,3,2,1,0:T(8,128)(2,1)}, u32[]{:S(2)}) copy-start(bf16[2,2,2,256,128]{4,3,2,1,0:T(8,128)(2,1)} %copy-done.1) | copy-start | bytes 1572868
  88.7 2.3 %copy-start.4 = (bf16[2,2,2,256,128]{4,3,2,1,0:T(8,128)(2,1)S(1)}, bf16[2,2,2,256,128]{4,3,2,1,0:T(8,128)(2,1)}, u32[]{:S(2)}) copy-start(bf16[2,2,2,256,128]{4,3,2,1,0:T(8,128)(2,1)} %copy-done.3) | copy-start | bytes 1572868
  88.7 2.3 %copy-start.6 = (bf16[2,2,2,256,128]{4,3,2,1,0:T(8,128)(2,1)S(1)}, bf16[2,2,2,256,128]{4,3,2,1,0:T(8,128)(2,1)}, u32[]{:S(2)}) copy-start(bf16[2,2,2,256,128]{4,3,2,1,0:T(8,128)(2,1)} %copy-done.5) | copy-start | bytes 1572868
  88.7 2.3 %copy-start.12 = (bf16[2,2,2,256,128]{4,3,2,1,0:T(8,128)(2,1)S(1)}, bf16[2,2,2,256,128]{4,3,2,1,0:T(8,128)(2,1)}, u32[]{:S(2)}) copy-start(bf16[2,2,2,256,128]{4,3,2,1,0:T(8,128)(2,1)} %copy-done.11) | copy-start | bytes 1572868
  88.8 25.5 %collective-permute-start.15 = (bf16[512,2048]{1,0:T(8,128)(2,1)}, bf16[512,2048]{1,0:T(8,128)(2,1)S(1)}, u32[]{:S(2)}, u32[]{:S(2)}) collective-permute-start(bf16[512,2048]{1,0:T(8,128)(2,1)} %shard_map.53.refs_9_.refs_2_), channel_id=1, source_target_pairs={{0,2},{2,0},{4,6},{6,4},{8,10},{10,8},{12,14},{14,12},{16,18},{18,... | collective-permute-start | bytes 6291464 | tf_op jit(solution)/shard_map/panel_pair/ppermute | solution.py:21
  88.8 24.6 %collective-permute-start.17 = (bf16[2,256,256]{2,1,0:T(8,128)(2,1)S(1)}, bf16[2,256,256]{2,1,0:T(8,128)(2,1)S(1)}, u32[]{:S(2)}, u32[]{:S(2)}) collective-permute-start(bf16[2,256,256]{2,1,0:T(8,128)(2,1)S(1)} %get-tuple-element.13.refs_1_), channel_id=1, source_target_pairs={{0,1},{1,0},{2,3},{3,2},{4,5},{5,4},{6,7},{7,6},{8,9},{9,8},{10,11... | collective-permute-start | bytes 786440 | tf_op jit(solution)/shard_map/same0/ppermute | solution.py:27
  90.4 23.3 %collective-permute-start.18 = (bf16[2,256,256]{2,1,0:T(8,128)(2,1)S(1)}, bf16[2,256,256]{2,1,0:T(8,128)(2,1)S(1)}, u32[]{:S(2)}, u32[]{:S(2)}) collective-permute-start(bf16[2,256,256]{2,1,0:T(8,128)(2,1)S(1)} %get-tuple-element.14), channel_id=1, source_target_pairs={{0,3},{1,2},{2,1},{3,0},{4,7},{5,6},{6,5},{7,4},{8,11},{9,10},{10,... | collective-permute-start | bytes 786440 | tf_op jit(solution)/shard_map/cross0/ppermute | solution.py:27
  90.7 23.6 %collective-permute-start.16 = (bf16[2,256,256]{2,1,0:T(8,128)(2,1)S(1)}, bf16[2,256,256]{2,1,0:T(8,128)(2,1)S(1)}, u32[]{:S(2)}, u32[]{:S(2)}) collective-permute-start(bf16[2,256,256]{2,1,0:T(8,128)(2,1)S(1)} %get-tuple-element.14), channel_id=1, source_target_pairs={{0,2},{2,0},{4,6},{6,4},{8,10},{10,8},{12,14},{14,12},{16,18},{18,... | collective-permute-start | bytes 786440 | tf_op jit(solution)/shard_map/pair0/ppermute | solution.py:21
  112.1 8.3 %collective-permute-start.14 = (bf16[2,256,256]{2,1,0:T(8,128)(2,1)S(1)}, bf16[2,256,256]{2,1,0:T(8,128)(2,1)S(1)}, u32[]{:S(2)}, u32[]{:S(2)}) collective-permute-start(bf16[2,256,256]{2,1,0:T(8,128)(2,1)S(1)} %get-tuple-element.12), channel_id=1, source_target_pairs={{0,3},{1,2},{2,1},{3,0},{4,7},{5,6},{6,5},{7,4},{8,11},{9,10},{10,... | collective-permute-start | bytes 786440 | tf_op jit(solution)/shard_map/cross1/ppermute | solution.py:27
  113.4 7.0 %collective-permute-start.13 = (bf16[2,256,256]{2,1,0:T(8,128)(2,1)S(1)}, bf16[2,256,256]{2,1,0:T(8,128)(2,1)S(1)}, u32[]{:S(2)}, u32[]{:S(2)}) collective-permute-start(bf16[2,256,256]{2,1,0:T(8,128)(2,1)S(1)} %get-tuple-element.12), channel_id=1, source_target_pairs={{0,2},{2,0},{4,6},{6,4},{8,10},{10,8},{12,14},{14,12},{16,18},{18,... | collective-permute-start | bytes 786440 | tf_op jit(solution)/shard_map/pair1/ppermute | solution.py:21
  113.8 12.6 %collective-permute-start.11 = (bf16[2,256,256]{2,1,0:T(8,128)(2,1)S(1)}, bf16[2,256,256]{2,1,0:T(8,128)(2,1)S(1)}, u32[]{:S(2)}, u32[]{:S(2)}) collective-permute-start(bf16[2,256,256]{2,1,0:T(8,128)(2,1)S(1)} %get-tuple-element.11.refs_2_), channel_id=1, source_target_pairs={{0,1},{1,0},{2,3},{3,2},{4,5},{5,4},{6,7},{7,6},{8,9},{9,8},{10,11... | collective-permute-start | bytes 786440 | tf_op jit(solution)/shard_map/same1/ppermute | solution.py:27

commit v15 on v14

--- a/solution.py
+++ b/solution.py
@@ -239,7 +239,7 @@
             ],
         ),
         out_shape=[out, out, jax.ShapeDtypeStruct((8, HD), jnp.float32)],
-        compiler_params=pltpu.CompilerParams(vmem_limit_bytes=24 * 1024 * 1024),
+        compiler_params=pltpu.CompilerParams(vmem_limit_bytes=20 * 1024 * 1024),
         cost_estimate=pl.CostEstimate(
             flops=work * 8, bytes_accessed=count * 64 * 1024, transcendentals=0
         ),
@@ -290,7 +290,7 @@
             num_scalar_prefetch=1, grid=(steps,), in_specs=specs, out_specs=spec
         ),
         out_shape=jax.ShapeDtypeStruct((2, tokens, features), dtype),
-        compiler_params=pltpu.CompilerParams(vmem_limit_bytes=40 * 1024 * 1024),
+        compiler_params=pltpu.CompilerParams(vmem_limit_bytes=24 * 1024 * 1024),
         cost_estimate=pl.CostEstimate(
             flops=2 * 2 * tokens * depth * features // 8,
             bytes_accessed=2 * depth * features // 8,

time: 130 us -> 131 us (level)
    unnamed x31 -> x35, local copies, waits for them, and re-layouts: 5.38 us -> 5.39 us
where the time goes in v15:
time: 131 us; the launch traced here: 130 us
  Pallas kernels  60.7 us (46%)
  waiting for transfers between devices  31.2 us (24%)
  starting transfers between devices  28.9 us (22%)
  local copies, waits for them, and re-layouts  7.12 us (5%)
  other arithmetic  1.93 us (1%)
    pallas_call x2, Pallas kernels, attend(): pl.pallas_call(lambda *refs: attend_kernel(tokens, *refs), grid_spec=pltp...  41.7 us
    ppermute x14, waiting for transfers between devices, moved(): return lax.ppermute(array, 'ctx', pairs)  27.3 us
    ppermute x14, starting transfers between devices, moved(): return lax.ppermute(array, 'ctx', pairs)  23.8 us
    pallas_call x3, Pallas kernels, project(): pl.pallas_call(lambda *refs: project_kernel(len(flat), len(used), before...  11.7 us
    pallas_call x3, Pallas kernels, copies(): pl.pallas_call(kernel, grid_spec=pltpu.PrefetchScalarGridSpec(num_scalar_...  7.27 us
    unnamed x35, local copies, waits for them, and re-layouts  5.39 us
    ppermute x5, starting transfers between devices, moved_both(): return lax.ppermute(array, ('ctx', 'fsdp'), pairs)  5.16 us
    ppermute x5, waiting for transfers between devices, moved_both(): return lax.ppermute(array, ('ctx', 'fsdp'), pairs)  3.81 us
  transfers between devices with their start and end apart: 19, of which 8 were waited for; matrix products, arithmetic and copies ran while one was open for 3% of the time, Pallas kernels for 43%

profile of v15, /device:TPU:0, one launch (start us, length us, event | category | flops | bytes accessed | tf_op | source)
XLA Modules:
  0.0 130.1 jit_solution(13416119496092321895)
XLA Ops:
  0.0 0.5 collective-permute-start.1
  0.5 0.7 pad_add_fusion.2.info.refs_0_
  1.1 3.5 %shard_map.46.refs_2_ = bf16[512,2048]{1,0:T(8,128)(2,1)} custom-call(s32[3]{0:T(128)} %pad_add_fusion.2.info.refs_0_, bf16[1024,4096]{1,0:T(8,128)(2,1)} %refs_3_.1), custom_call_target="tpu_custom_call" | custom-call | bytes 1048576 | tf_op jit(solution)/shard_map/pallas_call | solution.py:89
  4.6 1.9 %shard_map.47.refs_2_.refs_5_ = bf16[2,2,2,256,128]{4,3,2,1,0:T(8,128)(2,1)S(1)} custom-call(s32[3]{0:T(128)S(1)} %copy-done.13, bf16[2,2,256,1024]{3,2,1,0:T(8,128)(2,1)S(1)} %copy-done, bf16[2,2,256,1024]{3,2,1,0:T(8,128)(2,1)} %collective-permute-done.1.refs_1_.refs_4_, bf16[512,2048]{1,0:T(8,128)(2,1)} %shard_map.46.refs_2_), custom_call_target="tpu_custom_call" | custom-call | bytes 262144 | tf_op jit(solution)/shard_map/pallas_call | solution.py:89
  6.5 5.6 %collective-permute-start.5 = (bf16[2,2,2,256,128]{4,3,2,1,0:T(8,128)(2,1)S(1)}, bf16[2,2,2,256,128]{4,3,2,1,0:T(8,128)(2,1)}, u32[]{:S(2)}, u32[]{:S(2)}) collective-permute-start(bf16[2,2,2,256,128]{4,3,2,1,0:T(8,128)(2,1)S(1)} %shard_map.47.refs_2_.refs_5_), channel_id=1, source_target_pairs={{0,8},{2,10},{4,12},{6,14},{8,16},{10,18},{12,20},{14,22},{16,24},... | collective-permute-start | bytes 1572872 | tf_op jit(solution)/shard_map/near0/ppermute | solution.py:21
  12.2 1.5 %collective-permute-start.12 = (bf16[512,2048]{1,0:T(8,128)(2,1)}, bf16[512,2048]{1,0:T(8,128)(2,1)}, u32[]{:S(2)}, u32[]{:S(2)}) collective-permute-start(bf16[512,2048]{1,0:T(8,128)(2,1)} %shard_map.46.refs_2_), channel_id=1, source_target_pairs={{0,1},{1,0},{2,3},{3,2},{4,5},{5,4},{6,7},{7,6},{8,9},{9,8},{10,11... | collective-permute-start | bytes 6291464 | tf_op jit(solution)/shard_map/panel/ppermute | solution.py:27
  13.7 1.9 %shard_map.48.refs_5_ = bf16[2,2,2,256,128]{4,3,2,1,0:T(8,128)(2,1)S(1)} custom-call(s32[3]{0:T(128)S(1)} %copy-done.13, bf16[2,2,256,1024]{3,2,1,0:T(8,128)(2,1)S(1)} %copy-done, bf16[2,2,256,1024]{3,2,1,0:T(8,128)(2,1)} %collective-permute-done.1.refs_1_.refs_4_, bf16[2,2,2,256,128]{4,3,2,1,0:T(8,128)(2,1)S(1)} %shard_map.47.refs_2_.refs_5_), custom_call_target="tpu_custom_call" | custom-call | bytes 262144 | tf_op jit(solution)/shard_map/pallas_call | solution.py:89
  15.6 2.8 %collective-permute-start.2 = (bf16[2,2,2,256,128]{4,3,2,1,0:T(8,128)(2,1)S(1)}, bf16[2,2,2,256,128]{4,3,2,1,0:T(8,128)(2,1)S(1)}, u32[]{:S(2)}, u32[]{:S(2)}) collective-permute-start(bf16[2,2,2,256,128]{4,3,2,1,0:T(8,128)(2,1)S(1)} %shard_map.48.refs_5_), channel_id=1, source_target_pairs={{0,8},{2,10},{4,12},{6,14},{8,16},{10,18},{12,20},{14,22},{16,24},... | collective-permute-start | bytes 1572872 | tf_op jit(solution)/shard_map/near1/ppermute | solution.py:21
  18.4 5.2 %collective-permute-done.5.refs_6_ = bf16[2,2,2,256,128]{4,3,2,1,0:T(8,128)(2,1)} collective-permute-done((bf16[2,2,2,256,128]{4,3,2,1,0:T(8,128)(2,1)S(1)}, bf16[2,2,2,256,128]{4,3,2,1,0:T(8,128)(2,1)}, u32[]{:S(2)}, u32[]{:S(2)}) %collective-permute-start.5) | collective-permute-done | bytes 524320 | tf_op jit(solution)/shard_map/near0/ppermute | solution.py:21
  23.6 1.5 %collective-permute-start.7 = (bf16[2,2,2,256,128]{4,3,2,1,0:T(8,128)(2,1)}, bf16[2,2,2,256,128]{4,3,2,1,0:T(8,128)(2,1)S(1)}, u32[]{:S(2)}, u32[]{:S(2)}) collective-permute-start(bf16[2,2,2,256,128]{4,3,2,1,0:T(8,128)(2,1)} %collective-permute-done.5.refs_6_), channel_id=1, source_target_pairs={{0,4},{2,6},{4,0},{6,2},{8,12},{10,14},{12,8},{14,10},{16,20},{18,... | collective-permute-start | bytes 1572872 | tf_op jit(solution)/shard_map/nearx0/ppermute | solution.py:21
  25.1 4.5 %collective-permute-start.6 = (bf16[2,2,2,256,128]{4,3,2,1,0:T(8,128)(2,1)}, bf16[2,2,2,256,128]{4,3,2,1,0:T(8,128)(2,1)S(1)}, u32[]{:S(2)}, u32[]{:S(2)}) collective-permute-start(bf16[2,2,2,256,128]{4,3,2,1,0:T(8,128)(2,1)} %collective-permute-done.5.refs_6_), channel_id=1, source_target_pairs={{0,8},{2,10},{4,12},{6,14},{8,16},{10,18},{12,20},{14,22},{16,24},... | collective-permute-start | bytes 1572872 | tf_op jit(solution)/shard_map/far0/ppermute | solution.py:21
  29.7 5.1 %collective-permute-done.2.refs_6_ = bf16[2,2,2,256,128]{4,3,2,1,0:T(8,128)(2,1)S(1)} collective-permute-done((bf16[2,2,2,256,128]{4,3,2,1,0:T(8,128)(2,1)S(1)}, bf16[2,2,2,256,128]{4,3,2,1,0:T(8,128)(2,1)S(1)}, u32[]{:S(2)}, u32[]{:S(2)}) %collective-permute-start.2) | collective-permute-done | bytes 524320 | tf_op jit(solution)/shard_map/near1/ppermute | solution.py:21
  34.9 1.4 %collective-permute-done.7.refs_8_ = bf16[2,2,2,256,128]{4,3,2,1,0:T(8,128)(2,1)S(1)} collective-permute-done((bf16[2,2,2,256,128]{4,3,2,1,0:T(8,128)(2,1)}, bf16[2,2,2,256,128]{4,3,2,1,0:T(8,128)(2,1)S(1)}, u32[]{:S(2)}, u32[]{:S(2)}) %collective-permute-start.7) | collective-permute-done | bytes 524320 | tf_op jit(solution)/shard_map/nearx0/ppermute | solution.py:21
  36.3 1.5 %collective-permute-start.4 = (bf16[2,2,2,256,128]{4,3,2,1,0:T(8,128)(2,1)S(1)}, bf16[2,2,2,256,128]{4,3,2,1,0:T(8,128)(2,1)S(1)}, u32[]{:S(2)}, u32[]{:S(2)}) collective-permute-start(bf16[2,2,2,256,128]{4,3,2,1,0:T(8,128)(2,1)S(1)} %collective-permute-done.2.refs_6_), channel_id=1, source_target_pairs={{0,4},{2,6},{4,0},{6,2},{8,12},{10,14},{12,8},{14,10},{16,20},{18,... | collective-permute-start | bytes 1572872 | tf_op jit(solution)/shard_map/nearx1/ppermute | solution.py:21
  37.8 0.8 copy-done.7
  38.6 6.8 %collective-permute-done.6.refs_0_ = bf16[2,2,2,256,128]{4,3,2,1,0:T(8,128)(2,1)S(1)} collective-permute-done((bf16[2,2,2,256,128]{4,3,2,1,0:T(8,128)(2,1)}, bf16[2,2,2,256,128]{4,3,2,1,0:T(8,128)(2,1)S(1)}, u32[]{:S(2)}, u32[]{:S(2)}) %collective-permute-start.6) | collective-permute-done | bytes 524320 | tf_op jit(solution)/shard_map/far0/ppermute | solution.py:21
  45.5 1.6 %collective-permute-start.8 = (bf16[2,2,2,256,128]{4,3,2,1,0:T(8,128)(2,1)S(1)}, bf16[2,2,2,256,128]{4,3,2,1,0:T(8,128)(2,1)S(1)}, u32[]{:S(2)}, u32[]{:S(2)}) collective-permute-start(bf16[2,2,2,256,128]{4,3,2,1,0:T(8,128)(2,1)S(1)} %broadcast_select_fusion.1), channel_id=1, source_target_pairs={{0,4},{2,6},{4,0},{6,2},{8,12},{10,14},{12,8},{14,10},{16,20},{18,... | collective-permute-start | bytes 1572872 | tf_op jit(solution)/shard_map/extra0/ppermute | solution.py:21
  47.1 4.3 %collective-permute-start.3 = (bf16[2,2,2,256,128]{4,3,2,1,0:T(8,128)(2,1)S(1)}, bf16[2,2,2,256,128]{4,3,2,1,0:T(8,128)(2,1)S(1)}, u32[]{:S(2)}, u32[]{:S(2)}) collective-permute-start(bf16[2,2,2,256,128]{4,3,2,1,0:T(8,128)(2,1)S(1)} %collective-permute-done.2.refs_6_), channel_id=1, source_target_pairs={{0,8},{2,10},{4,12},{6,14},{8,16},{10,18},{12,20},{14,22},{16,24},... | collective-permute-start | bytes 1572872 | tf_op jit(solution)/shard_map/far1/ppermute | solution.py:21
  51.4 0.8 copy-done.11
  52.2 0.1 fusion.3
  52.4 8.1 %collective-permute-done.8.refs_9_ = bf16[2,2,2,256,128]{4,3,2,1,0:T(8,128)(2,1)S(1)} collective-permute-done((bf16[2,2,2,256,128]{4,3,2,1,0:T(8,128)(2,1)S(1)}, bf16[2,2,2,256,128]{4,3,2,1,0:T(8,128)(2,1)S(1)}, u32[]{:S(2)}, u32[]{:S(2)}) %collective-permute-start.8) | collective-permute-done | bytes 524320 | tf_op jit(solution)/shard_map/extra0/ppermute | solution.py:21
  60.4 0.8 copy-done.9
  61.2 0.6 collective-permute-done.3.refs_0_
  61.9 0.9 broadcast_select_fusion
  62.7 0.8 copy-done.1
  63.6 0.8 collective-permute-start.9
  64.6 0.1 copy.18
  64.9 0.1 copy.16
  65.0 0.1 broadcast_in_dim.16
  65.1 0.2 stack_reshape.6
  65.3 0.1 broadcast_in_dim.17
  65.4 0.2 stack_reshape.7
  65.7 1.0 copy-done.8
  66.7 1.0 copy-done.10
  67.8 20.6 %shard_map.51 = (bf16[2,256,256]{2,1,0:T(8,128)(2,1)S(1)}, bf16[2,256,256]{2,1,0:T(8,128)(2,1)S(1)}, f32[8,128]{1,0:T(8,128)S(1)}) custom-call(s32[3]{0:T(128)S(1)} %copy-done.13, bf16[2,256,1024]{2,1,0:T(8,128)(2,1)} %refs_1_.3, bf16[2,2,256,1024]{3,2,1,0:T(8,128)(2,1)S(1)} %copy-done, bf16[2,256,1024]{2,1,0:T(8,128)(2,1)} %collective-permute-done.refs_3_, ...), custom_call_target="tpu_custom_call" | custom-call | flops 41943040 | bytes 131072 | tf_op jit(solution)/shard_map/pallas_call | solution.py:224
  88.4 0.7 slice_bitcast_fusion.refs_1_
  89.1 1.6 %collective-permute-start.17 = (bf16[2,256,256]{2,1,0:T(8,128)(2,1)S(1)}, bf16[2,256,256]{2,1,0:T(8,128)(2,1)S(1)}, u32[]{:S(2)}, u32[]{:S(2)}) collective-permute-start(bf16[2,256,256]{2,1,0:T(8,128)(2,1)S(1)} %get-tuple-element.13.refs_1_), channel_id=1, source_target_pairs={{0,1},{1,0},{2,3},{3,2},{4,5},{5,4},{6,7},{7,6},{8,9},{9,8},{10,11... | collective-permute-start | bytes 786440 | tf_op jit(solution)/shard_map/same0/ppermute | solution.py:27
  90.7 0.3 collective-permute-start.18
  91.0 0.4 collective-permute-start.16
  91.3 21.1 %shard_map.52 = (bf16[2,256,256]{2,1,0:T(8,128)(2,1)S(1)}, bf16[2,256,256]{2,1,0:T(8,128)(2,1)S(1)}, f32[8,128]{1,0:T(8,128)}) custom-call(s32[3]{0:T(128)S(1)} %copy-done.13, bf16[2,256,1024]{2,1,0:T(8,128)(2,1)} %refs_1_.3, bf16[2,2,256,1024]{3,2,1,0:T(8,128)(2,1)S(1)} %copy-done, bf16[2,256,1024]{2,1,0:T(8,128)(2,1)} %collective-permute-done.refs_3_, ...), custom_call_target="tpu_custom_call" | custom-call | flops 41943040 | bytes 131072 | tf_op jit(solution)/shard_map/pallas_call | solution.py:224
  112.4 1.3 collective-permute-start.14
  113.7 0.4 collective-permute-start.13
  114.0 0.5 collective-permute-start.11
  114.6 5.5 %shard_map.54.refs_5_ = f32[2,256,2048]{2,1,0:T(8,128)S(1)} custom-call(s32[3]{0:T(128)S(1)} %copy-done.13, bf16[2,256,256]{2,1,0:T(8,128)(2,1)S(1)} %get-tuple-element.13.refs_1_, bf16[2,256,256]{2,1,0:T(8,128)(2,1)S(1)} %get-tuple-element.11.refs_2_, bf16[2,256,256]{2,1,0:T(8,128)(2,1)S(1)} %collective-permute-done.16.refs_3_, ...), custom_call_target="tpu_custom_call" | custom-call | flops 335544320 | bytes 655360 | tf_op jit(solution)/shard_map/pallas_call | solution.py:287
  120.1 0.6 collective-permute-done.14.refs_2_
  120.7 2.8 %shard_map.55.refs_3_ = f32[2,256,2048]{2,1,0:T(8,128)S(1)} custom-call(s32[3]{0:T(128)S(1)} %copy-done.13, bf16[2,256,256]{2,1,0:T(8,128)(2,1)S(1)} %collective-permute-done.13.refs_1_, bf16[2,256,256]{2,1,0:T(8,128)(2,1)S(1)} %collective-permute-done.14.refs_2_, bf16[1024,4096]{1,0:T(8,128)(2,1)S(1)} %bitcast.18, ...), custom_call_target="tpu_custom_call" | custom-call | flops 134217728 | bytes 262144 | tf_op jit(solution)/shard_map/pallas_call | solution.py:287
  123.4 3.2 %collective-permute-done.11.refs_1_ = bf16[2,256,256]{2,1,0:T(8,128)(2,1)S(1)} collective-permute-done((bf16[2,256,256]{2,1,0:T(8,128)(2,1)S(1)}, bf16[2,256,256]{2,1,0:T(8,128)(2,1)S(1)}, u32[]{:S(2)}, u32[]{:S(2)}) %collective-permute-start.11) | collective-permute-done | bytes 262176 | tf_op jit(solution)/shard_map/same1/ppermute | solution.py:27
  126.6 3.5 %shard_map.56 = bf16[2,256,2048]{2,1,0:T(8,128)(2,1)} custom-call(s32[3]{0:T(128)S(1)} %copy-done.13, bf16[2,256,256]{2,1,0:T(8,128)(2,1)S(1)} %collective-permute-done.11.refs_1_, bf16[512,2048]{1,0:T(8,128)(2,1)} %shard_map.53.refs_9_.refs_2_, f32[2,256,2048]{2,1,0:T(8,128)S(1)} %shard_map.55.refs_3_), custom_call_target="tpu_custom_call" | custom-call | flops 67108864 | bytes 131072 | tf_op jit(solution)/shard_map/pallas_call | solution.py:287
  (62 shorter events, 0.6 us)
Async XLA Ops:
  0.0 4.6 %collective-permute-start.1 = (bf16[2,2,256,1024]{3,2,1,0:T(8,128)(2,1)}, bf16[2,2,256,1024]{3,2,1,0:T(8,128)(2,1)}, u32[]{:S(2)}, u32[]{:S(2)}) collective-permute-start(bf16[2,2,256,1024]{3,2,1,0:T(8,128)(2,1)} %refs_2_.3), channel_id=1, source_target_pairs={{0,2},{2,0},{4,6},{6,4},{8,10},{10,8},{12,14},{14,12},{16,18},{18,... | collective-permute-start | bytes 6291464 | tf_op jit(solution)/shard_map/pair_kv/ppermute | solution.py:21
  1.1 3.5 %copy-start = (bf16[2,2,256,1024]{3,2,1,0:T(8,128)(2,1)S(1)}, bf16[2,2,256,1024]{3,2,1,0:T(8,128)(2,1)}, u32[]{:S(2)}) copy-start(bf16[2,2,256,1024]{3,2,1,0:T(8,128)(2,1)} %refs_2_.3) | copy-start | bytes 6291460
  1.1 3.5 %copy-start.13 = (s32[3]{0:T(128)S(1)}, s32[3]{0:T(128)}, u32[]{:S(2)}) copy-start(s32[3]{0:T(128)} %pad_add_fusion.2.info.refs_0_) | copy-start | bytes 40
  4.6 9.1 %copy-start.14 = (s32[4,32]{1,0:T(4,128)S(1)}, s32[4,32]{1,0:T(4,128)}, u32[]{:S(2)}) copy-start(s32[4,32]{1,0:T(4,128)} %param.6) | copy-start | bytes 1540
  6.5 17.1 %collective-permute-start.5 = (bf16[2,2,2,256,128]{4,3,2,1,0:T(8,128)(2,1)S(1)}, bf16[2,2,2,256,128]{4,3,2,1,0:T(8,128)(2,1)}, u32[]{:S(2)}, u32[]{:S(2)}) collective-permute-start(bf16[2,2,2,256,128]{4,3,2,1,0:T(8,128)(2,1)S(1)} %shard_map.47.refs_2_.refs_5_), channel_id=1, source_target_pairs={{0,8},{2,10},{4,12},{6,14},{8,16},{10,18},{12,20},{14,22},{16,24},... | collective-permute-start | bytes 1572872 | tf_op jit(solution)/shard_map/near0/ppermute | solution.py:21
  12.2 76.9 %collective-permute-start.12 = (bf16[512,2048]{1,0:T(8,128)(2,1)}, bf16[512,2048]{1,0:T(8,128)(2,1)}, u32[]{:S(2)}, u32[]{:S(2)}) collective-permute-start(bf16[512,2048]{1,0:T(8,128)(2,1)} %shard_map.46.refs_2_), channel_id=1, source_target_pairs={{0,1},{1,0},{2,3},{3,2},{4,5},{5,4},{6,7},{7,6},{8,9},{9,8},{10,11... | collective-permute-start | bytes 6291464 | tf_op jit(solution)/shard_map/panel/ppermute | solution.py:27
  13.7 33.4 %collective-permute-start.10 = (s32[4,32]{1,0:T(4,128)S(1)}, s32[4,32]{1,0:T(4,128)S(1)}, u32[]{:S(2)}, u32[]{:S(2)}) collective-permute-start(s32[4,32]{1,0:T(4,128)S(1)} %copy-done.14), channel_id=1, source_target_pairs={{0,2},{2,0},{4,6},{6,4},{8,10},{10,8},{12,14},{14,12},{16,18},{18,... | collective-permute-start | bytes 1544 | tf_op jit(solution)/shard_map/pair_mask/ppermute | solution.py:21
  15.6 47.1 %copy-start.3 = (bf16[2,2,2,256,128]{4,3,2,1,0:T(8,128)(2,1)}, bf16[2,2,2,256,128]{4,3,2,1,0:T(8,128)(2,1)S(1)}, u32[]{:S(2)}) copy-start(bf16[2,2,2,256,128]{4,3,2,1,0:T(8,128)(2,1)S(1)} %shard_map.48.refs_5_) | copy-start | bytes 1572868
  15.6 19.2 %collective-permute-start.2 = (bf16[2,2,2,256,128]{4,3,2,1,0:T(8,128)(2,1)S(1)}, bf16[2,2,2,256,128]{4,3,2,1,0:T(8,128)(2,1)S(1)}, u32[]{:S(2)}, u32[]{:S(2)}) collective-permute-start(bf16[2,2,2,256,128]{4,3,2,1,0:T(8,128)(2,1)S(1)} %shard_map.48.refs_5_), channel_id=1, source_target_pairs={{0,8},{2,10},{4,12},{6,14},{8,16},{10,18},{12,20},{14,22},{16,24},... | collective-permute-start | bytes 1572872 | tf_op jit(solution)/shard_map/near1/ppermute | solution.py:21
  23.6 12.6 %collective-permute-start.7 = (bf16[2,2,2,256,128]{4,3,2,1,0:T(8,128)(2,1)}, bf16[2,2,2,256,128]{4,3,2,1,0:T(8,128)(2,1)S(1)}, u32[]{:S(2)}, u32[]{:S(2)}) collective-permute-start(bf16[2,2,2,256,128]{4,3,2,1,0:T(8,128)(2,1)} %collective-permute-done.5.refs_6_), channel_id=1, source_target_pairs={{0,4},{2,6},{4,0},{6,2},{8,12},{10,14},{12,8},{14,10},{16,20},{18,... | collective-permute-start | bytes 1572872 | tf_op jit(solution)/shard_map/nearx0/ppermute | solution.py:21
  25.1 20.3 %collective-permute-start.6 = (bf16[2,2,2,256,128]{4,3,2,1,0:T(8,128)(2,1)}, bf16[2,2,2,256,128]{4,3,2,1,0:T(8,128)(2,1)S(1)}, u32[]{:S(2)}, u32[]{:S(2)}) collective-permute-start(bf16[2,2,2,256,128]{4,3,2,1,0:T(8,128)(2,1)} %collective-permute-done.5.refs_6_), channel_id=1, source_target_pairs={{0,8},{2,10},{4,12},{6,14},{8,16},{10,18},{12,20},{14,22},{16,24},... | collective-permute-start | bytes 1572872 | tf_op jit(solution)/shard_map/far0/ppermute | solution.py:21
  34.9 30.8 %collective-permute-start = (bf16[2,256,1024]{2,1,0:T(8,128)(2,1)}, bf16[2,256,1024]{2,1,0:T(8,128)(2,1)}, u32[]{:S(2)}, u32[]{:S(2)}) collective-permute-start(bf16[2,256,1024]{2,1,0:T(8,128)(2,1)} %refs_1_.3), channel_id=1, source_target_pairs={{0,2},{2,0},{4,6},{6,4},{8,10},{10,8},{12,14},{14,12},{16,18},{18,... | collective-permute-start | bytes 3145736 | tf_op jit(solution)/shard_map/pair_q/ppermute | solution.py:21
  36.3 16.1 %collective-permute-start.4 = (bf16[2,2,2,256,128]{4,3,2,1,0:T(8,128)(2,1)S(1)}, bf16[2,2,2,256,128]{4,3,2,1,0:T(8,128)(2,1)S(1)}, u32[]{:S(2)}, u32[]{:S(2)}) collective-permute-start(bf16[2,2,2,256,128]{4,3,2,1,0:T(8,128)(2,1)S(1)} %collective-permute-done.2.refs_6_), channel_id=1, source_target_pairs={{0,4},{2,6},{4,0},{6,2},{8,12},{10,14},{12,8},{14,10},{16,20},{18,... | collective-permute-start | bytes 1572872 | tf_op jit(solution)/shard_map/nearx1/ppermute | solution.py:21
  37.8 0.8 copy-start.7
  45.5 14.9 %collective-permute-start.8 = (bf16[2,2,2,256,128]{4,3,2,1,0:T(8,128)(2,1)S(1)}, bf16[2,2,2,256,128]{4,3,2,1,0:T(8,128)(2,1)S(1)}, u32[]{:S(2)}, u32[]{:S(2)}) collective-permute-start(bf16[2,2,2,256,128]{4,3,2,1,0:T(8,128)(2,1)S(1)} %broadcast_select_fusion.1), channel_id=1, source_target_pairs={{0,4},{2,6},{4,0},{6,2},{8,12},{10,14},{12,8},{14,10},{16,20},{18,... | collective-permute-start | bytes 1572872 | tf_op jit(solution)/shard_map/extra0/ppermute | solution.py:21
  47.1 14.8 %collective-permute-start.3 = (bf16[2,2,2,256,128]{4,3,2,1,0:T(8,128)(2,1)S(1)}, bf16[2,2,2,256,128]{4,3,2,1,0:T(8,128)(2,1)S(1)}, u32[]{:S(2)}, u32[]{:S(2)}) collective-permute-start(bf16[2,2,2,256,128]{4,3,2,1,0:T(8,128)(2,1)S(1)} %collective-permute-done.2.refs_6_), channel_id=1, source_target_pairs={{0,8},{2,10},{4,12},{6,14},{8,16},{10,18},{12,20},{14,22},{16,24},... | collective-permute-start | bytes 1572872 | tf_op jit(solution)/shard_map/far1/ppermute | solution.py:21
  51.4 0.8 copy-start.11
  52.3 12.1 %copy-start.5 = (bf16[2,2,2,256,128]{4,3,2,1,0:T(8,128)(2,1)}, bf16[2,2,2,256,128]{4,3,2,1,0:T(8,128)(2,1)S(1)}, u32[]{:S(2)}) copy-start(bf16[2,2,2,256,128]{4,3,2,1,0:T(8,128)(2,1)S(1)} %collective-permute-done.4.refs_8_) | copy-start | bytes 1572868
  60.4 0.8 copy-start.9
  62.7 0.8 copy-start.1
  63.6 24.8 %collective-permute-start.9 = (bf16[2,2,2,256,128]{4,3,2,1,0:T(8,128)(2,1)}, bf16[2,2,2,256,128]{4,3,2,1,0:T(8,128)(2,1)}, u32[]{:S(2)}, u32[]{:S(2)}) collective-permute-start(bf16[2,2,2,256,128]{4,3,2,1,0:T(8,128)(2,1)} %broadcast_select_fusion), channel_id=1, source_target_pairs={{0,4},{2,6},{4,0},{6,2},{8,12},{10,14},{12,8},{14,10},{16,20},{18,... | collective-permute-start | bytes 1572872 | tf_op jit(solution)/shard_map/extra1/ppermute | solution.py:21
  65.6 1.0 copy-start.8
  66.7 1.0 copy-start.10
  67.7 23.6 %copy-start.2 = (bf16[2,2,2,256,128]{4,3,2,1,0:T(8,128)(2,1)S(1)}, bf16[2,2,2,256,128]{4,3,2,1,0:T(8,128)(2,1)}, u32[]{:S(2)}) copy-start(bf16[2,2,2,256,128]{4,3,2,1,0:T(8,128)(2,1)} %copy-done.1) | copy-start | bytes 1572868
  67.7 23.6 %copy-start.4 = (bf16[2,2,2,256,128]{4,3,2,1,0:T(8,128)(2,1)S(1)}, bf16[2,2,2,256,128]{4,3,2,1,0:T(8,128)(2,1)}, u32[]{:S(2)}) copy-start(bf16[2,2,2,256,128]{4,3,2,1,0:T(8,128)(2,1)} %copy-done.3) | copy-start | bytes 1572868
  67.7 23.6 %copy-start.6 = (bf16[2,2,2,256,128]{4,3,2,1,0:T(8,128)(2,1)S(1)}, bf16[2,2,2,256,128]{4,3,2,1,0:T(8,128)(2,1)}, u32[]{:S(2)}) copy-start(bf16[2,2,2,256,128]{4,3,2,1,0:T(8,128)(2,1)} %copy-done.5) | copy-start | bytes 1572868
  67.7 23.6 %copy-start.12 = (bf16[2,2,2,256,128]{4,3,2,1,0:T(8,128)(2,1)S(1)}, bf16[2,2,2,256,128]{4,3,2,1,0:T(8,128)(2,1)}, u32[]{:S(2)}) copy-start(bf16[2,2,2,256,128]{4,3,2,1,0:T(8,128)(2,1)} %copy-done.11) | copy-start | bytes 1572868
  67.7 46.8 %slice-start = ((s8[8388608]{0:T(1024)(128)(4,1)}), s8[4194304]{0:T(1024)(128)(4,1)S(1)}, s32[]{:S(2)}) async-start(s8[8388608]{0:T(1024)(128)(4,1)} %bitcast.17), calls=%async_computation | async-start | bytes 8388608
  89.1 25.5 %slice-start.1 = ((s8[8388608]{0:T(1024)(128)(4,1)}), s8[4194304]{0:T(1024)(128)(4,1)S(1)}, s32[]{:S(2)}) async-start(s8[8388608]{0:T(1024)(128)(4,1)} %bitcast.17), calls=%async_computation.1 | async-start | bytes 8388608
  89.1 25.5 %collective-permute-start.15 = (bf16[512,2048]{1,0:T(8,128)(2,1)}, bf16[512,2048]{1,0:T(8,128)(2,1)S(1)}, u32[]{:S(2)}, u32[]{:S(2)}) collective-permute-start(bf16[512,2048]{1,0:T(8,128)(2,1)} %shard_map.53.refs_9_.refs_2_), channel_id=1, source_target_pairs={{0,2},{2,0},{4,6},{6,4},{8,10},{10,8},{12,14},{14,12},{16,18},{18,... | collective-permute-start | bytes 6291464 | tf_op jit(solution)/shard_map/panel_pair/ppermute | solution.py:21
  89.1 24.6 %collective-permute-start.17 = (bf16[2,256,256]{2,1,0:T(8,128)(2,1)S(1)}, bf16[2,256,256]{2,1,0:T(8,128)(2,1)S(1)}, u32[]{:S(2)}, u32[]{:S(2)}) collective-permute-start(bf16[2,256,256]{2,1,0:T(8,128)(2,1)S(1)} %get-tuple-element.13.refs_1_), channel_id=1, source_target_pairs={{0,1},{1,0},{2,3},{3,2},{4,5},{5,4},{6,7},{7,6},{8,9},{9,8},{10,11... | collective-permute-start | bytes 786440 | tf_op jit(solution)/shard_map/same0/ppermute | solution.py:27
  90.7 23.3 %collective-permute-start.18 = (bf16[2,256,256]{2,1,0:T(8,128)(2,1)S(1)}, bf16[2,256,256]{2,1,0:T(8,128)(2,1)S(1)}, u32[]{:S(2)}, u32[]{:S(2)}) collective-permute-start(bf16[2,256,256]{2,1,0:T(8,128)(2,1)S(1)} %get-tuple-element.14), channel_id=1, source_target_pairs={{0,3},{1,2},{2,1},{3,0},{4,7},{5,6},{6,5},{7,4},{8,11},{9,10},{10,... | collective-permute-start | bytes 786440 | tf_op jit(solution)/shard_map/cross0/ppermute | solution.py:27
  91.0 23.6 %collective-permute-start.16 = (bf16[2,256,256]{2,1,0:T(8,128)(2,1)S(1)}, bf16[2,256,256]{2,1,0:T(8,128)(2,1)S(1)}, u32[]{:S(2)}, u32[]{:S(2)}) collective-permute-start(bf16[2,256,256]{2,1,0:T(8,128)(2,1)S(1)} %get-tuple-element.14), channel_id=1, source_target_pairs={{0,2},{2,0},{4,6},{6,4},{8,10},{10,8},{12,14},{14,12},{16,18},{18,... | collective-permute-start | bytes 786440 | tf_op jit(solution)/shard_map/pair0/ppermute | solution.py:21
  112.4 8.3 %collective-permute-start.14 = (bf16[2,256,256]{2,1,0:T(8,128)(2,1)S(1)}, bf16[2,256,256]{2,1,0:T(8,128)(2,1)S(1)}, u32[]{:S(2)}, u32[]{:S(2)}) collective-permute-start(bf16[2,256,256]{2,1,0:T(8,128)(2,1)S(1)} %get-tuple-element.12), channel_id=1, source_target_pairs={{0,3},{1,2},{2,1},{3,0},{4,7},{5,6},{6,5},{7,4},{8,11},{9,10},{10,... | collective-permute-start | bytes 786440 | tf_op jit(solution)/shard_map/cross1/ppermute | solution.py:27
  113.7 7.0 %collective-permute-start.13 = (bf16[2,256,256]{2,1,0:T(8,128)(2,1)S(1)}, bf16[2,256,256]{2,1,0:T(8,128)(2,1)S(1)}, u32[]{:S(2)}, u32[]{:S(2)}) collective-permute-start(bf16[2,256,256]{2,1,0:T(8,128)(2,1)S(1)} %get-tuple-element.12), channel_id=1, source_target_pairs={{0,2},{2,0},{4,6},{6,4},{8,10},{10,8},{12,14},{14,12},{16,18},{18,... | collective-permute-start | bytes 786440 | tf_op jit(solution)/shard_map/pair1/ppermute | solution.py:21
  114.0 12.6 %collective-permute-start.11 = (bf16[2,256,256]{2,1,0:T(8,128)(2,1)S(1)}, bf16[2,256,256]{2,1,0:T(8,128)(2,1)S(1)}, u32[]{:S(2)}, u32[]{:S(2)}) collective-permute-start(bf16[2,256,256]{2,1,0:T(8,128)(2,1)S(1)} %get-tuple-element.11.refs_2_), channel_id=1, source_target_pairs={{0,1},{1,0},{2,3},{3,2},{4,5},{5,4},{6,7},{7,6},{8,9},{9,8},{10,11... | collective-permute-start | bytes 786440 | tf_op jit(solution)/shard_map/same1/ppermute | solution.py:27
